TPU v7x, 32 devices: a whole 2x2x4 slice. The times are simulated.
32 devices in a mesh: groups: 2 (over x), ctx: 16 (over z, y, core).
Axes of the slice: x: 2, y: 2, z: 4, core: 2. Of those that a mesh axis runs over, the one named last changes fastest.
Arguments:
- hidden: bfloat16 [256, 8192], P('groups', 'ctx'), parts along dimension 0, may hold values from -6 to 6
- attn_gain: bfloat16 [8192], P('ctx'), may hold values from 0.25 to 1.75
- q_weight: bfloat16 [8192, 8192], P(None, 'ctx'), may hold values from -0.0625 to 0.0625
- q_gain: bfloat16 [128], replicated, may hold values from 0.25 to 1.75
- key_cache: bfloat16 [49152, 1024], P(('groups', 'ctx')), parts along dimension 0, may hold values from -64 to 64
- value_cache: bfloat16 [49152, 1024], P(('groups', 'ctx')), parts along dimension 0, may hold values from -6 to 6
- block_limit: int32 [256], P('groups'), parts along dimension 0, may hold values from 0 to 191, as said below
- out_weight: bfloat16 [8192, 8192], P('ctx'), may hold values from -0.09375 to 0.09375
- next_gain: bfloat16 [8192], P('ctx'), may hold values from 0.25 to 1.75
- next_weight: bfloat16 [8192, 8192], P(None, 'ctx'), may hold values from -0.0625 to 0.0625
Outputs:
- new_hidden: bfloat16 [256, 8192], P('groups', 'ctx'), parts along dimension 0
- next_queries: bfloat16 [256, 8192], P('groups', 'ctx'), parts along dimension 0
There are 2 independent parts, one for each index of `groups`. A program takes and returns all parts, laid end to end along the dimension named above; an argument that names none is the same for every part. Nothing has to cross between parts.
Inputs may be any that keep to these rules, and one draw needn't show every extreme that they name: Text token i may attend the visual blocks 0 to block_limit[i], each of 128 visual tokens; some token reaches the last block and some only the first.
All inputs are finite; a program needn't handle non-finite values.
Results may differ from a plain program's by a relative error of at most 0.015.
Values may be sent and summed in bfloat16 or wider, within the bound.
No kernel may reach another device: no remote copies, remote signals or barrier semaphores. Data moves between devices by JAX's collectives and lax.ppermute only.
A program may use at most 64 MiB of HBM per device.

v0:
```python
import jax
import jax.numpy as jnp
from jax import lax
from jax.sharding import PartitionSpec as P

BLK = 128


EPSILON = 1e-05


def shifted(block, axis, distance):
    devices = range(lax.axis_size(axis))
    route = [((i - distance) % len(devices), i) for i in devices]
    return lax.ppermute(block, axis, route)


def normalize_project(share, gain_share, weight):
    whole, gains = (
        lax.all_gather(share, "ctx", axis=1, tiled=True),
        lax.all_gather(gain_share, "ctx", axis=0, tiled=True),
    )
    values = whole.astype(jnp.float32)
    factor = lax.rsqrt(jnp.mean(values * values, axis=1, keepdims=True) + EPSILON)
    normed = (values * factor * gains.astype(jnp.float32)).astype(jnp.bfloat16)
    return jnp.dot(normed, weight, preferred_element_type=jnp.float32)


def masked_scores(query_rows, keys, allowed, queries, heads_block, scale):
    scores = (
        lax.dot_general(
            query_rows, keys, (((1,), (1,)), ((), ())), preferred_element_type=jnp.float32
        )
        * scale
    )
    scores = scores.reshape(queries, heads_block, keys.shape[0])
    scores = jnp.where(allowed[:, None, :], scores, -jnp.inf)
    return scores.reshape(queries * heads_block, keys.shape[0])


def on_device(
    hidden,
    attn_gain,
    q_weight,
    q_gain,
    key_cache,
    value_cache,
    block_limit,
    out_weight,
    next_gain,
    next_weight,
):
    queries = hidden.shape[0]
    head_dim = q_gain.shape[0]
    devices = lax.axis_size("ctx")
    query = normalize_project(hidden, attn_gain, q_weight)
    heads_here = query.shape[1] // head_dim
    heads_total = heads_here * devices
    kv_heads = key_cache.shape[1] // head_dim
    group_size = heads_total // kv_heads
    shaped = query.reshape(queries, heads_here, head_dim)
    head_mean = jnp.mean(shaped * shaped, axis=-1, keepdims=True)
    query_normed = (shaped * lax.rsqrt(head_mean + EPSILON) * q_gain.astype(jnp.float32)).astype(
        jnp.bfloat16
    )
    local_tokens = key_cache.shape[0]
    device = lax.axis_index("ctx")
    blocks_here = (device * local_tokens + jnp.arange(local_tokens, dtype=jnp.int32)) // BLK
    allowed = blocks_here[None, :] <= block_limit[:, None]
    scale = head_dim ** (-0.5)
    count_rows = queries * heads_here

    def visit(step, carry):
        travelling, sums, peak, total = carry
        anchor = (device - step) % devices
        group = anchor * heads_here // group_size
        keys = lax.dynamic_slice_in_dim(key_cache, group * head_dim, head_dim, 1)
        values = lax.dynamic_slice_in_dim(value_cache, group * head_dim, head_dim, 1)
        scores = masked_scores(travelling, keys, allowed, queries, heads_here, scale)
        fresh = jnp.maximum(peak, jnp.max(scores, axis=1))
        expo = jnp.exp(scores - fresh[:, None])
        decay = jnp.exp(peak - fresh)
        total = total * decay + jnp.sum(expo, axis=1)
        sums = sums * decay[:, None] + jnp.dot(
            expo.astype(jnp.bfloat16), values, preferred_element_type=jnp.float32
        )
        travelling = shifted(travelling, "ctx", 1)
        sums, fresh, total = (
            shifted(sums.astype(jnp.bfloat16), "ctx", 1).astype(sums.dtype),
            shifted(fresh.astype(jnp.bfloat16), "ctx", 1).astype(fresh.dtype),
            shifted(total.astype(jnp.bfloat16), "ctx", 1).astype(total.dtype),
        )
        return (travelling, sums, fresh, total)

    start_state = (
        query_normed.reshape(count_rows, head_dim),
        jnp.zeros((count_rows, head_dim), jnp.float32),
        jnp.full((count_rows,), -1e30, jnp.float32),
        jnp.zeros((count_rows,), jnp.float32),
    )
    _, sums, peak, total = lax.fori_loop(0, devices, visit, start_state)
    attended = (sums / total[:, None]).astype(jnp.bfloat16).reshape(queries, heads_here * head_dim)
    mixed = lax.psum_scatter(
        lax.dot_general(
            out_weight, attended, (((0,), (1,)), ((), ())), preferred_element_type=jnp.float32
        ),
        "ctx",
        scatter_dimension=0,
        tiled=True,
    )
    new_hidden = (hidden.astype(jnp.float32) + mixed.T).astype(jnp.bfloat16)
    next_queries = normalize_project(new_hidden, next_gain, next_weight).astype(jnp.bfloat16)
    return (new_hidden, next_queries)


def solution(mesh):
    in_specs = (
        P("groups", "ctx"),
        P("ctx"),
        P(None, "ctx"),
        P(),
        P(("groups", "ctx"), None),
        P(("groups", "ctx"), None),
        P("groups"),
        P("ctx", None),
        P("ctx"),
        P(None, "ctx"),
    )
    out_specs = (P("groups", "ctx"), P("groups", "ctx"))
    return jax.shard_map(
        on_device, mesh=mesh, in_specs=in_specs, out_specs=out_specs, check_vma=False
    )
```

profile of v0, /device:TPU:0, one launch (start us, length us, event | category | flops | bytes accessed | tf_op | source)
XLA Modules:
  0.0 440.6 jit_solution(16993364083367760374)
XLA Ops:
  8.7 23.1 %all-gather = bf16[16,1,512]{2,1,0:T(2,128)(2,1)S(1)} all-gather(bf16[1,1,512]{2,1,0:T(2,128)(2,1)S(1)} %reshape.86), channel_id=1, replica_groups=mesh['groups'=2,'ctx'=16] {'ctx'}, dimensions={0}, use_global_device_ids=true | all-gather | bytes 17408 | tf_op jit(solution)/shard_map/all_gather | solution.py:21
  32.5 21.6 %all-gather.5.cloned.1.call-done = bf16[128,8192]{1,0:T(8,128)(2,1)} async-done(((bf16[128,512]{1,0:T(8,128)(2,1)}), bf16[128,8192]{1,0:T(8,128)(2,1)}) %all-gather.5.cloned.1.call-update) | async-done | bytes 2097168 | tf_op jit(solution)/shard_map/all_gather | solution.py:20
  54.1 2.1 fusion.21
  56.2 5.3 %fusion.44 = (f32[128,512]{1,0:T(8,128)S(1)}, f32[128,512]{1,0:T(8,128)S(1)}) fusion(bf16[8192,512]{1,0:T(8,128)(2,1)} %param.14, bf16[128,8192]{1,0:T(8,128)(2,1)} %all-gather.5.cloned.1.call-done, f32[8192]{0:T(1024)S(1)} %bitcast.19, f32[128]{0:T(128)S(1)} %add_rsqrt_fusion.2), kind=kOutput, calls=%fused_computation.58 | convolution fusion | flops 1078001664 | bytes 11043328 | tf_op jit(solution)/shard_map/dot_general | solution.py:26
  62.1 243.6 %while.22 = (s32[]{:T(128)}, bf16[512,128]{1,0:T(8,128)(2,1)S(1)}, f32[512,128]{1,0:T(8,128)S(1)}, f32[512]{0:T(512)S(1)}, f32[512]{0:T(512)S(1)}, /*index=5*/s3...) while((s32[]{:T(128)}, bf16[512,128]{1,0:T(8,128)(2,1)S(1)}, ...), condition=%wide.region_5.6_spmd.clone, body=%wide.region_2.5_spmd.clone.sunk | while | flops 408687136 | bytes 17614000 | solution.py:101
  63.9 0.9 copy.15
  64.8 1.7 fusion.61
  67.0 1.7 fusion.65
  69.0 1.1 collective-permute-start
  70.3 1.0 collective-permute-start.2
  71.3 6.0 %collective-permute-done.3 = bf16[512]{0:T(512)(128)(2,1)S(1)} collective-permute-done((bf16[512]{0:T(512)(128)(2,1)S(1)}, bf16[512]{0:T(512)(128)(2,1)S(1)}, u32[]{:S(2)}, u32[]{:S(2)}) %collective-permute-start.3) | collective-permute-done | bytes 1056 | tf_op jit(solution)/shard_map/while/body/eval_jaxpr/ppermute | solution.py:15
  80.0 1.7 fusion.61
  82.2 1.7 fusion.65
  84.7 7.8 %collective-permute-done.3 = bf16[512]{0:T(512)(128)(2,1)S(1)} collective-permute-done((bf16[512]{0:T(512)(128)(2,1)S(1)}, bf16[512]{0:T(512)(128)(2,1)S(1)}, u32[]{:S(2)}, u32[]{:S(2)}) %collective-permute-start.3) | collective-permute-done | bytes 1056 | tf_op jit(solution)/shard_map/while/body/eval_jaxpr/ppermute | solution.py:15
  95.3 1.7 fusion.61
  97.5 1.7 fusion.65
  99.4 8.3 %collective-permute-done.3 = bf16[512]{0:T(512)(128)(2,1)S(1)} collective-permute-done((bf16[512]{0:T(512)(128)(2,1)S(1)}, bf16[512]{0:T(512)(128)(2,1)S(1)}, u32[]{:S(2)}, u32[]{:S(2)}) %collective-permute-start.3) | collective-permute-done | bytes 1056 | tf_op jit(solution)/shard_map/while/body/eval_jaxpr/ppermute | solution.py:15
  109.6 0.9 copy.15
  110.5 1.7 fusion.61
  112.7 1.7 fusion.65
  114.6 8.3 %collective-permute-done.3 = bf16[512]{0:T(512)(128)(2,1)S(1)} collective-permute-done((bf16[512]{0:T(512)(128)(2,1)S(1)}, bf16[512]{0:T(512)(128)(2,1)S(1)}, u32[]{:S(2)}, u32[]{:S(2)}) %collective-permute-start.3) | collective-permute-done | bytes 1056 | tf_op jit(solution)/shard_map/while/body/eval_jaxpr/ppermute | solution.py:15
  125.7 1.7 fusion.61
  127.9 1.7 fusion.65
  129.9 8.3 %collective-permute-done.3 = bf16[512]{0:T(512)(128)(2,1)S(1)} collective-permute-done((bf16[512]{0:T(512)(128)(2,1)S(1)}, bf16[512]{0:T(512)(128)(2,1)S(1)}, u32[]{:S(2)}, u32[]{:S(2)}) %collective-permute-start.3) | collective-permute-done | bytes 1056 | tf_op jit(solution)/shard_map/while/body/eval_jaxpr/ppermute | solution.py:15
  140.9 1.7 fusion.61
  143.1 1.7 fusion.65
  145.1 8.3 %collective-permute-done.3 = bf16[512]{0:T(512)(128)(2,1)S(1)} collective-permute-done((bf16[512]{0:T(512)(128)(2,1)S(1)}, bf16[512]{0:T(512)(128)(2,1)S(1)}, u32[]{:S(2)}, u32[]{:S(2)}) %collective-permute-start.3) | collective-permute-done | bytes 1056 | tf_op jit(solution)/shard_map/while/body/eval_jaxpr/ppermute | solution.py:15
  156.2 1.7 fusion.61
  158.4 1.7 fusion.65
  160.3 8.3 %collective-permute-done.3 = bf16[512]{0:T(512)(128)(2,1)S(1)} collective-permute-done((bf16[512]{0:T(512)(128)(2,1)S(1)}, bf16[512]{0:T(512)(128)(2,1)S(1)}, u32[]{:S(2)}, u32[]{:S(2)}) %collective-permute-start.3) | collective-permute-done | bytes 1056 | tf_op jit(solution)/shard_map/while/body/eval_jaxpr/ppermute | solution.py:15
  171.4 1.7 fusion.61
  173.6 1.7 fusion.65
  175.5 8.3 %collective-permute-done.3 = bf16[512]{0:T(512)(128)(2,1)S(1)} collective-permute-done((bf16[512]{0:T(512)(128)(2,1)S(1)}, bf16[512]{0:T(512)(128)(2,1)S(1)}, u32[]{:S(2)}, u32[]{:S(2)}) %collective-permute-start.3) | collective-permute-done | bytes 1056 | tf_op jit(solution)/shard_map/while/body/eval_jaxpr/ppermute | solution.py:15
  186.6 1.7 fusion.61
  188.8 1.7 fusion.65
  190.8 8.3 %collective-permute-done.3 = bf16[512]{0:T(512)(128)(2,1)S(1)} collective-permute-done((bf16[512]{0:T(512)(128)(2,1)S(1)}, bf16[512]{0:T(512)(128)(2,1)S(1)}, u32[]{:S(2)}, u32[]{:S(2)}) %collective-permute-start.3) | collective-permute-done | bytes 1056 | tf_op jit(solution)/shard_map/while/body/eval_jaxpr/ppermute | solution.py:15
  201.8 1.7 fusion.61
  204.0 1.7 fusion.65
  206.0 8.3 %collective-permute-done.3 = bf16[512]{0:T(512)(128)(2,1)S(1)} collective-permute-done((bf16[512]{0:T(512)(128)(2,1)S(1)}, bf16[512]{0:T(512)(128)(2,1)S(1)}, u32[]{:S(2)}, u32[]{:S(2)}) %collective-permute-start.3) | collective-permute-done | bytes 1056 | tf_op jit(solution)/shard_map/while/body/eval_jaxpr/ppermute | solution.py:15
  217.0 1.7 fusion.61
  219.2 1.7 fusion.65
  221.2 8.3 %collective-permute-done.3 = bf16[512]{0:T(512)(128)(2,1)S(1)} collective-permute-done((bf16[512]{0:T(512)(128)(2,1)S(1)}, bf16[512]{0:T(512)(128)(2,1)S(1)}, u32[]{:S(2)}, u32[]{:S(2)}) %collective-permute-start.3) | collective-permute-done | bytes 1056 | tf_op jit(solution)/shard_map/while/body/eval_jaxpr/ppermute | solution.py:15
  232.3 1.7 fusion.61
  234.5 1.7 fusion.65
  236.4 8.3 %collective-permute-done.3 = bf16[512]{0:T(512)(128)(2,1)S(1)} collective-permute-done((bf16[512]{0:T(512)(128)(2,1)S(1)}, bf16[512]{0:T(512)(128)(2,1)S(1)}, u32[]{:S(2)}, u32[]{:S(2)}) %collective-permute-start.3) | collective-permute-done | bytes 1056 | tf_op jit(solution)/shard_map/while/body/eval_jaxpr/ppermute | solution.py:15
  247.5 1.7 fusion.61
  249.7 1.7 fusion.65
  251.6 8.3 %collective-permute-done.3 = bf16[512]{0:T(512)(128)(2,1)S(1)} collective-permute-done((bf16[512]{0:T(512)(128)(2,1)S(1)}, bf16[512]{0:T(512)(128)(2,1)S(1)}, u32[]{:S(2)}, u32[]{:S(2)}) %collective-permute-start.3) | collective-permute-done | bytes 1056 | tf_op jit(solution)/shard_map/while/body/eval_jaxpr/ppermute | solution.py:15
  262.7 1.7 fusion.61
  264.9 1.7 fusion.65
  266.9 8.3 %collective-permute-done.3 = bf16[512]{0:T(512)(128)(2,1)S(1)} collective-permute-done((bf16[512]{0:T(512)(128)(2,1)S(1)}, bf16[512]{0:T(512)(128)(2,1)S(1)}, u32[]{:S(2)}, u32[]{:S(2)}) %collective-permute-start.3) | collective-permute-done | bytes 1056 | tf_op jit(solution)/shard_map/while/body/eval_jaxpr/ppermute | solution.py:15
  277.9 1.7 fusion.61
  280.1 1.7 fusion.65
  282.1 8.3 %collective-permute-done.3 = bf16[512]{0:T(512)(128)(2,1)S(1)} collective-permute-done((bf16[512]{0:T(512)(128)(2,1)S(1)}, bf16[512]{0:T(512)(128)(2,1)S(1)}, u32[]{:S(2)}, u32[]{:S(2)}) %collective-permute-start.3) | collective-permute-done | bytes 1056 | tf_op jit(solution)/shard_map/while/body/eval_jaxpr/ppermute | solution.py:15
  293.2 1.7 fusion.61
  295.4 1.7 fusion.65
  297.3 8.3 %collective-permute-done.3 = bf16[512]{0:T(512)(128)(2,1)S(1)} collective-permute-done((bf16[512]{0:T(512)(128)(2,1)S(1)}, bf16[512]{0:T(512)(128)(2,1)S(1)}, u32[]{:S(2)}, u32[]{:S(2)}) %collective-permute-start.3) | collective-permute-done | bytes 1056 | tf_op jit(solution)/shard_map/while/body/eval_jaxpr/ppermute | solution.py:15
  306.0 6.6 %convolution_bitcast_fusion = f32[8192,128]{0,1:T(8,128)} fusion(bf16[128,512]{1,0:T(8,128)(2,1)S(1)} %reshape.85, bf16[512,8192]{1,0:T(8,128)(2,1)} %param.19), kind=kOutput, calls=%fused_computation.22 | convolution fusion | flops 1073741824 | bytes 12713984 | tf_op jit(solution)/shard_map/dot_general | solution.py:104
  312.6 70.2 %reduce-scatter.2.cloned.1.call-done = f32[512,128]{0,1:T(8,128)} async-done(((f32[8192,128]{0,1:T(8,128)}), f32[512,128]{0,1:T(8,128)}) %reduce-scatter.2.cloned.1.call-update) | async-done | bytes 262160 | tf_op jit(solution)/shard_map/reduce_scatter | solution.py:103
  382.8 1.6 fusion.38
  384.5 19.2 %all-gather.1 = bf16[16,1,512]{2,1,0:T(2,128)(2,1)S(1)} all-gather(bf16[1,1,512]{2,1,0:T(2,128)(2,1)S(1)} %reshape.88), channel_id=1, replica_groups=mesh['groups'=2,'ctx'=16] {'ctx'}, dimensions={0}, use_global_device_ids=true | all-gather | bytes 17408 | tf_op jit(solution)/shard_map/all_gather | solution.py:21
  403.7 22.3 %all-gather.7.cloned.1.call-done = bf16[128,8192]{1,0:T(8,128)(2,1)} async-done(((bf16[128,512]{1,0:T(8,128)(2,1)}), bf16[128,8192]{1,0:T(8,128)(2,1)}) %all-gather.7.cloned.1.call-update) | async-done | bytes 2097168 | tf_op jit(solution)/shard_map/all_gather | solution.py:20
  426.0 2.1 fusion.24
  428.1 6.0 %fusion.35 = bf16[128,512]{1,0:T(8,128)(2,1)} fusion(bf16[8192,512]{1,0:T(8,128)(2,1)} %param.21, bf16[128,8192]{1,0:T(8,128)(2,1)} %all-gather.7.cloned.1.call-done, f32[8192]{0:T(1024)S(1)} %bitcast.20, f32[128]{0:T(128)S(1)} %add_rsqrt_fusion.1), kind=kOutput, calls=%fused_computation.39 | convolution fusion | flops 1078001664 | bytes 10650112 | tf_op jit(solution)/shard_map/dot_general | solution.py:26
  (315 shorter events, 56.0 us)
Async XLA Ops:
  7.2 46.9 %all-gather.5.cloned.1.call-start = ((), (), s32[]{:S(2)}) async-start(), calls=%async_computation.1 | async-start | bytes 2228224 | tf_op jit(solution)/shard_map/all_gather | solution.py:20
  7.9 374.9 %reduce-scatter.2.cloned.1.call-start = ((), (), s32[]{:S(2)}) async-start(), calls=%async_computation.2 | async-start | bytes 4456448 | tf_op jit(solution)/shard_map/reduce_scatter | solution.py:103
  68.7 8.6 %collective-permute-start.1 = (bf16[512,128]{1,0:T(8,128)(2,1)S(1)}, bf16[512,128]{1,0:T(8,128)(2,1)S(1)}, u32[]{:S(2)}, u32[]{:S(2)}) collective-permute-start(bf16[512,128]{1,0:T(8,128)(2,1)S(1)} %fusion.65), channel_id=1, source_target_pairs={{15,0},{0,1},{1,2},{2,3},{3,4},{4,5},{5,6},{6,7},{7,8},{8,9},{9,10... | collective-permute-start | bytes 393224 | tf_op jit(solution)/shard_map/while/body/eval_jaxpr/ppermute | solution.py:15
  83.9 8.6 %collective-permute-start.1 = (bf16[512,128]{1,0:T(8,128)(2,1)S(1)}, bf16[512,128]{1,0:T(8,128)(2,1)S(1)}, u32[]{:S(2)}, u32[]{:S(2)}) collective-permute-start(bf16[512,128]{1,0:T(8,128)(2,1)S(1)} %fusion.65), channel_id=1, source_target_pairs={{15,0},{0,1},{1,2},{2,3},{3,4},{4,5},{5,6},{6,7},{7,8},{8,9},{9,10... | collective-permute-start | bytes 393224 | tf_op jit(solution)/shard_map/while/body/eval_jaxpr/ppermute | solution.py:15
  84.0 8.6 %collective-permute-start = (bf16[512,128]{1,0:T(8,128)(2,1)S(1)}, bf16[512,128]{1,0:T(8,128)(2,1)S(1)}, u32[]{:S(2)}, u32[]{:S(2)}) collective-permute-start(bf16[512,128]{1,0:T(8,128)(2,1)S(1)} %copy.22), channel_id=1, source_target_pairs={{15,0},{0,1},{1,2},{2,3},{3,4},{4,5},{5,6},{6,7},{7,8},{8,9},{9,10... | collective-permute-start | bytes 393224 | tf_op jit(solution)/shard_map/while/body/eval_jaxpr/ppermute | solution.py:15
  84.1 8.5 %collective-permute-start.3 = (bf16[512]{0:T(512)(128)(2,1)S(1)}, bf16[512]{0:T(512)(128)(2,1)S(1)}, u32[]{:S(2)}, u32[]{:S(2)}) collective-permute-start(bf16[512]{0:T(512)(128)(2,1)S(1)} %get-tuple-element.365), channel_id=1, source_target_pairs={{15,0},{0,1},{1,2},{2,3},{3,4},{4,5},{5,6},{6,7},{7,8},{8,9},{9,10... | collective-permute-start | bytes 3080 | tf_op jit(solution)/shard_map/while/body/eval_jaxpr/ppermute | solution.py:15
  84.1 8.4 %collective-permute-start.2 = (bf16[512]{0:T(512)(128)(2,1)S(1)}, bf16[512]{0:T(512)(128)(2,1)S(1)}, u32[]{:S(2)}, u32[]{:S(2)}) collective-permute-start(bf16[512]{0:T(512)(128)(2,1)S(1)} %get-tuple-element.364), channel_id=1, source_target_pairs={{15,0},{0,1},{1,2},{2,3},{3,4},{4,5},{5,6},{6,7},{7,8},{8,9},{9,10... | collective-permute-start | bytes 3080 | tf_op jit(solution)/shard_map/while/body/eval_jaxpr/ppermute | solution.py:15
  99.2 8.6 %collective-permute-start.1 = (bf16[512,128]{1,0:T(8,128)(2,1)S(1)}, bf16[512,128]{1,0:T(8,128)(2,1)S(1)}, u32[]{:S(2)}, u32[]{:S(2)}) collective-permute-start(bf16[512,128]{1,0:T(8,128)(2,1)S(1)} %fusion.65), channel_id=1, source_target_pairs={{15,0},{0,1},{1,2},{2,3},{3,4},{4,5},{5,6},{6,7},{7,8},{8,9},{9,10... | collective-permute-start | bytes 393224 | tf_op jit(solution)/shard_map/while/body/eval_jaxpr/ppermute | solution.py:15
  99.2 8.6 %collective-permute-start = (bf16[512,128]{1,0:T(8,128)(2,1)S(1)}, bf16[512,128]{1,0:T(8,128)(2,1)S(1)}, u32[]{:S(2)}, u32[]{:S(2)}) collective-permute-start(bf16[512,128]{1,0:T(8,128)(2,1)S(1)} %copy.22), channel_id=1, source_target_pairs={{15,0},{0,1},{1,2},{2,3},{3,4},{4,5},{5,6},{6,7},{7,8},{8,9},{9,10... | collective-permute-start | bytes 393224 | tf_op jit(solution)/shard_map/while/body/eval_jaxpr/ppermute | solution.py:15
  99.3 8.5 %collective-permute-start.3 = (bf16[512]{0:T(512)(128)(2,1)S(1)}, bf16[512]{0:T(512)(128)(2,1)S(1)}, u32[]{:S(2)}, u32[]{:S(2)}) collective-permute-start(bf16[512]{0:T(512)(128)(2,1)S(1)} %get-tuple-element.365), channel_id=1, source_target_pairs={{15,0},{0,1},{1,2},{2,3},{3,4},{4,5},{5,6},{6,7},{7,8},{8,9},{9,10... | collective-permute-start | bytes 3080 | tf_op jit(solution)/shard_map/while/body/eval_jaxpr/ppermute | solution.py:15
  99.4 8.4 %collective-permute-start.2 = (bf16[512]{0:T(512)(128)(2,1)S(1)}, bf16[512]{0:T(512)(128)(2,1)S(1)}, u32[]{:S(2)}, u32[]{:S(2)}) collective-permute-start(bf16[512]{0:T(512)(128)(2,1)S(1)} %get-tuple-element.364), channel_id=1, source_target_pairs={{15,0},{0,1},{1,2},{2,3},{3,4},{4,5},{5,6},{6,7},{7,8},{8,9},{9,10... | collective-permute-start | bytes 3080 | tf_op jit(solution)/shard_map/while/body/eval_jaxpr/ppermute | solution.py:15
  114.4 8.6 %collective-permute-start.1 = (bf16[512,128]{1,0:T(8,128)(2,1)S(1)}, bf16[512,128]{1,0:T(8,128)(2,1)S(1)}, u32[]{:S(2)}, u32[]{:S(2)}) collective-permute-start(bf16[512,128]{1,0:T(8,128)(2,1)S(1)} %fusion.65), channel_id=1, source_target_pairs={{15,0},{0,1},{1,2},{2,3},{3,4},{4,5},{5,6},{6,7},{7,8},{8,9},{9,10... | collective-permute-start | bytes 393224 | tf_op jit(solution)/shard_map/while/body/eval_jaxpr/ppermute | solution.py:15
  114.4 8.6 %collective-permute-start = (bf16[512,128]{1,0:T(8,128)(2,1)S(1)}, bf16[512,128]{1,0:T(8,128)(2,1)S(1)}, u32[]{:S(2)}, u32[]{:S(2)}) collective-permute-start(bf16[512,128]{1,0:T(8,128)(2,1)S(1)} %copy.22), channel_id=1, source_target_pairs={{15,0},{0,1},{1,2},{2,3},{3,4},{4,5},{5,6},{6,7},{7,8},{8,9},{9,10... | collective-permute-start | bytes 393224 | tf_op jit(solution)/shard_map/while/body/eval_jaxpr/ppermute | solution.py:15
  114.5 8.5 %collective-permute-start.3 = (bf16[512]{0:T(512)(128)(2,1)S(1)}, bf16[512]{0:T(512)(128)(2,1)S(1)}, u32[]{:S(2)}, u32[]{:S(2)}) collective-permute-start(bf16[512]{0:T(512)(128)(2,1)S(1)} %get-tuple-element.365), channel_id=1, source_target_pairs={{15,0},{0,1},{1,2},{2,3},{3,4},{4,5},{5,6},{6,7},{7,8},{8,9},{9,10... | collective-permute-start | bytes 3080 | tf_op jit(solution)/shard_map/while/body/eval_jaxpr/ppermute | solution.py:15
  114.6 8.4 %collective-permute-start.2 = (bf16[512]{0:T(512)(128)(2,1)S(1)}, bf16[512]{0:T(512)(128)(2,1)S(1)}, u32[]{:S(2)}, u32[]{:S(2)}) collective-permute-start(bf16[512]{0:T(512)(128)(2,1)S(1)} %get-tuple-element.364), channel_id=1, source_target_pairs={{15,0},{0,1},{1,2},{2,3},{3,4},{4,5},{5,6},{6,7},{7,8},{8,9},{9,10... | collective-permute-start | bytes 3080 | tf_op jit(solution)/shard_map/while/body/eval_jaxpr/ppermute | solution.py:15
  129.6 8.6 %collective-permute-start.1 = (bf16[512,128]{1,0:T(8,128)(2,1)S(1)}, bf16[512,128]{1,0:T(8,128)(2,1)S(1)}, u32[]{:S(2)}, u32[]{:S(2)}) collective-permute-start(bf16[512,128]{1,0:T(8,128)(2,1)S(1)} %fusion.65), channel_id=1, source_target_pairs={{15,0},{0,1},{1,2},{2,3},{3,4},{4,5},{5,6},{6,7},{7,8},{8,9},{9,10... | collective-permute-start | bytes 393224 | tf_op jit(solution)/shard_map/while/body/eval_jaxpr/ppermute | solution.py:15
  129.7 8.6 %collective-permute-start = (bf16[512,128]{1,0:T(8,128)(2,1)S(1)}, bf16[512,128]{1,0:T(8,128)(2,1)S(1)}, u32[]{:S(2)}, u32[]{:S(2)}) collective-permute-start(bf16[512,128]{1,0:T(8,128)(2,1)S(1)} %copy.22), channel_id=1, source_target_pairs={{15,0},{0,1},{1,2},{2,3},{3,4},{4,5},{5,6},{6,7},{7,8},{8,9},{9,10... | collective-permute-start | bytes 393224 | tf_op jit(solution)/shard_map/while/body/eval_jaxpr/ppermute | solution.py:15
  129.7 8.5 %collective-permute-start.3 = (bf16[512]{0:T(512)(128)(2,1)S(1)}, bf16[512]{0:T(512)(128)(2,1)S(1)}, u32[]{:S(2)}, u32[]{:S(2)}) collective-permute-start(bf16[512]{0:T(512)(128)(2,1)S(1)} %get-tuple-element.365), channel_id=1, source_target_pairs={{15,0},{0,1},{1,2},{2,3},{3,4},{4,5},{5,6},{6,7},{7,8},{8,9},{9,10... | collective-permute-start | bytes 3080 | tf_op jit(solution)/shard_map/while/body/eval_jaxpr/ppermute | solution.py:15
  129.8 8.4 %collective-permute-start.2 = (bf16[512]{0:T(512)(128)(2,1)S(1)}, bf16[512]{0:T(512)(128)(2,1)S(1)}, u32[]{:S(2)}, u32[]{:S(2)}) collective-permute-start(bf16[512]{0:T(512)(128)(2,1)S(1)} %get-tuple-element.364), channel_id=1, source_target_pairs={{15,0},{0,1},{1,2},{2,3},{3,4},{4,5},{5,6},{6,7},{7,8},{8,9},{9,10... | collective-permute-start | bytes 3080 | tf_op jit(solution)/shard_map/while/body/eval_jaxpr/ppermute | solution.py:15
  144.8 8.6 %collective-permute-start.1 = (bf16[512,128]{1,0:T(8,128)(2,1)S(1)}, bf16[512,128]{1,0:T(8,128)(2,1)S(1)}, u32[]{:S(2)}, u32[]{:S(2)}) collective-permute-start(bf16[512,128]{1,0:T(8,128)(2,1)S(1)} %fusion.65), channel_id=1, source_target_pairs={{15,0},{0,1},{1,2},{2,3},{3,4},{4,5},{5,6},{6,7},{7,8},{8,9},{9,10... | collective-permute-start | bytes 393224 | tf_op jit(solution)/shard_map/while/body/eval_jaxpr/ppermute | solution.py:15
  144.9 8.6 %collective-permute-start = (bf16[512,128]{1,0:T(8,128)(2,1)S(1)}, bf16[512,128]{1,0:T(8,128)(2,1)S(1)}, u32[]{:S(2)}, u32[]{:S(2)}) collective-permute-start(bf16[512,128]{1,0:T(8,128)(2,1)S(1)} %copy.22), channel_id=1, source_target_pairs={{15,0},{0,1},{1,2},{2,3},{3,4},{4,5},{5,6},{6,7},{7,8},{8,9},{9,10... | collective-permute-start | bytes 393224 | tf_op jit(solution)/shard_map/while/body/eval_jaxpr/ppermute | solution.py:15
  145.0 8.5 %collective-permute-start.3 = (bf16[512]{0:T(512)(128)(2,1)S(1)}, bf16[512]{0:T(512)(128)(2,1)S(1)}, u32[]{:S(2)}, u32[]{:S(2)}) collective-permute-start(bf16[512]{0:T(512)(128)(2,1)S(1)} %get-tuple-element.365), channel_id=1, source_target_pairs={{15,0},{0,1},{1,2},{2,3},{3,4},{4,5},{5,6},{6,7},{7,8},{8,9},{9,10... | collective-permute-start | bytes 3080 | tf_op jit(solution)/shard_map/while/body/eval_jaxpr/ppermute | solution.py:15
  145.0 8.4 %collective-permute-start.2 = (bf16[512]{0:T(512)(128)(2,1)S(1)}, bf16[512]{0:T(512)(128)(2,1)S(1)}, u32[]{:S(2)}, u32[]{:S(2)}) collective-permute-start(bf16[512]{0:T(512)(128)(2,1)S(1)} %get-tuple-element.364), channel_id=1, source_target_pairs={{15,0},{0,1},{1,2},{2,3},{3,4},{4,5},{5,6},{6,7},{7,8},{8,9},{9,10... | collective-permute-start | bytes 3080 | tf_op jit(solution)/shard_map/while/body/eval_jaxpr/ppermute | solution.py:15
  160.0 8.6 %collective-permute-start.1 = (bf16[512,128]{1,0:T(8,128)(2,1)S(1)}, bf16[512,128]{1,0:T(8,128)(2,1)S(1)}, u32[]{:S(2)}, u32[]{:S(2)}) collective-permute-start(bf16[512,128]{1,0:T(8,128)(2,1)S(1)} %fusion.65), channel_id=1, source_target_pairs={{15,0},{0,1},{1,2},{2,3},{3,4},{4,5},{5,6},{6,7},{7,8},{8,9},{9,10... | collective-permute-start | bytes 393224 | tf_op jit(solution)/shard_map/while/body/eval_jaxpr/ppermute | solution.py:15
  160.1 8.6 %collective-permute-start = (bf16[512,128]{1,0:T(8,128)(2,1)S(1)}, bf16[512,128]{1,0:T(8,128)(2,1)S(1)}, u32[]{:S(2)}, u32[]{:S(2)}) collective-permute-start(bf16[512,128]{1,0:T(8,128)(2,1)S(1)} %copy.22), channel_id=1, source_target_pairs={{15,0},{0,1},{1,2},{2,3},{3,4},{4,5},{5,6},{6,7},{7,8},{8,9},{9,10... | collective-permute-start | bytes 393224 | tf_op jit(solution)/shard_map/while/body/eval_jaxpr/ppermute | solution.py:15
  160.2 8.5 %collective-permute-start.3 = (bf16[512]{0:T(512)(128)(2,1)S(1)}, bf16[512]{0:T(512)(128)(2,1)S(1)}, u32[]{:S(2)}, u32[]{:S(2)}) collective-permute-start(bf16[512]{0:T(512)(128)(2,1)S(1)} %get-tuple-element.365), channel_id=1, source_target_pairs={{15,0},{0,1},{1,2},{2,3},{3,4},{4,5},{5,6},{6,7},{7,8},{8,9},{9,10... | collective-permute-start | bytes 3080 | tf_op jit(solution)/shard_map/while/body/eval_jaxpr/ppermute | solution.py:15
  160.2 8.4 %collective-permute-start.2 = (bf16[512]{0:T(512)(128)(2,1)S(1)}, bf16[512]{0:T(512)(128)(2,1)S(1)}, u32[]{:S(2)}, u32[]{:S(2)}) collective-permute-start(bf16[512]{0:T(512)(128)(2,1)S(1)} %get-tuple-element.364), channel_id=1, source_target_pairs={{15,0},{0,1},{1,2},{2,3},{3,4},{4,5},{5,6},{6,7},{7,8},{8,9},{9,10... | collective-permute-start | bytes 3080 | tf_op jit(solution)/shard_map/while/body/eval_jaxpr/ppermute | solution.py:15
  175.3 8.6 %collective-permute-start.1 = (bf16[512,128]{1,0:T(8,128)(2,1)S(1)}, bf16[512,128]{1,0:T(8,128)(2,1)S(1)}, u32[]{:S(2)}, u32[]{:S(2)}) collective-permute-start(bf16[512,128]{1,0:T(8,128)(2,1)S(1)} %fusion.65), channel_id=1, source_target_pairs={{15,0},{0,1},{1,2},{2,3},{3,4},{4,5},{5,6},{6,7},{7,8},{8,9},{9,10... | collective-permute-start | bytes 393224 | tf_op jit(solution)/shard_map/while/body/eval_jaxpr/ppermute | solution.py:15
  175.3 8.6 %collective-permute-start = (bf16[512,128]{1,0:T(8,128)(2,1)S(1)}, bf16[512,128]{1,0:T(8,128)(2,1)S(1)}, u32[]{:S(2)}, u32[]{:S(2)}) collective-permute-start(bf16[512,128]{1,0:T(8,128)(2,1)S(1)} %copy.22), channel_id=1, source_target_pairs={{15,0},{0,1},{1,2},{2,3},{3,4},{4,5},{5,6},{6,7},{7,8},{8,9},{9,10... | collective-permute-start | bytes 393224 | tf_op jit(solution)/shard_map/while/body/eval_jaxpr/ppermute | solution.py:15
  175.4 8.5 %collective-permute-start.3 = (bf16[512]{0:T(512)(128)(2,1)S(1)}, bf16[512]{0:T(512)(128)(2,1)S(1)}, u32[]{:S(2)}, u32[]{:S(2)}) collective-permute-start(bf16[512]{0:T(512)(128)(2,1)S(1)} %get-tuple-element.365), channel_id=1, source_target_pairs={{15,0},{0,1},{1,2},{2,3},{3,4},{4,5},{5,6},{6,7},{7,8},{8,9},{9,10... | collective-permute-start | bytes 3080 | tf_op jit(solution)/shard_map/while/body/eval_jaxpr/ppermute | solution.py:15
  175.5 8.4 %collective-permute-start.2 = (bf16[512]{0:T(512)(128)(2,1)S(1)}, bf16[512]{0:T(512)(128)(2,1)S(1)}, u32[]{:S(2)}, u32[]{:S(2)}) collective-permute-start(bf16[512]{0:T(512)(128)(2,1)S(1)} %get-tuple-element.364), channel_id=1, source_target_pairs={{15,0},{0,1},{1,2},{2,3},{3,4},{4,5},{5,6},{6,7},{7,8},{8,9},{9,10... | collective-permute-start | bytes 3080 | tf_op jit(solution)/shard_map/while/body/eval_jaxpr/ppermute | solution.py:15
  190.5 8.6 %collective-permute-start.1 = (bf16[512,128]{1,0:T(8,128)(2,1)S(1)}, bf16[512,128]{1,0:T(8,128)(2,1)S(1)}, u32[]{:S(2)}, u32[]{:S(2)}) collective-permute-start(bf16[512,128]{1,0:T(8,128)(2,1)S(1)} %fusion.65), channel_id=1, source_target_pairs={{15,0},{0,1},{1,2},{2,3},{3,4},{4,5},{5,6},{6,7},{7,8},{8,9},{9,10... | collective-permute-start | bytes 393224 | tf_op jit(solution)/shard_map/while/body/eval_jaxpr/ppermute | solution.py:15
  190.6 8.6 %collective-permute-start = (bf16[512,128]{1,0:T(8,128)(2,1)S(1)}, bf16[512,128]{1,0:T(8,128)(2,1)S(1)}, u32[]{:S(2)}, u32[]{:S(2)}) collective-permute-start(bf16[512,128]{1,0:T(8,128)(2,1)S(1)} %copy.22), channel_id=1, source_target_pairs={{15,0},{0,1},{1,2},{2,3},{3,4},{4,5},{5,6},{6,7},{7,8},{8,9},{9,10... | collective-permute-start | bytes 393224 | tf_op jit(solution)/shard_map/while/body/eval_jaxpr/ppermute | solution.py:15
  190.6 8.5 %collective-permute-start.3 = (bf16[512]{0:T(512)(128)(2,1)S(1)}, bf16[512]{0:T(512)(128)(2,1)S(1)}, u32[]{:S(2)}, u32[]{:S(2)}) collective-permute-start(bf16[512]{0:T(512)(128)(2,1)S(1)} %get-tuple-element.365), channel_id=1, source_target_pairs={{15,0},{0,1},{1,2},{2,3},{3,4},{4,5},{5,6},{6,7},{7,8},{8,9},{9,10... | collective-permute-start | bytes 3080 | tf_op jit(solution)/shard_map/while/body/eval_jaxpr/ppermute | solution.py:15
  190.7 8.4 %collective-permute-start.2 = (bf16[512]{0:T(512)(128)(2,1)S(1)}, bf16[512]{0:T(512)(128)(2,1)S(1)}, u32[]{:S(2)}, u32[]{:S(2)}) collective-permute-start(bf16[512]{0:T(512)(128)(2,1)S(1)} %get-tuple-element.364), channel_id=1, source_target_pairs={{15,0},{0,1},{1,2},{2,3},{3,4},{4,5},{5,6},{6,7},{7,8},{8,9},{9,10... | collective-permute-start | bytes 3080 | tf_op jit(solution)/shard_map/while/body/eval_jaxpr/ppermute | solution.py:15
  205.7 8.6 %collective-permute-start.1 = (bf16[512,128]{1,0:T(8,128)(2,1)S(1)}, bf16[512,128]{1,0:T(8,128)(2,1)S(1)}, u32[]{:S(2)}, u32[]{:S(2)}) collective-permute-start(bf16[512,128]{1,0:T(8,128)(2,1)S(1)} %fusion.65), channel_id=1, source_target_pairs={{15,0},{0,1},{1,2},{2,3},{3,4},{4,5},{5,6},{6,7},{7,8},{8,9},{9,10... | collective-permute-start | bytes 393224 | tf_op jit(solution)/shard_map/while/body/eval_jaxpr/ppermute | solution.py:15
  205.8 8.6 %collective-permute-start = (bf16[512,128]{1,0:T(8,128)(2,1)S(1)}, bf16[512,128]{1,0:T(8,128)(2,1)S(1)}, u32[]{:S(2)}, u32[]{:S(2)}) collective-permute-start(bf16[512,128]{1,0:T(8,128)(2,1)S(1)} %copy.22), channel_id=1, source_target_pairs={{15,0},{0,1},{1,2},{2,3},{3,4},{4,5},{5,6},{6,7},{7,8},{8,9},{9,10... | collective-permute-start | bytes 393224 | tf_op jit(solution)/shard_map/while/body/eval_jaxpr/ppermute | solution.py:15
  205.8 8.5 %collective-permute-start.3 = (bf16[512]{0:T(512)(128)(2,1)S(1)}, bf16[512]{0:T(512)(128)(2,1)S(1)}, u32[]{:S(2)}, u32[]{:S(2)}) collective-permute-start(bf16[512]{0:T(512)(128)(2,1)S(1)} %get-tuple-element.365), channel_id=1, source_target_pairs={{15,0},{0,1},{1,2},{2,3},{3,4},{4,5},{5,6},{6,7},{7,8},{8,9},{9,10... | collective-permute-start | bytes 3080 | tf_op jit(solution)/shard_map/while/body/eval_jaxpr/ppermute | solution.py:15
  205.9 8.4 %collective-permute-start.2 = (bf16[512]{0:T(512)(128)(2,1)S(1)}, bf16[512]{0:T(512)(128)(2,1)S(1)}, u32[]{:S(2)}, u32[]{:S(2)}) collective-permute-start(bf16[512]{0:T(512)(128)(2,1)S(1)} %get-tuple-element.364), channel_id=1, source_target_pairs={{15,0},{0,1},{1,2},{2,3},{3,4},{4,5},{5,6},{6,7},{7,8},{8,9},{9,10... | collective-permute-start | bytes 3080 | tf_op jit(solution)/shard_map/while/body/eval_jaxpr/ppermute | solution.py:15
  220.9 8.6 %collective-permute-start.1 = (bf16[512,128]{1,0:T(8,128)(2,1)S(1)}, bf16[512,128]{1,0:T(8,128)(2,1)S(1)}, u32[]{:S(2)}, u32[]{:S(2)}) collective-permute-start(bf16[512,128]{1,0:T(8,128)(2,1)S(1)} %fusion.65), channel_id=1, source_target_pairs={{15,0},{0,1},{1,2},{2,3},{3,4},{4,5},{5,6},{6,7},{7,8},{8,9},{9,10... | collective-permute-start | bytes 393224 | tf_op jit(solution)/shard_map/while/body/eval_jaxpr/ppermute | solution.py:15
  221.0 8.6 %collective-permute-start = (bf16[512,128]{1,0:T(8,128)(2,1)S(1)}, bf16[512,128]{1,0:T(8,128)(2,1)S(1)}, u32[]{:S(2)}, u32[]{:S(2)}) collective-permute-start(bf16[512,128]{1,0:T(8,128)(2,1)S(1)} %copy.22), channel_id=1, source_target_pairs={{15,0},{0,1},{1,2},{2,3},{3,4},{4,5},{5,6},{6,7},{7,8},{8,9},{9,10... | collective-permute-start | bytes 393224 | tf_op jit(solution)/shard_map/while/body/eval_jaxpr/ppermute | solution.py:15
  221.1 8.5 %collective-permute-start.3 = (bf16[512]{0:T(512)(128)(2,1)S(1)}, bf16[512]{0:T(512)(128)(2,1)S(1)}, u32[]{:S(2)}, u32[]{:S(2)}) collective-permute-start(bf16[512]{0:T(512)(128)(2,1)S(1)} %get-tuple-element.365), channel_id=1, source_target_pairs={{15,0},{0,1},{1,2},{2,3},{3,4},{4,5},{5,6},{6,7},{7,8},{8,9},{9,10... | collective-permute-start | bytes 3080 | tf_op jit(solution)/shard_map/while/body/eval_jaxpr/ppermute | solution.py:15
  221.1 8.4 %collective-permute-start.2 = (bf16[512]{0:T(512)(128)(2,1)S(1)}, bf16[512]{0:T(512)(128)(2,1)S(1)}, u32[]{:S(2)}, u32[]{:S(2)}) collective-permute-start(bf16[512]{0:T(512)(128)(2,1)S(1)} %get-tuple-element.364), channel_id=1, source_target_pairs={{15,0},{0,1},{1,2},{2,3},{3,4},{4,5},{5,6},{6,7},{7,8},{8,9},{9,10... | collective-permute-start | bytes 3080 | tf_op jit(solution)/shard_map/while/body/eval_jaxpr/ppermute | solution.py:15
  236.2 8.6 %collective-permute-start.1 = (bf16[512,128]{1,0:T(8,128)(2,1)S(1)}, bf16[512,128]{1,0:T(8,128)(2,1)S(1)}, u32[]{:S(2)}, u32[]{:S(2)}) collective-permute-start(bf16[512,128]{1,0:T(8,128)(2,1)S(1)} %fusion.65), channel_id=1, source_target_pairs={{15,0},{0,1},{1,2},{2,3},{3,4},{4,5},{5,6},{6,7},{7,8},{8,9},{9,10... | collective-permute-start | bytes 393224 | tf_op jit(solution)/shard_map/while/body/eval_jaxpr/ppermute | solution.py:15
  236.2 8.6 %collective-permute-start = (bf16[512,128]{1,0:T(8,128)(2,1)S(1)}, bf16[512,128]{1,0:T(8,128)(2,1)S(1)}, u32[]{:S(2)}, u32[]{:S(2)}) collective-permute-start(bf16[512,128]{1,0:T(8,128)(2,1)S(1)} %copy.22), channel_id=1, source_target_pairs={{15,0},{0,1},{1,2},{2,3},{3,4},{4,5},{5,6},{6,7},{7,8},{8,9},{9,10... | collective-permute-start | bytes 393224 | tf_op jit(solution)/shard_map/while/body/eval_jaxpr/ppermute | solution.py:15
  236.3 8.5 %collective-permute-start.3 = (bf16[512]{0:T(512)(128)(2,1)S(1)}, bf16[512]{0:T(512)(128)(2,1)S(1)}, u32[]{:S(2)}, u32[]{:S(2)}) collective-permute-start(bf16[512]{0:T(512)(128)(2,1)S(1)} %get-tuple-element.365), channel_id=1, source_target_pairs={{15,0},{0,1},{1,2},{2,3},{3,4},{4,5},{5,6},{6,7},{7,8},{8,9},{9,10... | collective-permute-start | bytes 3080 | tf_op jit(solution)/shard_map/while/body/eval_jaxpr/ppermute | solution.py:15
  236.4 8.4 %collective-permute-start.2 = (bf16[512]{0:T(512)(128)(2,1)S(1)}, bf16[512]{0:T(512)(128)(2,1)S(1)}, u32[]{:S(2)}, u32[]{:S(2)}) collective-permute-start(bf16[512]{0:T(512)(128)(2,1)S(1)} %get-tuple-element.364), channel_id=1, source_target_pairs={{15,0},{0,1},{1,2},{2,3},{3,4},{4,5},{5,6},{6,7},{7,8},{8,9},{9,10... | collective-permute-start | bytes 3080 | tf_op jit(solution)/shard_map/while/body/eval_jaxpr/ppermute | solution.py:15
  251.4 8.6 %collective-permute-start.1 = (bf16[512,128]{1,0:T(8,128)(2,1)S(1)}, bf16[512,128]{1,0:T(8,128)(2,1)S(1)}, u32[]{:S(2)}, u32[]{:S(2)}) collective-permute-start(bf16[512,128]{1,0:T(8,128)(2,1)S(1)} %fusion.65), channel_id=1, source_target_pairs={{15,0},{0,1},{1,2},{2,3},{3,4},{4,5},{5,6},{6,7},{7,8},{8,9},{9,10... | collective-permute-start | bytes 393224 | tf_op jit(solution)/shard_map/while/body/eval_jaxpr/ppermute | solution.py:15
  251.4 8.6 %collective-permute-start = (bf16[512,128]{1,0:T(8,128)(2,1)S(1)}, bf16[512,128]{1,0:T(8,128)(2,1)S(1)}, u32[]{:S(2)}, u32[]{:S(2)}) collective-permute-start(bf16[512,128]{1,0:T(8,128)(2,1)S(1)} %copy.22), channel_id=1, source_target_pairs={{15,0},{0,1},{1,2},{2,3},{3,4},{4,5},{5,6},{6,7},{7,8},{8,9},{9,10... | collective-permute-start | bytes 393224 | tf_op jit(solution)/shard_map/while/body/eval_jaxpr/ppermute | solution.py:15
  251.5 8.5 %collective-permute-start.3 = (bf16[512]{0:T(512)(128)(2,1)S(1)}, bf16[512]{0:T(512)(128)(2,1)S(1)}, u32[]{:S(2)}, u32[]{:S(2)}) collective-permute-start(bf16[512]{0:T(512)(128)(2,1)S(1)} %get-tuple-element.365), channel_id=1, source_target_pairs={{15,0},{0,1},{1,2},{2,3},{3,4},{4,5},{5,6},{6,7},{7,8},{8,9},{9,10... | collective-permute-start | bytes 3080 | tf_op jit(solution)/shard_map/while/body/eval_jaxpr/ppermute | solution.py:15
  251.6 8.4 %collective-permute-start.2 = (bf16[512]{0:T(512)(128)(2,1)S(1)}, bf16[512]{0:T(512)(128)(2,1)S(1)}, u32[]{:S(2)}, u32[]{:S(2)}) collective-permute-start(bf16[512]{0:T(512)(128)(2,1)S(1)} %get-tuple-element.364), channel_id=1, source_target_pairs={{15,0},{0,1},{1,2},{2,3},{3,4},{4,5},{5,6},{6,7},{7,8},{8,9},{9,10... | collective-permute-start | bytes 3080 | tf_op jit(solution)/shard_map/while/body/eval_jaxpr/ppermute | solution.py:15
  266.6 8.6 %collective-permute-start.1 = (bf16[512,128]{1,0:T(8,128)(2,1)S(1)}, bf16[512,128]{1,0:T(8,128)(2,1)S(1)}, u32[]{:S(2)}, u32[]{:S(2)}) collective-permute-start(bf16[512,128]{1,0:T(8,128)(2,1)S(1)} %fusion.65), channel_id=1, source_target_pairs={{15,0},{0,1},{1,2},{2,3},{3,4},{4,5},{5,6},{6,7},{7,8},{8,9},{9,10... | collective-permute-start | bytes 393224 | tf_op jit(solution)/shard_map/while/body/eval_jaxpr/ppermute | solution.py:15
  266.7 8.6 %collective-permute-start = (bf16[512,128]{1,0:T(8,128)(2,1)S(1)}, bf16[512,128]{1,0:T(8,128)(2,1)S(1)}, u32[]{:S(2)}, u32[]{:S(2)}) collective-permute-start(bf16[512,128]{1,0:T(8,128)(2,1)S(1)} %copy.22), channel_id=1, source_target_pairs={{15,0},{0,1},{1,2},{2,3},{3,4},{4,5},{5,6},{6,7},{7,8},{8,9},{9,10... | collective-permute-start | bytes 393224 | tf_op jit(solution)/shard_map/while/body/eval_jaxpr/ppermute | solution.py:15
  266.7 8.5 %collective-permute-start.3 = (bf16[512]{0:T(512)(128)(2,1)S(1)}, bf16[512]{0:T(512)(128)(2,1)S(1)}, u32[]{:S(2)}, u32[]{:S(2)}) collective-permute-start(bf16[512]{0:T(512)(128)(2,1)S(1)} %get-tuple-element.365), channel_id=1, source_target_pairs={{15,0},{0,1},{1,2},{2,3},{3,4},{4,5},{5,6},{6,7},{7,8},{8,9},{9,10... | collective-permute-start | bytes 3080 | tf_op jit(solution)/shard_map/while/body/eval_jaxpr/ppermute | solution.py:15
  266.8 8.4 %collective-permute-start.2 = (bf16[512]{0:T(512)(128)(2,1)S(1)}, bf16[512]{0:T(512)(128)(2,1)S(1)}, u32[]{:S(2)}, u32[]{:S(2)}) collective-permute-start(bf16[512]{0:T(512)(128)(2,1)S(1)} %get-tuple-element.364), channel_id=1, source_target_pairs={{15,0},{0,1},{1,2},{2,3},{3,4},{4,5},{5,6},{6,7},{7,8},{8,9},{9,10... | collective-permute-start | bytes 3080 | tf_op jit(solution)/shard_map/while/body/eval_jaxpr/ppermute | solution.py:15
  281.8 8.6 %collective-permute-start.1 = (bf16[512,128]{1,0:T(8,128)(2,1)S(1)}, bf16[512,128]{1,0:T(8,128)(2,1)S(1)}, u32[]{:S(2)}, u32[]{:S(2)}) collective-permute-start(bf16[512,128]{1,0:T(8,128)(2,1)S(1)} %fusion.65), channel_id=1, source_target_pairs={{15,0},{0,1},{1,2},{2,3},{3,4},{4,5},{5,6},{6,7},{7,8},{8,9},{9,10... | collective-permute-start | bytes 393224 | tf_op jit(solution)/shard_map/while/body/eval_jaxpr/ppermute | solution.py:15
  281.9 8.6 %collective-permute-start = (bf16[512,128]{1,0:T(8,128)(2,1)S(1)}, bf16[512,128]{1,0:T(8,128)(2,1)S(1)}, u32[]{:S(2)}, u32[]{:S(2)}) collective-permute-start(bf16[512,128]{1,0:T(8,128)(2,1)S(1)} %copy.22), channel_id=1, source_target_pairs={{15,0},{0,1},{1,2},{2,3},{3,4},{4,5},{5,6},{6,7},{7,8},{8,9},{9,10... | collective-permute-start | bytes 393224 | tf_op jit(solution)/shard_map/while/body/eval_jaxpr/ppermute | solution.py:15
  282.0 8.5 %collective-permute-start.3 = (bf16[512]{0:T(512)(128)(2,1)S(1)}, bf16[512]{0:T(512)(128)(2,1)S(1)}, u32[]{:S(2)}, u32[]{:S(2)}) collective-permute-start(bf16[512]{0:T(512)(128)(2,1)S(1)} %get-tuple-element.365), channel_id=1, source_target_pairs={{15,0},{0,1},{1,2},{2,3},{3,4},{4,5},{5,6},{6,7},{7,8},{8,9},{9,10... | collective-permute-start | bytes 3080 | tf_op jit(solution)/shard_map/while/body/eval_jaxpr/ppermute | solution.py:15
  282.0 8.4 %collective-permute-start.2 = (bf16[512]{0:T(512)(128)(2,1)S(1)}, bf16[512]{0:T(512)(128)(2,1)S(1)}, u32[]{:S(2)}, u32[]{:S(2)}) collective-permute-start(bf16[512]{0:T(512)(128)(2,1)S(1)} %get-tuple-element.364), channel_id=1, source_target_pairs={{15,0},{0,1},{1,2},{2,3},{3,4},{4,5},{5,6},{6,7},{7,8},{8,9},{9,10... | collective-permute-start | bytes 3080 | tf_op jit(solution)/shard_map/while/body/eval_jaxpr/ppermute | solution.py:15
  297.0 8.6 %collective-permute-start.1 = (bf16[512,128]{1,0:T(8,128)(2,1)S(1)}, bf16[512,128]{1,0:T(8,128)(2,1)S(1)}, u32[]{:S(2)}, u32[]{:S(2)}) collective-permute-start(bf16[512,128]{1,0:T(8,128)(2,1)S(1)} %fusion.65), channel_id=1, source_target_pairs={{15,0},{0,1},{1,2},{2,3},{3,4},{4,5},{5,6},{6,7},{7,8},{8,9},{9,10... | collective-permute-start | bytes 393224 | tf_op jit(solution)/shard_map/while/body/eval_jaxpr/ppermute | solution.py:15
  297.1 8.6 %collective-permute-start = (bf16[512,128]{1,0:T(8,128)(2,1)S(1)}, bf16[512,128]{1,0:T(8,128)(2,1)S(1)}, u32[]{:S(2)}, u32[]{:S(2)}) collective-permute-start(bf16[512,128]{1,0:T(8,128)(2,1)S(1)} %copy.22), channel_id=1, source_target_pairs={{15,0},{0,1},{1,2},{2,3},{3,4},{4,5},{5,6},{6,7},{7,8},{8,9},{9,10... | collective-permute-start | bytes 393224 | tf_op jit(solution)/shard_map/while/body/eval_jaxpr/ppermute | solution.py:15
  297.2 8.5 %collective-permute-start.3 = (bf16[512]{0:T(512)(128)(2,1)S(1)}, bf16[512]{0:T(512)(128)(2,1)S(1)}, u32[]{:S(2)}, u32[]{:S(2)}) collective-permute-start(bf16[512]{0:T(512)(128)(2,1)S(1)} %get-tuple-element.365), channel_id=1, source_target_pairs={{15,0},{0,1},{1,2},{2,3},{3,4},{4,5},{5,6},{6,7},{7,8},{8,9},{9,10... | collective-permute-start | bytes 3080 | tf_op jit(solution)/shard_map/while/body/eval_jaxpr/ppermute | solution.py:15
  297.2 8.4 %collective-permute-start.2 = (bf16[512]{0:T(512)(128)(2,1)S(1)}, bf16[512]{0:T(512)(128)(2,1)S(1)}, u32[]{:S(2)}, u32[]{:S(2)}) collective-permute-start(bf16[512]{0:T(512)(128)(2,1)S(1)} %get-tuple-element.364), channel_id=1, source_target_pairs={{15,0},{0,1},{1,2},{2,3},{3,4},{4,5},{5,6},{6,7},{7,8},{8,9},{9,10... | collective-permute-start | bytes 3080 | tf_op jit(solution)/shard_map/while/body/eval_jaxpr/ppermute | solution.py:15
  312.6 113.4 %all-gather.7.cloned.1.call-start = ((), (), s32[]{:S(2)}) async-start(), calls=%async_computation.3 | async-start | bytes 2228224 | tf_op jit(solution)/shard_map/all_gather | solution.py:20
  (6 other events, 170.7 us)
Sparse Core Ops, SparseCore 0:
  10.2 43.8 all-gather.4
  312.7 70.0 reduce-scatter.1
  385.8 40.1 all-gather.6
where the time goes:
time: 442 us; the launch traced here: 441 us
  waiting for transfers between devices  245 us (55%)
  matrix products  71.6 us (16%)
  blocking collectives  42.3 us (10%)
  local copies, waits for them, and re-layouts  39.4 us (9%)
  other arithmetic  18.6 us (4%)
  between operations  13.9 us (3%)
  starting transfers between devices  6.7 us (2%)
    ppermute x64, waiting for transfers between devices, shifted(): return lax.ppermute(block, axis, route)  131 us
    reduce_scatter x1, waiting for transfers between devices, on_device(): lax.psum_scatter(lax.dot_general(out_weight, attended, (((0,), (1,)), (()...  70.2 us
    all_gather x2, waiting for transfers between devices, normalize_project(): lax.all_gather(share, 'ctx', axis=1, tiled=True)  43.8 us
    all_gather x2, blocking collectives, normalize_project(): lax.all_gather(gain_share, 'ctx', axis=0, tiled=True)  42.3 us
    broadcast_in_dim x48, local copies, waits for them, and re-layouts, masked_scores(): scores = jnp.where(allowed[:, None, :], scores, -jnp.inf)  38.2 us
    dot_general x16, matrix products, visit(): jnp.dot(expo.astype(jnp.bfloat16), values, preferred_element_type=jnp.flo...  26.9 us
    dot_general x16, matrix products, masked_scores(): lax.dot_general(query_rows, keys, (((1,), (1,)), ((), ())), preferred_ele...  26.8 us
    dot_general x2, matrix products, normalize_project(): return jnp.dot(normed, weight, preferred_element_type=jnp.float32)  11.3 us
  transfers between devices with their start and end apart: 67, of which 19 were waited for; matrix products, arithmetic and copies ran while one was open for 0% of the time, Pallas kernels for 0%

commit v1 on v0

v1 whole, which is shorter than its diff:
```python
import functools
import math

import jax
import jax.numpy as jnp
from jax import lax
from jax.experimental import pallas as pl
from jax.experimental.pallas import tpu as pltpu
from jax.sharding import PartitionSpec as P

BLK = 128
EPSILON = 1e-05
MASKED = -1e30
LANES = 128
TILE = 16
BF16 = jnp.bfloat16
F32 = jnp.float32
VMEM = pl.BlockSpec(memory_space=pltpu.VMEM)
ANYWHERE = pl.BlockSpec(memory_space=pl.ANY)
SCALARS = pl.BlockSpec(memory_space=pltpu.SMEM)


class Ring:
    def __init__(self, devices, columns):
        self.chips = devices // 2
        if columns == 2 and self.chips % 2 == 0:
            self.order = list(range(0, self.chips, 2)) + list(range(1, self.chips, 2))[::-1]
        else:
            self.order = list(range(self.chips))
        self.snake = columns == 2 and self.chips % 2 == 0
        self.device = lax.axis_index("ctx")
        self.core = self.device % 2
        self.chip = self.device // 2
        if self.snake:
            self.place = jnp.where(
                self.chip % 2 == 0, self.chip // 2, self.chips - 1 - self.chip // 2
            )
        else:
            self.place = self.chip
        self.sign = 1 - 2 * self.core

    def owner(self, rounds):
        place = (self.place - self.sign * rounds + self.chips) % self.chips
        if not self.snake:
            return place
        half = self.chips // 2
        return jnp.where(place < half, 2 * place, 2 * (self.chips - 1 - place) + 1)

    def send(self, block, step):
        route = []
        for place in range(self.chips):
            for core in (0, 1):
                to = self.order[(place + (step if core == 0 else -step)) % self.chips]
                route.append((self.order[place] * 2 + core, to * 2 + core))
        return lax.ppermute(block, "ctx", sorted(route))

    def swap(self, block):
        return lax.ppermute(block, "ctx", [(i, i ^ 1) for i in range(2 * self.chips)])

    def in_order(self, own, other, axis):
        first = jnp.where(self.core == 0, own, other)
        second = jnp.where(self.core == 0, other, own)
        return jnp.concatenate([first, second], axis=axis)


def stat_rows(rows):
    return -(-3 * (rows // LANES) // TILE) * TILE


def diagonal():
    shape = (LANES, LANES)
    return lax.broadcasted_iota(jnp.int32, shape, 0) == lax.broadcasted_iota(jnp.int32, shape, 1)


def pack_stats(stats):
    high = [x.astype(BF16).astype(F32) for x in stats]
    rest = [x - h for x, h in zip(stats, high)]
    middle = [x.astype(BF16).astype(F32) for x in rest]
    low = [x - h for x, h in zip(rest, middle)]
    parts = high + middle + low
    parts += [jnp.zeros_like(stats[0])] * (-len(parts) % TILE)
    return jnp.concatenate(parts, axis=0).astype(BF16)


def unpack_stats(packed, blocks):
    packed = packed.astype(F32)
    return packed[:blocks] + packed[blocks : 2 * blocks] + packed[2 * blocks : 3 * blocks]


def attend_kernel(chunk, group, q, bias, k0, k1, v0, v1, out, kbuf, vbuf, sems):
    tokens = k0.shape[0]
    rows = q.shape[0]
    columns = pl.ds(pl.multiple_of(group[0] * LANES, LANES), LANES)
    copies = []
    for i, (source, buffer) in enumerate(((k0, kbuf), (k1, kbuf), (v0, vbuf), (v1, vbuf))):
        copy = pltpu.make_async_copy(
            source.at[:, columns],
            buffer.at[pl.ds((i % 2) * tokens, tokens), pl.ds(0, LANES)],
            sems.at[i],
        )
        copy.start()
        copies.append(copy)
    shape = (2 * tokens, LANES)
    block = lax.broadcasted_iota(jnp.int32, shape, 0) // BLK
    lane = lax.broadcasted_iota(jnp.int32, shape, 1)
    kbuf[:, LANES:] = (block == lane).astype(F32).astype(BF16)
    vbuf[:, LANES:] = jnp.ones(shape, BF16)
    for copy in copies:
        copy.wait()
    diag = diagonal()
    biases = jnp.concatenate([bias[...]] * (chunk // bias.shape[0]), axis=0)
    stats = []
    for start in range(0, rows, chunk):
        query = jnp.concatenate([q[pl.ds(start, chunk), :], biases], axis=1)
        scores = lax.dot_general(
            query, kbuf[...], (((1,), (1,)), ((), ())), preferred_element_type=F32
        )
        peak = jnp.max(scores, axis=1, keepdims=True)
        weights = jnp.exp2(scores - peak).astype(BF16)
        sums = jnp.dot(weights, vbuf[...], preferred_element_type=F32)
        total = sums[:, LANES:]
        out[pl.ds(start, chunk), :] = (sums[:, :LANES] / total).astype(BF16)
        level = peak + jnp.log2(total)
        for b in range(chunk // LANES):
            part = level[b * LANES : (b + 1) * LANES]
            stats.append(jnp.sum(jnp.where(diag, part, 0.0), axis=0, keepdims=True))
    out[pl.ds(rows, stat_rows(rows)), :] = pack_stats(stats)


def attend(group, q, bias, cache):
    rows, width = q.shape
    tokens = cache[0].shape[0]
    chunk = math.gcd(rows, 256)
    return pl.pallas_call(
        functools.partial(attend_kernel, chunk),
        out_shape=jax.ShapeDtypeStruct((rows + stat_rows(rows), width), BF16),
        in_specs=[SCALARS, VMEM, VMEM] + [ANYWHERE] * 4,
        out_specs=VMEM,
        scratch_shapes=[
            pltpu.VMEM((2 * tokens, 2 * LANES), BF16),
            pltpu.VMEM((2 * tokens, 2 * LANES), BF16),
            pltpu.SemaphoreType.DMA((4,)),
        ],
        compiler_params=pltpu.CompilerParams(vmem_limit_bytes=40 * 1024 * 1024),
        cost_estimate=pl.CostEstimate(
            flops=16 * rows * tokens * width,
            bytes_accessed=8 * tokens * width,
            transcendentals=2 * rows * tokens,
        ),
        name="attend",
    )(group, q, bias, *cache)


def merged(diag, one, one_stat, two, two_stat):
    peak = jnp.maximum(one_stat, two_stat)
    one_part, two_part = jnp.exp2(one_stat - peak), jnp.exp2(two_stat - peak)
    total = one_part + two_part
    share = jnp.sum(jnp.where(diag, one_part / total, 0.0), axis=1, keepdims=True)
    one, two = one.astype(F32), two.astype(F32)
    return two + share * (one - two), peak + jnp.log2(total)


def merge_kernel(one, two, out):
    rows = out.shape[0] * LANES // (LANES + 3)
    rows -= rows % LANES
    while rows + stat_rows(rows) > out.shape[0]:
        rows -= LANES
    blocks = rows // LANES
    one_rows = rows
    while one_rows + stat_rows(one_rows) > one.shape[0]:
        one_rows -= LANES
    one_blocks = one_rows // LANES
    diag = diagonal()
    one_stats = unpack_stats(one[pl.ds(one_rows, stat_rows(one_rows)), :], one_blocks)
    two_stats = unpack_stats(two[pl.ds(rows, stat_rows(rows)), :], blocks)
    stats = []
    for b in range(blocks):
        here = pl.ds(b * LANES, LANES)
        if b < one_blocks:
            value, stat = merged(
                diag, one[here, :], one_stats[b : b + 1], two[here, :], two_stats[b : b + 1]
            )
            out[here, :] = value.astype(BF16)
        else:
            out[here, :] = two[here, :]
            stat = two_stats[b : b + 1]
        stats.append(stat)
    out[pl.ds(rows, stat_rows(rows)), :] = pack_stats(stats)


def merge(one, two):
    return pl.pallas_call(
        merge_kernel,
        out_shape=jax.ShapeDtypeStruct(two.shape, BF16),
        in_specs=[VMEM, VMEM],
        out_specs=VMEM,
        cost_estimate=pl.CostEstimate(
            flops=8 * two.size, bytes_accessed=6 * two.size, transcendentals=0
        ),
        name="merge",
    )(one, two)


def finish_kernel(queries, mine, other, out):
    width = mine.shape[1]
    rows = out.shape[0] * out.shape[1] // width
    blocks = rows // LANES
    diag = diagonal()
    mine_stats = unpack_stats(mine[pl.ds(rows, stat_rows(rows)), :], blocks)
    other_stats = unpack_stats(other[pl.ds(rows, stat_rows(rows)), :], blocks)
    for b in range(blocks):
        far = (b + blocks // 2) % blocks
        value, _ = merged(
            diag,
            mine[pl.ds(b * LANES, LANES), :],
            mine_stats[b : b + 1],
            other[pl.ds(far * LANES, LANES), :],
            other_stats[far : far + 1],
        )
        for part in range(LANES // queries):
            head = (b * LANES) // queries + part
            out[:, pl.ds(head * width, width)] = value[
                part * queries : (part + 1) * queries
            ].astype(BF16)


def finish(queries, mine, other, heads):
    width = mine.shape[1]
    return pl.pallas_call(
        functools.partial(finish_kernel, queries),
        out_shape=jax.ShapeDtypeStruct((queries, heads * width), BF16),
        in_specs=[VMEM, VMEM],
        out_specs=VMEM,
        cost_estimate=pl.CostEstimate(
            flops=8 * mine.size, bytes_accessed=6 * mine.size, transcendentals=0
        ),
        name="finish",
    )(mine, other)


def gather_project(ring, block, gain_of, weight):
    width = block.shape[1]
    rows = block.shape[0]

    def add(sums, squares, part, start, gains):
        values = part.astype(F32)
        scaled = (values * gains.astype(F32)).astype(BF16)
        piece = lax.dynamic_slice_in_dim(weight, start, part.shape[1], 0)
        return (
            sums + jnp.dot(scaled, piece, preferred_element_type=F32),
            squares + jnp.sum(values * values, axis=1, keepdims=True),
        )

    sums = jnp.zeros((rows, weight.shape[1]), F32)
    squares = jnp.zeros((rows, 1), F32)
    sums, squares = add(sums, squares, block, ring.owner(0) * width, gain_of(0, None, block))
    rounds = ring.chips // 2
    travelling = block
    for step in range(1, rounds + 1):
        last = step == rounds
        if last:
            half = width // 2
            travelling = lax.dynamic_slice_in_dim(travelling, ring.core * half, half, 1)
        travelling = ring.send(travelling, 1)
        opposite = ring.swap(travelling)
        if last:
            base = ring.owner(rounds) * width
            near, far = ring.core * half, (1 - ring.core) * half
            sums, squares = add(sums, squares, travelling, base + near, gain_of(step, near, travelling))
            sums, squares = add(sums, squares, opposite, base + far, gain_of(step, far, opposite))
        else:
            sums, squares = add(
                sums, squares, travelling, ring.owner(step) * width, gain_of(step, None, travelling)
            )
            sums, squares = add(
                sums, squares, opposite, ring.owner(-step) * width, gain_of(-step, None, opposite)
            )
    factor = lax.rsqrt(squares / weight.shape[0] + EPSILON)
    return sums * factor


def layer(ring, hidden, gains, weights, q_gain, bias, cache):
    attn_gain, next_gain = gains
    q_weight, out_weight, other_weight, next_weight = weights
    queries, here = hidden.shape
    head_dim = q_gain.shape[0]
    heads_here = q_weight.shape[1] // head_dim
    chip_heads = 2 * heads_here
    kv_heads = cache[0].shape[1] // head_dim
    group_size = heads_here * 2 * ring.chips // kv_heads
    rounds = ring.chips // 2

    def gain_of(gain):
        def get(step, offset, part):
            owner = ring.owner(step)
            start = owner * 2 * here + (0 if offset is None else offset)
            return lax.dynamic_slice_in_dim(gain, start, part.shape[1], 0)[None, :]

        return get

    block = ring.in_order(hidden, ring.swap(hidden), 1)
    query = gather_project(ring, block, gain_of(attn_gain), q_weight)
    shaped = query.reshape(queries, heads_here, head_dim)
    mean = jnp.mean(shaped * shaped, axis=-1, keepdims=True)
    scale = head_dim**-0.5 * math.log2(math.e)
    normed = (
        shaped * lax.rsqrt(mean + EPSILON) * (q_gain.astype(F32) * scale)
    ).astype(BF16)
    own_heads = normed.transpose(1, 0, 2).reshape(heads_here * queries, head_dim)
    travelling = jnp.concatenate([own_heads, ring.swap(own_heads)], axis=0)

    def partial(step, rows):
        group = (ring.owner(step) * chip_heads // group_size).astype(jnp.int32)
        return attend(group[None], rows, bias, cache)

    partials = [partial(0, own_heads)]
    for step in range(1, rounds + 1):
        if step == rounds:
            travelling = travelling[: heads_here * queries]
        travelling = ring.send(travelling, 1)
        partials.append(partial(step, travelling))
    running = partials[rounds]
    for step in range(rounds - 1, 0, -1):
        running = merge(ring.send(running, -1), partials[step])
    running = ring.send(running, -1)
    running = merge(partials[0], running)
    attended = finish(queries, running, ring.swap(running), chip_heads)
    own, other = jnp.split(attended, 2, axis=1)

    def mix(rows, weight, start, size):
        piece = lax.dynamic_slice_in_dim(weight, start, size, 1)
        return jnp.dot(rows, piece, preferred_element_type=F32)

    def mixed(step):
        start, size = ring.owner(step) * 2 * here, 2 * here
        if step == rounds:
            start, size = start + ring.core * here, here
        return mix(own, out_weight, start, size) + mix(other, other_weight, start, size)

    running = mixed(rounds)
    for step in range(rounds - 1, -1, -1):
        got = ring.send(running.astype(BF16), -1).astype(F32)
        if step == rounds - 1:
            zero = jnp.zeros_like(got)
            got = ring.in_order(got, zero, 1)
        if step:
            running = got + mixed(step)
        else:
            running = got + mix(own, out_weight, ring.owner(0) * 2 * here, 2 * here)
    running = running.astype(BF16)
    total = running.astype(F32) + ring.swap(running).astype(F32)
    new_block = (block.astype(F32) + total).astype(BF16)
    new_hidden = lax.dynamic_slice_in_dim(new_block, ring.core * here, here, 1)
    following = gather_project(ring, new_block, gain_of(next_gain), next_weight)
    return new_hidden, following.astype(BF16)


def gather_small(ring, block):
    blocks = {}
    whole = jnp.zeros((block.shape[0], ring.chips * block.shape[1]), block.dtype)
    rounds = ring.chips // 2
    travelling = block
    whole = lax.dynamic_update_slice_in_dim(whole, block, ring.owner(0) * block.shape[1], 1)
    for step in range(1, rounds + 1):
        travelling = ring.send(travelling, 1)
        opposite = ring.swap(travelling)
        for at, part in ((step, travelling), (-step, opposite)):
            whole = lax.dynamic_update_slice_in_dim(whole, part, ring.owner(at) * block.shape[1], 1)
    return whole


def on_device(
    streams,
    columns,
    hidden,
    attn_gain,
    q_weight,
    q_gain,
    key_cache,
    value_cache,
    block_limit,
    out_weight,
    next_gain,
    next_weight,
):
    ring = Ring(lax.axis_size("ctx"), columns)
    queries = hidden.shape[0]
    small = jnp.stack([attn_gain, next_gain])
    small = ring.in_order(small, ring.swap(small), 1)
    gains = gather_small(ring, small)
    tokens = key_cache.shape[0]
    cache = (key_cache, ring.swap(key_cache), value_cache, ring.swap(value_cache))
    other_weight = ring.swap(out_weight)
    lanes = jnp.arange(LANES, dtype=jnp.int32)
    own_blocks = tokens // BLK
    block = jnp.where(
        lanes < own_blocks,
        ring.device * own_blocks + lanes,
        (ring.device + ring.sign) * own_blocks + lanes - own_blocks,
    )
    bias = jnp.where(block[None, :] <= block_limit[:, None], 0.0, MASKED).astype(BF16)
    weights = (q_weight, out_weight, other_weight, next_weight)
    size = queries // streams
    outs = [
        layer(
            ring,
            hidden[i * size : (i + 1) * size],
            (gains[0], gains[1]),
            weights,
            q_gain,
            bias[i * size : (i + 1) * size],
            cache,
        )
        for i in range(streams)
    ]
    return tuple(jnp.concatenate(parts, axis=0) for parts in zip(*outs))


def solution(mesh):
    in_specs = (
        P("groups", "ctx"),
        P("ctx"),
        P(None, "ctx"),
        P(),
        P(("groups", "ctx"), None),
        P(("groups", "ctx"), None),
        P("groups"),
        P("ctx", None),
        P("ctx"),
        P(None, "ctx"),
    )
    out_specs = (P("groups", "ctx"), P("groups", "ctx"))
    columns = 2 if mesh.shape["groups"] == 2 else 1
    return jax.shard_map(
        functools.partial(on_device, 1, columns),
        mesh=mesh,
        in_specs=in_specs,
        out_specs=out_specs,
        check_vma=False,
    )
```

time: 442 us -> 211 us (0.48)
  waiting for transfers between devices: 245 us -> 85.1 us
  matrix products: 71.6 us -> 25.5 us
  blocking collectives: 42.3 us -> 0 us
  Pallas kernels: 0 us -> 37.6 us
  starting transfers between devices: 6.7 us -> 38.4 us
  local copies, waits for them, and re-layouts: 39.4 us -> 17.5 us
  other arithmetic: 18.6 us -> 4.75 us
  between operations: 13.9 us -> 1.23 us
    reduce_scatter x1 -> x0, waiting for transfers between devices: 70.2 us -> none  [on_device(): lax.psum_scatter(lax.dot_general(out_weight, attended, (((0,), (1,)), (()...]
    dot_general x35 -> x27, matrix products: 71.6 us -> 25.5 us  [the longest x9 13.8 us: mix(): return jnp.dot(rows, piece, preferred_element_type=F32)]
    ppermute x64 -> x44, waiting for transfers between devices: 131 us -> 85.1 us  [the longest x24 66.2 us: send(): return lax.ppermute(block, 'ctx', sorted(route))]
    all_gather x2 -> x0, waiting for transfers between devices: 43.8 us -> none  [normalize_project(): lax.all_gather(share, 'ctx', axis=1, tiled=True)]
    all_gather x2 -> x0, blocking collectives: 42.3 us -> none  [normalize_project(): lax.all_gather(gain_share, 'ctx', axis=0, tiled=True)]
    broadcast_in_dim x48 -> x1, local copies, waits for them, and re-layouts: 38.2 us -> 0.02 us  [gather_small(): jnp.zeros((block.shape[0], ring.chips * block.shape[1]), block.dtype)]
    pallas_call x0 -> x10, Pallas kernels: none -> 37.6 us  [the longest x5 27.8 us: attend(): pl.pallas_call(functools.partial(attend_kernel, chunk), out_shape=jax.Sha...]
    ppermute x64 -> x44, starting transfers between devices: 6.58 us -> 38.4 us  [the longest x24 36.5 us: send(): return lax.ppermute(block, 'ctx', sorted(route))]
  transfers between devices with their start and end apart: 67 -> 44, of which waited for: 19 -> 27; matrix products, arithmetic and copies ran while one was open for 0% -> 12% of each run, Pallas kernels for 0% -> 18%
where the time goes in v1:
time: 211 us; the launch traced here: 210 us
  waiting for transfers between devices  85.1 us (40%)
  starting transfers between devices  38.4 us (18%)
  Pallas kernels  37.6 us (18%)
  matrix products  25.5 us (12%)
  local copies, waits for them, and re-layouts  17.5 us (8%)
  other arithmetic  4.75 us (2%)
    ppermute x24, waiting for transfers between devices, send(): return lax.ppermute(block, 'ctx', sorted(route))  66.2 us
    ppermute x24, starting transfers between devices, send(): return lax.ppermute(block, 'ctx', sorted(route))  36.5 us
    pallas_call x5, Pallas kernels, attend(): pl.pallas_call(functools.partial(attend_kernel, chunk), out_shape=jax.Sha...  27.8 us
    ppermute x20, waiting for transfers between devices, swap(): lax.ppermute(block, 'ctx', [(i, i ^ 1) for i in range(2 * self.chips)])  18.9 us
    dot_general x9, matrix products, mix(): return jnp.dot(rows, piece, preferred_element_type=F32)  13.8 us
    unnamed x40, local copies, waits for them, and re-layouts  12.7 us
    dot_general x18, matrix products, add(): jnp.dot(scaled, piece, preferred_element_type=F32)  11.6 us
    pallas_call x4, Pallas kernels, merge(): pl.pallas_call(merge_kernel, out_shape=jax.ShapeDtypeStruct(two.shape, BF...  7.76 us
  transfers between devices with their start and end apart: 44, of which 27 were waited for; matrix products, arithmetic and copies ran while one was open for 12% of the time, Pallas kernels for 18%

profile of v1, /device:TPU:0, one launch (start us, length us, event | category | flops | bytes accessed | tf_op | source)
XLA Modules:
  0.0 210.1 jit_solution(8057677695922402101)
XLA Ops:
  3.9 3.1 %collective-permute-start.2 = (bf16[2,1024]{1,0:T(2,128)(2,1)S(1)}, bf16[2,1024]{1,0:T(2,128)(2,1)S(1)}, u32[]{:S(2)}, u32[]{:S(2)}) collective-permute-start(bf16[2,1024]{1,0:T(2,128)(2,1)S(1)} %get-tuple-element.28), channel_id=1, source_target_pairs={{0,4},{1,3},{2,0},{3,7},{4,8},{5,1},{6,2},{7,11},{8,12},{9,5},{10,... | collective-permute-start | bytes 12296 | tf_op jit(solution)/shard_map/ppermute | solution.py:55
  7.0 1.5 collective-permute-done.2
  8.5 2.1 collective-permute-start.4
  10.6 1.5 collective-permute-done.4
  12.9 2.9 %collective-permute-start.6 = (bf16[2,1024]{1,0:T(2,128)(2,1)S(1)}, bf16[2,1024]{1,0:T(2,128)(2,1)S(1)}, u32[]{:S(2)}, u32[]{:S(2)}) collective-permute-start(bf16[2,1024]{1,0:T(2,128)(2,1)S(1)} %collective-permute-done.4), channel_id=1, source_target_pairs={{0,4},{1,3},{2,0},{3,7},{4,8},{5,1},{6,2},{7,11},{8,12},{9,5},{10,... | collective-permute-start | bytes 12296 | tf_op jit(solution)/shard_map/ppermute | solution.py:55
  15.9 1.5 collective-permute-done.6
  17.4 2.1 collective-permute-start.8
  21.0 11.7 %collective-permute-done.9 = bf16[2,1024]{1,0:T(2,128)(2,1)S(1)} collective-permute-done((bf16[2,1024]{1,0:T(2,128)(2,1)S(1)}, bf16[2,1024]{1,0:T(2,128)(2,1)S(1)}, u32[]{:S(2)}, u32[]{:S(2)}) %collective-permute-start.9) | collective-permute-done | bytes 4128 | tf_op jit(solution)/shard_map/ppermute | solution.py:58
  34.4 1.6 collective-permute-start.10
  36.2 1.5 fusion.39
  37.7 3.1 %collective-permute-done.10 = bf16[128,1024]{1,0:T(8,128)(2,1)S(1)} collective-permute-done((bf16[128,1024]{1,0:T(8,128)(2,1)S(1)}, bf16[128,1024]{1,0:T(8,128)(2,1)S(1)}, u32[]{:S(2)}, u32[]{:S(2)}) %collective-permute-start.10) | collective-permute-done | bytes 262176 | tf_op jit(solution)/shard_map/ppermute | solution.py:55
  40.8 1.6 collective-permute-start.12
  42.5 1.5 convolution_add_fusion.13
  44.1 3.1 %collective-permute-done.12 = bf16[128,1024]{1,0:T(8,128)(2,1)S(1)} collective-permute-done((bf16[128,1024]{1,0:T(8,128)(2,1)S(1)}, bf16[128,1024]{1,0:T(8,128)(2,1)S(1)}, u32[]{:S(2)}, u32[]{:S(2)}) %collective-permute-start.12) | collective-permute-done | bytes 262176 | tf_op jit(solution)/shard_map/ppermute | solution.py:55
  47.2 1.6 collective-permute-start.14
  48.9 1.5 fusion.35
  50.7 1.5 fusion.7
  52.2 1.4 collective-permute-done.14
  53.6 1.6 collective-permute-start.16
  56.2 2.4 %collective-permute-done.16 = bf16[128,512]{1,0:T(8,128)(2,1)S(1)} collective-permute-done((bf16[128,512]{1,0:T(8,128)(2,1)S(1)}, bf16[128,512]{1,0:T(8,128)(2,1)S(1)}, u32[]{:S(2)}, u32[]{:S(2)}) %collective-permute-start.16) | collective-permute-done | bytes 131104 | tf_op jit(solution)/shard_map/ppermute | solution.py:55
  64.5 1.6 collective-permute-start.21
  66.1 4.8 %collective-permute-done.21.q = bf16[1024,128]{1,0:T(8,128)(2,1)S(1)} collective-permute-done((bf16[1024,128]{1,0:T(8,128)(2,1)S(1)}, bf16[1024,128]{1,0:T(8,128)(2,1)S(1)}, u32[]{:S(2)}, u32[]{:S(2)}) %collective-permute-start.21) | collective-permute-done | bytes 262176 | tf_op jit(solution)/shard_map/ppermute | solution.py:55
  70.9 1.6 collective-permute-start.22
  73.2 4.2 %collective-permute-done.22.q = bf16[1024,128]{1,0:T(8,128)(2,1)} collective-permute-done((bf16[1024,128]{1,0:T(8,128)(2,1)S(1)}, bf16[1024,128]{1,0:T(8,128)(2,1)}, u32[]{:S(2)}, u32[]{:S(2)}) %collective-permute-start.22) | collective-permute-done | bytes 262176 | tf_op jit(solution)/shard_map/ppermute | solution.py:55
  77.4 1.6 collective-permute-start.23
  78.9 5.1 %collective-permute-done.23.q = bf16[1024,128]{1,0:T(8,128)(2,1)} collective-permute-done((bf16[1024,128]{1,0:T(8,128)(2,1)}, bf16[1024,128]{1,0:T(8,128)(2,1)}, u32[]{:S(2)}, u32[]{:S(2)}) %collective-permute-start.23) | collective-permute-done | bytes 262176 | tf_op jit(solution)/shard_map/ppermute | solution.py:55
  85.0 1.6 collective-permute-start.24
  86.7 3.3 %collective-permute-done.24.q = bf16[512,128]{1,0:T(8,128)(2,1)S(1)} collective-permute-done((bf16[512,128]{1,0:T(8,128)(2,1)S(1)}, bf16[512,128]{1,0:T(8,128)(2,1)S(1)}, u32[]{:S(2)}, u32[]{:S(2)}) %collective-permute-start.24) | collective-permute-done | bytes 131104 | tf_op jit(solution)/shard_map/ppermute | solution.py:55
  90.0 1.9 copy-done.1
  91.9 4.1 %attend.6 = bf16[528,128]{1,0:T(8,128)(2,1)S(1)} custom-call(s32[1]{0:T(128)} %bitcast.12.group, bf16[512,128]{1,0:T(8,128)(2,1)S(1)} %collective-permute-done.24.q, bf16[128,128]{1,0:T(8,128)(2,1)S(1)} %select_convert_fusion.bias, bf16[1536,1024]{1,0:T(8,128)(2,1)S(1)} %copy-done, bf16[1536,1024]{1,0:T(8,128)(2,1)} %collective-permute-done.18.k1, ...), custom_call_target="tpu_custom_call" | custom-call | flops 1610612736 | bytes 1572864 | tf_op jit(solution)/shard_map/attend/pallas_call | solution.py:134
  96.0 1.6 collective-permute-start.25
  97.7 6.8 %attend.7.two = bf16[1056,128]{1,0:T(8,128)(2,1)S(1)} custom-call(s32[1]{0:T(128)} %bitcast.13.group, bf16[1024,128]{1,0:T(8,128)(2,1)} %collective-permute-done.23.q, bf16[128,128]{1,0:T(8,128)(2,1)S(1)} %select_convert_fusion.bias, bf16[1536,1024]{1,0:T(8,128)(2,1)S(1)} %copy-done, bf16[1536,1024]{1,0:T(8,128)(2,1)} %collective-permute-done.18.k1, ...), custom_call_target="tpu_custom_call" | custom-call | flops 3221225472 | bytes 1572864 | tf_op jit(solution)/shard_map/attend/pallas_call | solution.py:134
  105.2 1.9 merge.4
  107.1 1.6 collective-permute-start.26
  108.6 1.9 copy-done.2
  110.5 6.8 %attend.8.two = bf16[1056,128]{1,0:T(8,128)(2,1)S(1)} custom-call(s32[1]{0:T(128)} %bitcast.14.group, bf16[1024,128]{1,0:T(8,128)(2,1)} %collective-permute-done.22.q, bf16[128,128]{1,0:T(8,128)(2,1)S(1)} %select_convert_fusion.bias, bf16[1536,1024]{1,0:T(8,128)(2,1)S(1)} %copy-done, bf16[1536,1024]{1,0:T(8,128)(2,1)} %collective-permute-done.18.k1, ...), custom_call_target="tpu_custom_call" | custom-call | flops 3221225472 | bytes 1572864 | tf_op jit(solution)/shard_map/attend/pallas_call | solution.py:134
  118.1 2.0 merge.5
  120.0 1.6 collective-permute-start.27
  121.6 1.9 copy-done.3
  124.5 6.0 %attend.9.two = bf16[1056,128]{1,0:T(8,128)(2,1)S(1)} custom-call(s32[1]{0:T(128)} %bitcast.15.group, bf16[1024,128]{1,0:T(8,128)(2,1)S(1)} %copy-done.10, bf16[128,128]{1,0:T(8,128)(2,1)S(1)} %select_convert_fusion.bias, bf16[1536,1024]{1,0:T(8,128)(2,1)S(1)} %copy-done, bf16[1536,1024]{1,0:T(8,128)(2,1)} %collective-permute-done.18.k1, ...), custom_call_target="tpu_custom_call" | custom-call | flops 3221225472 | bytes 1572864 | tf_op jit(solution)/shard_map/attend/pallas_call | solution.py:134
  131.2 2.0 merge.6
  134.3 1.9 copy-done.4
  136.2 4.1 %attend.5.one = bf16[528,128]{1,0:T(8,128)(2,1)S(1)} custom-call(s32[1]{0:T(128)} %bitcast.group, bf16[512,128]{1,0:T(8,128)(2,1)S(1)} %bitcast.28, bf16[128,128]{1,0:T(8,128)(2,1)S(1)} %select_convert_fusion.bias, bf16[1536,1024]{1,0:T(8,128)(2,1)S(1)} %copy-done, bf16[1536,1024]{1,0:T(8,128)(2,1)} %collective-permute-done.18.k1, ...), custom_call_target="tpu_custom_call" | custom-call | flops 1610612736 | bytes 1572864 | tf_op jit(solution)/shard_map/attend/pallas_call | solution.py:134
  141.0 1.9 merge.7.mine
  143.0 1.8 collective-permute-done.29.other
  145.4 2.0 finish.1
  147.4 1.4 fusion.74
  148.9 1.5 fusion.8
  151.4 1.6 fusion.28
  153.0 2.4 %collective-permute-done.31 = bf16[128,512]{1,0:T(8,128)(2,1)S(1)} collective-permute-done((bf16[128,512]{1,0:T(8,128)(2,1)S(1)}, bf16[128,512]{1,0:T(8,128)(2,1)S(1)}, u32[]{:S(2)}, u32[]{:S(2)}) %collective-permute-start.31) | collective-permute-done | bytes 131104 | tf_op jit(solution)/shard_map/ppermute | solution.py:55
  155.4 1.6 fusion.70
  158.1 1.6 fusion.25
  159.7 3.8 %collective-permute-done.32 = bf16[128,1024]{1,0:T(8,128)(2,1)S(1)} collective-permute-done((bf16[128,1024]{1,0:T(8,128)(2,1)S(1)}, bf16[128,1024]{1,0:T(8,128)(2,1)S(1)}, u32[]{:S(2)}, u32[]{:S(2)}) %collective-permute-start.32) | collective-permute-done | bytes 262176 | tf_op jit(solution)/shard_map/ppermute | solution.py:55
  163.5 1.5 add_convert_fusion.2
  166.0 1.5 fusion.22
  167.6 3.9 %collective-permute-done.33 = bf16[128,1024]{1,0:T(8,128)(2,1)S(1)} collective-permute-done((bf16[128,1024]{1,0:T(8,128)(2,1)S(1)}, bf16[128,1024]{1,0:T(8,128)(2,1)S(1)}, u32[]{:S(2)}, u32[]{:S(2)}) %collective-permute-start.33) | collective-permute-done | bytes 262176 | tf_op jit(solution)/shard_map/ppermute | solution.py:55
  171.5 1.5 add_convert_fusion.1
  174.0 5.4 %collective-permute-done.34 = bf16[128,1024]{1,0:T(8,128)(2,1)S(1)} collective-permute-done((bf16[128,1024]{1,0:T(8,128)(2,1)S(1)}, bf16[128,1024]{1,0:T(8,128)(2,1)S(1)}, u32[]{:S(2)}, u32[]{:S(2)}) %collective-permute-start.34) | collective-permute-done | bytes 262176 | tf_op jit(solution)/shard_map/ppermute | solution.py:55
  179.4 1.5 add_convert_fusion
  181.1 1.4 collective-permute-done.35
  184.9 4.6 %collective-permute-done.36 = bf16[128,1024]{1,0:T(8,128)(2,1)S(1)} collective-permute-done((bf16[128,1024]{1,0:T(8,128)(2,1)S(1)}, bf16[128,1024]{1,0:T(8,128)(2,1)S(1)}, u32[]{:S(2)}, u32[]{:S(2)}) %collective-permute-start.36) | collective-permute-done | bytes 262176 | tf_op jit(solution)/shard_map/ppermute | solution.py:55
  190.7 5.1 %collective-permute-done.38 = bf16[128,1024]{1,0:T(8,128)(2,1)S(1)} collective-permute-done((bf16[128,1024]{1,0:T(8,128)(2,1)S(1)}, bf16[128,1024]{1,0:T(8,128)(2,1)S(1)}, u32[]{:S(2)}, u32[]{:S(2)}) %collective-permute-start.38) | collective-permute-done | bytes 262176 | tf_op jit(solution)/shard_map/ppermute | solution.py:55
  197.6 4.6 %collective-permute-done.40 = bf16[128,1024]{1,0:T(8,128)(2,1)S(1)} collective-permute-done((bf16[128,1024]{1,0:T(8,128)(2,1)S(1)}, bf16[128,1024]{1,0:T(8,128)(2,1)S(1)}, u32[]{:S(2)}, u32[]{:S(2)}) %collective-permute-start.40) | collective-permute-done | bytes 262176 | tf_op jit(solution)/shard_map/ppermute | solution.py:55
  204.0 3.2 %collective-permute-done.42 = bf16[128,512]{1,0:T(8,128)(2,1)S(1)} collective-permute-done((bf16[128,512]{1,0:T(8,128)(2,1)S(1)}, bf16[128,512]{1,0:T(8,128)(2,1)S(1)}, u32[]{:S(2)}, u32[]{:S(2)}) %collective-permute-start.42) | collective-permute-done | bytes 131104 | tf_op jit(solution)/shard_map/ppermute | solution.py:55
  (157 shorter events, 36.2 us)
Async XLA Ops:
  0.6 32.8 %collective-permute-start = (bf16[128,512]{1,0:T(8,128)(2,1)}, bf16[128,512]{1,0:T(8,128)(2,1)S(1)}, u32[]{:S(2)}, u32[]{:S(2)}) collective-permute-start(bf16[128,512]{1,0:T(8,128)(2,1)} %param.10), channel_id=1, source_target_pairs={{0,1},{1,0},{2,3},{3,2},{4,5},{5,4},{6,7},{7,6},{8,9},{9,8},{10,11... | collective-permute-start | bytes 393224 | tf_op jit(solution)/shard_map/ppermute | solution.py:58
  2.5 1.3 collective-permute-start.1
  2.6 87.3 %collective-permute-start.18 = (bf16[1536,1024]{1,0:T(8,128)(2,1)}, bf16[1536,1024]{1,0:T(8,128)(2,1)}, u32[]{:S(2)}, u32[]{:S(2)}) collective-permute-start(bf16[1536,1024]{1,0:T(8,128)(2,1)} %k0.9), channel_id=1, source_target_pairs={{0,1},{1,0},{2,3},{3,2},{4,5},{5,4},{6,7},{7,6},{8,9},{9,8},{10,11... | collective-permute-start | bytes 9437192 | tf_op jit(solution)/shard_map/ppermute | solution.py:58
  3.1 86.9 %collective-permute-start.19 = (bf16[1536,1024]{1,0:T(8,128)(2,1)}, bf16[1536,1024]{1,0:T(8,128)(2,1)}, u32[]{:S(2)}, u32[]{:S(2)}) collective-permute-start(bf16[1536,1024]{1,0:T(8,128)(2,1)} %v0.9), channel_id=1, source_target_pairs={{0,1},{1,0},{2,3},{3,2},{4,5},{5,4},{6,7},{7,6},{8,9},{9,8},{10,11... | collective-permute-start | bytes 9437192 | tf_op jit(solution)/shard_map/ppermute | solution.py:58
  3.9 4.6 %collective-permute-start.2 = (bf16[2,1024]{1,0:T(2,128)(2,1)S(1)}, bf16[2,1024]{1,0:T(2,128)(2,1)S(1)}, u32[]{:S(2)}, u32[]{:S(2)}) collective-permute-start(bf16[2,1024]{1,0:T(2,128)(2,1)S(1)} %get-tuple-element.28), channel_id=1, source_target_pairs={{0,4},{1,3},{2,0},{3,7},{4,8},{5,1},{6,2},{7,11},{8,12},{9,5},{10,... | collective-permute-start | bytes 12296 | tf_op jit(solution)/shard_map/ppermute | solution.py:55
  7.0 48.2 %copy-start.11 = (bf16[8192,512]{1,0:T(8,128)(2,1)S(1)}, bf16[8192,512]{1,0:T(8,128)(2,1)}, u32[]{:S(2)}) copy-start(bf16[8192,512]{1,0:T(8,128)(2,1)} %param.12) | copy-start | bytes 25165828
  8.5 4.4 %collective-permute-start.3 = (bf16[2,1024]{1,0:T(2,128)(2,1)S(1)}, bf16[2,1024]{1,0:T(2,128)(2,1)S(1)}, u32[]{:S(2)}, u32[]{:S(2)}) collective-permute-start(bf16[2,1024]{1,0:T(2,128)(2,1)S(1)} %collective-permute-done.2), channel_id=1, source_target_pairs={{0,1},{1,0},{2,3},{3,2},{4,5},{5,4},{6,7},{7,6},{8,9},{9,8},{10,11... | collective-permute-start | bytes 12296 | tf_op jit(solution)/shard_map/ppermute | solution.py:58
  8.5 3.6 %collective-permute-start.4 = (bf16[2,1024]{1,0:T(2,128)(2,1)S(1)}, bf16[2,1024]{1,0:T(2,128)(2,1)S(1)}, u32[]{:S(2)}, u32[]{:S(2)}) collective-permute-start(bf16[2,1024]{1,0:T(2,128)(2,1)S(1)} %collective-permute-done.2), channel_id=1, source_target_pairs={{0,4},{1,3},{2,0},{3,7},{4,8},{5,1},{6,2},{7,11},{8,12},{9,5},{10,... | collective-permute-start | bytes 12296 | tf_op jit(solution)/shard_map/ppermute | solution.py:55
  12.1 5.3 %collective-permute-start.5 = (bf16[2,1024]{1,0:T(2,128)(2,1)S(1)}, bf16[2,1024]{1,0:T(2,128)(2,1)S(1)}, u32[]{:S(2)}, u32[]{:S(2)}) collective-permute-start(bf16[2,1024]{1,0:T(2,128)(2,1)S(1)} %collective-permute-done.4), channel_id=1, source_target_pairs={{0,1},{1,0},{2,3},{3,2},{4,5},{5,4},{6,7},{7,6},{8,9},{9,8},{10,11... | collective-permute-start | bytes 12296 | tf_op jit(solution)/shard_map/ppermute | solution.py:58
  12.9 4.5 %collective-permute-start.6 = (bf16[2,1024]{1,0:T(2,128)(2,1)S(1)}, bf16[2,1024]{1,0:T(2,128)(2,1)S(1)}, u32[]{:S(2)}, u32[]{:S(2)}) collective-permute-start(bf16[2,1024]{1,0:T(2,128)(2,1)S(1)} %collective-permute-done.4), channel_id=1, source_target_pairs={{0,4},{1,3},{2,0},{3,7},{4,8},{5,1},{6,2},{7,11},{8,12},{9,5},{10,... | collective-permute-start | bytes 12296 | tf_op jit(solution)/shard_map/ppermute | solution.py:55
  17.4 2.1 %collective-permute-start.7 = (bf16[2,1024]{1,0:T(2,128)(2,1)S(1)}, bf16[2,1024]{1,0:T(2,128)(2,1)S(1)}, u32[]{:S(2)}, u32[]{:S(2)}) collective-permute-start(bf16[2,1024]{1,0:T(2,128)(2,1)S(1)} %collective-permute-done.6), channel_id=1, source_target_pairs={{0,1},{1,0},{2,3},{3,2},{4,5},{5,4},{6,7},{7,6},{8,9},{9,8},{10,11... | collective-permute-start | bytes 12296 | tf_op jit(solution)/shard_map/ppermute | solution.py:58
  17.4 3.6 %collective-permute-start.8 = (bf16[2,1024]{1,0:T(2,128)(2,1)S(1)}, bf16[2,1024]{1,0:T(2,128)(2,1)S(1)}, u32[]{:S(2)}, u32[]{:S(2)}) collective-permute-start(bf16[2,1024]{1,0:T(2,128)(2,1)S(1)} %collective-permute-done.6), channel_id=1, source_target_pairs={{0,4},{1,3},{2,0},{3,7},{4,8},{5,1},{6,2},{7,11},{8,12},{9,5},{10,... | collective-permute-start | bytes 12296 | tf_op jit(solution)/shard_map/ppermute | solution.py:55
  19.5 128.0 %collective-permute-start.30 = (bf16[512,8192]{1,0:T(8,128)(2,1)}, bf16[512,8192]{1,0:T(8,128)(2,1)}, u32[]{:S(2)}, u32[]{:S(2)}) collective-permute-start(bf16[512,8192]{1,0:T(8,128)(2,1)} %param.17), channel_id=1, source_target_pairs={{0,1},{1,0},{2,3},{3,2},{4,5},{5,4},{6,7},{7,6},{8,9},{9,8},{10,11... | collective-permute-start | bytes 25165832 | tf_op jit(solution)/shard_map/ppermute | solution.py:58
  21.0 11.7 %collective-permute-start.9 = (bf16[2,1024]{1,0:T(2,128)(2,1)S(1)}, bf16[2,1024]{1,0:T(2,128)(2,1)S(1)}, u32[]{:S(2)}, u32[]{:S(2)}) collective-permute-start(bf16[2,1024]{1,0:T(2,128)(2,1)S(1)} %collective-permute-done.8), channel_id=1, source_target_pairs={{0,1},{1,0},{2,3},{3,2},{4,5},{5,4},{6,7},{7,6},{8,9},{9,8},{10,11... | collective-permute-start | bytes 12296 | tf_op jit(solution)/shard_map/ppermute | solution.py:58
  34.4 1.8 copy-start.13
  34.4 6.4 %collective-permute-start.10 = (bf16[128,1024]{1,0:T(8,128)(2,1)S(1)}, bf16[128,1024]{1,0:T(8,128)(2,1)S(1)}, u32[]{:S(2)}, u32[]{:S(2)}) collective-permute-start(bf16[128,1024]{1,0:T(8,128)(2,1)S(1)} %pad_maximum_fusion), channel_id=1, source_target_pairs={{0,4},{1,3},{2,0},{3,7},{4,8},{5,1},{6,2},{7,11},{8,12},{9,5},{10,... | collective-permute-start | bytes 786440 | tf_op jit(solution)/shard_map/ppermute | solution.py:55
  40.8 6.4 %collective-permute-start.12 = (bf16[128,1024]{1,0:T(8,128)(2,1)S(1)}, bf16[128,1024]{1,0:T(8,128)(2,1)S(1)}, u32[]{:S(2)}, u32[]{:S(2)}) collective-permute-start(bf16[128,1024]{1,0:T(8,128)(2,1)S(1)} %collective-permute-done.10), channel_id=1, source_target_pairs={{0,4},{1,3},{2,0},{3,7},{4,8},{5,1},{6,2},{7,11},{8,12},{9,5},{10,... | collective-permute-start | bytes 786440 | tf_op jit(solution)/shard_map/ppermute | solution.py:55
  42.4 8.0 %collective-permute-start.11 = (bf16[128,1024]{1,0:T(8,128)(2,1)S(1)}, bf16[128,1024]{1,0:T(8,128)(2,1)S(1)}, u32[]{:S(2)}, u32[]{:S(2)}) collective-permute-start(bf16[128,1024]{1,0:T(8,128)(2,1)S(1)} %collective-permute-done.10), channel_id=1, source_target_pairs={{0,1},{1,0},{2,3},{3,2},{4,5},{5,4},{6,7},{7,6},{8,9},{9,8},{10,11... | collective-permute-start | bytes 786440 | tf_op jit(solution)/shard_map/ppermute | solution.py:58
  44.1 42.5 %copy-start.17 = (s32[128]{0:T(128)S(1)}, s32[128]{0:T(128)}, u32[]{:S(2)}) copy-start(s32[128]{0:T(128)} %param.16) | copy-start | bytes 1540
  44.1 45.9 %copy-start = (bf16[1536,1024]{1,0:T(8,128)(2,1)S(1)}, bf16[1536,1024]{1,0:T(8,128)(2,1)}, u32[]{:S(2)}) copy-start(bf16[1536,1024]{1,0:T(8,128)(2,1)} %k0.9) | copy-start | bytes 9437188
  47.2 6.4 %collective-permute-start.14 = (bf16[128,1024]{1,0:T(8,128)(2,1)S(1)}, bf16[128,1024]{1,0:T(8,128)(2,1)S(1)}, u32[]{:S(2)}, u32[]{:S(2)}) collective-permute-start(bf16[128,1024]{1,0:T(8,128)(2,1)S(1)} %collective-permute-done.12), channel_id=1, source_target_pairs={{0,4},{1,3},{2,0},{3,7},{4,8},{5,1},{6,2},{7,11},{8,12},{9,5},{10,... | collective-permute-start | bytes 786440 | tf_op jit(solution)/shard_map/ppermute | solution.py:55
  50.5 5.1 %collective-permute-start.13 = (bf16[128,1024]{1,0:T(8,128)(2,1)S(1)}, bf16[128,1024]{1,0:T(8,128)(2,1)S(1)}, u32[]{:S(2)}, u32[]{:S(2)}) collective-permute-start(bf16[128,1024]{1,0:T(8,128)(2,1)S(1)} %collective-permute-done.12), channel_id=1, source_target_pairs={{0,1},{1,0},{2,3},{3,2},{4,5},{5,4},{6,7},{7,6},{8,9},{9,8},{10,11... | collective-permute-start | bytes 786440 | tf_op jit(solution)/shard_map/ppermute | solution.py:58
  53.6 5.0 %collective-permute-start.16 = (bf16[128,512]{1,0:T(8,128)(2,1)S(1)}, bf16[128,512]{1,0:T(8,128)(2,1)S(1)}, u32[]{:S(2)}, u32[]{:S(2)}) collective-permute-start(bf16[128,512]{1,0:T(8,128)(2,1)S(1)} %constant_dynamic-slice_fusion.13), channel_id=1, source_target_pairs={{0,4},{1,3},{2,0},{3,7},{4,8},{5,1},{6,2},{7,11},{8,12},{9,5},{10,... | collective-permute-start | bytes 393224 | tf_op jit(solution)/shard_map/ppermute | solution.py:55
  55.5 4.5 %collective-permute-start.15 = (bf16[128,1024]{1,0:T(8,128)(2,1)S(1)}, bf16[128,1024]{1,0:T(8,128)(2,1)S(1)}, u32[]{:S(2)}, u32[]{:S(2)}) collective-permute-start(bf16[128,1024]{1,0:T(8,128)(2,1)S(1)} %collective-permute-done.14), channel_id=1, source_target_pairs={{0,1},{1,0},{2,3},{3,2},{4,5},{5,4},{6,7},{7,6},{8,9},{9,8},{10,11... | collective-permute-start | bytes 786440 | tf_op jit(solution)/shard_map/ppermute | solution.py:58
  58.6 1.3 collective-permute-start.17
  63.0 1.4 collective-permute-start.20
  64.5 6.4 %collective-permute-start.21 = (bf16[1024,128]{1,0:T(8,128)(2,1)S(1)}, bf16[1024,128]{1,0:T(8,128)(2,1)S(1)}, u32[]{:S(2)}, u32[]{:S(2)}) collective-permute-start(bf16[1024,128]{1,0:T(8,128)(2,1)S(1)} %pad_maximum_fusion.1), channel_id=1, source_target_pairs={{0,4},{1,3},{2,0},{3,7},{4,8},{5,1},{6,2},{7,11},{8,12},{9,5},{10,... | collective-permute-start | bytes 786440 | tf_op jit(solution)/shard_map/ppermute | solution.py:55
  70.9 6.5 %collective-permute-start.22 = (bf16[1024,128]{1,0:T(8,128)(2,1)S(1)}, bf16[1024,128]{1,0:T(8,128)(2,1)}, u32[]{:S(2)}, u32[]{:S(2)}) collective-permute-start(bf16[1024,128]{1,0:T(8,128)(2,1)S(1)} %collective-permute-done.21.q), channel_id=1, source_target_pairs={{0,4},{1,3},{2,0},{3,7},{4,8},{5,1},{6,2},{7,11},{8,12},{9,5},{10,... | collective-permute-start | bytes 786440 | tf_op jit(solution)/shard_map/ppermute | solution.py:55
  72.5 0.7 copy-start.9
  77.4 6.7 %collective-permute-start.23 = (bf16[1024,128]{1,0:T(8,128)(2,1)}, bf16[1024,128]{1,0:T(8,128)(2,1)}, u32[]{:S(2)}, u32[]{:S(2)}) collective-permute-start(bf16[1024,128]{1,0:T(8,128)(2,1)} %collective-permute-done.22.q), channel_id=1, source_target_pairs={{0,4},{1,3},{2,0},{3,7},{4,8},{5,1},{6,2},{7,11},{8,12},{9,5},{10,... | collective-permute-start | bytes 786440 | tf_op jit(solution)/shard_map/ppermute | solution.py:55
  85.0 5.0 %collective-permute-start.24 = (bf16[512,128]{1,0:T(8,128)(2,1)S(1)}, bf16[512,128]{1,0:T(8,128)(2,1)S(1)}, u32[]{:S(2)}, u32[]{:S(2)}) collective-permute-start(bf16[512,128]{1,0:T(8,128)(2,1)S(1)} %slice.13), channel_id=1, source_target_pairs={{0,4},{1,3},{2,0},{3,7},{4,8},{5,1},{6,2},{7,11},{8,12},{9,5},{10,... | collective-permute-start | bytes 393224 | tf_op jit(solution)/shard_map/ppermute | solution.py:55
  90.0 1.9 copy-start.1
  96.0 9.1 %collective-permute-start.25 = (bf16[528,128]{1,0:T(8,128)(2,1)S(1)}, bf16[528,128]{1,0:T(8,128)(2,1)}, u32[]{:S(2)}, u32[]{:S(2)}) collective-permute-start(bf16[528,128]{1,0:T(8,128)(2,1)S(1)} %attend.6), channel_id=1, source_target_pairs={{0,2},{1,5},{2,6},{3,1},{4,0},{5,9},{6,10},{7,3},{8,4},{9,13},{10,... | collective-permute-start | bytes 405512 | tf_op jit(solution)/shard_map/ppermute | solution.py:55
  104.5 0.7 copy-start.7
  107.1 11.0 %collective-permute-start.26 = (bf16[1056,128]{1,0:T(8,128)(2,1)}, bf16[1056,128]{1,0:T(8,128)(2,1)}, u32[]{:S(2)}, u32[]{:S(2)}) collective-permute-start(bf16[1056,128]{1,0:T(8,128)(2,1)} %merge.4), channel_id=1, source_target_pairs={{0,2},{1,5},{2,6},{3,1},{4,0},{5,9},{6,10},{7,3},{8,4},{9,13},{10,... | collective-permute-start | bytes 811016 | tf_op jit(solution)/shard_map/ppermute | solution.py:55
  108.6 1.9 copy-start.2
  117.3 0.7 copy-start.5
  120.0 11.1 %collective-permute-start.27 = (bf16[1056,128]{1,0:T(8,128)(2,1)}, bf16[1056,128]{1,0:T(8,128)(2,1)}, u32[]{:S(2)}, u32[]{:S(2)}) collective-permute-start(bf16[1056,128]{1,0:T(8,128)(2,1)} %merge.5), channel_id=1, source_target_pairs={{0,2},{1,5},{2,6},{3,1},{4,0},{5,9},{6,10},{7,3},{8,4},{9,13},{10,... | collective-permute-start | bytes 811016 | tf_op jit(solution)/shard_map/ppermute | solution.py:55
  121.6 1.9 copy-start.3
  123.5 0.9 copy-start.10
  130.4 0.7 copy-start.6
  133.1 7.9 %collective-permute-start.28 = (bf16[1056,128]{1,0:T(8,128)(2,1)}, bf16[1056,128]{1,0:T(8,128)(2,1)}, u32[]{:S(2)}, u32[]{:S(2)}) collective-permute-start(bf16[1056,128]{1,0:T(8,128)(2,1)} %merge.6), channel_id=1, source_target_pairs={{0,2},{1,5},{2,6},{3,1},{4,0},{5,9},{6,10},{7,3},{8,4},{9,13},{10,... | collective-permute-start | bytes 811016 | tf_op jit(solution)/shard_map/ppermute | solution.py:55
  134.3 1.9 copy-start.4
  140.4 0.7 copy-start.8
  143.0 1.8 collective-permute-start.29
  144.7 0.7 copy-start.15
  147.4 16.1 %copy-start.12 = (bf16[128,1024]{1,0:T(8,128)(2,1)S(1)}, bf16[128,1024]{1,0:T(8,128)(2,1)}, u32[]{:S(2)}) copy-start(bf16[128,1024]{1,0:T(8,128)(2,1)} %finish.1) | copy-start | bytes 786436
  147.4 33.6 %copy-start.16 = (bf16[1,8192]{1,0:T(2,128)(2,1)S(1)}, bf16[1,8192]{1,0:T(2,128)(2,1)}, u32[]{:S(2)}) copy-start(bf16[1,8192]{1,0:T(2,128)(2,1)} %get-tuple-element.17) | copy-start | bytes 49156
  147.4 35.1 %copy-start.14 = (bf16[128,512]{1,0:T(8,128)(2,1)S(1)}, bf16[128,512]{1,0:T(8,128)(2,1)}, u32[]{:S(2)}) copy-start(bf16[128,512]{1,0:T(8,128)(2,1)} %copy-done.13) | copy-start | bytes 393220
  148.8 35.7 %slice-start = ((s8[8388608]{0:T(1024)(128)(4,1)}), s8[4194304]{0:T(1024)(128)(4,1)S(1)}, s32[]{:S(2)}) async-start(s8[8388608]{0:T(1024)(128)(4,1)} %bitcast.29), calls=%async_computation | async-start | bytes 8388608
  150.3 5.0 %collective-permute-start.31 = (bf16[128,512]{1,0:T(8,128)(2,1)S(1)}, bf16[128,512]{1,0:T(8,128)(2,1)S(1)}, u32[]{:S(2)}, u32[]{:S(2)}) collective-permute-start(bf16[128,512]{1,0:T(8,128)(2,1)S(1)} %fusion.8), channel_id=1, source_target_pairs={{0,2},{1,5},{2,6},{3,1},{4,0},{5,9},{6,10},{7,3},{8,4},{9,13},{10,... | collective-permute-start | bytes 393224 | tf_op jit(solution)/shard_map/ppermute | solution.py:55
  157.1 6.4 %collective-permute-start.32 = (bf16[128,1024]{1,0:T(8,128)(2,1)S(1)}, bf16[128,1024]{1,0:T(8,128)(2,1)S(1)}, u32[]{:S(2)}, u32[]{:S(2)}) collective-permute-start(bf16[128,1024]{1,0:T(8,128)(2,1)S(1)} %fusion.70), channel_id=1, source_target_pairs={{0,2},{1,5},{2,6},{3,1},{4,0},{5,9},{6,10},{7,3},{8,4},{9,13},{10,... | collective-permute-start | bytes 786440 | tf_op jit(solution)/shard_map/ppermute | solution.py:55
  159.7 24.9 %slice-start.1 = ((s8[8388608]{0:T(1024)(128)(4,1)}), s8[4194304]{0:T(1024)(128)(4,1)S(1)}, s32[]{:S(2)}) async-start(s8[8388608]{0:T(1024)(128)(4,1)} %bitcast.29), calls=%async_computation.1 | async-start | bytes 8388608
  165.0 6.4 %collective-permute-start.33 = (bf16[128,1024]{1,0:T(8,128)(2,1)S(1)}, bf16[128,1024]{1,0:T(8,128)(2,1)S(1)}, u32[]{:S(2)}, u32[]{:S(2)}) collective-permute-start(bf16[128,1024]{1,0:T(8,128)(2,1)S(1)} %add_convert_fusion.2), channel_id=1, source_target_pairs={{0,2},{1,5},{2,6},{3,1},{4,0},{5,9},{6,10},{7,3},{8,4},{9,13},{10,... | collective-permute-start | bytes 786440 | tf_op jit(solution)/shard_map/ppermute | solution.py:55
  173.0 6.4 %collective-permute-start.34 = (bf16[128,1024]{1,0:T(8,128)(2,1)S(1)}, bf16[128,1024]{1,0:T(8,128)(2,1)S(1)}, u32[]{:S(2)}, u32[]{:S(2)}) collective-permute-start(bf16[128,1024]{1,0:T(8,128)(2,1)S(1)} %add_convert_fusion.1), channel_id=1, source_target_pairs={{0,2},{1,5},{2,6},{3,1},{4,0},{5,9},{6,10},{7,3},{8,4},{9,13},{10,... | collective-permute-start | bytes 786440 | tf_op jit(solution)/shard_map/ppermute | solution.py:55
  181.0 1.6 collective-permute-start.35
  182.8 6.7 %collective-permute-start.36 = (bf16[128,1024]{1,0:T(8,128)(2,1)S(1)}, bf16[128,1024]{1,0:T(8,128)(2,1)S(1)}, u32[]{:S(2)}, u32[]{:S(2)}) collective-permute-start(bf16[128,1024]{1,0:T(8,128)(2,1)S(1)} %get-tuple-element.3), channel_id=1, source_target_pairs={{0,4},{1,3},{2,0},{3,7},{4,8},{5,1},{6,2},{7,11},{8,12},{9,5},{10,... | collective-permute-start | bytes 786440 | tf_op jit(solution)/shard_map/ppermute | solution.py:55
  189.5 6.4 %collective-permute-start.38 = (bf16[128,1024]{1,0:T(8,128)(2,1)S(1)}, bf16[128,1024]{1,0:T(8,128)(2,1)S(1)}, u32[]{:S(2)}, u32[]{:S(2)}) collective-permute-start(bf16[128,1024]{1,0:T(8,128)(2,1)S(1)} %collective-permute-done.36), channel_id=1, source_target_pairs={{0,4},{1,3},{2,0},{3,7},{4,8},{5,1},{6,2},{7,11},{8,12},{9,5},{10,... | collective-permute-start | bytes 786440 | tf_op jit(solution)/shard_map/ppermute | solution.py:55
  190.3 6.8 %collective-permute-start.37 = (bf16[128,1024]{1,0:T(8,128)(2,1)S(1)}, bf16[128,1024]{1,0:T(8,128)(2,1)S(1)}, u32[]{:S(2)}, u32[]{:S(2)}) collective-permute-start(bf16[128,1024]{1,0:T(8,128)(2,1)S(1)} %collective-permute-done.36), channel_id=1, source_target_pairs={{0,1},{1,0},{2,3},{3,2},{4,5},{5,4},{6,7},{7,6},{8,9},{9,8},{10,11... | collective-permute-start | bytes 786440 | tf_op jit(solution)/shard_map/ppermute | solution.py:58
  195.8 6.4 %collective-permute-start.40 = (bf16[128,1024]{1,0:T(8,128)(2,1)S(1)}, bf16[128,1024]{1,0:T(8,128)(2,1)S(1)}, u32[]{:S(2)}, u32[]{:S(2)}) collective-permute-start(bf16[128,1024]{1,0:T(8,128)(2,1)S(1)} %collective-permute-done.38), channel_id=1, source_target_pairs={{0,4},{1,3},{2,0},{3,7},{4,8},{5,1},{6,2},{7,11},{8,12},{9,5},{10,... | collective-permute-start | bytes 786440 | tf_op jit(solution)/shard_map/ppermute | solution.py:55
  196.6 6.8 %collective-permute-start.39 = (bf16[128,1024]{1,0:T(8,128)(2,1)S(1)}, bf16[128,1024]{1,0:T(8,128)(2,1)S(1)}, u32[]{:S(2)}, u32[]{:S(2)}) collective-permute-start(bf16[128,1024]{1,0:T(8,128)(2,1)S(1)} %collective-permute-done.38), channel_id=1, source_target_pairs={{0,1},{1,0},{2,3},{3,2},{4,5},{5,4},{6,7},{7,6},{8,9},{9,8},{10,11... | collective-permute-start | bytes 786440 | tf_op jit(solution)/shard_map/ppermute | solution.py:58
  202.2 5.0 %collective-permute-start.42 = (bf16[128,512]{1,0:T(8,128)(2,1)S(1)}, bf16[128,512]{1,0:T(8,128)(2,1)S(1)}, u32[]{:S(2)}, u32[]{:S(2)}) collective-permute-start(bf16[128,512]{1,0:T(8,128)(2,1)S(1)} %constant_dynamic-slice_fusion.2), channel_id=1, source_target_pairs={{0,4},{1,3},{2,0},{3,7},{4,8},{5,1},{6,2},{7,11},{8,12},{9,5},{10,... | collective-permute-start | bytes 393224 | tf_op jit(solution)/shard_map/ppermute | solution.py:55
  203.1 5.6 %collective-permute-start.41 = (bf16[128,1024]{1,0:T(8,128)(2,1)S(1)}, bf16[128,1024]{1,0:T(8,128)(2,1)S(1)}, u32[]{:S(2)}, u32[]{:S(2)}) collective-permute-start(bf16[128,1024]{1,0:T(8,128)(2,1)S(1)} %collective-permute-done.40), channel_id=1, source_target_pairs={{0,1},{1,0},{2,3},{3,2},{4,5},{5,4},{6,7},{7,6},{8,9},{9,8},{10,11... | collective-permute-start | bytes 786440 | tf_op jit(solution)/shard_map/ppermute | solution.py:58
  207.2 1.3 collective-permute-start.43

commit v2 on v0

v2 whole, which is shorter than its diff:
```python
import functools
import math

import jax
import jax.numpy as jnp
from jax import lax
from jax.experimental import pallas as pl
from jax.experimental.pallas import tpu as pltpu
from jax.sharding import PartitionSpec as P

BLK = 128
EPSILON = 1e-05
MASKED = -1e30
LANES = 128
TILE = 16
BF16 = jnp.bfloat16
F32 = jnp.float32
VMEM = pl.BlockSpec(memory_space=pltpu.VMEM)
ANYWHERE = pl.BlockSpec(memory_space=pl.ANY)
SCALARS = pl.BlockSpec(memory_space=pltpu.SMEM)


FREE = pl.CostEstimate(flops=0, bytes_accessed=0, transcendentals=0)


class Ring:
    def __init__(self, devices, columns):
        self.chips = devices // 2
        self.rounds = self.chips // 2
        self.snake = columns == 2 and self.chips % 2 == 0
        if self.snake:
            self.order = list(range(0, self.chips, 2)) + list(range(1, self.chips, 2))[::-1]
        else:
            self.order = list(range(self.chips))

    def locate(self, key_share):
        device = lax.axis_index("ctx")
        core, chip = device % 2, device // 2
        half = self.chips // 2
        if self.snake:
            place = jnp.where(chip % 2 == 0, chip // 2, self.chips - 1 - chip // 2)
        else:
            place = chip
        names, values = ["self", "pair"], [device, device + 1 - 2 * core]
        for step in range(-self.rounds, self.rounds + 1):
            owner = (place - (1 - 2 * core) * step + self.chips) % self.chips
            if self.snake:
                owner = jnp.where(owner < half, 2 * owner, 2 * (self.chips - 1 - owner) + 1)
            names += [(step, True), (step, False), step]
            values += [2 * owner + core, 2 * owner + 1 - core, owner // key_share]
        values = lax.optimization_barrier([x.astype(jnp.int32) for x in values])
        self.numbers = dict(zip(names, values))
        return values

    def number(self, name):
        return self.numbers[name].reshape(1)

    def send(self, block, way):
        route = []
        for place in range(self.chips):
            for core in (0, 1):
                to = self.order[(place + (way if core == 0 else -way)) % self.chips]
                route.append((self.order[place] * 2 + core, to * 2 + core))
        return lax.ppermute(block, "ctx", sorted(route))

    def swap(self, block):
        return lax.ppermute(block, "ctx", [(i, i ^ 1) for i in range(2 * self.chips)])


def after(value, *others):
    return lax.optimization_barrier((value, *others))[0]


def near(x):
    return pltpu.with_memory_space_constraint(x, pltpu.VMEM)


def far(x):
    return pltpu.with_memory_space_constraint(x, pltpu.HBM)


def limit(megabytes):
    return pltpu.CompilerParams(vmem_limit_bytes=megabytes * 1024 * 1024)


def stat_rows(rows):
    return -(-3 * (rows // LANES) // TILE) * TILE


def diagonal():
    shape = (LANES, LANES)
    return lax.broadcasted_iota(jnp.int32, shape, 0) == lax.broadcasted_iota(jnp.int32, shape, 1)


def pack_stats(stats):
    high = [x.astype(BF16).astype(F32) for x in stats]
    rest = [x - h for x, h in zip(stats, high)]
    middle = [x.astype(BF16).astype(F32) for x in rest]
    low = [x - h for x, h in zip(rest, middle)]
    parts = high + middle + low
    parts += [jnp.zeros_like(stats[0])] * (-len(parts) % TILE)
    return jnp.concatenate(parts, axis=0).astype(BF16)


def unpack_stats(ref, rows):
    blocks = rows // LANES
    packed = ref[pl.ds(rows, stat_rows(rows)), :].astype(F32)
    return packed[:blocks] + packed[blocks : 2 * blocks] + packed[2 * blocks : 3 * blocks]


def fetch_columns(group, sources, targets, sems):
    columns = pl.ds(pl.multiple_of(group * LANES, LANES), LANES)
    tokens = sources[0].shape[0]
    copies = []
    for i, source in enumerate(sources):
        target = targets[i // 2].at[pl.ds((i % 2) * tokens, tokens), :]
        copies.append(pltpu.make_async_copy(source.at[:, columns], target, sems.at[i]))
        copies[-1].start()
    return copies


def prepare_kernel(this, pair, weight, last, weight_out, onehot, bias, sem):
    copy = pltpu.make_async_copy(weight, weight_out, sem)
    copy.start()
    shape = onehot.shape
    block = lax.broadcasted_iota(jnp.int32, shape, 0) // BLK
    lane = lax.broadcasted_iota(jnp.int32, shape, 1)
    onehot[...] = (block == lane).astype(F32).astype(BF16)
    blocks = shape[0] // BLK // 2
    lane = lax.broadcasted_iota(jnp.int32, bias.shape, 1)
    place = jnp.where(
        lane < blocks, this[0] * blocks + lane, (pair[0] - 1) * blocks + lane
    )
    bias[...] = jnp.where(place <= last[...], 0.0, MASKED).astype(BF16)
    copy.wait()


def prepare(ring, weight, last, tokens):
    queries = last.shape[0]
    return pl.pallas_call(
        prepare_kernel,
        out_shape=[
            pltpu.VMEM(weight.shape, BF16),
            pltpu.VMEM((tokens, LANES), BF16),
            pltpu.VMEM((queries, LANES), BF16),
        ],
        in_specs=[SCALARS, SCALARS, ANYWHERE, VMEM],
        out_specs=[VMEM] * 3,
        scratch_shapes=[pltpu.SemaphoreType.DMA],
        compiler_params=limit(8),
        cost_estimate=FREE,
        name="prepare",
    )(ring.number("self"), ring.number("pair"), far(weight), near(last))


def stage_kernel(source, target, sem):
    copy = pltpu.make_async_copy(source, target, sem)
    copy.start()
    copy.wait()


def stage(weight):
    return pl.pallas_call(
        stage_kernel,
        out_shape=pltpu.VMEM(weight.shape, weight.dtype),
        in_specs=[ANYWHERE],
        out_specs=VMEM,
        scratch_shapes=[pltpu.SemaphoreType.DMA],
        compiler_params=limit(8),
        cost_estimate=FREE,
        name="stage",
    )(far(weight))


def fetch_kernel(head, k0, k1, v0, v1, key, value, sems):
    for copy in fetch_columns(head[0], (k0, k1, v0, v1), (key, value), sems):
        copy.wait()


def fetch(head, cache):
    shape = pltpu.VMEM((2 * cache[0].shape[0], LANES), BF16)
    return pl.pallas_call(
        fetch_kernel,
        out_shape=[shape, shape],
        in_specs=[SCALARS] + [ANYWHERE] * 4,
        out_specs=[VMEM] * 2,
        scratch_shapes=[pltpu.SemaphoreType.DMA((4,))],
        compiler_params=limit(8),
        cost_estimate=FREE,
        name="fetch",
    )(head, far(cache[0]), cache[1], far(cache[2]), cache[3])


def attend_kernel(chunk, parts, following, q, bias, onehot, key, value, k0, k1, v0, v1, *refs):
    outs, (next_key, next_value, sems) = refs[:parts], refs[parts:]
    copies = fetch_columns(following[0], (k0, k1, v0, v1), (next_key, next_value), sems)
    rows = q.shape[0] // parts
    diag = diagonal()
    biases = jnp.concatenate([bias[...]] * (chunk // bias.shape[0]), axis=0)
    for part, out in enumerate(outs):
        stats = []
        for start in range(0, rows, chunk):
            query = jnp.concatenate(
                [q[pl.ds(part * rows + start, chunk), :], biases], axis=1
            )
            keys = jnp.concatenate([key[...], onehot[...]], axis=1)
            scores = lax.dot_general(
                query, keys, (((1,), (1,)), ((), ())), preferred_element_type=F32
            )
            peak = jnp.max(scores, axis=1, keepdims=True)
            weights = jnp.exp2(scores - peak).astype(BF16)
            values = jnp.concatenate([value[...], jnp.ones(value.shape, BF16)], axis=1)
            sums = jnp.dot(weights, values, preferred_element_type=F32)
            total = sums[:, LANES:]
            out[pl.ds(start, chunk), :] = (sums[:, :LANES] / total).astype(BF16)
            level = peak + jnp.log2(total)
            for b in range(chunk // LANES):
                block = level[b * LANES : (b + 1) * LANES]
                stats.append(jnp.sum(jnp.where(diag, block, 0.0), axis=0, keepdims=True))
        out[pl.ds(rows, stat_rows(rows)), :] = pack_stats(stats)
    for copy in copies:
        copy.wait()


def attend(following, q, parts, bias, onehot, head, cache):
    rows, width = q.shape[0] // parts, q.shape[1]
    chunk = math.gcd(rows, 256)
    shape = pltpu.VMEM(head[0].shape, BF16)
    out = pl.pallas_call(
        functools.partial(attend_kernel, chunk, parts),
        out_shape=[pltpu.VMEM((rows + stat_rows(rows), width), BF16)] * parts + [shape, shape],
        in_specs=[SCALARS] + [VMEM] * 5 + [ANYWHERE] * 4,
        out_specs=[VMEM] * (parts + 2),
        scratch_shapes=[pltpu.SemaphoreType.DMA((4,))],
        compiler_params=limit(16),
        cost_estimate=FREE,
        name="attend",
    )(following, *[near(x) for x in (q, bias, onehot, *head)], far(cache[0]), cache[1], far(cache[2]), cache[3])
    return out[:parts], out[parts:]


def spread(diag, row):
    high = row.astype(BF16).astype(F32)
    ones = jnp.ones((LANES, LANES), BF16)
    return sum(
        jnp.dot(jnp.where(diag, x, 0.0).astype(BF16), ones, preferred_element_type=F32)
        for x in (high, row - high)
    )


def merged(diag, block, one, one_stat, two, two_stat):
    peak = jnp.maximum(one_stat, two_stat)
    one_part, two_part = jnp.exp2(one_stat - peak), jnp.exp2(two_stat - peak)
    total = one_part + two_part
    share = spread(diag, one_part / total)
    here = pl.ds(block * LANES, LANES)
    one, two = one[here, :].astype(F32), two[here, :].astype(F32)
    return two + share * (one - two), peak + jnp.log2(total)


def merge_kernel(rows, one, two, out):
    diag = diagonal()
    one_stats, two_stats = unpack_stats(one, rows), unpack_stats(two, rows)
    stats = []
    for b in range(rows // LANES):
        value, stat = merged(diag, b, one, one_stats[b : b + 1], two, two_stats[b : b + 1])
        out[pl.ds(b * LANES, LANES), :] = value.astype(BF16)
        stats.append(stat)
    out[pl.ds(rows, stat_rows(rows)), :] = pack_stats(stats)


def merge(rows, one, two):
    return pl.pallas_call(
        functools.partial(merge_kernel, rows),
        out_shape=pltpu.VMEM(two.shape, BF16),
        in_specs=[VMEM, VMEM],
        out_specs=VMEM,
        cost_estimate=FREE,
        compiler_params=limit(8),
        name="merge",
    )(near(one), near(two))


def finish_kernel(rows, queries, *refs):
    diag = diagonal()
    for half in range(2):
        parts, out = refs[3 * half : 3 * half + 3], refs[6 + half]
        width = parts[0].shape[1]
        stats = [unpack_stats(part, rows) for part in parts]
        for b in range(rows // LANES):
            here = pl.ds(b * LANES, LANES)
            levels = [stat[b : b + 1] for stat in stats]
            peak = functools.reduce(jnp.maximum, levels)
            shares = [jnp.exp2(level - peak) for level in levels]
            total = sum(shares)
            value = sum(
                spread(diag, share / total) * part[here, :].astype(F32)
                for share, part in zip(shares, parts)
            ).astype(BF16)
            for piece in range(LANES // queries):
                head = (b * LANES) // queries + piece
                out[:, pl.ds(head * width, width)] = value[piece * queries : (piece + 1) * queries]


def finish(rows, queries, own, other):
    width = own[0].shape[1]
    shape = pltpu.VMEM((queries, rows // queries * width), BF16)
    return pl.pallas_call(
        functools.partial(finish_kernel, rows, queries),
        out_shape=[shape, shape],
        in_specs=[VMEM] * 6,
        out_specs=[VMEM] * 2,
        cost_estimate=FREE,
        compiler_params=limit(8),
        name="finish",
    )(*[near(x) for x in (*own, *other)])


def head_norm_kernel(features, scale, sums, squares, gain, out):
    queries = sums.shape[0]
    width = gain.shape[1]
    factor = lax.rsqrt(jnp.sum(squares[...], axis=1, keepdims=True) / features + EPSILON)
    gains = gain[...].astype(F32) * scale
    for head in range(sums.shape[1] // width):
        value = sums[:, pl.ds(head * width, width)] * factor
        mean = jnp.mean(value * value, axis=1, keepdims=True)
        out[pl.ds(head * queries, queries), :] = (
            value * lax.rsqrt(mean + EPSILON) * gains
        ).astype(BF16)


def head_norm(sums, squares, gain, features):
    queries, width = sums.shape[0], gain.shape[0]
    heads = sums.shape[1] // width
    return pl.pallas_call(
        functools.partial(head_norm_kernel, features, width**-0.5 * math.log2(math.e)),
        out_shape=pltpu.VMEM((heads * queries, width), BF16),
        in_specs=[VMEM] * 3,
        out_specs=VMEM,
        cost_estimate=FREE,
        compiler_params=limit(8),
        name="head_norm",
    )(near(sums), near(squares), near(gain[None, :]))


def project_kernel(count, queries, carried, begun, *refs):
    blocks, parts = refs[:count], refs[count : 2 * count]
    gains, row = (parts, queries) if carried else (refs[2 * count : 3 * count], queries + 1)
    rest = refs[(2 if carried else 3) * count :]
    weight, state, (sums, squares) = rest[0], rest[1:-2], rest[-2:]
    total, square = (state[0][...], state[1][...]) if begun else (0.0, 0.0)
    for block, part, gain in zip(blocks, parts, gains):
        width = part.shape[1]
        values = part[...][:queries].astype(F32)
        scaled = (values * gain[...][row : row + 1].astype(F32)).astype(BF16)
        piece = weight[pl.ds(pl.multiple_of(block[0] * width, width), width), :]
        total += jnp.dot(scaled, piece, preferred_element_type=F32)
        for lane in range(0, width, LANES):
            square += values[:, lane : lane + LANES] * values[:, lane : lane + LANES]
    sums[...] = total
    squares[...] = square


def project(queries, blocks, parts, gains, weight, state):
    arrays = [*parts, *(gains or ()), weight, *(state or ())]
    return pl.pallas_call(
        functools.partial(project_kernel, len(parts), queries, not gains, bool(state)),
        out_shape=[
            pltpu.VMEM((queries, weight.shape[1]), F32),
            pltpu.VMEM((queries, LANES), F32),
        ],
        in_specs=[SCALARS] * len(blocks) + [VMEM] * len(arrays),
        out_specs=[VMEM] * 2,
        compiler_params=limit(8),
        cost_estimate=FREE,
        name="project",
    )(*blocks, *[near(x) for x in arrays])


def gather_project(ring, queries, own, other, carriers, weight, beside=()):
    arrived, waiting, state = {}, [], None
    for step in range(ring.rounds + 1):
        last = step == ring.rounds
        parts = [(step, True, own)] + ([] if last else [(step, False, other)])
        if not last:
            own = ring.send(own if state is None else after(own, state[0]), 1)
        if step < ring.rounds - 1:
            other = ring.send(other, 1)
        if step > 0:
            for _, mine, part in list(parts):
                opposite = ring.swap(part)
                if step == 1 and mine and beside:
                    opposite, *beside[:] = lax.optimization_barrier((opposite, *beside))
                parts.append((-step, not mine, opposite))
        for at, mine, part in parts:
            arrived[at, mine] = part
            waiting.append((at, mine))
        if last or step % 3 == 2:
            state = project(
                queries,
                [ring.number(name) for name in waiting],
                [arrived[name] for name in waiting],
                carriers and [carriers[name] for name in waiting],
                weight,
                state,
            )
            waiting = []
    return state[0], state[1], arrived


def mix_kernel(count, *refs):
    blocks, (one, two, one_weight, two_weight) = refs[:count], refs[count : count + 4]
    outs, (pieces, sems) = refs[count + 4 : -2], refs[-2:]
    width = outs[0].shape[1]
    copies = []
    for i, block in enumerate(blocks):
        columns = pl.ds(pl.multiple_of(block[0] * width, width), width)
        for j, weight in enumerate((one_weight, two_weight)):
            copies.append(
                pltpu.make_async_copy(weight.at[:, columns], pieces.at[i, j], sems.at[i, j])
            )
            copies[-1].start()
    for i, out in enumerate(outs):
        value = 0.0
        for j, rows in enumerate((one, two)):
            copies[2 * i + j].wait()
            value += jnp.dot(rows[...], pieces[i, j], preferred_element_type=F32)
        out[...] = value.astype(out.dtype)


def mix(blocks, width, kind, one, two, one_weight, two_weight):
    queries, depth = one.shape
    return pl.pallas_call(
        functools.partial(mix_kernel, len(blocks)),
        out_shape=[pltpu.VMEM((queries, width), kind)] * len(blocks),
        in_specs=[SCALARS] * len(blocks) + [VMEM, VMEM, ANYWHERE, ANYWHERE],
        out_specs=[VMEM] * len(blocks),
        scratch_shapes=[
            pltpu.VMEM((len(blocks), 2, depth, width), BF16),
            pltpu.SemaphoreType.DMA((len(blocks), 2)),
        ],
        compiler_params=limit(16),
        cost_estimate=FREE,
        name="mix",
    )(*blocks, near(one), near(two), far(one_weight), two_weight)


def add_kernel(*refs):
    rows = refs[-1].shape[0]
    refs[-1][...] = sum(ref[...][:rows].astype(F32) for ref in refs[:-1]).astype(BF16)


def add(*parts):
    return pl.pallas_call(
        add_kernel,
        out_shape=pltpu.VMEM(parts[0].shape, BF16),
        in_specs=[VMEM] * len(parts),
        out_specs=VMEM,
        compiler_params=limit(8),
        cost_estimate=FREE,
        name="add",
    )(*[near(x) for x in parts])


def join_kernel(one, two, out):
    rows = one.shape[0]
    out[:rows] = one[...]
    out[rows:] = two[...]


def join(one, two):
    return pl.pallas_call(
        join_kernel,
        out_shape=pltpu.VMEM((2 * one.shape[0], one.shape[1]), one.dtype),
        in_specs=[VMEM, VMEM],
        out_specs=VMEM,
        compiler_params=limit(8),
        cost_estimate=FREE,
        name="join",
    )(near(one), near(two))


def first_half_kernel(both, out):
    out[...] = both[: out.shape[0]]


def first_half(both):
    return pl.pallas_call(
        first_half_kernel,
        out_shape=pltpu.VMEM((both.shape[0] // 2, both.shape[1]), both.dtype),
        in_specs=[VMEM],
        out_specs=VMEM,
        compiler_params=limit(8),
        cost_estimate=FREE,
        name="first_half",
    )(near(both))


def on_device(
    columns,
    hidden,
    attn_gain,
    q_weight,
    q_gain,
    key_cache,
    value_cache,
    block_limit,
    out_weight,
    next_gain,
    next_weight,
):
    ring = Ring(lax.axis_size("ctx"), columns)
    rounds = ring.rounds
    queries, here = hidden.shape
    features = q_weight.shape[0]
    head_dim = q_gain.shape[0]
    heads_here = q_weight.shape[1] // head_dim
    rows = heads_here * queries
    kv_heads = key_cache.shape[1] // head_dim
    group_size = heads_here * 2 * ring.chips // kv_heads

    numbers = ring.locate(group_size // (2 * heads_here))

    row = jnp.arange(queries + 2, dtype=jnp.int32)[:, None]
    own = jnp.where(
        row < queries,
        jnp.pad(hidden, ((0, 2), (0, 0))),
        jnp.where(row == queries, attn_gain[None, :], next_gain[None, :]),
    )
    last = jnp.broadcast_to(block_limit[:, None], (queries, LANES))
    own, last = after(own, *numbers), after(last, *numbers)
    other, other_keys = lax.optimization_barrier((ring.swap(own), ring.swap(key_cache)))
    beside = [ring.swap(value_cache)]
    near_weight, onehot, bias = prepare(ring, q_weight, last, 2 * key_cache.shape[0])
    sums, squares, carriers = gather_project(
        ring, queries, own, other, None, near_weight, beside
    )
    cache = (key_cache, other_keys, value_cache, *beside)
    own_heads = head_norm(sums, squares, q_gain, features)
    travelling = join(own_heads, ring.swap(own_heads))
    other_weight = ring.swap(after(out_weight, travelling))

    partials = []
    done = own_heads
    head = fetch(ring.number(0), cache)
    for step in range(rounds + 1):
        if step < rounds:
            block = travelling if step < rounds - 1 else first_half(travelling)
            coming = ring.send(after(block, done), 1)
        following = ring.number(min(step + 1, rounds))
        if step == 0:
            parts, head = attend(following, own_heads, 1, bias, onehot, head, cache)
            local_other = ring.swap(parts[0])
        else:
            count = 2 if step < rounds else 1
            parts, head = attend(following, travelling, count, bias, onehot, head, cache)
        partials.append(parts)
        done = parts[0]
        travelling = coming
    own = ring.send(partials[rounds][0], -1)
    other = ring.send(partials[rounds - 1][1], -1)
    for step in range(rounds - 1, 0, -1):
        own = ring.send(merge(rows, own, partials[step][0]), -1)
        if step > 1:
            other = ring.send(merge(rows, other, partials[step - 1][1]), -1)
    own_far, other_far = ring.swap(own), ring.swap(other)
    attended, attended_other = finish(
        rows, queries, (own, other_far, partials[0][0]), (other, own_far, local_other)
    )

    def mixed(kind, places):
        blocks = [ring.number(place) for place in places]
        weights = (out_weight, other_weight)
        parts = mix(blocks, here, kind, attended, attended_other, *weights)
        return dict(zip(places, parts))

    first = [(rounds, True), (rounds - 1, False)]
    places = [(step, mine) for step in range(rounds - 1, -1, -1) for mine in (True, False)]
    shares = mixed(BF16, first)
    own, other = (ring.send(shares[place], -1) for place in first)
    shares = mixed(F32, [place for place in places if place not in first])
    near_weight = stage(after(next_weight, shares[0, True]))
    for step in range(rounds - 1, 0, -1):
        if step == rounds - 2:
            own, near_weight = lax.optimization_barrier((own, near_weight))
        own = ring.send(add(shares[step, True], own), -1)
        if step > 1:
            other = ring.send(add(shares[step - 1, False], other), -1)
    own_far, other_far = ring.swap(own), ring.swap(other)
    new_own = add(shares[0, True], own, other_far, carriers[0, True])
    new_other = add(shares[0, False], other, own_far, carriers[0, False])

    sums, squares, _ = gather_project(
        ring, queries, new_own, new_other, carriers, near_weight
    )
    factor = lax.rsqrt(jnp.sum(squares, axis=1, keepdims=True) / features + EPSILON)
    return new_own, (sums * factor).astype(BF16)


def solution(mesh):
    in_specs = (
        P("groups", "ctx"),
        P("ctx"),
        P(None, "ctx"),
        P(),
        P(("groups", "ctx"), None),
        P(("groups", "ctx"), None),
        P("groups"),
        P("ctx", None),
        P("ctx"),
        P(None, "ctx"),
    )
    out_specs = (P("groups", "ctx"), P("groups", "ctx"))
    columns = 2 if mesh.shape["groups"] == 2 else 1
    return jax.shard_map(
        functools.partial(on_device, columns),
        mesh=mesh,
        in_specs=in_specs,
        out_specs=out_specs,
        check_vma=False,
    )
```

time: 442 us -> 140 us (0.32)
  waiting for transfers between devices: 245 us -> 50.2 us
  matrix products: 71.6 us -> 0 us
  blocking collectives: 42.3 us -> 0 us
  Pallas kernels: 0 us -> 40.9 us
  local copies, waits for them, and re-layouts: 39.4 us -> 1.4 us
  starting transfers between devices: 6.7 us -> 44 us
  other arithmetic: 18.6 us -> 1.9 us
  between operations: 13.9 us -> 1.02 us
    ppermute x64 -> x56, waiting for transfers between devices: 131 us -> 50.2 us  [the longest x32 40.4 us: send(): return lax.ppermute(block, 'ctx', sorted(route))]
    dot_general x35 -> x0, matrix products: 71.6 us -> none  [the longest x16 26.9 us: visit(): jnp.dot(expo.astype(jnp.bfloat16), values, preferred_element_type=jnp.flo...]
    reduce_scatter x1 -> x0, waiting for transfers between devices: 70.2 us -> none  [on_device(): lax.psum_scatter(lax.dot_general(out_weight, attended, (((0,), (1,)), (()...]
    all_gather x2 -> x0, waiting for transfers between devices: 43.8 us -> none  [normalize_project(): lax.all_gather(share, 'ctx', axis=1, tiled=True)]
    all_gather x2 -> x0, blocking collectives: 42.3 us -> none  [normalize_project(): lax.all_gather(gain_share, 'ctx', axis=0, tiled=True)]
    pallas_call x0 -> x30, Pallas kernels: none -> 40.9 us  [the longest x5 22.1 us: attend(): pl.pallas_call(functools.partial(attend_kernel, chunk, parts), out_shape=...]
    broadcast_in_dim x48 -> x1, local copies, waits for them, and re-layouts: 38.2 us -> 0.73 us  [on_device(): last = jnp.broadcast_to(block_limit[:, None], (queries, LANES))]
    ppermute x64 -> x56, starting transfers between devices: 6.58 us -> 44 us  [the longest x32 41 us: send(): return lax.ppermute(block, 'ctx', sorted(route))]
  transfers between devices with their start and end apart: 67 -> 56, of which waited for: 19 -> 30; matrix products, arithmetic and copies ran while one was open for 0% -> 2% of each run, Pallas kernels for 0% -> 27%
where the time goes in v2:
time: 140 us; the launch traced here: 139 us
  waiting for transfers between devices  50.2 us (36%)
  starting transfers between devices  44 us (31%)
  Pallas kernels  40.9 us (29%)
  other arithmetic  1.9 us (1%)
    ppermute x32, starting transfers between devices, send(): return lax.ppermute(block, 'ctx', sorted(route))  41 us
    ppermute x32, waiting for transfers between devices, send(): return lax.ppermute(block, 'ctx', sorted(route))  40.4 us
    pallas_call x5, Pallas kernels, attend(): pl.pallas_call(functools.partial(attend_kernel, chunk, parts), out_shape=...  22.1 us
    ppermute x24, waiting for transfers between devices, swap(): lax.ppermute(block, 'ctx', [(i, i ^ 1) for i in range(2 * self.chips)])  9.72 us
    pallas_call x2, Pallas kernels, mix(): pl.pallas_call(functools.partial(mix_kernel, len(blocks)), out_shape=[plt...  5.45 us
    pallas_call x1, Pallas kernels, prepare(): pl.pallas_call(prepare_kernel, out_shape=[pltpu.VMEM(weight.shape, BF16),...  3.4 us
    pallas_call x1, Pallas kernels, stage(): pl.pallas_call(stage_kernel, out_shape=pltpu.VMEM(weight.shape, weight.dt...  3.39 us
    pallas_call x4, Pallas kernels, project(): pl.pallas_call(functools.partial(project_kernel, len(parts), queries, not...  3.02 us
  transfers between devices with their start and end apart: 56, of which 30 were waited for; matrix products, arithmetic and copies ran while one was open for 2% of the time, Pallas kernels for 27%

profile of v2, /device:TPU:0, one launch (start us, length us, event | category | flops | bytes accessed | tf_op | source)
XLA Modules:
  0.0 139.4 jit_solution(13614003742839387949)
XLA Ops:
  1.2 1.0 select_select_fusion.refs_10_.refs_3_.refs_20_
  2.8 2.7 %collective-permute-start = (bf16[130,512]{1,0:T(8,128)(2,1)S(1)}, bf16[130,512]{1,0:T(8,128)(2,1)S(1)}, u32[]{:S(2)}, u32[]{:S(2)}) collective-permute-start(bf16[130,512]{1,0:T(8,128)(2,1)S(1)} %select_select_fusion.refs_10_.refs_3_.refs_20_), channel_id=1, source_target_pairs={{0,4},{1,3},{2,0},{3,7},{4,8},{5,1},{6,2},{7,11},{8,12},{9,5},{10,... | collective-permute-start | bytes 399368 | tf_op jit(solution)/shard_map/ppermute | solution.py:64
  5.4 5.1 %collective-permute-done.3.refs_11_.refs_3_.refs_21_ = bf16[130,512]{1,0:T(8,128)(2,1)S(1)} collective-permute-done((bf16[130,512]{1,0:T(8,128)(2,1)S(1)}, bf16[130,512]{1,0:T(8,128)(2,1)S(1)}, u32[]{:S(2)}, u32[]{:S(2)}) %collective-permute-start.3) | collective-permute-done | bytes 133152 | tf_op jit(solution)/shard_map/ppermute | solution.py:67
  10.5 2.9 %collective-permute-start.5 = (bf16[130,512]{1,0:T(8,128)(2,1)S(1)}, bf16[130,512]{1,0:T(8,128)(2,1)S(1)}, u32[]{:S(2)}, u32[]{:S(2)}) collective-permute-start(bf16[130,512]{1,0:T(8,128)(2,1)S(1)} %collective-permute-done.3.refs_11_.refs_3_.refs_21_), channel_id=1, source_target_pairs={{0,4},{1,3},{2,0},{3,7},{4,8},{5,1},{6,2},{7,11},{8,12},{9,5},{10,... | collective-permute-start | bytes 399368 | tf_op jit(solution)/shard_map/ppermute | solution.py:64
  13.5 1.6 %collective-permute-start.1 = (bf16[130,512]{1,0:T(8,128)(2,1)S(1)}, bf16[130,512]{1,0:T(8,128)(2,1)S(1)}, u32[]{:S(2)}, u32[]{:S(2)}) collective-permute-start(bf16[130,512]{1,0:T(8,128)(2,1)S(1)} %collective-permute-done.refs_12_.refs_22_), channel_id=1, source_target_pairs={{0,4},{1,3},{2,0},{3,7},{4,8},{5,1},{6,2},{7,11},{8,12},{9,5},{10,... | collective-permute-start | bytes 399368 | tf_op jit(solution)/shard_map/ppermute | solution.py:64
  15.0 1.4 %collective-permute-done.5.refs_13_.refs_23_ = bf16[130,512]{1,0:T(8,128)(2,1)S(1)} collective-permute-done((bf16[130,512]{1,0:T(8,128)(2,1)S(1)}, bf16[130,512]{1,0:T(8,128)(2,1)S(1)}, u32[]{:S(2)}, u32[]{:S(2)}) %collective-permute-start.5) | collective-permute-done | bytes 133152 | tf_op jit(solution)/shard_map/ppermute | solution.py:64
  16.4 2.1 %collective-permute-start.6 = (bf16[130,512]{1,0:T(8,128)(2,1)S(1)}, bf16[130,512]{1,0:T(8,128)(2,1)S(1)}, u32[]{:S(2)}, u32[]{:S(2)}) collective-permute-start(bf16[130,512]{1,0:T(8,128)(2,1)S(1)} %collective-permute-done.5.refs_13_.refs_23_), channel_id=1, source_target_pairs={{0,4},{1,3},{2,0},{3,7},{4,8},{5,1},{6,2},{7,11},{8,12},{9,5},{10,... | collective-permute-start | bytes 399368 | tf_op jit(solution)/shard_map/ppermute | solution.py:64
  19.0 2.5 %collective-permute-done.6.refs_17_.refs_27_ = bf16[130,512]{1,0:T(8,128)(2,1)S(1)} collective-permute-done((bf16[130,512]{1,0:T(8,128)(2,1)S(1)}, bf16[130,512]{1,0:T(8,128)(2,1)S(1)}, u32[]{:S(2)}, u32[]{:S(2)}) %collective-permute-start.6) | collective-permute-done | bytes 133152 | tf_op jit(solution)/shard_map/ppermute | solution.py:64
  21.5 2.1 %collective-permute-start.2 = (bf16[130,512]{1,0:T(8,128)(2,1)S(1)}, bf16[130,512]{1,0:T(8,128)(2,1)S(1)}, u32[]{:S(2)}, u32[]{:S(2)}) collective-permute-start(bf16[130,512]{1,0:T(8,128)(2,1)S(1)} %collective-permute-done.1.refs_16_.refs_26_), channel_id=1, source_target_pairs={{0,4},{1,3},{2,0},{3,7},{4,8},{5,1},{6,2},{7,11},{8,12},{9,5},{10,... | collective-permute-start | bytes 399368 | tf_op jit(solution)/shard_map/ppermute | solution.py:64
  23.6 0.7 broadcast_in_dim.49.last
  24.3 3.4 %prepare.1 = (bf16[8192,512]{1,0:T(8,128)(2,1)S(1)}, bf16[3072,128]{1,0:T(8,128)(2,1)S(1)}, bf16[128,128]{1,0:T(8,128)(2,1)S(1)}) custom-call(s32[1]{0:T(128)} %bitcast.17.this, s32[1]{0:T(128)} %bitcast.18.pair, bf16[8192,512]{1,0:T(8,128)(2,1)} %weight.1, s32[128,128]{1,0:T(8,128)S(1)} %broadcast_in_dim.49.last), custom_call_target="tpu_custom_call" | custom-call | tf_op jit(solution)/shard_map/prepare/pallas_call | solution.py:140
  27.7 1.6 %collective-permute-start.7 = (bf16[130,512]{1,0:T(8,128)(2,1)S(1)}, bf16[130,512]{1,0:T(8,128)(2,1)S(1)}, u32[]{:S(2)}, u32[]{:S(2)}) collective-permute-start(bf16[130,512]{1,0:T(8,128)(2,1)S(1)} %collective-permute-done.6.refs_17_.refs_27_), channel_id=1, source_target_pairs={{0,4},{1,3},{2,0},{3,7},{4,8},{5,1},{6,2},{7,11},{8,12},{9,5},{10,... | collective-permute-start | bytes 399368 | tf_op jit(solution)/shard_map/ppermute | solution.py:64
  29.4 0.9 project.4
  30.3 1.6 %collective-permute-start.15 = (bf16[130,512]{1,0:T(8,128)(2,1)S(1)}, bf16[130,512]{1,0:T(8,128)(2,1)S(1)}, u32[]{:S(2)}, u32[]{:S(2)}) collective-permute-start(bf16[130,512]{1,0:T(8,128)(2,1)S(1)} %collective-permute-done.2.refs_6_.refs_12_), channel_id=1, source_target_pairs={{0,4},{1,3},{2,0},{3,7},{4,8},{5,1},{6,2},{7,11},{8,12},{9,5},{10,... | collective-permute-start | bytes 399368 | tf_op jit(solution)/shard_map/ppermute | solution.py:64
  32.0 0.9 collective-permute-done.7.refs_7_.refs_13_
  32.8 2.6 %collective-permute-done.15.refs_10_.refs_16_ = bf16[130,512]{1,0:T(8,128)(2,1)S(1)} collective-permute-done((bf16[130,512]{1,0:T(8,128)(2,1)S(1)}, bf16[130,512]{1,0:T(8,128)(2,1)S(1)}, u32[]{:S(2)}, u32[]{:S(2)}) %collective-permute-start.15) | collective-permute-done | bytes 133152 | tf_op jit(solution)/shard_map/ppermute | solution.py:64
  35.5 1.3 collective-permute-done.16.refs_11_.refs_17_
  37.9 1.2 collective-permute-done.17.two
  39.4 1.6 %collective-permute-start.18 = (bf16[1024,128]{1,0:T(8,128)(2,1)S(1)}, bf16[1024,128]{1,0:T(8,128)(2,1)S(1)}, u32[]{:S(2)}, u32[]{:S(2)}) collective-permute-start(bf16[1024,128]{1,0:T(8,128)(2,1)S(1)} %join.1), channel_id=1, source_target_pairs={{0,4},{1,3},{2,0},{3,7},{4,8},{5,1},{6,2},{7,11},{8,12},{9,5},{10,... | collective-permute-start | bytes 786440 | tf_op jit(solution)/shard_map/ppermute | solution.py:64
  40.9 1.3 fetch.1
  42.3 3.1 %attend.5 = (bf16[528,128]{1,0:T(8,128)(2,1)S(1)}, bf16[3072,128]{1,0:T(8,128)(2,1)S(1)}, bf16[3072,128]{1,0:T(8,128)(2,1)S(1)}) custom-call(s32[1]{0:T(128)} %bitcast.20.following, bf16[512,128]{1,0:T(8,128)(2,1)S(1)} %head_norm.1.one.q, bf16[128,128]{1,0:T(8,128)(2,1)S(1)} %get-tuple-element.127.bias, bf16[3072,128]{1,0:T(8,128)(2,1)S(1)} %get-tuple-element.128.onehot, ...), custom_call_target="tpu_custom_call" | custom-call | tf_op jit(solution)/shard_map/attend/pallas_call | solution.py:229
  45.7 1.6 %collective-permute-start.19 = (bf16[1024,128]{1,0:T(8,128)(2,1)S(1)}, bf16[1024,128]{1,0:T(8,128)(2,1)S(1)}, u32[]{:S(2)}, u32[]{:S(2)}) collective-permute-start(bf16[1024,128]{1,0:T(8,128)(2,1)S(1)} %collective-permute-done.18.q), channel_id=1, source_target_pairs={{0,4},{1,3},{2,0},{3,7},{4,8},{5,1},{6,2},{7,11},{8,12},{9,5},{10,... | collective-permute-start | bytes 786440 | tf_op jit(solution)/shard_map/ppermute | solution.py:64
  47.3 4.9 %attend.6 = (bf16[528,128]{1,0:T(8,128)(2,1)S(1)}, bf16[528,128]{1,0:T(8,128)(2,1)S(1)}, bf16[3072,128]{1,0:T(8,128)(2,1)S(1)}, bf16[3072,128]{1,0:T(8,128)(2,1)S(1)}) custom-call(s32[1]{0:T(128)} %bitcast.22.following, bf16[1024,128]{1,0:T(8,128)(2,1)S(1)} %collective-permute-done.18.q, bf16[128,128]{1,0:T(8,128)(2,1)S(1)} %get-tuple-element.127.bias, ...), custom_call_target="tpu_custom_call" | custom-call | tf_op jit(solution)/shard_map/attend/pallas_call | solution.py:229
  52.3 1.8 %collective-permute-start.20 = (bf16[1024,128]{1,0:T(8,128)(2,1)S(1)}, bf16[1024,128]{1,0:T(8,128)(2,1)S(1)}, u32[]{:S(2)}, u32[]{:S(2)}) collective-permute-start(bf16[1024,128]{1,0:T(8,128)(2,1)S(1)} %collective-permute-done.19.q), channel_id=1, source_target_pairs={{0,4},{1,3},{2,0},{3,7},{4,8},{5,1},{6,2},{7,11},{8,12},{9,5},{10,... | collective-permute-start | bytes 786440 | tf_op jit(solution)/shard_map/ppermute | solution.py:64
  54.0 4.9 %attend.7 = (bf16[528,128]{1,0:T(8,128)(2,1)S(1)}, bf16[528,128]{1,0:T(8,128)(2,1)S(1)}, bf16[3072,128]{1,0:T(8,128)(2,1)S(1)}, bf16[3072,128]{1,0:T(8,128)(2,1)S(1)}) custom-call(s32[1]{0:T(128)} %bitcast.23.following, bf16[1024,128]{1,0:T(8,128)(2,1)S(1)} %collective-permute-done.19.q, bf16[128,128]{1,0:T(8,128)(2,1)S(1)} %get-tuple-element.127.bias, ...), custom_call_target="tpu_custom_call" | custom-call | tf_op jit(solution)/shard_map/attend/pallas_call | solution.py:229
  59.0 1.5 %collective-permute-start.21 = (bf16[512,128]{1,0:T(8,128)(2,1)S(1)}, bf16[512,128]{1,0:T(8,128)(2,1)S(1)}, u32[]{:S(2)}, u32[]{:S(2)}) collective-permute-start(bf16[512,128]{1,0:T(8,128)(2,1)S(1)} %first_half.1), channel_id=1, source_target_pairs={{0,4},{1,3},{2,0},{3,7},{4,8},{5,1},{6,2},{7,11},{8,12},{9,5},{10,... | collective-permute-start | bytes 393224 | tf_op jit(solution)/shard_map/ppermute | solution.py:64
  60.5 4.9 %attend.8 = (bf16[528,128]{1,0:T(8,128)(2,1)S(1)}, bf16[528,128]{1,0:T(8,128)(2,1)S(1)}, bf16[3072,128]{1,0:T(8,128)(2,1)S(1)}, bf16[3072,128]{1,0:T(8,128)(2,1)S(1)}) custom-call(s32[1]{0:T(128)} %bitcast.7.following, bf16[1024,128]{1,0:T(8,128)(2,1)S(1)} %collective-permute-done.20.both.q, bf16[128,128]{1,0:T(8,128)(2,1)S(1)} %get-tuple-element.127.bias, ...), custom_call_target="tpu_custom_call" | custom-call | tf_op jit(solution)/shard_map/attend/pallas_call | solution.py:229
  65.4 4.3 %attend.9 = (bf16[528,128]{1,0:T(8,128)(2,1)S(1)}, bf16[3072,128]{1,0:T(8,128)(2,1)}, bf16[3072,128]{1,0:T(8,128)(2,1)}) custom-call(s32[1]{0:T(128)} %bitcast.7.following, bf16[512,128]{1,0:T(8,128)(2,1)S(1)} %collective-permute-done.21.q, bf16[128,128]{1,0:T(8,128)(2,1)S(1)} %get-tuple-element.127.bias, bf16[3072,128]{1,0:T(8,128)(2,1)S(1)} %get-tuple-element.128.onehot, ...), custom_call_target="tpu_custom_call" | custom-call | tf_op jit(solution)/shard_map/attend/pallas_call | solution.py:229
  69.6 0.7 collective-permute-start.22
  70.8 3.9 %collective-permute-done.22.one = bf16[528,128]{1,0:T(8,128)(2,1)S(1)} collective-permute-done((bf16[528,128]{1,0:T(8,128)(2,1)S(1)}, bf16[528,128]{1,0:T(8,128)(2,1)S(1)}, u32[]{:S(2)}, u32[]{:S(2)}) %collective-permute-start.22) | collective-permute-done | bytes 135200 | tf_op jit(solution)/shard_map/ppermute | solution.py:64
  74.9 0.7 collective-permute-start.23
  76.4 0.7 collective-permute-start.27
  77.1 3.0 %collective-permute-done.23.one = bf16[528,128]{1,0:T(8,128)(2,1)S(1)} collective-permute-done((bf16[528,128]{1,0:T(8,128)(2,1)S(1)}, bf16[528,128]{1,0:T(8,128)(2,1)S(1)}, u32[]{:S(2)}, u32[]{:S(2)}) %collective-permute-start.23) | collective-permute-done | bytes 135200 | tf_op jit(solution)/shard_map/ppermute | solution.py:64
  80.2 0.7 collective-permute-start.24
  81.7 0.7 collective-permute-start.28
  82.3 3.0 %collective-permute-done.24.one = bf16[528,128]{1,0:T(8,128)(2,1)S(1)} collective-permute-done((bf16[528,128]{1,0:T(8,128)(2,1)S(1)}, bf16[528,128]{1,0:T(8,128)(2,1)S(1)}, u32[]{:S(2)}, u32[]{:S(2)}) %collective-permute-start.24) | collective-permute-done | bytes 135200 | tf_op jit(solution)/shard_map/ppermute | solution.py:64
  85.5 0.7 collective-permute-start.25
  86.8 3.8 %collective-permute-done.25.refs_0_ = bf16[528,128]{1,0:T(8,128)(2,1)S(1)} collective-permute-done((bf16[528,128]{1,0:T(8,128)(2,1)S(1)}, bf16[528,128]{1,0:T(8,128)(2,1)S(1)}, u32[]{:S(2)}, u32[]{:S(2)}) %collective-permute-start.25) | collective-permute-done | bytes 135200 | tf_op jit(solution)/shard_map/ppermute | solution.py:64
  90.6 1.3 collective-permute-done.30.refs_4_
  92.6 1.8 %mix.3 = (bf16[128,512]{1,0:T(8,128)(2,1)S(1)}, bf16[128,512]{1,0:T(8,128)(2,1)S(1)}) custom-call(s32[1]{0:T(128)} %bitcast.11.refs_4_.refs_0_, s32[1]{0:T(128)} %bitcast.8.refs_1_, bf16[128,512]{1,0:T(8,128)(2,1)S(1)} %get-tuple-element.152.refs_7_.refs_2_, bf16[128,512]{1,0:T(8,128)(2,1)S(1)} %get-tuple-element.153.refs_8_.refs_3_, ...), custom_call_target="tpu_custom_call" | custom-call | tf_op jit(solution)/shard_map/mix/pallas_call | solution.py:433
  95.5 3.6 %mix.2 = (f32[128,512]{1,0:T(8,128)S(1)}, f32[128,512]{1,0:T(8,128)S(1)}, f32[128,512]{1,0:T(8,128)S(1)}, f32[128,512]{1,0:T(8,128)S(1)}, f32[128,512]{1,0:T(8,1...) custom-call(s32[1]{0:T(128)} %bitcast.refs_0_, s32[1]{0:T(128)} %bitcast.1.refs_6_.refs_1_, ...), custom_call_target="tpu_custom_call" | custom-call | tf_op jit(solution)/shard_map/mix/pallas_call | solution.py:433
  100.1 3.4 %stage.1.refs_30_.refs_18_ = bf16[8192,512]{1,0:T(8,128)(2,1)S(1)} custom-call(bf16[8192,512]{1,0:T(8,128)(2,1)} %source), custom_call_target="tpu_custom_call" | custom-call | tf_op jit(solution)/shard_map/stage/pallas_call | solution.py:163
  103.5 0.9 collective-permute-start.38
  104.5 1.4 %collective-permute-start.35 = (bf16[128,512]{1,0:T(8,128)(2,1)S(1)}, bf16[128,512]{1,0:T(8,128)(2,1)S(1)}, u32[]{:S(2)}, u32[]{:S(2)}) collective-permute-start(bf16[128,512]{1,0:T(8,128)(2,1)S(1)} %add.229), channel_id=1, source_target_pairs={{0,2},{1,5},{2,6},{3,1},{4,0},{5,9},{6,10},{7,3},{8,4},{9,13},{10,... | collective-permute-start | bytes 393224 | tf_op jit(solution)/shard_map/ppermute | solution.py:64
  105.9 2.7 %collective-permute-done.38.refs_1_ = bf16[128,512]{1,0:T(8,128)(2,1)S(1)} collective-permute-done((bf16[128,512]{1,0:T(8,128)(2,1)S(1)}, bf16[128,512]{1,0:T(8,128)(2,1)S(1)}, u32[]{:S(2)}, u32[]{:S(2)}) %collective-permute-start.38) | collective-permute-done | bytes 131104 | tf_op jit(solution)/shard_map/ppermute | solution.py:64
  108.6 0.9 collective-permute-start.39
  110.0 1.0 collective-permute-start.36
  110.9 2.6 %collective-permute-done.39.refs_1_ = bf16[128,512]{1,0:T(8,128)(2,1)S(1)} collective-permute-done((bf16[128,512]{1,0:T(8,128)(2,1)S(1)}, bf16[128,512]{1,0:T(8,128)(2,1)S(1)}, u32[]{:S(2)}, u32[]{:S(2)}) %collective-permute-start.39) | collective-permute-done | bytes 131104 | tf_op jit(solution)/shard_map/ppermute | solution.py:64
  113.6 1.4 %collective-permute-done.36.refs_1_ = bf16[128,512]{1,0:T(8,128)(2,1)S(1)} collective-permute-done((bf16[128,512]{1,0:T(8,128)(2,1)S(1)}, bf16[128,512]{1,0:T(8,128)(2,1)S(1)}, u32[]{:S(2)}, u32[]{:S(2)}) %collective-permute-start.36) | collective-permute-done | bytes 131104 | tf_op jit(solution)/shard_map/ppermute | solution.py:64
  115.1 1.5 %collective-permute-start.41 = (bf16[128,512]{1,0:T(8,128)(2,1)S(1)}, bf16[128,512]{1,0:T(8,128)(2,1)S(1)}, u32[]{:S(2)}, u32[]{:S(2)}) collective-permute-start(bf16[128,512]{1,0:T(8,128)(2,1)S(1)} %add.233.refs_10_), channel_id=1, source_target_pairs={{0,4},{1,3},{2,0},{3,7},{4,8},{5,1},{6,2},{7,11},{8,12},{9,5},{10,... | collective-permute-start | bytes 393224 | tf_op jit(solution)/shard_map/ppermute | solution.py:64
  116.6 1.4 collective-permute-start.45
  118.0 2.1 %collective-permute-done.41.refs_12_ = bf16[128,512]{1,0:T(8,128)(2,1)S(1)} collective-permute-done((bf16[128,512]{1,0:T(8,128)(2,1)S(1)}, bf16[128,512]{1,0:T(8,128)(2,1)S(1)}, u32[]{:S(2)}, u32[]{:S(2)}) %collective-permute-start.41) | collective-permute-done | bytes 131104 | tf_op jit(solution)/shard_map/ppermute | solution.py:64
  120.1 1.4 %collective-permute-start.42 = (bf16[128,512]{1,0:T(8,128)(2,1)S(1)}, bf16[128,512]{1,0:T(8,128)(2,1)S(1)}, u32[]{:S(2)}, u32[]{:S(2)}) collective-permute-start(bf16[128,512]{1,0:T(8,128)(2,1)S(1)} %collective-permute-done.41.refs_12_), channel_id=1, source_target_pairs={{0,4},{1,3},{2,0},{3,7},{4,8},{5,1},{6,2},{7,11},{8,12},{9,5},{10,... | collective-permute-start | bytes 393224 | tf_op jit(solution)/shard_map/ppermute | solution.py:64
  121.6 1.3 collective-permute-start.46
  123.5 1.6 %collective-permute-done.42.refs_16_ = bf16[128,512]{1,0:T(8,128)(2,1)S(1)} collective-permute-done((bf16[128,512]{1,0:T(8,128)(2,1)S(1)}, bf16[128,512]{1,0:T(8,128)(2,1)S(1)}, u32[]{:S(2)}, u32[]{:S(2)}) %collective-permute-start.42) | collective-permute-done | bytes 131104 | tf_op jit(solution)/shard_map/ppermute | solution.py:64
  125.0 1.6 %collective-permute-done.46.refs_17_ = bf16[128,512]{1,0:T(8,128)(2,1)S(1)} collective-permute-done((bf16[128,512]{1,0:T(8,128)(2,1)S(1)}, bf16[128,512]{1,0:T(8,128)(2,1)S(1)}, u32[]{:S(2)}, u32[]{:S(2)}) %collective-permute-start.46) | collective-permute-done | bytes 131104 | tf_op jit(solution)/shard_map/ppermute | solution.py:64
  126.6 1.3 collective-permute-start.43
  127.9 1.4 %collective-permute-start.47 = (bf16[128,512]{1,0:T(8,128)(2,1)S(1)}, bf16[128,512]{1,0:T(8,128)(2,1)S(1)}, u32[]{:S(2)}, u32[]{:S(2)}) collective-permute-start(bf16[128,512]{1,0:T(8,128)(2,1)S(1)} %collective-permute-done.46.refs_17_), channel_id=1, source_target_pairs={{0,4},{1,3},{2,0},{3,7},{4,8},{5,1},{6,2},{7,11},{8,12},{9,5},{10,... | collective-permute-start | bytes 393224 | tf_op jit(solution)/shard_map/ppermute | solution.py:64
  129.4 0.9 project.6
  130.3 1.3 collective-permute-done.43.refs_6_
  131.6 1.3 collective-permute-start.54
  133.4 3.1 %collective-permute-done.54.refs_10_ = bf16[128,512]{1,0:T(8,128)(2,1)S(1)} collective-permute-done((bf16[128,512]{1,0:T(8,128)(2,1)S(1)}, bf16[128,512]{1,0:T(8,128)(2,1)S(1)}, u32[]{:S(2)}, u32[]{:S(2)}) %collective-permute-start.54) | collective-permute-done | bytes 131104 | tf_op jit(solution)/shard_map/ppermute | solution.py:64
  137.2 0.7 collective-permute-done.55.refs_11_
  138.6 0.8 multiply_convert_fusion
  (92 shorter events, 12.7 us)
Async XLA Ops:
  0.6 9.9 %collective-permute-start.4 = (bf16[1536,1024]{1,0:T(8,128)(2,1)}, bf16[1536,1024]{1,0:T(8,128)(2,1)S(1)}, u32[]{:S(2)}, u32[]{:S(2)}) collective-permute-start(bf16[1536,1024]{1,0:T(8,128)(2,1)} %k0.11), channel_id=1, source_target_pairs={{0,1},{1,0},{2,3},{3,2},{4,5},{5,4},{6,7},{7,6},{8,9},{9,8},{10,11... | collective-permute-start | bytes 9437192 | tf_op jit(solution)/shard_map/ppermute | solution.py:67
  1.1 26.6 %collective-permute-start.11 = (bf16[1536,1024]{1,0:T(8,128)(2,1)}, bf16[1536,1024]{1,0:T(8,128)(2,1)}, u32[]{:S(2)}, u32[]{:S(2)}) collective-permute-start(bf16[1536,1024]{1,0:T(8,128)(2,1)} %v0.11), channel_id=1, source_target_pairs={{0,1},{1,0},{2,3},{3,2},{4,5},{5,4},{6,7},{7,6},{8,9},{9,8},{10,11... | collective-permute-start | bytes 9437192 | tf_op jit(solution)/shard_map/ppermute | solution.py:67
  2.3 8.2 %collective-permute-start.3 = (bf16[130,512]{1,0:T(8,128)(2,1)S(1)}, bf16[130,512]{1,0:T(8,128)(2,1)S(1)}, u32[]{:S(2)}, u32[]{:S(2)}) collective-permute-start(bf16[130,512]{1,0:T(8,128)(2,1)S(1)} %select_select_fusion.refs_10_.refs_3_.refs_20_), channel_id=1, source_target_pairs={{0,1},{1,0},{2,3},{3,2},{4,5},{5,4},{6,7},{7,6},{8,9},{9,8},{10,11... | collective-permute-start | bytes 399368 | tf_op jit(solution)/shard_map/ppermute | solution.py:67
  2.8 10.7 %collective-permute-start = (bf16[130,512]{1,0:T(8,128)(2,1)S(1)}, bf16[130,512]{1,0:T(8,128)(2,1)S(1)}, u32[]{:S(2)}, u32[]{:S(2)}) collective-permute-start(bf16[130,512]{1,0:T(8,128)(2,1)S(1)} %select_select_fusion.refs_10_.refs_3_.refs_20_), channel_id=1, source_target_pairs={{0,4},{1,3},{2,0},{3,7},{4,8},{5,1},{6,2},{7,11},{8,12},{9,5},{10,... | collective-permute-start | bytes 399368 | tf_op jit(solution)/shard_map/ppermute | solution.py:64
  10.5 5.9 %collective-permute-start.5 = (bf16[130,512]{1,0:T(8,128)(2,1)S(1)}, bf16[130,512]{1,0:T(8,128)(2,1)S(1)}, u32[]{:S(2)}, u32[]{:S(2)}) collective-permute-start(bf16[130,512]{1,0:T(8,128)(2,1)S(1)} %collective-permute-done.3.refs_11_.refs_3_.refs_21_), channel_id=1, source_target_pairs={{0,4},{1,3},{2,0},{3,7},{4,8},{5,1},{6,2},{7,11},{8,12},{9,5},{10,... | collective-permute-start | bytes 399368 | tf_op jit(solution)/shard_map/ppermute | solution.py:64
  13.5 5.1 %collective-permute-start.1 = (bf16[130,512]{1,0:T(8,128)(2,1)S(1)}, bf16[130,512]{1,0:T(8,128)(2,1)S(1)}, u32[]{:S(2)}, u32[]{:S(2)}) collective-permute-start(bf16[130,512]{1,0:T(8,128)(2,1)S(1)} %collective-permute-done.refs_12_.refs_22_), channel_id=1, source_target_pairs={{0,4},{1,3},{2,0},{3,7},{4,8},{5,1},{6,2},{7,11},{8,12},{9,5},{10,... | collective-permute-start | bytes 399368 | tf_op jit(solution)/shard_map/ppermute | solution.py:64
  16.4 5.1 %collective-permute-start.6 = (bf16[130,512]{1,0:T(8,128)(2,1)S(1)}, bf16[130,512]{1,0:T(8,128)(2,1)S(1)}, u32[]{:S(2)}, u32[]{:S(2)}) collective-permute-start(bf16[130,512]{1,0:T(8,128)(2,1)S(1)} %collective-permute-done.5.refs_13_.refs_23_), channel_id=1, source_target_pairs={{0,4},{1,3},{2,0},{3,7},{4,8},{5,1},{6,2},{7,11},{8,12},{9,5},{10,... | collective-permute-start | bytes 399368 | tf_op jit(solution)/shard_map/ppermute | solution.py:64
  18.5 3.0 %collective-permute-start.10 = (bf16[130,512]{1,0:T(8,128)(2,1)S(1)}, bf16[130,512]{1,0:T(8,128)(2,1)S(1)}, u32[]{:S(2)}, u32[]{:S(2)}) collective-permute-start(bf16[130,512]{1,0:T(8,128)(2,1)S(1)} %collective-permute-done.refs_12_.refs_22_), channel_id=1, source_target_pairs={{0,1},{1,0},{2,3},{3,2},{4,5},{5,4},{6,7},{7,6},{8,9},{9,8},{10,11... | collective-permute-start | bytes 399368 | tf_op jit(solution)/shard_map/ppermute | solution.py:67
  18.5 10.8 %collective-permute-start.13 = (bf16[130,512]{1,0:T(8,128)(2,1)S(1)}, bf16[130,512]{1,0:T(8,128)(2,1)S(1)}, u32[]{:S(2)}, u32[]{:S(2)}) collective-permute-start(bf16[130,512]{1,0:T(8,128)(2,1)S(1)} %collective-permute-done.1.refs_16_.refs_26_), channel_id=1, source_target_pairs={{0,1},{1,0},{2,3},{3,2},{4,5},{5,4},{6,7},{7,6},{8,9},{9,8},{10,11... | collective-permute-start | bytes 399368 | tf_op jit(solution)/shard_map/ppermute | solution.py:67
  19.0 10.3 %collective-permute-start.12 = (bf16[130,512]{1,0:T(8,128)(2,1)S(1)}, bf16[130,512]{1,0:T(8,128)(2,1)S(1)}, u32[]{:S(2)}, u32[]{:S(2)}) collective-permute-start(bf16[130,512]{1,0:T(8,128)(2,1)S(1)} %collective-permute-done.5.refs_13_.refs_23_), channel_id=1, source_target_pairs={{0,1},{1,0},{2,3},{3,2},{4,5},{5,4},{6,7},{7,6},{8,9},{9,8},{10,11... | collective-permute-start | bytes 399368 | tf_op jit(solution)/shard_map/ppermute | solution.py:67
  21.5 7.9 %collective-permute-start.14 = (bf16[130,512]{1,0:T(8,128)(2,1)S(1)}, bf16[130,512]{1,0:T(8,128)(2,1)S(1)}, u32[]{:S(2)}, u32[]{:S(2)}) collective-permute-start(bf16[130,512]{1,0:T(8,128)(2,1)S(1)} %collective-permute-done.6.refs_17_.refs_27_), channel_id=1, source_target_pairs={{0,1},{1,0},{2,3},{3,2},{4,5},{5,4},{6,7},{7,6},{8,9},{9,8},{10,11... | collective-permute-start | bytes 399368 | tf_op jit(solution)/shard_map/ppermute | solution.py:67
  21.5 8.8 %collective-permute-start.2 = (bf16[130,512]{1,0:T(8,128)(2,1)S(1)}, bf16[130,512]{1,0:T(8,128)(2,1)S(1)}, u32[]{:S(2)}, u32[]{:S(2)}) collective-permute-start(bf16[130,512]{1,0:T(8,128)(2,1)S(1)} %collective-permute-done.1.refs_16_.refs_26_), channel_id=1, source_target_pairs={{0,4},{1,3},{2,0},{3,7},{4,8},{5,1},{6,2},{7,11},{8,12},{9,5},{10,... | collective-permute-start | bytes 399368 | tf_op jit(solution)/shard_map/ppermute | solution.py:64
  27.7 5.1 %collective-permute-start.7 = (bf16[130,512]{1,0:T(8,128)(2,1)S(1)}, bf16[130,512]{1,0:T(8,128)(2,1)S(1)}, u32[]{:S(2)}, u32[]{:S(2)}) collective-permute-start(bf16[130,512]{1,0:T(8,128)(2,1)S(1)} %collective-permute-done.6.refs_17_.refs_27_), channel_id=1, source_target_pairs={{0,4},{1,3},{2,0},{3,7},{4,8},{5,1},{6,2},{7,11},{8,12},{9,5},{10,... | collective-permute-start | bytes 399368 | tf_op jit(solution)/shard_map/ppermute | solution.py:64
  29.4 8.1 %copy-start = (bf16[128]{0:T(256)(128)(2,1)S(1)}, bf16[128]{0:T(256)(128)(2,1)}, u32[]{:S(2)}) copy-start(bf16[128]{0:T(256)(128)(2,1)} %param.13) | copy-start | bytes 772
  29.4 9.7 %slice-start = ((s8[8388608]{0:T(1024)(128)(4,1)}), s8[4194304]{0:T(1024)(128)(4,1)S(1)}, s32[]{:S(2)}) async-start(s8[8388608]{0:T(1024)(128)(4,1)} %bitcast.25), calls=%async_computation | async-start | bytes 8388608
  30.3 5.1 %collective-permute-start.15 = (bf16[130,512]{1,0:T(8,128)(2,1)S(1)}, bf16[130,512]{1,0:T(8,128)(2,1)S(1)}, u32[]{:S(2)}, u32[]{:S(2)}) collective-permute-start(bf16[130,512]{1,0:T(8,128)(2,1)S(1)} %collective-permute-done.2.refs_6_.refs_12_), channel_id=1, source_target_pairs={{0,4},{1,3},{2,0},{3,7},{4,8},{5,1},{6,2},{7,11},{8,12},{9,5},{10,... | collective-permute-start | bytes 399368 | tf_op jit(solution)/shard_map/ppermute | solution.py:64
  32.0 3.5 %collective-permute-start.8 = (bf16[130,512]{1,0:T(8,128)(2,1)S(1)}, bf16[130,512]{1,0:T(8,128)(2,1)S(1)}, u32[]{:S(2)}, u32[]{:S(2)}) collective-permute-start(bf16[130,512]{1,0:T(8,128)(2,1)S(1)} %collective-permute-done.2.refs_6_.refs_12_), channel_id=1, source_target_pairs={{0,1},{1,0},{2,3},{3,2},{4,5},{5,4},{6,7},{7,6},{8,9},{9,8},{10,11... | collective-permute-start | bytes 399368 | tf_op jit(solution)/shard_map/ppermute | solution.py:67
  32.8 2.6 %collective-permute-start.9 = (bf16[130,512]{1,0:T(8,128)(2,1)S(1)}, bf16[130,512]{1,0:T(8,128)(2,1)S(1)}, u32[]{:S(2)}, u32[]{:S(2)}) collective-permute-start(bf16[130,512]{1,0:T(8,128)(2,1)S(1)} %collective-permute-done.7.refs_7_.refs_13_), channel_id=1, source_target_pairs={{0,1},{1,0},{2,3},{3,2},{4,5},{5,4},{6,7},{7,6},{8,9},{9,8},{10,11... | collective-permute-start | bytes 399368 | tf_op jit(solution)/shard_map/ppermute | solution.py:67
  35.4 1.4 collective-permute-start.16
  36.8 2.3 %slice-start.1 = ((s8[8388608]{0:T(1024)(128)(4,1)}), s8[4194304]{0:T(1024)(128)(4,1)S(1)}, s32[]{:S(2)}) async-start(s8[8388608]{0:T(1024)(128)(4,1)} %bitcast.25), calls=%async_computation.1 | async-start | bytes 8388608
  37.7 1.4 %collective-permute-start.17 = (bf16[512,128]{1,0:T(8,128)(2,1)S(1)}, bf16[512,128]{1,0:T(8,128)(2,1)S(1)}, u32[]{:S(2)}, u32[]{:S(2)}) collective-permute-start(bf16[512,128]{1,0:T(8,128)(2,1)S(1)} %head_norm.1.one.q), channel_id=1, source_target_pairs={{0,1},{1,0},{2,3},{3,2},{4,5},{5,4},{6,7},{7,6},{8,9},{9,8},{10,11... | collective-permute-start | bytes 393224 | tf_op jit(solution)/shard_map/ppermute | solution.py:67
  39.2 53.4 %collective-permute-start.32 = (bf16[512,8192]{1,0:T(8,128)(2,1)S(1)}, bf16[512,8192]{1,0:T(8,128)(2,1)S(1)}, u32[]{:S(2)}, u32[]{:S(2)}) collective-permute-start(bf16[512,8192]{1,0:T(8,128)(2,1)S(1)} %bitcast.26), channel_id=1, source_target_pairs={{0,1},{1,0},{2,3},{3,2},{4,5},{5,4},{6,7},{7,6},{8,9},{9,8},{10,11... | collective-permute-start | bytes 25165832 | tf_op jit(solution)/shard_map/ppermute | solution.py:67
  39.4 6.4 %collective-permute-start.18 = (bf16[1024,128]{1,0:T(8,128)(2,1)S(1)}, bf16[1024,128]{1,0:T(8,128)(2,1)S(1)}, u32[]{:S(2)}, u32[]{:S(2)}) collective-permute-start(bf16[1024,128]{1,0:T(8,128)(2,1)S(1)} %join.1), channel_id=1, source_target_pairs={{0,4},{1,3},{2,0},{3,7},{4,8},{5,1},{6,2},{7,11},{8,12},{9,5},{10,... | collective-permute-start | bytes 786440 | tf_op jit(solution)/shard_map/ppermute | solution.py:64
  45.7 6.5 %collective-permute-start.19 = (bf16[1024,128]{1,0:T(8,128)(2,1)S(1)}, bf16[1024,128]{1,0:T(8,128)(2,1)S(1)}, u32[]{:S(2)}, u32[]{:S(2)}) collective-permute-start(bf16[1024,128]{1,0:T(8,128)(2,1)S(1)} %collective-permute-done.18.q), channel_id=1, source_target_pairs={{0,4},{1,3},{2,0},{3,7},{4,8},{5,1},{6,2},{7,11},{8,12},{9,5},{10,... | collective-permute-start | bytes 786440 | tf_op jit(solution)/shard_map/ppermute | solution.py:64
  52.3 6.7 %collective-permute-start.20 = (bf16[1024,128]{1,0:T(8,128)(2,1)S(1)}, bf16[1024,128]{1,0:T(8,128)(2,1)S(1)}, u32[]{:S(2)}, u32[]{:S(2)}) collective-permute-start(bf16[1024,128]{1,0:T(8,128)(2,1)S(1)} %collective-permute-done.19.q), channel_id=1, source_target_pairs={{0,4},{1,3},{2,0},{3,7},{4,8},{5,1},{6,2},{7,11},{8,12},{9,5},{10,... | collective-permute-start | bytes 786440 | tf_op jit(solution)/shard_map/ppermute | solution.py:64
  59.0 6.4 %collective-permute-start.21 = (bf16[512,128]{1,0:T(8,128)(2,1)S(1)}, bf16[512,128]{1,0:T(8,128)(2,1)S(1)}, u32[]{:S(2)}, u32[]{:S(2)}) collective-permute-start(bf16[512,128]{1,0:T(8,128)(2,1)S(1)} %first_half.1), channel_id=1, source_target_pairs={{0,4},{1,3},{2,0},{3,7},{4,8},{5,1},{6,2},{7,11},{8,12},{9,5},{10,... | collective-permute-start | bytes 393224 | tf_op jit(solution)/shard_map/ppermute | solution.py:64
  69.6 5.1 %collective-permute-start.22 = (bf16[528,128]{1,0:T(8,128)(2,1)S(1)}, bf16[528,128]{1,0:T(8,128)(2,1)S(1)}, u32[]{:S(2)}, u32[]{:S(2)}) collective-permute-start(bf16[528,128]{1,0:T(8,128)(2,1)S(1)} %get-tuple-element.147), channel_id=1, source_target_pairs={{0,2},{1,5},{2,6},{3,1},{4,0},{5,9},{6,10},{7,3},{8,4},{9,13},{10,... | collective-permute-start | bytes 405512 | tf_op jit(solution)/shard_map/ppermute | solution.py:64
  70.3 5.9 %collective-permute-start.26 = (bf16[528,128]{1,0:T(8,128)(2,1)S(1)}, bf16[528,128]{1,0:T(8,128)(2,1)S(1)}, u32[]{:S(2)}, u32[]{:S(2)}) collective-permute-start(bf16[528,128]{1,0:T(8,128)(2,1)S(1)} %get-tuple-element.149), channel_id=1, source_target_pairs={{0,2},{1,5},{2,6},{3,1},{4,0},{5,9},{6,10},{7,3},{8,4},{9,13},{10,... | collective-permute-start | bytes 405512 | tf_op jit(solution)/shard_map/ppermute | solution.py:64
  74.9 5.1 %collective-permute-start.23 = (bf16[528,128]{1,0:T(8,128)(2,1)S(1)}, bf16[528,128]{1,0:T(8,128)(2,1)S(1)}, u32[]{:S(2)}, u32[]{:S(2)}) collective-permute-start(bf16[528,128]{1,0:T(8,128)(2,1)S(1)} %merge.5), channel_id=1, source_target_pairs={{0,2},{1,5},{2,6},{3,1},{4,0},{5,9},{6,10},{7,3},{8,4},{9,13},{10,... | collective-permute-start | bytes 405512 | tf_op jit(solution)/shard_map/ppermute | solution.py:64
  76.4 5.1 %collective-permute-start.27 = (bf16[528,128]{1,0:T(8,128)(2,1)S(1)}, bf16[528,128]{1,0:T(8,128)(2,1)S(1)}, u32[]{:S(2)}, u32[]{:S(2)}) collective-permute-start(bf16[528,128]{1,0:T(8,128)(2,1)S(1)} %merge.8), channel_id=1, source_target_pairs={{0,2},{1,5},{2,6},{3,1},{4,0},{5,9},{6,10},{7,3},{8,4},{9,13},{10,... | collective-permute-start | bytes 405512 | tf_op jit(solution)/shard_map/ppermute | solution.py:64
  80.2 5.1 %collective-permute-start.24 = (bf16[528,128]{1,0:T(8,128)(2,1)S(1)}, bf16[528,128]{1,0:T(8,128)(2,1)S(1)}, u32[]{:S(2)}, u32[]{:S(2)}) collective-permute-start(bf16[528,128]{1,0:T(8,128)(2,1)S(1)} %merge.6), channel_id=1, source_target_pairs={{0,2},{1,5},{2,6},{3,1},{4,0},{5,9},{6,10},{7,3},{8,4},{9,13},{10,... | collective-permute-start | bytes 405512 | tf_op jit(solution)/shard_map/ppermute | solution.py:64
  81.7 5.1 %collective-permute-start.28 = (bf16[528,128]{1,0:T(8,128)(2,1)S(1)}, bf16[528,128]{1,0:T(8,128)(2,1)S(1)}, u32[]{:S(2)}, u32[]{:S(2)}) collective-permute-start(bf16[528,128]{1,0:T(8,128)(2,1)S(1)} %merge.9), channel_id=1, source_target_pairs={{0,2},{1,5},{2,6},{3,1},{4,0},{5,9},{6,10},{7,3},{8,4},{9,13},{10,... | collective-permute-start | bytes 405512 | tf_op jit(solution)/shard_map/ppermute | solution.py:64
  85.5 5.1 %collective-permute-start.25 = (bf16[528,128]{1,0:T(8,128)(2,1)S(1)}, bf16[528,128]{1,0:T(8,128)(2,1)S(1)}, u32[]{:S(2)}, u32[]{:S(2)}) collective-permute-start(bf16[528,128]{1,0:T(8,128)(2,1)S(1)} %merge.7), channel_id=1, source_target_pairs={{0,2},{1,5},{2,6},{3,1},{4,0},{5,9},{6,10},{7,3},{8,4},{9,13},{10,... | collective-permute-start | bytes 405512 | tf_op jit(solution)/shard_map/ppermute | solution.py:64
  86.2 4.4 %collective-permute-start.31 = (bf16[528,128]{1,0:T(8,128)(2,1)S(1)}, bf16[528,128]{1,0:T(8,128)(2,1)S(1)}, u32[]{:S(2)}, u32[]{:S(2)}) collective-permute-start(bf16[528,128]{1,0:T(8,128)(2,1)S(1)} %get-tuple-element.133.refs_2_), channel_id=1, source_target_pairs={{0,1},{1,0},{2,3},{3,2},{4,5},{5,4},{6,7},{7,6},{8,9},{9,8},{10,11... | collective-permute-start | bytes 405512 | tf_op jit(solution)/shard_map/ppermute | solution.py:67
  86.8 3.9 %collective-permute-start.29 = (bf16[528,128]{1,0:T(8,128)(2,1)S(1)}, bf16[528,128]{1,0:T(8,128)(2,1)S(1)}, u32[]{:S(2)}, u32[]{:S(2)}) collective-permute-start(bf16[528,128]{1,0:T(8,128)(2,1)S(1)} %collective-permute-done.28.refs_3_), channel_id=1, source_target_pairs={{0,1},{1,0},{2,3},{3,2},{4,5},{5,4},{6,7},{7,6},{8,9},{9,8},{10,11... | collective-permute-start | bytes 405512 | tf_op jit(solution)/shard_map/ppermute | solution.py:67
  90.6 1.4 collective-permute-start.30
  94.4 5.0 %collective-permute-start.33 = (bf16[128,512]{1,0:T(8,128)(2,1)S(1)}, bf16[128,512]{1,0:T(8,128)(2,1)S(1)}, u32[]{:S(2)}, u32[]{:S(2)}) collective-permute-start(bf16[128,512]{1,0:T(8,128)(2,1)S(1)} %get-tuple-element.159), channel_id=1, source_target_pairs={{0,2},{1,5},{2,6},{3,1},{4,0},{5,9},{6,10},{7,3},{8,4},{9,13},{10,... | collective-permute-start | bytes 393224 | tf_op jit(solution)/shard_map/ppermute | solution.py:64
  95.0 8.4 %collective-permute-start.37 = (bf16[128,512]{1,0:T(8,128)(2,1)S(1)}, bf16[128,512]{1,0:T(8,128)(2,1)S(1)}, u32[]{:S(2)}, u32[]{:S(2)}) collective-permute-start(bf16[128,512]{1,0:T(8,128)(2,1)S(1)} %get-tuple-element.164), channel_id=1, source_target_pairs={{0,2},{1,5},{2,6},{3,1},{4,0},{5,9},{6,10},{7,3},{8,4},{9,13},{10,... | collective-permute-start | bytes 393224 | tf_op jit(solution)/shard_map/ppermute | solution.py:64
  99.4 5.0 %collective-permute-start.34 = (bf16[128,512]{1,0:T(8,128)(2,1)S(1)}, bf16[128,512]{1,0:T(8,128)(2,1)S(1)}, u32[]{:S(2)}, u32[]{:S(2)}) collective-permute-start(bf16[128,512]{1,0:T(8,128)(2,1)S(1)} %add.228), channel_id=1, source_target_pairs={{0,2},{1,5},{2,6},{3,1},{4,0},{5,9},{6,10},{7,3},{8,4},{9,13},{10,... | collective-permute-start | bytes 393224 | tf_op jit(solution)/shard_map/ppermute | solution.py:64
  103.5 5.0 %collective-permute-start.38 = (bf16[128,512]{1,0:T(8,128)(2,1)S(1)}, bf16[128,512]{1,0:T(8,128)(2,1)S(1)}, u32[]{:S(2)}, u32[]{:S(2)}) collective-permute-start(bf16[128,512]{1,0:T(8,128)(2,1)S(1)} %add.231), channel_id=1, source_target_pairs={{0,2},{1,5},{2,6},{3,1},{4,0},{5,9},{6,10},{7,3},{8,4},{9,13},{10,... | collective-permute-start | bytes 393224 | tf_op jit(solution)/shard_map/ppermute | solution.py:64
  104.5 5.5 %collective-permute-start.35 = (bf16[128,512]{1,0:T(8,128)(2,1)S(1)}, bf16[128,512]{1,0:T(8,128)(2,1)S(1)}, u32[]{:S(2)}, u32[]{:S(2)}) collective-permute-start(bf16[128,512]{1,0:T(8,128)(2,1)S(1)} %add.229), channel_id=1, source_target_pairs={{0,2},{1,5},{2,6},{3,1},{4,0},{5,9},{6,10},{7,3},{8,4},{9,13},{10,... | collective-permute-start | bytes 393224 | tf_op jit(solution)/shard_map/ppermute | solution.py:64
  108.6 5.0 %collective-permute-start.39 = (bf16[128,512]{1,0:T(8,128)(2,1)S(1)}, bf16[128,512]{1,0:T(8,128)(2,1)S(1)}, u32[]{:S(2)}, u32[]{:S(2)}) collective-permute-start(bf16[128,512]{1,0:T(8,128)(2,1)S(1)} %add.232), channel_id=1, source_target_pairs={{0,2},{1,5},{2,6},{3,1},{4,0},{5,9},{6,10},{7,3},{8,4},{9,13},{10,... | collective-permute-start | bytes 393224 | tf_op jit(solution)/shard_map/ppermute | solution.py:64
  110.0 5.0 %collective-permute-start.36 = (bf16[128,512]{1,0:T(8,128)(2,1)S(1)}, bf16[128,512]{1,0:T(8,128)(2,1)S(1)}, u32[]{:S(2)}, u32[]{:S(2)}) collective-permute-start(bf16[128,512]{1,0:T(8,128)(2,1)S(1)} %add.230), channel_id=1, source_target_pairs={{0,2},{1,5},{2,6},{3,1},{4,0},{5,9},{6,10},{7,3},{8,4},{9,13},{10,... | collective-permute-start | bytes 393224 | tf_op jit(solution)/shard_map/ppermute | solution.py:64
  113.6 1.4 %collective-permute-start.40 = (bf16[128,512]{1,0:T(8,128)(2,1)S(1)}, bf16[128,512]{1,0:T(8,128)(2,1)S(1)}, u32[]{:S(2)}, u32[]{:S(2)}) collective-permute-start(bf16[128,512]{1,0:T(8,128)(2,1)S(1)} %collective-permute-done.39.refs_1_), channel_id=1, source_target_pairs={{0,1},{1,0},{2,3},{3,2},{4,5},{5,4},{6,7},{7,6},{8,9},{9,8},{10,11... | collective-permute-start | bytes 393224 | tf_op jit(solution)/shard_map/ppermute | solution.py:67
  115.0 1.6 %collective-permute-start.44 = (bf16[128,512]{1,0:T(8,128)(2,1)S(1)}, bf16[128,512]{1,0:T(8,128)(2,1)S(1)}, u32[]{:S(2)}, u32[]{:S(2)}) collective-permute-start(bf16[128,512]{1,0:T(8,128)(2,1)S(1)} %collective-permute-done.36.refs_1_), channel_id=1, source_target_pairs={{0,1},{1,0},{2,3},{3,2},{4,5},{5,4},{6,7},{7,6},{8,9},{9,8},{10,11... | collective-permute-start | bytes 393224 | tf_op jit(solution)/shard_map/ppermute | solution.py:67
  115.1 5.0 %collective-permute-start.41 = (bf16[128,512]{1,0:T(8,128)(2,1)S(1)}, bf16[128,512]{1,0:T(8,128)(2,1)S(1)}, u32[]{:S(2)}, u32[]{:S(2)}) collective-permute-start(bf16[128,512]{1,0:T(8,128)(2,1)S(1)} %add.233.refs_10_), channel_id=1, source_target_pairs={{0,4},{1,3},{2,0},{3,7},{4,8},{5,1},{6,2},{7,11},{8,12},{9,5},{10,... | collective-permute-start | bytes 393224 | tf_op jit(solution)/shard_map/ppermute | solution.py:64
  116.6 5.0 %collective-permute-start.45 = (bf16[128,512]{1,0:T(8,128)(2,1)S(1)}, bf16[128,512]{1,0:T(8,128)(2,1)S(1)}, u32[]{:S(2)}, u32[]{:S(2)}) collective-permute-start(bf16[128,512]{1,0:T(8,128)(2,1)S(1)} %add.234.refs_11_), channel_id=1, source_target_pairs={{0,4},{1,3},{2,0},{3,7},{4,8},{5,1},{6,2},{7,11},{8,12},{9,5},{10,... | collective-permute-start | bytes 393224 | tf_op jit(solution)/shard_map/ppermute | solution.py:64
  120.1 5.0 %collective-permute-start.42 = (bf16[128,512]{1,0:T(8,128)(2,1)S(1)}, bf16[128,512]{1,0:T(8,128)(2,1)S(1)}, u32[]{:S(2)}, u32[]{:S(2)}) collective-permute-start(bf16[128,512]{1,0:T(8,128)(2,1)S(1)} %collective-permute-done.41.refs_12_), channel_id=1, source_target_pairs={{0,4},{1,3},{2,0},{3,7},{4,8},{5,1},{6,2},{7,11},{8,12},{9,5},{10,... | collective-permute-start | bytes 393224 | tf_op jit(solution)/shard_map/ppermute | solution.py:64
  121.6 5.0 %collective-permute-start.46 = (bf16[128,512]{1,0:T(8,128)(2,1)S(1)}, bf16[128,512]{1,0:T(8,128)(2,1)S(1)}, u32[]{:S(2)}, u32[]{:S(2)}) collective-permute-start(bf16[128,512]{1,0:T(8,128)(2,1)S(1)} %collective-permute-done.45.refs_13_), channel_id=1, source_target_pairs={{0,4},{1,3},{2,0},{3,7},{4,8},{5,1},{6,2},{7,11},{8,12},{9,5},{10,... | collective-permute-start | bytes 393224 | tf_op jit(solution)/shard_map/ppermute | solution.py:64
  123.0 5.0 %collective-permute-start.50 = (bf16[128,512]{1,0:T(8,128)(2,1)S(1)}, bf16[128,512]{1,0:T(8,128)(2,1)S(1)}, u32[]{:S(2)}, u32[]{:S(2)}) collective-permute-start(bf16[128,512]{1,0:T(8,128)(2,1)S(1)} %collective-permute-done.41.refs_12_), channel_id=1, source_target_pairs={{0,1},{1,0},{2,3},{3,2},{4,5},{5,4},{6,7},{7,6},{8,9},{9,8},{10,11... | collective-permute-start | bytes 393224 | tf_op jit(solution)/shard_map/ppermute | solution.py:67
  123.0 6.4 %collective-permute-start.51 = (bf16[128,512]{1,0:T(8,128)(2,1)S(1)}, bf16[128,512]{1,0:T(8,128)(2,1)S(1)}, u32[]{:S(2)}, u32[]{:S(2)}) collective-permute-start(bf16[128,512]{1,0:T(8,128)(2,1)S(1)} %collective-permute-done.45.refs_13_), channel_id=1, source_target_pairs={{0,1},{1,0},{2,3},{3,2},{4,5},{5,4},{6,7},{7,6},{8,9},{9,8},{10,11... | collective-permute-start | bytes 393224 | tf_op jit(solution)/shard_map/ppermute | solution.py:67
  125.0 4.3 %collective-permute-start.52 = (bf16[128,512]{1,0:T(8,128)(2,1)S(1)}, bf16[128,512]{1,0:T(8,128)(2,1)S(1)}, u32[]{:S(2)}, u32[]{:S(2)}) collective-permute-start(bf16[128,512]{1,0:T(8,128)(2,1)S(1)} %collective-permute-done.42.refs_16_), channel_id=1, source_target_pairs={{0,1},{1,0},{2,3},{3,2},{4,5},{5,4},{6,7},{7,6},{8,9},{9,8},{10,11... | collective-permute-start | bytes 393224 | tf_op jit(solution)/shard_map/ppermute | solution.py:67
  126.6 2.8 %collective-permute-start.53 = (bf16[128,512]{1,0:T(8,128)(2,1)S(1)}, bf16[128,512]{1,0:T(8,128)(2,1)S(1)}, u32[]{:S(2)}, u32[]{:S(2)}) collective-permute-start(bf16[128,512]{1,0:T(8,128)(2,1)S(1)} %collective-permute-done.46.refs_17_), channel_id=1, source_target_pairs={{0,1},{1,0},{2,3},{3,2},{4,5},{5,4},{6,7},{7,6},{8,9},{9,8},{10,11... | collective-permute-start | bytes 393224 | tf_op jit(solution)/shard_map/ppermute | solution.py:67
  126.6 5.0 %collective-permute-start.43 = (bf16[128,512]{1,0:T(8,128)(2,1)S(1)}, bf16[128,512]{1,0:T(8,128)(2,1)S(1)}, u32[]{:S(2)}, u32[]{:S(2)}) collective-permute-start(bf16[128,512]{1,0:T(8,128)(2,1)S(1)} %collective-permute-done.42.refs_16_), channel_id=1, source_target_pairs={{0,4},{1,3},{2,0},{3,7},{4,8},{5,1},{6,2},{7,11},{8,12},{9,5},{10,... | collective-permute-start | bytes 393224 | tf_op jit(solution)/shard_map/ppermute | solution.py:64
  127.9 5.1 %collective-permute-start.47 = (bf16[128,512]{1,0:T(8,128)(2,1)S(1)}, bf16[128,512]{1,0:T(8,128)(2,1)S(1)}, u32[]{:S(2)}, u32[]{:S(2)}) collective-permute-start(bf16[128,512]{1,0:T(8,128)(2,1)S(1)} %collective-permute-done.46.refs_17_), channel_id=1, source_target_pairs={{0,4},{1,3},{2,0},{3,7},{4,8},{5,1},{6,2},{7,11},{8,12},{9,5},{10,... | collective-permute-start | bytes 393224 | tf_op jit(solution)/shard_map/ppermute | solution.py:64
  131.6 5.0 %collective-permute-start.54 = (bf16[128,512]{1,0:T(8,128)(2,1)S(1)}, bf16[128,512]{1,0:T(8,128)(2,1)S(1)}, u32[]{:S(2)}, u32[]{:S(2)}) collective-permute-start(bf16[128,512]{1,0:T(8,128)(2,1)S(1)} %collective-permute-done.43.refs_6_), channel_id=1, source_target_pairs={{0,4},{1,3},{2,0},{3,7},{4,8},{5,1},{6,2},{7,11},{8,12},{9,5},{10,... | collective-permute-start | bytes 393224 | tf_op jit(solution)/shard_map/ppermute | solution.py:64
  132.9 4.3 %collective-permute-start.48 = (bf16[128,512]{1,0:T(8,128)(2,1)S(1)}, bf16[128,512]{1,0:T(8,128)(2,1)S(1)}, u32[]{:S(2)}, u32[]{:S(2)}) collective-permute-start(bf16[128,512]{1,0:T(8,128)(2,1)S(1)} %collective-permute-done.43.refs_6_), channel_id=1, source_target_pairs={{0,1},{1,0},{2,3},{3,2},{4,5},{5,4},{6,7},{7,6},{8,9},{9,8},{10,11... | collective-permute-start | bytes 393224 | tf_op jit(solution)/shard_map/ppermute | solution.py:67
  133.0 4.2 %collective-permute-start.49 = (bf16[128,512]{1,0:T(8,128)(2,1)S(1)}, bf16[128,512]{1,0:T(8,128)(2,1)S(1)}, u32[]{:S(2)}, u32[]{:S(2)}) collective-permute-start(bf16[128,512]{1,0:T(8,128)(2,1)S(1)} %collective-permute-done.47.refs_7_), channel_id=1, source_target_pairs={{0,1},{1,0},{2,3},{3,2},{4,5},{5,4},{6,7},{7,6},{8,9},{9,8},{10,11... | collective-permute-start | bytes 393224 | tf_op jit(solution)/shard_map/ppermute | solution.py:67
  136.6 1.3 collective-permute-start.55

commit v3 on v2

--- a/solution.py
+++ b/solution.py
@@ -36,18 +36,20 @@
     def locate(self, key_share):
         device = lax.axis_index("ctx")
         core, chip = device % 2, device // 2
-        half = self.chips // 2
+        middle = self.chips // 2
         if self.snake:
             place = jnp.where(chip % 2 == 0, chip // 2, self.chips - 1 - chip // 2)
         else:
             place = chip
+        sign = 1 - 2 * ((core + place) % 2)
         names, values = ["self", "pair"], [device, device + 1 - 2 * core]
         for step in range(-self.rounds, self.rounds + 1):
-            owner = (place - (1 - 2 * core) * step + self.chips) % self.chips
+            owner = (place - sign * step + self.chips) % self.chips
             if self.snake:
-                owner = jnp.where(owner < half, 2 * owner, 2 * (self.chips - 1 - owner) + 1)
+                owner = jnp.where(owner < middle, 2 * owner, 2 * (self.chips - 1 - owner) + 1)
             names += [(step, True), (step, False), step]
-            values += [2 * owner + core, 2 * owner + 1 - core, owner // key_share]
+            half = core if step % 2 == 0 else 1 - core
+            values += [2 * owner + half, 2 * owner + 1 - half, owner // key_share]
         values = lax.optimization_barrier([x.astype(jnp.int32) for x in values])
         self.numbers = dict(zip(names, values))
         return values
@@ -59,8 +61,9 @@
         route = []
         for place in range(self.chips):
             for core in (0, 1):
-                to = self.order[(place + (way if core == 0 else -way)) % self.chips]
-                route.append((self.order[place] * 2 + core, to * 2 + core))
+                ahead = way if (core + place) % 2 == 0 else -way
+                to = self.order[(place + ahead) % self.chips]
+                route.append((self.order[place] * 2 + core, to * 2 + 1 - core))
         return lax.ppermute(block, "ctx", sorted(route))
 
     def swap(self, block):
@@ -119,9 +122,7 @@
     return copies
 
 
-def prepare_kernel(this, pair, weight, last, weight_out, onehot, bias, sem):
-    copy = pltpu.make_async_copy(weight, weight_out, sem)
-    copy.start()
+def prepare_kernel(this, pair, last, onehot, bias):
     shape = onehot.shape
     block = lax.broadcasted_iota(jnp.int32, shape, 0) // BLK
     lane = lax.broadcasted_iota(jnp.int32, shape, 1)
@@ -132,25 +133,22 @@
         lane < blocks, this[0] * blocks + lane, (pair[0] - 1) * blocks + lane
     )
     bias[...] = jnp.where(place <= last[...], 0.0, MASKED).astype(BF16)
-    copy.wait()
-
-
-def prepare(ring, weight, last, tokens):
+
+
+def prepare(ring, last, tokens):
     queries = last.shape[0]
     return pl.pallas_call(
         prepare_kernel,
         out_shape=[
-            pltpu.VMEM(weight.shape, BF16),
             pltpu.VMEM((tokens, LANES), BF16),
             pltpu.VMEM((queries, LANES), BF16),
         ],
-        in_specs=[SCALARS, SCALARS, ANYWHERE, VMEM],
-        out_specs=[VMEM] * 3,
-        scratch_shapes=[pltpu.SemaphoreType.DMA],
+        in_specs=[SCALARS, SCALARS, VMEM],
+        out_specs=[VMEM] * 2,
         compiler_params=limit(8),
         cost_estimate=FREE,
         name="prepare",
-    )(ring.number("self"), ring.number("pair"), far(weight), near(last))
+    )(ring.number("self"), ring.number("pair"), near(last))
 
 
 def stage_kernel(source, target, sem):
@@ -191,9 +189,14 @@
     )(head, far(cache[0]), cache[1], far(cache[2]), cache[3])
 
 
-def attend_kernel(chunk, parts, following, q, bias, onehot, key, value, k0, k1, v0, v1, *refs):
-    outs, (next_key, next_value, sems) = refs[:parts], refs[parts:]
-    copies = fetch_columns(following[0], (k0, k1, v0, v1), (next_key, next_value), sems)
+def attend_kernel(chunk, parts, q, bias, onehot, key, value, *refs):
+    copies = []
+    if len(refs) > parts:
+        following, *cache = refs[:5]
+        outs, (next_key, next_value, sems) = refs[5 : 5 + parts], refs[5 + parts :]
+        copies = fetch_columns(following[0], cache, (next_key, next_value), sems)
+    else:
+        outs = refs
     rows = q.shape[0] // parts
     diag = diagonal()
     biases = jnp.concatenate([bias[...]] * (chunk // bias.shape[0]), axis=0)
@@ -225,17 +228,24 @@
 def attend(following, q, parts, bias, onehot, head, cache):
     rows, width = q.shape[0] // parts, q.shape[1]
     chunk = math.gcd(rows, 256)
-    shape = pltpu.VMEM(head[0].shape, BF16)
+    shapes = [pltpu.VMEM((rows + stat_rows(rows), width), BF16)] * parts
+    arrays = [near(x) for x in (q, bias, onehot, *head)]
+    specs, scratch = [VMEM] * 5, []
+    if following is not None:
+        shapes += [pltpu.VMEM(head[0].shape, BF16)] * 2
+        arrays += [following, far(cache[0]), cache[1], far(cache[2]), cache[3]]
+        specs += [SCALARS] + [ANYWHERE] * 4
+        scratch = [pltpu.SemaphoreType.DMA((4,))]
     out = pl.pallas_call(
         functools.partial(attend_kernel, chunk, parts),
-        out_shape=[pltpu.VMEM((rows + stat_rows(rows), width), BF16)] * parts + [shape, shape],
-        in_specs=[SCALARS] + [VMEM] * 5 + [ANYWHERE] * 4,
-        out_specs=[VMEM] * (parts + 2),
-        scratch_shapes=[pltpu.SemaphoreType.DMA((4,))],
+        out_shape=shapes,
+        in_specs=specs,
+        out_specs=[VMEM] * len(shapes),
+        scratch_shapes=scratch,
         compiler_params=limit(16),
         cost_estimate=FREE,
         name="attend",
-    )(following, *[near(x) for x in (q, bias, onehot, *head)], far(cache[0]), cache[1], far(cache[2]), cache[3])
+    )(*arrays)
     return out[:parts], out[parts:]
 
 
@@ -316,39 +326,14 @@
     )(*[near(x) for x in (*own, *other)])
 
 
-def head_norm_kernel(features, scale, sums, squares, gain, out):
-    queries = sums.shape[0]
-    width = gain.shape[1]
-    factor = lax.rsqrt(jnp.sum(squares[...], axis=1, keepdims=True) / features + EPSILON)
-    gains = gain[...].astype(F32) * scale
-    for head in range(sums.shape[1] // width):
-        value = sums[:, pl.ds(head * width, width)] * factor
-        mean = jnp.mean(value * value, axis=1, keepdims=True)
-        out[pl.ds(head * queries, queries), :] = (
-            value * lax.rsqrt(mean + EPSILON) * gains
-        ).astype(BF16)
-
-
-def head_norm(sums, squares, gain, features):
-    queries, width = sums.shape[0], gain.shape[0]
-    heads = sums.shape[1] // width
-    return pl.pallas_call(
-        functools.partial(head_norm_kernel, features, width**-0.5 * math.log2(math.e)),
-        out_shape=pltpu.VMEM((heads * queries, width), BF16),
-        in_specs=[VMEM] * 3,
-        out_specs=VMEM,
-        cost_estimate=FREE,
-        compiler_params=limit(8),
-        name="head_norm",
-    )(near(sums), near(squares), near(gain[None, :]))
-
-
-def project_kernel(count, queries, carried, begun, *refs):
+def project_kernel(count, queries, features, scale, carried, begun, *refs):
     blocks, parts = refs[:count], refs[count : 2 * count]
     gains, row = (parts, queries) if carried else (refs[2 * count : 3 * count], queries + 1)
-    rest = refs[(2 if carried else 3) * count :]
-    weight, state, (sums, squares) = rest[0], rest[1:-2], rest[-2:]
-    total, square = (state[0][...], state[1][...]) if begun else (0.0, 0.0)
+    weight, *rest = refs[(2 if carried else 3) * count :]
+    total, square = 0.0, 0.0
+    if begun:
+        total, square = rest[0][...], rest[1][...]
+    rest = rest[2 if begun else 0 :]
     for block, part, gain in zip(blocks, parts, gains):
         width = part.shape[1]
         values = part[...][:queries].astype(F32)
@@ -357,92 +342,102 @@
         total += jnp.dot(scaled, piece, preferred_element_type=F32)
         for lane in range(0, width, LANES):
             square += values[:, lane : lane + LANES] * values[:, lane : lane + LANES]
-    sums[...] = total
-    squares[...] = square
-
-
-def project(queries, blocks, parts, gains, weight, state):
+    if not features:
+        rest[0][...] = total
+        rest[1][...] = square
+        return
+    factor = lax.rsqrt(jnp.sum(square, axis=1, keepdims=True) / features + EPSILON)
+    if scale is None:
+        rest[0][...] = (total * factor).astype(BF16)
+        return
+    gain, out = rest
+    width = gain.shape[1]
+    for head in range(total.shape[1] // width):
+        value = total[:, head * width : (head + 1) * width] * factor
+        mean = jnp.mean(value * value, axis=1, keepdims=True)
+        out[pl.ds(head * queries, queries), :] = (
+            value * lax.rsqrt(mean + EPSILON) * (gain[...].astype(F32) * scale)
+        ).astype(BF16)
+
+
+def project(queries, blocks, parts, gains, weight, state, last=False, head_gain=None):
     arrays = [*parts, *(gains or ()), weight, *(state or ())]
-    return pl.pallas_call(
-        functools.partial(project_kernel, len(parts), queries, not gains, bool(state)),
-        out_shape=[
-            pltpu.VMEM((queries, weight.shape[1]), F32),
-            pltpu.VMEM((queries, LANES), F32),
-        ],
+    width, scale = weight.shape[1], None
+    shapes = [pltpu.VMEM((queries, width), F32), pltpu.VMEM((queries, LANES), F32)]
+    if head_gain is not None:
+        arrays.append(head_gain[None, :])
+        depth = head_gain.shape[0]
+        scale = depth**-0.5 * math.log2(math.e)
+        shapes = [pltpu.VMEM((width // depth * queries, depth), BF16)]
+    elif last:
+        shapes = [jax.ShapeDtypeStruct((queries, width), BF16)]
+    features = weight.shape[0] if last else 0
+    return pl.pallas_call(
+        functools.partial(
+            project_kernel, len(parts), queries, features, scale, not gains, bool(state)
+        ),
+        out_shape=shapes,
         in_specs=[SCALARS] * len(blocks) + [VMEM] * len(arrays),
-        out_specs=[VMEM] * 2,
+        out_specs=[VMEM] * len(shapes),
         compiler_params=limit(8),
         cost_estimate=FREE,
         name="project",
     )(*blocks, *[near(x) for x in arrays])
 
 
-def gather_project(ring, queries, own, other, carriers, weight, beside=()):
-    arrived, waiting, state = {}, [], None
+def gather_project(ring, queries, own, other, carriers, weight, beside=None, head_gain=None):
+    arrived, waiting, swapped, state = {}, [], [], None
+
+    def flush(names, state, **how):
+        return project(
+            queries,
+            [ring.number(name) for name in names],
+            [arrived[name] for name in names],
+            carriers and [carriers[name] for name in names],
+            weight,
+            state,
+            **how,
+        )
+
     for step in range(ring.rounds + 1):
-        last = step == ring.rounds
-        parts = [(step, True, own)] + ([] if last else [(step, False, other)])
-        if not last:
-            own = ring.send(own if state is None else after(own, state[0]), 1)
+        halves = (True, False) if step < ring.rounds else (True,)
+        for mine, part in zip(halves, (own, other)):
+            arrived[step, mine] = part
+            waiting.append((step, mine))
+        if step < ring.rounds:
+            own = after(own, *(beside or {}).get(step + 1, ()), *(state or ()))
+            own = ring.send(own, 1)
         if step < ring.rounds - 1:
             other = ring.send(other, 1)
-        if step > 0:
-            for _, mine, part in list(parts):
-                opposite = ring.swap(part)
-                if step == 1 and mine and beside:
-                    opposite, *beside[:] = lax.optimization_barrier((opposite, *beside))
-                parts.append((-step, not mine, opposite))
-        for at, mine, part in parts:
-            arrived[at, mine] = part
-            waiting.append((at, mine))
-        if last or step % 3 == 2:
-            state = project(
-                queries,
-                [ring.number(name) for name in waiting],
-                [arrived[name] for name in waiting],
-                carriers and [carriers[name] for name in waiting],
-                weight,
-                state,
-            )
-            waiting = []
-    return state[0], state[1], arrived
+        for mine in halves if step else ():
+            arrived[-step, not mine] = ring.swap(arrived[step, mine])
+            swapped.append((-step, not mine))
+        if carriers and step % 3 == 2 and step < ring.rounds:
+            state, waiting = flush(waiting, state), []
+    (result,) = flush(waiting + swapped, state, last=True, head_gain=head_gain)
+    return result, arrived
 
 
 def mix_kernel(count, *refs):
     blocks, (one, two, one_weight, two_weight) = refs[:count], refs[count : count + 4]
-    outs, (pieces, sems) = refs[count + 4 : -2], refs[-2:]
-    width = outs[0].shape[1]
-    copies = []
-    for i, block in enumerate(blocks):
+    for block, out in zip(blocks, refs[count + 4 :]):
+        width = out.shape[1]
         columns = pl.ds(pl.multiple_of(block[0] * width, width), width)
-        for j, weight in enumerate((one_weight, two_weight)):
-            copies.append(
-                pltpu.make_async_copy(weight.at[:, columns], pieces.at[i, j], sems.at[i, j])
-            )
-            copies[-1].start()
-    for i, out in enumerate(outs):
-        value = 0.0
-        for j, rows in enumerate((one, two)):
-            copies[2 * i + j].wait()
-            value += jnp.dot(rows[...], pieces[i, j], preferred_element_type=F32)
+        value = jnp.dot(one[...], one_weight[:, columns], preferred_element_type=F32)
+        value += jnp.dot(two[...], two_weight[:, columns], preferred_element_type=F32)
         out[...] = value.astype(out.dtype)
 
 
 def mix(blocks, width, kind, one, two, one_weight, two_weight):
-    queries, depth = one.shape
     return pl.pallas_call(
         functools.partial(mix_kernel, len(blocks)),
-        out_shape=[pltpu.VMEM((queries, width), kind)] * len(blocks),
-        in_specs=[SCALARS] * len(blocks) + [VMEM, VMEM, ANYWHERE, ANYWHERE],
+        out_shape=[pltpu.VMEM((one.shape[0], width), kind)] * len(blocks),
+        in_specs=[SCALARS] * len(blocks) + [VMEM] * 4,
         out_specs=[VMEM] * len(blocks),
-        scratch_shapes=[
-            pltpu.VMEM((len(blocks), 2, depth, width), BF16),
-            pltpu.SemaphoreType.DMA((len(blocks), 2)),
-        ],
-        compiler_params=limit(16),
+        compiler_params=limit(8),
         cost_estimate=FREE,
         name="mix",
-    )(*blocks, near(one), near(two), far(one_weight), two_weight)
+    )(*blocks, *[near(x) for x in (one, two, one_weight, two_weight)])
 
 
 def add_kernel(*refs):
@@ -512,7 +507,6 @@
     ring = Ring(lax.axis_size("ctx"), columns)
     rounds = ring.rounds
     queries, here = hidden.shape
-    features = q_weight.shape[0]
     head_dim = q_gain.shape[0]
     heads_here = q_weight.shape[1] // head_dim
     rows = heads_here * queries
@@ -529,25 +523,28 @@
     )
     last = jnp.broadcast_to(block_limit[:, None], (queries, LANES))
     own, last = after(own, *numbers), after(last, *numbers)
-    other, other_keys = lax.optimization_barrier((ring.swap(own), ring.swap(key_cache)))
-    beside = [ring.swap(value_cache)]
-    near_weight, onehot, bias = prepare(ring, q_weight, last, 2 * key_cache.shape[0])
-    sums, squares, carriers = gather_project(
-        ring, queries, own, other, None, near_weight, beside
+    other = ring.swap(own)
+    other_keys = ring.swap(after(key_cache, other))
+    other_values = ring.swap(after(value_cache, other))
+    cache = (key_cache, other_keys, value_cache, other_values)
+    onehot, bias = prepare(ring, last, 2 * key_cache.shape[0])
+    head = fetch(ring.number(0), cache)
+    beside = {rounds - 1: (other_keys,), rounds: (*head, bias)}
+    own_heads, carriers = gather_project(
+        ring, queries, own, other, None, q_weight, beside, q_gain
     )
-    cache = (key_cache, other_keys, value_cache, *beside)
-    own_heads = head_norm(sums, squares, q_gain, features)
-    travelling = join(own_heads, ring.swap(own_heads))
-    other_weight = ring.swap(after(out_weight, travelling))
+    other_heads = ring.swap(own_heads)
+    other_weight = ring.swap(after(out_weight, other_heads))
 
     partials = []
     done = own_heads
-    head = fetch(ring.number(0), cache)
     for step in range(rounds + 1):
-        if step < rounds:
+        if step == 0:
+            coming = join(ring.send(own_heads, 1), ring.send(other_heads, 1))
+        elif step < rounds:
             block = travelling if step < rounds - 1 else first_half(travelling)
             coming = ring.send(after(block, done), 1)
-        following = ring.number(min(step + 1, rounds))
+        following = ring.number(step + 1) if step < rounds else None
         if step == 0:
             parts, head = attend(following, own_heads, 1, bias, onehot, head, cache)
             local_other = ring.swap(parts[0])
@@ -576,25 +573,17 @@
 
     first = [(rounds, True), (rounds - 1, False)]
     places = [(step, mine) for step in range(rounds - 1, -1, -1) for mine in (True, False)]
-    shares = mixed(BF16, first)
+    shares = mixed(BF16, first) | mixed(F32, [place for place in places if place not in first])
     own, other = (ring.send(shares[place], -1) for place in first)
-    shares = mixed(F32, [place for place in places if place not in first])
-    near_weight = stage(after(next_weight, shares[0, True]))
     for step in range(rounds - 1, 0, -1):
-        if step == rounds - 2:
-            own, near_weight = lax.optimization_barrier((own, near_weight))
         own = ring.send(add(shares[step, True], own), -1)
         if step > 1:
             other = ring.send(add(shares[step - 1, False], other), -1)
     own_far, other_far = ring.swap(own), ring.swap(other)
     new_own = add(shares[0, True], own, other_far, carriers[0, True])
     new_other = add(shares[0, False], other, own_far, carriers[0, False])
-
-    sums, squares, _ = gather_project(
-        ring, queries, new_own, new_other, carriers, near_weight
-    )
-    factor = lax.rsqrt(jnp.sum(squares, axis=1, keepdims=True) / features + EPSILON)
-    return new_own, (sums * factor).astype(BF16)
+    next_queries, _ = gather_project(ring, queries, new_own, new_other, carriers, next_weight)
+    return new_own, next_queries
 
 
 def solution(mesh):

time: 140 us -> 121 us (0.86)
  waiting for transfers between devices: 50.2 us -> 35.5 us
  Pallas kernels: 40.9 us -> 30.2 us
  starting transfers between devices: 44 us -> 51.5 us
    ppermute x32 -> x33, waiting for transfers between devices: 40.4 us -> 31.2 us  [send(): return lax.ppermute(block, 'ctx', sorted(route))]
    ppermute x24, starting transfers between devices: 3 us -> 10.2 us  [swap(): lax.ppermute(block, 'ctx', [(i, i ^ 1) for i in range(2 * self.chips)])]
    pallas_call x7 -> x4, Pallas kernels: 10 us -> 4.07 us  [the longest x3 3.82 us: project(): pl.pallas_call(functools.partial(project_kernel, len(parts), queries, fea...]
    ppermute x24, waiting for transfers between devices: 9.72 us -> 4.3 us  [swap(): lax.ppermute(block, 'ctx', [(i, i ^ 1) for i in range(2 * self.chips)])]
    pallas_call x2, Pallas kernels: 5.45 us -> 1.69 us  [mix(): pl.pallas_call(functools.partial(mix_kernel, len(blocks)), out_shape=[plt...]
    ppermute x32 -> x33, starting transfers between devices: 41 us -> 41.3 us  [send(): return lax.ppermute(block, 'ctx', sorted(route))]
  transfers between devices with their start and end apart: 56 -> 57, of which waited for: 30 -> 26; matrix products, arithmetic and copies ran while one was open for 2% -> 1% of each run, Pallas kernels for 27% -> 22%
where the time goes in v3:
time: 121 us
  starting transfers between devices  51.5 us (43%)
  waiting for transfers between devices  35.5 us (29%)
  Pallas kernels  30.2 us (25%)
  local copies, waits for them, and re-layouts  1.41 us (1%)
  between operations  1.33 us (1%)
    ppermute x33, starting transfers between devices, send(): return lax.ppermute(block, 'ctx', sorted(route))  41.3 us
    ppermute x33, waiting for transfers between devices, send(): return lax.ppermute(block, 'ctx', sorted(route))  31.2 us
    pallas_call x5, Pallas kernels, attend(): pl.pallas_call(functools.partial(attend_kernel, chunk, parts), out_shape=...  21.1 us
    ppermute x24, starting transfers between devices, swap(): lax.ppermute(block, 'ctx', [(i, i ^ 1) for i in range(2 * self.chips)])  10.2 us
    ppermute x24, waiting for transfers between devices, swap(): lax.ppermute(block, 'ctx', [(i, i ^ 1) for i in range(2 * self.chips)])  4.3 us
    pallas_call x3, Pallas kernels, project(): pl.pallas_call(functools.partial(project_kernel, len(parts), queries, fea...  3.82 us
  transfers between devices with their start and end apart: 57, of which 26 were waited for; matrix products, arithmetic and copies ran while one was open for 1% of the time, Pallas kernels for 22%

profile of v3, /device:TPU:0, one launch (start us, length us, event | category | flops | bytes accessed | tf_op | source)
XLA Modules:
  0.0 121.1 jit_solution(4559423920611977680)
XLA Ops:
  1.0 1.2 select_select_fusion.refs_16_.refs_3_.refs_12_
  2.7 1.0 collective-permute-done.refs_17_.refs_3_.refs_13_
  4.2 2.7 %collective-permute-start.1 = (bf16[130,512]{1,0:T(8,128)(2,1)S(1)}, bf16[130,512]{1,0:T(8,128)(2,1)S(1)}, u32[]{:S(2)}, u32[]{:S(2)}) collective-permute-start(bf16[130,512]{1,0:T(8,128)(2,1)S(1)} %select_select_fusion.refs_16_.refs_3_.refs_12_), channel_id=1, source_target_pairs={{0,5},{1,2},{2,7},{3,0},{4,1},{5,8},{6,3},{7,10},{8,13},{9,4},{10,... | collective-permute-start | bytes 399368 | tf_op jit(solution)/shard_map/ppermute | solution.py:67
  6.9 1.5 %collective-permute-start.2 = (bf16[130,512]{1,0:T(8,128)(2,1)S(1)}, bf16[130,512]{1,0:T(8,128)(2,1)S(1)}, u32[]{:S(2)}, u32[]{:S(2)}) collective-permute-start(bf16[130,512]{1,0:T(8,128)(2,1)S(1)} %collective-permute-done.refs_17_.refs_3_.refs_13_), channel_id=1, source_target_pairs={{0,5},{1,2},{2,7},{3,0},{4,1},{5,8},{6,3},{7,10},{8,13},{9,4},{10,... | collective-permute-start | bytes 399368 | tf_op jit(solution)/shard_map/ppermute | solution.py:67
  8.5 1.1 collective-permute-done.1.refs_18_.refs_14_
  9.6 2.1 %collective-permute-start.3 = (bf16[130,512]{1,0:T(8,128)(2,1)S(1)}, bf16[130,512]{1,0:T(8,128)(2,1)S(1)}, u32[]{:S(2)}, u32[]{:S(2)}) collective-permute-start(bf16[130,512]{1,0:T(8,128)(2,1)S(1)} %collective-permute-done.1.refs_18_.refs_14_), channel_id=1, source_target_pairs={{0,5},{1,2},{2,7},{3,0},{4,1},{5,8},{6,3},{7,10},{8,13},{9,4},{10,... | collective-permute-start | bytes 399368 | tf_op jit(solution)/shard_map/ppermute | solution.py:67
  11.7 1.2 %collective-permute-start.4 = (bf16[130,512]{1,0:T(8,128)(2,1)S(1)}, bf16[130,512]{1,0:T(8,128)(2,1)S(1)}, u32[]{:S(2)}, u32[]{:S(2)}) collective-permute-start(bf16[130,512]{1,0:T(8,128)(2,1)S(1)} %collective-permute-done.2.refs_19_.refs_15_), channel_id=1, source_target_pairs={{0,5},{1,2},{2,7},{3,0},{4,1},{5,8},{6,3},{7,10},{8,13},{9,4},{10,... | collective-permute-start | bytes 399368 | tf_op jit(solution)/shard_map/ppermute | solution.py:67
  13.0 1.4 %collective-permute-done.3.refs_20_.refs_16_ = bf16[130,512]{1,0:T(8,128)(2,1)S(1)} collective-permute-done((bf16[130,512]{1,0:T(8,128)(2,1)S(1)}, bf16[130,512]{1,0:T(8,128)(2,1)S(1)}, u32[]{:S(2)}, u32[]{:S(2)}) %collective-permute-start.3) | collective-permute-done | bytes 133152 | tf_op jit(solution)/shard_map/ppermute | solution.py:67
  14.4 2.1 %collective-permute-start.6 = (bf16[130,512]{1,0:T(8,128)(2,1)S(1)}, bf16[130,512]{1,0:T(8,128)(2,1)S(1)}, u32[]{:S(2)}, u32[]{:S(2)}) collective-permute-start(bf16[130,512]{1,0:T(8,128)(2,1)S(1)} %collective-permute-done.3.refs_20_.refs_16_), channel_id=1, source_target_pairs={{0,5},{1,2},{2,7},{3,0},{4,1},{5,8},{6,3},{7,10},{8,13},{9,4},{10,... | collective-permute-start | bytes 399368 | tf_op jit(solution)/shard_map/ppermute | solution.py:67
  18.0 1.0 collective-permute-start.7
  19.0 1.3 %fetch.1 = (bf16[3072,128]{1,0:T(8,128)(2,1)S(1)}, bf16[3072,128]{1,0:T(8,128)(2,1)S(1)}) custom-call(s32[1]{0:T(128)} %bitcast.16.head, bf16[1536,1024]{1,0:T(8,128)(2,1)} %refs_1_.7, bf16[1536,1024]{1,0:T(8,128)(2,1)S(1)} %collective-permute-done.5.k1.refs_2_, bf16[1536,1024]{1,0:T(8,128)(2,1)} %refs_3_.7, ...), custom_call_target="tpu_custom_call" | custom-call | tf_op jit(solution)/shard_map/fetch/pallas_call | solution.py:180
  20.3 2.0 %collective-permute-start.9 = (bf16[130,512]{1,0:T(8,128)(2,1)S(1)}, bf16[130,512]{1,0:T(8,128)(2,1)S(1)}, u32[]{:S(2)}, u32[]{:S(2)}) collective-permute-start(bf16[130,512]{1,0:T(8,128)(2,1)S(1)} %collective-permute-done.6.refs_22_.refs_20_), channel_id=1, source_target_pairs={{0,5},{1,2},{2,7},{3,0},{4,1},{5,8},{6,3},{7,10},{8,13},{9,4},{10,... | collective-permute-start | bytes 399368 | tf_op jit(solution)/shard_map/ppermute | solution.py:67
  23.3 1.6 %collective-permute-done.9.refs_24_.refs_22_ = bf16[130,512]{1,0:T(8,128)(2,1)S(1)} collective-permute-done((bf16[130,512]{1,0:T(8,128)(2,1)S(1)}, bf16[130,512]{1,0:T(8,128)(2,1)S(1)}, u32[]{:S(2)}, u32[]{:S(2)}) %collective-permute-start.9) | collective-permute-done | bytes 133152 | tf_op jit(solution)/shard_map/ppermute | solution.py:67
  25.6 1.0 collective-permute-done.16.refs_31_.refs_29_
  26.6 1.5 %project.3.q = bf16[512,128]{1,0:T(8,128)(2,1)S(1)} custom-call(s32[1]{0:T(128)} %bitcast.5.refs_0_.refs_5_, s32[1]{0:T(128)} %bitcast.6.refs_1_.refs_6_, s32[1]{0:T(128)} %bitcast.3.refs_2_.refs_3_, s32[1]{0:T(128)} %bitcast.4.refs_3_.refs_4_, s32[1]{0:T(128)} %bitcast.1.refs_4_.refs_1_, s32[1]{0:T(128)} %bitcast.2.refs_5_.refs_2_, s32[1]{0:T(128)} %bitcast.refs_6_.refs_0_, ...), custom_call_target="tpu_custom_call" | custom-call | tf_op jit(solution)/shard_map/project/pallas_call | solution.py:375
  28.5 1.0 collective-permute-done.18
  29.9 1.4 %collective-permute-start.17 = (bf16[512,128]{1,0:T(8,128)(2,1)S(1)}, bf16[512,128]{1,0:T(8,128)(2,1)S(1)}, u32[]{:S(2)}, u32[]{:S(2)}) collective-permute-start(bf16[512,128]{1,0:T(8,128)(2,1)S(1)} %project.3.q), channel_id=1, source_target_pairs={{0,5},{1,2},{2,7},{3,0},{4,1},{5,8},{6,3},{7,10},{8,13},{9,4},{10,... | collective-permute-start | bytes 393224 | tf_op jit(solution)/shard_map/ppermute | solution.py:67
  31.3 0.9 collective-permute-start.19
  32.2 3.1 %attend.5 = (bf16[528,128]{1,0:T(8,128)(2,1)S(1)}, bf16[3072,128]{1,0:T(8,128)(2,1)S(1)}, bf16[3072,128]{1,0:T(8,128)(2,1)S(1)}) custom-call(bf16[512,128]{1,0:T(8,128)(2,1)S(1)} %project.3.q, bf16[128,128]{1,0:T(8,128)(2,1)S(1)} %get-tuple-element.110.bias, bf16[3072,128]{1,0:T(8,128)(2,1)S(1)} %get-tuple-element.112.onehot, ...), custom_call_target="tpu_custom_call" | custom-call | tf_op jit(solution)/shard_map/attend/pallas_call | solution.py:239
  35.7 1.4 %collective-permute-start.20 = (bf16[1024,128]{1,0:T(8,128)(2,1)S(1)}, bf16[1024,128]{1,0:T(8,128)(2,1)S(1)}, u32[]{:S(2)}, u32[]{:S(2)}) collective-permute-start(bf16[1024,128]{1,0:T(8,128)(2,1)S(1)} %join.1.q), channel_id=1, source_target_pairs={{0,5},{1,2},{2,7},{3,0},{4,1},{5,8},{6,3},{7,10},{8,13},{9,4},{10,... | collective-permute-start | bytes 786440 | tf_op jit(solution)/shard_map/ppermute | solution.py:67
  37.1 5.0 %attend.6 = (bf16[528,128]{1,0:T(8,128)(2,1)S(1)}, bf16[528,128]{1,0:T(8,128)(2,1)S(1)}, bf16[3072,128]{1,0:T(8,128)(2,1)S(1)}, bf16[3072,128]{1,0:T(8,128)(2,1)S(1)}) custom-call(bf16[1024,128]{1,0:T(8,128)(2,1)S(1)} %join.1.q, bf16[128,128]{1,0:T(8,128)(2,1)S(1)} %get-tuple-element.110.bias, bf16[3072,128]{1,0:T(8,128)(2,1)S(1)} %get-tuple-element.112.onehot, ...), custom_call_target="tpu_custom_call" | custom-call | tf_op jit(solution)/shard_map/attend/pallas_call | solution.py:239
  42.2 1.1 collective-permute-start.21
  43.3 5.0 %attend.7 = (bf16[528,128]{1,0:T(8,128)(2,1)S(1)}, bf16[528,128]{1,0:T(8,128)(2,1)S(1)}, bf16[3072,128]{1,0:T(8,128)(2,1)S(1)}, bf16[3072,128]{1,0:T(8,128)(2,1)S(1)}) custom-call(bf16[1024,128]{1,0:T(8,128)(2,1)S(1)} %collective-permute-done.20.q, bf16[128,128]{1,0:T(8,128)(2,1)S(1)} %get-tuple-element.110.bias, ...), custom_call_target="tpu_custom_call" | custom-call | tf_op jit(solution)/shard_map/attend/pallas_call | solution.py:239
  48.4 1.1 collective-permute-start.22
  49.4 5.0 %attend.8 = (bf16[528,128]{1,0:T(8,128)(2,1)S(1)}, bf16[528,128]{1,0:T(8,128)(2,1)S(1)}, bf16[3072,128]{1,0:T(8,128)(2,1)S(1)}, bf16[3072,128]{1,0:T(8,128)(2,1)S(1)}) custom-call(bf16[1024,128]{1,0:T(8,128)(2,1)S(1)} %collective-permute-done.21.both.q, bf16[128,128]{1,0:T(8,128)(2,1)S(1)} %get-tuple-element.110.bias, ...), custom_call_target="tpu_custom_call" | custom-call | tf_op jit(solution)/shard_map/attend/pallas_call | solution.py:239
  54.4 2.9 %attend.9 = bf16[528,128]{1,0:T(8,128)(2,1)S(1)} custom-call(bf16[512,128]{1,0:T(8,128)(2,1)S(1)} %collective-permute-done.22.q, bf16[128,128]{1,0:T(8,128)(2,1)S(1)} %get-tuple-element.110.bias, bf16[3072,128]{1,0:T(8,128)(2,1)S(1)} %get-tuple-element.112.onehot, bf16[3072,128]{1,0:T(8,128)(2,1)S(1)} %get-tuple-element.125.key, ...), custom_call_target="tpu_custom_call" | custom-call | tf_op jit(solution)/shard_map/attend/pallas_call | solution.py:239
  57.4 1.0 collective-permute-start.23
  58.4 0.8 collective-permute-start.27
  59.2 2.9 %collective-permute-done.23.one = bf16[528,128]{1,0:T(8,128)(2,1)S(1)} collective-permute-done((bf16[528,128]{1,0:T(8,128)(2,1)S(1)}, bf16[528,128]{1,0:T(8,128)(2,1)S(1)}, u32[]{:S(2)}, u32[]{:S(2)}) %collective-permute-start.23) | collective-permute-done | bytes 135200 | tf_op jit(solution)/shard_map/ppermute | solution.py:67
  62.3 1.1 collective-permute-start.24
  63.7 1.1 collective-permute-start.28
  64.8 2.0 %collective-permute-done.24.one = bf16[528,128]{1,0:T(8,128)(2,1)S(1)} collective-permute-done((bf16[528,128]{1,0:T(8,128)(2,1)S(1)}, bf16[528,128]{1,0:T(8,128)(2,1)S(1)}, u32[]{:S(2)}, u32[]{:S(2)}) %collective-permute-start.24) | collective-permute-done | bytes 135200 | tf_op jit(solution)/shard_map/ppermute | solution.py:67
  67.0 1.4 %collective-permute-start.25 = (bf16[528,128]{1,0:T(8,128)(2,1)S(1)}, bf16[528,128]{1,0:T(8,128)(2,1)S(1)}, u32[]{:S(2)}, u32[]{:S(2)}) collective-permute-start(bf16[528,128]{1,0:T(8,128)(2,1)S(1)} %merge.6), channel_id=1, source_target_pairs={{0,3},{1,4},{2,1},{3,6},{4,9},{5,0},{6,11},{7,2},{8,5},{9,12},{10,... | collective-permute-start | bytes 405512 | tf_op jit(solution)/shard_map/ppermute | solution.py:67
  68.6 1.0 collective-permute-start.29
  69.7 2.1 %collective-permute-done.25.one = bf16[528,128]{1,0:T(8,128)(2,1)S(1)} collective-permute-done((bf16[528,128]{1,0:T(8,128)(2,1)S(1)}, bf16[528,128]{1,0:T(8,128)(2,1)S(1)}, u32[]{:S(2)}, u32[]{:S(2)}) %collective-permute-start.25) | collective-permute-done | bytes 135200 | tf_op jit(solution)/shard_map/ppermute | solution.py:67
  72.0 1.4 %collective-permute-start.26 = (bf16[528,128]{1,0:T(8,128)(2,1)S(1)}, bf16[528,128]{1,0:T(8,128)(2,1)S(1)}, u32[]{:S(2)}, u32[]{:S(2)}) collective-permute-start(bf16[528,128]{1,0:T(8,128)(2,1)S(1)} %merge.7), channel_id=1, source_target_pairs={{0,3},{1,4},{2,1},{3,6},{4,9},{5,0},{6,11},{7,2},{8,5},{9,12},{10,... | collective-permute-start | bytes 405512 | tf_op jit(solution)/shard_map/ppermute | solution.py:67
  74.0 2.8 %collective-permute-done.26.refs_0_ = bf16[528,128]{1,0:T(8,128)(2,1)S(1)} collective-permute-done((bf16[528,128]{1,0:T(8,128)(2,1)S(1)}, bf16[528,128]{1,0:T(8,128)(2,1)S(1)}, u32[]{:S(2)}, u32[]{:S(2)}) %collective-permute-start.26) | collective-permute-done | bytes 135200 | tf_op jit(solution)/shard_map/ppermute | solution.py:67
  76.8 0.8 collective-permute-start.31
  77.6 1.0 collective-permute-done.31.refs_4_
  80.4 1.2 collective-permute-start.38
  81.6 1.2 %mix.2 = (f32[128,512]{1,0:T(8,128)S(1)}, f32[128,512]{1,0:T(8,128)S(1)}, f32[128,512]{1,0:T(8,128)S(1)}, f32[128,512]{1,0:T(8,128)S(1)}, f32[128,512]{1,0:T(8,1...) custom-call(s32[1]{0:T(128)} %bitcast.refs_6_.refs_0_, s32[1]{0:T(128)} %bitcast.1.refs_4_.refs_1_, ...), custom_call_target="tpu_custom_call" | custom-call | tf_op jit(solution)/shard_map/mix/pallas_call | solution.py:432
  82.8 1.3 %collective-permute-done.34.refs_1_ = bf16[128,512]{1,0:T(8,128)(2,1)S(1)} collective-permute-done((bf16[128,512]{1,0:T(8,128)(2,1)S(1)}, bf16[128,512]{1,0:T(8,128)(2,1)S(1)}, u32[]{:S(2)}, u32[]{:S(2)}) %collective-permute-start.34) | collective-permute-done | bytes 131104 | tf_op jit(solution)/shard_map/ppermute | solution.py:67
  84.1 1.0 collective-permute-start.35
  86.2 2.3 %collective-permute-done.35.refs_1_ = bf16[128,512]{1,0:T(8,128)(2,1)S(1)} collective-permute-done((bf16[128,512]{1,0:T(8,128)(2,1)S(1)}, bf16[128,512]{1,0:T(8,128)(2,1)S(1)}, u32[]{:S(2)}, u32[]{:S(2)}) %collective-permute-start.35) | collective-permute-done | bytes 131104 | tf_op jit(solution)/shard_map/ppermute | solution.py:67
  88.6 1.3 %collective-permute-start.36 = (bf16[128,512]{1,0:T(8,128)(2,1)S(1)}, bf16[128,512]{1,0:T(8,128)(2,1)S(1)}, u32[]{:S(2)}, u32[]{:S(2)}) collective-permute-start(bf16[128,512]{1,0:T(8,128)(2,1)S(1)} %add.222), channel_id=1, source_target_pairs={{0,3},{1,4},{2,1},{3,6},{4,9},{5,0},{6,11},{7,2},{8,5},{9,12},{10,... | collective-permute-start | bytes 393224 | tf_op jit(solution)/shard_map/ppermute | solution.py:67
  90.0 1.0 collective-permute-start.40
  91.0 2.2 %collective-permute-done.36.refs_1_ = bf16[128,512]{1,0:T(8,128)(2,1)S(1)} collective-permute-done((bf16[128,512]{1,0:T(8,128)(2,1)S(1)}, bf16[128,512]{1,0:T(8,128)(2,1)S(1)}, u32[]{:S(2)}, u32[]{:S(2)}) %collective-permute-start.36) | collective-permute-done | bytes 131104 | tf_op jit(solution)/shard_map/ppermute | solution.py:67
  93.3 1.4 %collective-permute-start.37 = (bf16[128,512]{1,0:T(8,128)(2,1)S(1)}, bf16[128,512]{1,0:T(8,128)(2,1)S(1)}, u32[]{:S(2)}, u32[]{:S(2)}) collective-permute-start(bf16[128,512]{1,0:T(8,128)(2,1)S(1)} %add.223), channel_id=1, source_target_pairs={{0,3},{1,4},{2,1},{3,6},{4,9},{5,0},{6,11},{7,2},{8,5},{9,12},{10,... | collective-permute-start | bytes 393224 | tf_op jit(solution)/shard_map/ppermute | solution.py:67
  94.7 0.8 collective-permute-start.41
  95.4 2.6 %collective-permute-done.37.refs_1_ = bf16[128,512]{1,0:T(8,128)(2,1)S(1)} collective-permute-done((bf16[128,512]{1,0:T(8,128)(2,1)S(1)}, bf16[128,512]{1,0:T(8,128)(2,1)S(1)}, u32[]{:S(2)}, u32[]{:S(2)}) %collective-permute-start.37) | collective-permute-done | bytes 131104 | tf_op jit(solution)/shard_map/ppermute | solution.py:67
  98.0 0.8 collective-permute-start.45
  98.9 1.0 collective-permute-start.42
  99.9 1.3 %collective-permute-start.46 = (bf16[128,512]{1,0:T(8,128)(2,1)S(1)}, bf16[128,512]{1,0:T(8,128)(2,1)S(1)}, u32[]{:S(2)}, u32[]{:S(2)}) collective-permute-start(bf16[128,512]{1,0:T(8,128)(2,1)S(1)} %add.227.refs_7_), channel_id=1, source_target_pairs={{0,5},{1,2},{2,7},{3,0},{4,1},{5,8},{6,3},{7,10},{8,13},{9,4},{10,... | collective-permute-start | bytes 393224 | tf_op jit(solution)/shard_map/ppermute | solution.py:67
  101.2 2.1 %collective-permute-done.42.refs_8_ = bf16[128,512]{1,0:T(8,128)(2,1)S(1)} collective-permute-done((bf16[128,512]{1,0:T(8,128)(2,1)S(1)}, bf16[128,512]{1,0:T(8,128)(2,1)S(1)}, u32[]{:S(2)}, u32[]{:S(2)}) %collective-permute-start.42) | collective-permute-done | bytes 131104 | tf_op jit(solution)/shard_map/ppermute | solution.py:67
  103.3 1.2 %collective-permute-start.43 = (bf16[128,512]{1,0:T(8,128)(2,1)S(1)}, bf16[128,512]{1,0:T(8,128)(2,1)S(1)}, u32[]{:S(2)}, u32[]{:S(2)}) collective-permute-start(bf16[128,512]{1,0:T(8,128)(2,1)S(1)} %collective-permute-done.42.refs_8_), channel_id=1, source_target_pairs={{0,5},{1,2},{2,7},{3,0},{4,1},{5,8},{6,3},{7,10},{8,13},{9,4},{10,... | collective-permute-start | bytes 393224 | tf_op jit(solution)/shard_map/ppermute | solution.py:67
  104.7 1.1 collective-permute-start.47
  105.8 1.9 %collective-permute-done.43.refs_10_ = bf16[128,512]{1,0:T(8,128)(2,1)S(1)} collective-permute-done((bf16[128,512]{1,0:T(8,128)(2,1)S(1)}, bf16[128,512]{1,0:T(8,128)(2,1)S(1)}, u32[]{:S(2)}, u32[]{:S(2)}) %collective-permute-start.43) | collective-permute-done | bytes 131104 | tf_op jit(solution)/shard_map/ppermute | solution.py:67
  107.7 1.5 %collective-permute-start.44 = (bf16[128,512]{1,0:T(8,128)(2,1)S(1)}, bf16[128,512]{1,0:T(8,128)(2,1)S(1)}, u32[]{:S(2)}, u32[]{:S(2)}) collective-permute-start(bf16[128,512]{1,0:T(8,128)(2,1)S(1)} %collective-permute-done.43.refs_10_), channel_id=1, source_target_pairs={{0,5},{1,2},{2,7},{3,0},{4,1},{5,8},{6,3},{7,10},{8,13},{9,4},{10,... | collective-permute-start | bytes 393224 | tf_op jit(solution)/shard_map/ppermute | solution.py:67
  110.4 1.7 %collective-permute-done.44.refs_10_ = bf16[128,512]{1,0:T(8,128)(2,1)S(1)} collective-permute-done((bf16[128,512]{1,0:T(8,128)(2,1)S(1)}, bf16[128,512]{1,0:T(8,128)(2,1)S(1)}, u32[]{:S(2)}, u32[]{:S(2)}) %collective-permute-start.44) | collective-permute-done | bytes 131104 | tf_op jit(solution)/shard_map/ppermute | solution.py:67
  112.1 1.5 %collective-permute-start.49 = (bf16[128,512]{1,0:T(8,128)(2,1)S(1)}, bf16[128,512]{1,0:T(8,128)(2,1)S(1)}, u32[]{:S(2)}, u32[]{:S(2)}) collective-permute-start(bf16[128,512]{1,0:T(8,128)(2,1)S(1)} %collective-permute-done.44.refs_10_), channel_id=1, source_target_pairs={{0,5},{1,2},{2,7},{3,0},{4,1},{5,8},{6,3},{7,10},{8,13},{9,4},{10,... | collective-permute-start | bytes 393224 | tf_op jit(solution)/shard_map/ppermute | solution.py:67
  113.7 0.9 collective-permute-start.52
  115.0 1.4 %collective-permute-done.49.refs_12_ = bf16[128,512]{1,0:T(8,128)(2,1)S(1)} collective-permute-done((bf16[128,512]{1,0:T(8,128)(2,1)S(1)}, bf16[128,512]{1,0:T(8,128)(2,1)S(1)}, u32[]{:S(2)}, u32[]{:S(2)}) %collective-permute-start.49) | collective-permute-done | bytes 131104 | tf_op jit(solution)/shard_map/ppermute | solution.py:67
  116.5 0.9 collective-permute-start.56
  119.5 1.6 %project.5 = bf16[128,512]{1,0:T(8,128)(2,1)} custom-call(s32[1]{0:T(128)} %bitcast.refs_6_.refs_0_, s32[1]{0:T(128)} %bitcast.7.refs_7_.refs_1_, s32[1]{0:T(128)} %bitcast.8.refs_8_.refs_0_.refs_2_, s32[1]{0:T(128)} %bitcast.9.refs_9_.refs_3_, s32[1]{0:T(128)} %bitcast.10.refs_10_.refs_4_, s32[1]{0:T(128)} %bitcast.11.refs_11_.refs_5_, ...), custom_call_target="tpu_custom_call" | custom-call | tf_op jit(solution)/shard_map/project/pallas_call | solution.py:375
  (95 shorter events, 14.5 us)
Async XLA Ops:
  0.6 25.9 %copy-start.1 = (bf16[128]{0:T(256)(128)(2,1)S(1)}, bf16[128]{0:T(256)(128)(2,1)}, u32[]{:S(2)}) copy-start(bf16[128]{0:T(256)(128)(2,1)} %param.13) | copy-start | bytes 772
  1.0 25.5 %copy-start = (bf16[8192,512]{1,0:T(8,128)(2,1)S(1)}, bf16[8192,512]{1,0:T(8,128)(2,1)}, u32[]{:S(2)}) copy-start(bf16[8192,512]{1,0:T(8,128)(2,1)} %refs_32_.1) | copy-start | bytes 25165828
  2.2 1.5 %collective-permute-start = (bf16[130,512]{1,0:T(8,128)(2,1)S(1)}, bf16[130,512]{1,0:T(8,128)(2,1)S(1)}, u32[]{:S(2)}, u32[]{:S(2)}) collective-permute-start(bf16[130,512]{1,0:T(8,128)(2,1)S(1)} %select_select_fusion.refs_16_.refs_3_.refs_12_), channel_id=1, source_target_pairs={{0,1},{1,0},{2,3},{3,2},{4,5},{5,4},{6,7},{7,6},{8,9},{9,8},{10,11... | collective-permute-start | bytes 399368 | tf_op jit(solution)/shard_map/ppermute | solution.py:70
  3.7 10.7 %collective-permute-start.5 = (bf16[1536,1024]{1,0:T(8,128)(2,1)}, bf16[1536,1024]{1,0:T(8,128)(2,1)S(1)}, u32[]{:S(2)}, u32[]{:S(2)}) collective-permute-start(bf16[1536,1024]{1,0:T(8,128)(2,1)} %refs_1_.7), channel_id=1, source_target_pairs={{0,1},{1,0},{2,3},{3,2},{4,5},{5,4},{6,7},{7,6},{8,9},{9,8},{10,11... | collective-permute-start | bytes 9437192 | tf_op jit(solution)/shard_map/ppermute | solution.py:70
  4.1 14.9 %collective-permute-start.8 = (bf16[1536,1024]{1,0:T(8,128)(2,1)}, bf16[1536,1024]{1,0:T(8,128)(2,1)S(1)}, u32[]{:S(2)}, u32[]{:S(2)}) collective-permute-start(bf16[1536,1024]{1,0:T(8,128)(2,1)} %refs_3_.7), channel_id=1, source_target_pairs={{0,1},{1,0},{2,3},{3,2},{4,5},{5,4},{6,7},{7,6},{8,9},{9,8},{10,11... | collective-permute-start | bytes 9437192 | tf_op jit(solution)/shard_map/ppermute | solution.py:70
  4.2 5.4 %collective-permute-start.1 = (bf16[130,512]{1,0:T(8,128)(2,1)S(1)}, bf16[130,512]{1,0:T(8,128)(2,1)S(1)}, u32[]{:S(2)}, u32[]{:S(2)}) collective-permute-start(bf16[130,512]{1,0:T(8,128)(2,1)S(1)} %select_select_fusion.refs_16_.refs_3_.refs_12_), channel_id=1, source_target_pairs={{0,5},{1,2},{2,7},{3,0},{4,1},{5,8},{6,3},{7,10},{8,13},{9,4},{10,... | collective-permute-start | bytes 399368 | tf_op jit(solution)/shard_map/ppermute | solution.py:67
  6.9 4.8 %collective-permute-start.2 = (bf16[130,512]{1,0:T(8,128)(2,1)S(1)}, bf16[130,512]{1,0:T(8,128)(2,1)S(1)}, u32[]{:S(2)}, u32[]{:S(2)}) collective-permute-start(bf16[130,512]{1,0:T(8,128)(2,1)S(1)} %collective-permute-done.refs_17_.refs_3_.refs_13_), channel_id=1, source_target_pairs={{0,5},{1,2},{2,7},{3,0},{4,1},{5,8},{6,3},{7,10},{8,13},{9,4},{10,... | collective-permute-start | bytes 399368 | tf_op jit(solution)/shard_map/ppermute | solution.py:67
  9.6 4.8 %collective-permute-start.3 = (bf16[130,512]{1,0:T(8,128)(2,1)S(1)}, bf16[130,512]{1,0:T(8,128)(2,1)S(1)}, u32[]{:S(2)}, u32[]{:S(2)}) collective-permute-start(bf16[130,512]{1,0:T(8,128)(2,1)S(1)} %collective-permute-done.1.refs_18_.refs_14_), channel_id=1, source_target_pairs={{0,5},{1,2},{2,7},{3,0},{4,1},{5,8},{6,3},{7,10},{8,13},{9,4},{10,... | collective-permute-start | bytes 399368 | tf_op jit(solution)/shard_map/ppermute | solution.py:67
  11.7 6.3 %collective-permute-start.4 = (bf16[130,512]{1,0:T(8,128)(2,1)S(1)}, bf16[130,512]{1,0:T(8,128)(2,1)S(1)}, u32[]{:S(2)}, u32[]{:S(2)}) collective-permute-start(bf16[130,512]{1,0:T(8,128)(2,1)S(1)} %collective-permute-done.2.refs_19_.refs_15_), channel_id=1, source_target_pairs={{0,5},{1,2},{2,7},{3,0},{4,1},{5,8},{6,3},{7,10},{8,13},{9,4},{10,... | collective-permute-start | bytes 399368 | tf_op jit(solution)/shard_map/ppermute | solution.py:67
  14.4 5.9 %collective-permute-start.6 = (bf16[130,512]{1,0:T(8,128)(2,1)S(1)}, bf16[130,512]{1,0:T(8,128)(2,1)S(1)}, u32[]{:S(2)}, u32[]{:S(2)}) collective-permute-start(bf16[130,512]{1,0:T(8,128)(2,1)S(1)} %collective-permute-done.3.refs_20_.refs_16_), channel_id=1, source_target_pairs={{0,5},{1,2},{2,7},{3,0},{4,1},{5,8},{6,3},{7,10},{8,13},{9,4},{10,... | collective-permute-start | bytes 399368 | tf_op jit(solution)/shard_map/ppermute | solution.py:67
  17.5 4.9 %collective-permute-start.10 = (bf16[130,512]{1,0:T(8,128)(2,1)S(1)}, bf16[130,512]{1,0:T(8,128)(2,1)S(1)}, u32[]{:S(2)}, u32[]{:S(2)}) collective-permute-start(bf16[130,512]{1,0:T(8,128)(2,1)S(1)} %collective-permute-done.1.refs_18_.refs_14_), channel_id=1, source_target_pairs={{0,1},{1,0},{2,3},{3,2},{4,5},{5,4},{6,7},{7,6},{8,9},{9,8},{10,11... | collective-permute-start | bytes 399368 | tf_op jit(solution)/shard_map/ppermute | solution.py:70
  17.5 5.4 %collective-permute-start.11 = (bf16[130,512]{1,0:T(8,128)(2,1)S(1)}, bf16[130,512]{1,0:T(8,128)(2,1)S(1)}, u32[]{:S(2)}, u32[]{:S(2)}) collective-permute-start(bf16[130,512]{1,0:T(8,128)(2,1)S(1)} %collective-permute-done.2.refs_19_.refs_15_), channel_id=1, source_target_pairs={{0,1},{1,0},{2,3},{3,2},{4,5},{5,4},{6,7},{7,6},{8,9},{9,8},{10,11... | collective-permute-start | bytes 399368 | tf_op jit(solution)/shard_map/ppermute | solution.py:70
  18.0 4.8 %collective-permute-start.7 = (bf16[130,512]{1,0:T(8,128)(2,1)S(1)}, bf16[130,512]{1,0:T(8,128)(2,1)S(1)}, u32[]{:S(2)}, u32[]{:S(2)}) collective-permute-start(bf16[130,512]{1,0:T(8,128)(2,1)S(1)} %collective-permute-done.4.refs_21_.refs_17_), channel_id=1, source_target_pairs={{0,5},{1,2},{2,7},{3,0},{4,1},{5,8},{6,3},{7,10},{8,13},{9,4},{10,... | collective-permute-start | bytes 399368 | tf_op jit(solution)/shard_map/ppermute | solution.py:67
  19.0 10.5 %slice-start = ((s8[8388608]{0:T(1024)(128)(4,1)}), s8[4194304]{0:T(1024)(128)(4,1)S(1)}, s32[]{:S(2)}) async-start(s8[8388608]{0:T(1024)(128)(4,1)} %bitcast.24), calls=%async_computation | async-start | bytes 8388608
  19.0 10.5 %slice-start.1 = ((s8[8388608]{0:T(1024)(128)(4,1)}), s8[4194304]{0:T(1024)(128)(4,1)S(1)}, s32[]{:S(2)}) async-start(s8[8388608]{0:T(1024)(128)(4,1)} %bitcast.24), calls=%async_computation.1 | async-start | bytes 8388608
  20.3 4.6 %collective-permute-start.9 = (bf16[130,512]{1,0:T(8,128)(2,1)S(1)}, bf16[130,512]{1,0:T(8,128)(2,1)S(1)}, u32[]{:S(2)}, u32[]{:S(2)}) collective-permute-start(bf16[130,512]{1,0:T(8,128)(2,1)S(1)} %collective-permute-done.6.refs_22_.refs_20_), channel_id=1, source_target_pairs={{0,5},{1,2},{2,7},{3,0},{4,1},{5,8},{6,3},{7,10},{8,13},{9,4},{10,... | collective-permute-start | bytes 399368 | tf_op jit(solution)/shard_map/ppermute | solution.py:67
  22.3 3.2 %collective-permute-start.12 = (bf16[130,512]{1,0:T(8,128)(2,1)S(1)}, bf16[130,512]{1,0:T(8,128)(2,1)S(1)}, u32[]{:S(2)}, u32[]{:S(2)}) collective-permute-start(bf16[130,512]{1,0:T(8,128)(2,1)S(1)} %collective-permute-done.3.refs_20_.refs_16_), channel_id=1, source_target_pairs={{0,1},{1,0},{2,3},{3,2},{4,5},{5,4},{6,7},{7,6},{8,9},{9,8},{10,11... | collective-permute-start | bytes 399368 | tf_op jit(solution)/shard_map/ppermute | solution.py:70
  22.3 3.2 %collective-permute-start.13 = (bf16[130,512]{1,0:T(8,128)(2,1)S(1)}, bf16[130,512]{1,0:T(8,128)(2,1)S(1)}, u32[]{:S(2)}, u32[]{:S(2)}) collective-permute-start(bf16[130,512]{1,0:T(8,128)(2,1)S(1)} %collective-permute-done.4.refs_21_.refs_17_), channel_id=1, source_target_pairs={{0,1},{1,0},{2,3},{3,2},{4,5},{5,4},{6,7},{7,6},{8,9},{9,8},{10,11... | collective-permute-start | bytes 399368 | tf_op jit(solution)/shard_map/ppermute | solution.py:70
  22.8 2.7 %collective-permute-start.15 = (bf16[130,512]{1,0:T(8,128)(2,1)S(1)}, bf16[130,512]{1,0:T(8,128)(2,1)S(1)}, u32[]{:S(2)}, u32[]{:S(2)}) collective-permute-start(bf16[130,512]{1,0:T(8,128)(2,1)S(1)} %collective-permute-done.7.refs_23_.refs_21_), channel_id=1, source_target_pairs={{0,1},{1,0},{2,3},{3,2},{4,5},{5,4},{6,7},{7,6},{8,9},{9,8},{10,11... | collective-permute-start | bytes 399368 | tf_op jit(solution)/shard_map/ppermute | solution.py:70
  22.9 2.7 %collective-permute-start.14 = (bf16[130,512]{1,0:T(8,128)(2,1)S(1)}, bf16[130,512]{1,0:T(8,128)(2,1)S(1)}, u32[]{:S(2)}, u32[]{:S(2)}) collective-permute-start(bf16[130,512]{1,0:T(8,128)(2,1)S(1)} %collective-permute-done.6.refs_22_.refs_20_), channel_id=1, source_target_pairs={{0,1},{1,0},{2,3},{3,2},{4,5},{5,4},{6,7},{7,6},{8,9},{9,8},{10,11... | collective-permute-start | bytes 399368 | tf_op jit(solution)/shard_map/ppermute | solution.py:70
  24.9 1.6 %collective-permute-start.16 = (bf16[130,512]{1,0:T(8,128)(2,1)S(1)}, bf16[130,512]{1,0:T(8,128)(2,1)S(1)}, u32[]{:S(2)}, u32[]{:S(2)}) collective-permute-start(bf16[130,512]{1,0:T(8,128)(2,1)S(1)} %collective-permute-done.9.refs_24_.refs_22_), channel_id=1, source_target_pairs={{0,1},{1,0},{2,3},{3,2},{4,5},{5,4},{6,7},{7,6},{8,9},{9,8},{10,11... | collective-permute-start | bytes 399368 | tf_op jit(solution)/shard_map/ppermute | solution.py:70
  28.1 1.4 %collective-permute-start.18 = (bf16[512,128]{1,0:T(8,128)(2,1)S(1)}, bf16[512,128]{1,0:T(8,128)(2,1)S(1)}, u32[]{:S(2)}, u32[]{:S(2)}) collective-permute-start(bf16[512,128]{1,0:T(8,128)(2,1)S(1)} %project.3.q), channel_id=1, source_target_pairs={{0,1},{1,0},{2,3},{3,2},{4,5},{5,4},{6,7},{7,6},{8,9},{9,8},{10,11... | collective-permute-start | bytes 393224 | tf_op jit(solution)/shard_map/ppermute | solution.py:70
  29.5 49.6 %collective-permute-start.33 = (bf16[512,8192]{1,0:T(8,128)(2,1)S(1)}, bf16[512,8192]{1,0:T(8,128)(2,1)S(1)}, u32[]{:S(2)}, u32[]{:S(2)}) collective-permute-start(bf16[512,8192]{1,0:T(8,128)(2,1)S(1)} %bitcast.25), channel_id=1, source_target_pairs={{0,1},{1,0},{2,3},{3,2},{4,5},{5,4},{6,7},{7,6},{8,9},{9,8},{10,11... | collective-permute-start | bytes 25165832 | tf_op jit(solution)/shard_map/ppermute | solution.py:70
  29.9 5.4 %collective-permute-start.17 = (bf16[512,128]{1,0:T(8,128)(2,1)S(1)}, bf16[512,128]{1,0:T(8,128)(2,1)S(1)}, u32[]{:S(2)}, u32[]{:S(2)}) collective-permute-start(bf16[512,128]{1,0:T(8,128)(2,1)S(1)} %project.3.q), channel_id=1, source_target_pairs={{0,5},{1,2},{2,7},{3,0},{4,1},{5,8},{6,3},{7,10},{8,13},{9,4},{10,... | collective-permute-start | bytes 393224 | tf_op jit(solution)/shard_map/ppermute | solution.py:67
  31.3 4.4 %collective-permute-start.19 = (bf16[512,128]{1,0:T(8,128)(2,1)S(1)}, bf16[512,128]{1,0:T(8,128)(2,1)S(1)}, u32[]{:S(2)}, u32[]{:S(2)}) collective-permute-start(bf16[512,128]{1,0:T(8,128)(2,1)S(1)} %collective-permute-done.18), channel_id=1, source_target_pairs={{0,5},{1,2},{2,7},{3,0},{4,1},{5,8},{6,3},{7,10},{8,13},{9,4},{10,... | collective-permute-start | bytes 393224 | tf_op jit(solution)/shard_map/ppermute | solution.py:67
  35.7 6.5 %collective-permute-start.20 = (bf16[1024,128]{1,0:T(8,128)(2,1)S(1)}, bf16[1024,128]{1,0:T(8,128)(2,1)S(1)}, u32[]{:S(2)}, u32[]{:S(2)}) collective-permute-start(bf16[1024,128]{1,0:T(8,128)(2,1)S(1)} %join.1.q), channel_id=1, source_target_pairs={{0,5},{1,2},{2,7},{3,0},{4,1},{5,8},{6,3},{7,10},{8,13},{9,4},{10,... | collective-permute-start | bytes 786440 | tf_op jit(solution)/shard_map/ppermute | solution.py:67
  42.2 6.2 %collective-permute-start.21 = (bf16[1024,128]{1,0:T(8,128)(2,1)S(1)}, bf16[1024,128]{1,0:T(8,128)(2,1)S(1)}, u32[]{:S(2)}, u32[]{:S(2)}) collective-permute-start(bf16[1024,128]{1,0:T(8,128)(2,1)S(1)} %collective-permute-done.20.q), channel_id=1, source_target_pairs={{0,5},{1,2},{2,7},{3,0},{4,1},{5,8},{6,3},{7,10},{8,13},{9,4},{10,... | collective-permute-start | bytes 786440 | tf_op jit(solution)/shard_map/ppermute | solution.py:67
  48.4 6.0 %collective-permute-start.22 = (bf16[512,128]{1,0:T(8,128)(2,1)S(1)}, bf16[512,128]{1,0:T(8,128)(2,1)S(1)}, u32[]{:S(2)}, u32[]{:S(2)}) collective-permute-start(bf16[512,128]{1,0:T(8,128)(2,1)S(1)} %first_half.1), channel_id=1, source_target_pairs={{0,5},{1,2},{2,7},{3,0},{4,1},{5,8},{6,3},{7,10},{8,13},{9,4},{10,... | collective-permute-start | bytes 393224 | tf_op jit(solution)/shard_map/ppermute | solution.py:67
  57.4 4.7 %collective-permute-start.23 = (bf16[528,128]{1,0:T(8,128)(2,1)S(1)}, bf16[528,128]{1,0:T(8,128)(2,1)S(1)}, u32[]{:S(2)}, u32[]{:S(2)}) collective-permute-start(bf16[528,128]{1,0:T(8,128)(2,1)S(1)} %attend.9), channel_id=1, source_target_pairs={{0,3},{1,4},{2,1},{3,6},{4,9},{5,0},{6,11},{7,2},{8,5},{9,12},{10,... | collective-permute-start | bytes 405512 | tf_op jit(solution)/shard_map/ppermute | solution.py:67
  58.4 5.1 %collective-permute-start.27 = (bf16[528,128]{1,0:T(8,128)(2,1)S(1)}, bf16[528,128]{1,0:T(8,128)(2,1)S(1)}, u32[]{:S(2)}, u32[]{:S(2)}) collective-permute-start(bf16[528,128]{1,0:T(8,128)(2,1)S(1)} %get-tuple-element.128), channel_id=1, source_target_pairs={{0,3},{1,4},{2,1},{3,6},{4,9},{5,0},{6,11},{7,2},{8,5},{9,12},{10,... | collective-permute-start | bytes 405512 | tf_op jit(solution)/shard_map/ppermute | solution.py:67
  62.3 4.5 %collective-permute-start.24 = (bf16[528,128]{1,0:T(8,128)(2,1)S(1)}, bf16[528,128]{1,0:T(8,128)(2,1)S(1)}, u32[]{:S(2)}, u32[]{:S(2)}) collective-permute-start(bf16[528,128]{1,0:T(8,128)(2,1)S(1)} %merge.5), channel_id=1, source_target_pairs={{0,3},{1,4},{2,1},{3,6},{4,9},{5,0},{6,11},{7,2},{8,5},{9,12},{10,... | collective-permute-start | bytes 405512 | tf_op jit(solution)/shard_map/ppermute | solution.py:67
  63.7 4.7 %collective-permute-start.28 = (bf16[528,128]{1,0:T(8,128)(2,1)S(1)}, bf16[528,128]{1,0:T(8,128)(2,1)S(1)}, u32[]{:S(2)}, u32[]{:S(2)}) collective-permute-start(bf16[528,128]{1,0:T(8,128)(2,1)S(1)} %merge.8), channel_id=1, source_target_pairs={{0,3},{1,4},{2,1},{3,6},{4,9},{5,0},{6,11},{7,2},{8,5},{9,12},{10,... | collective-permute-start | bytes 405512 | tf_op jit(solution)/shard_map/ppermute | solution.py:67
  67.0 4.7 %collective-permute-start.25 = (bf16[528,128]{1,0:T(8,128)(2,1)S(1)}, bf16[528,128]{1,0:T(8,128)(2,1)S(1)}, u32[]{:S(2)}, u32[]{:S(2)}) collective-permute-start(bf16[528,128]{1,0:T(8,128)(2,1)S(1)} %merge.6), channel_id=1, source_target_pairs={{0,3},{1,4},{2,1},{3,6},{4,9},{5,0},{6,11},{7,2},{8,5},{9,12},{10,... | collective-permute-start | bytes 405512 | tf_op jit(solution)/shard_map/ppermute | solution.py:67
  68.6 4.8 %collective-permute-start.29 = (bf16[528,128]{1,0:T(8,128)(2,1)S(1)}, bf16[528,128]{1,0:T(8,128)(2,1)S(1)}, u32[]{:S(2)}, u32[]{:S(2)}) collective-permute-start(bf16[528,128]{1,0:T(8,128)(2,1)S(1)} %merge.9), channel_id=1, source_target_pairs={{0,3},{1,4},{2,1},{3,6},{4,9},{5,0},{6,11},{7,2},{8,5},{9,12},{10,... | collective-permute-start | bytes 405512 | tf_op jit(solution)/shard_map/ppermute | solution.py:67
  72.0 4.8 %collective-permute-start.26 = (bf16[528,128]{1,0:T(8,128)(2,1)S(1)}, bf16[528,128]{1,0:T(8,128)(2,1)S(1)}, u32[]{:S(2)}, u32[]{:S(2)}) collective-permute-start(bf16[528,128]{1,0:T(8,128)(2,1)S(1)} %merge.7), channel_id=1, source_target_pairs={{0,3},{1,4},{2,1},{3,6},{4,9},{5,0},{6,11},{7,2},{8,5},{9,12},{10,... | collective-permute-start | bytes 405512 | tf_op jit(solution)/shard_map/ppermute | solution.py:67
  73.4 4.2 %collective-permute-start.32 = (bf16[528,128]{1,0:T(8,128)(2,1)S(1)}, bf16[528,128]{1,0:T(8,128)(2,1)S(1)}, u32[]{:S(2)}, u32[]{:S(2)}) collective-permute-start(bf16[528,128]{1,0:T(8,128)(2,1)S(1)} %get-tuple-element.113.refs_2_), channel_id=1, source_target_pairs={{0,1},{1,0},{2,3},{3,2},{4,5},{5,4},{6,7},{7,6},{8,9},{9,8},{10,11... | collective-permute-start | bytes 405512 | tf_op jit(solution)/shard_map/ppermute | solution.py:70
  73.4 4.2 %collective-permute-start.30 = (bf16[528,128]{1,0:T(8,128)(2,1)S(1)}, bf16[528,128]{1,0:T(8,128)(2,1)S(1)}, u32[]{:S(2)}, u32[]{:S(2)}) collective-permute-start(bf16[528,128]{1,0:T(8,128)(2,1)S(1)} %collective-permute-done.29.refs_3_), channel_id=1, source_target_pairs={{0,1},{1,0},{2,3},{3,2},{4,5},{5,4},{6,7},{7,6},{8,9},{9,8},{10,11... | collective-permute-start | bytes 405512 | tf_op jit(solution)/shard_map/ppermute | solution.py:70
  76.8 1.8 %collective-permute-start.31 = (bf16[528,128]{1,0:T(8,128)(2,1)S(1)}, bf16[528,128]{1,0:T(8,128)(2,1)S(1)}, u32[]{:S(2)}, u32[]{:S(2)}) collective-permute-start(bf16[528,128]{1,0:T(8,128)(2,1)S(1)} %collective-permute-done.26.refs_0_), channel_id=1, source_target_pairs={{0,1},{1,0},{2,3},{3,2},{4,5},{5,4},{6,7},{7,6},{8,9},{9,8},{10,11... | collective-permute-start | bytes 405512 | tf_op jit(solution)/shard_map/ppermute | solution.py:70
  79.7 4.4 %collective-permute-start.34 = (bf16[128,512]{1,0:T(8,128)(2,1)S(1)}, bf16[128,512]{1,0:T(8,128)(2,1)S(1)}, u32[]{:S(2)}, u32[]{:S(2)}) collective-permute-start(bf16[128,512]{1,0:T(8,128)(2,1)S(1)} %get-tuple-element.138), channel_id=1, source_target_pairs={{0,3},{1,4},{2,1},{3,6},{4,9},{5,0},{6,11},{7,2},{8,5},{9,12},{10,... | collective-permute-start | bytes 393224 | tf_op jit(solution)/shard_map/ppermute | solution.py:67
  80.4 29.4 %slice-start.2 = ((s8[8388608]{0:T(1024)(128)(4,1)}), s8[4194304]{0:T(1024)(128)(4,1)S(1)}, s32[]{:S(2)}) async-start(s8[8388608]{0:T(1024)(128)(4,1)} %bitcast.26), calls=%async_computation.2 | async-start | bytes 8388608
  80.4 29.4 %slice-start.3 = ((s8[8388608]{0:T(1024)(128)(4,1)}), s8[4194304]{0:T(1024)(128)(4,1)S(1)}, s32[]{:S(2)}) async-start(s8[8388608]{0:T(1024)(128)(4,1)} %bitcast.26), calls=%async_computation.3 | async-start | bytes 8388608
  80.4 5.2 %collective-permute-start.38 = (bf16[128,512]{1,0:T(8,128)(2,1)S(1)}, bf16[128,512]{1,0:T(8,128)(2,1)S(1)}, u32[]{:S(2)}, u32[]{:S(2)}) collective-permute-start(bf16[128,512]{1,0:T(8,128)(2,1)S(1)} %get-tuple-element.141), channel_id=1, source_target_pairs={{0,3},{1,4},{2,1},{3,6},{4,9},{5,0},{6,11},{7,2},{8,5},{9,12},{10,... | collective-permute-start | bytes 393224 | tf_op jit(solution)/shard_map/ppermute | solution.py:67
  84.1 4.4 %collective-permute-start.35 = (bf16[128,512]{1,0:T(8,128)(2,1)S(1)}, bf16[128,512]{1,0:T(8,128)(2,1)S(1)}, u32[]{:S(2)}, u32[]{:S(2)}) collective-permute-start(bf16[128,512]{1,0:T(8,128)(2,1)S(1)} %add.221), channel_id=1, source_target_pairs={{0,3},{1,4},{2,1},{3,6},{4,9},{5,0},{6,11},{7,2},{8,5},{9,12},{10,... | collective-permute-start | bytes 393224 | tf_op jit(solution)/shard_map/ppermute | solution.py:67
  85.5 4.4 %collective-permute-start.39 = (bf16[128,512]{1,0:T(8,128)(2,1)S(1)}, bf16[128,512]{1,0:T(8,128)(2,1)S(1)}, u32[]{:S(2)}, u32[]{:S(2)}) collective-permute-start(bf16[128,512]{1,0:T(8,128)(2,1)S(1)} %add.224), channel_id=1, source_target_pairs={{0,3},{1,4},{2,1},{3,6},{4,9},{5,0},{6,11},{7,2},{8,5},{9,12},{10,... | collective-permute-start | bytes 393224 | tf_op jit(solution)/shard_map/ppermute | solution.py:67
  88.6 4.6 %collective-permute-start.36 = (bf16[128,512]{1,0:T(8,128)(2,1)S(1)}, bf16[128,512]{1,0:T(8,128)(2,1)S(1)}, u32[]{:S(2)}, u32[]{:S(2)}) collective-permute-start(bf16[128,512]{1,0:T(8,128)(2,1)S(1)} %add.222), channel_id=1, source_target_pairs={{0,3},{1,4},{2,1},{3,6},{4,9},{5,0},{6,11},{7,2},{8,5},{9,12},{10,... | collective-permute-start | bytes 393224 | tf_op jit(solution)/shard_map/ppermute | solution.py:67
  90.0 4.7 %collective-permute-start.40 = (bf16[128,512]{1,0:T(8,128)(2,1)S(1)}, bf16[128,512]{1,0:T(8,128)(2,1)S(1)}, u32[]{:S(2)}, u32[]{:S(2)}) collective-permute-start(bf16[128,512]{1,0:T(8,128)(2,1)S(1)} %add.225), channel_id=1, source_target_pairs={{0,3},{1,4},{2,1},{3,6},{4,9},{5,0},{6,11},{7,2},{8,5},{9,12},{10,... | collective-permute-start | bytes 393224 | tf_op jit(solution)/shard_map/ppermute | solution.py:67
  93.3 4.7 %collective-permute-start.37 = (bf16[128,512]{1,0:T(8,128)(2,1)S(1)}, bf16[128,512]{1,0:T(8,128)(2,1)S(1)}, u32[]{:S(2)}, u32[]{:S(2)}) collective-permute-start(bf16[128,512]{1,0:T(8,128)(2,1)S(1)} %add.223), channel_id=1, source_target_pairs={{0,3},{1,4},{2,1},{3,6},{4,9},{5,0},{6,11},{7,2},{8,5},{9,12},{10,... | collective-permute-start | bytes 393224 | tf_op jit(solution)/shard_map/ppermute | solution.py:67
  94.7 4.1 %collective-permute-start.41 = (bf16[128,512]{1,0:T(8,128)(2,1)S(1)}, bf16[128,512]{1,0:T(8,128)(2,1)S(1)}, u32[]{:S(2)}, u32[]{:S(2)}) collective-permute-start(bf16[128,512]{1,0:T(8,128)(2,1)S(1)} %collective-permute-done.40.refs_1_), channel_id=1, source_target_pairs={{0,1},{1,0},{2,3},{3,2},{4,5},{5,4},{6,7},{7,6},{8,9},{9,8},{10,11... | collective-permute-start | bytes 393224 | tf_op jit(solution)/shard_map/ppermute | solution.py:70
  98.0 1.9 %collective-permute-start.45 = (bf16[128,512]{1,0:T(8,128)(2,1)S(1)}, bf16[128,512]{1,0:T(8,128)(2,1)S(1)}, u32[]{:S(2)}, u32[]{:S(2)}) collective-permute-start(bf16[128,512]{1,0:T(8,128)(2,1)S(1)} %collective-permute-done.37.refs_1_), channel_id=1, source_target_pairs={{0,1},{1,0},{2,3},{3,2},{4,5},{5,4},{6,7},{7,6},{8,9},{9,8},{10,11... | collective-permute-start | bytes 393224 | tf_op jit(solution)/shard_map/ppermute | solution.py:70
  98.9 4.4 %collective-permute-start.42 = (bf16[128,512]{1,0:T(8,128)(2,1)S(1)}, bf16[128,512]{1,0:T(8,128)(2,1)S(1)}, u32[]{:S(2)}, u32[]{:S(2)}) collective-permute-start(bf16[128,512]{1,0:T(8,128)(2,1)S(1)} %add.226.refs_6_), channel_id=1, source_target_pairs={{0,5},{1,2},{2,7},{3,0},{4,1},{5,8},{6,3},{7,10},{8,13},{9,4},{10,... | collective-permute-start | bytes 393224 | tf_op jit(solution)/shard_map/ppermute | solution.py:67
  99.9 4.8 %collective-permute-start.46 = (bf16[128,512]{1,0:T(8,128)(2,1)S(1)}, bf16[128,512]{1,0:T(8,128)(2,1)S(1)}, u32[]{:S(2)}, u32[]{:S(2)}) collective-permute-start(bf16[128,512]{1,0:T(8,128)(2,1)S(1)} %add.227.refs_7_), channel_id=1, source_target_pairs={{0,5},{1,2},{2,7},{3,0},{4,1},{5,8},{6,3},{7,10},{8,13},{9,4},{10,... | collective-permute-start | bytes 393224 | tf_op jit(solution)/shard_map/ppermute | solution.py:67
  103.3 4.4 %collective-permute-start.43 = (bf16[128,512]{1,0:T(8,128)(2,1)S(1)}, bf16[128,512]{1,0:T(8,128)(2,1)S(1)}, u32[]{:S(2)}, u32[]{:S(2)}) collective-permute-start(bf16[128,512]{1,0:T(8,128)(2,1)S(1)} %collective-permute-done.42.refs_8_), channel_id=1, source_target_pairs={{0,5},{1,2},{2,7},{3,0},{4,1},{5,8},{6,3},{7,10},{8,13},{9,4},{10,... | collective-permute-start | bytes 393224 | tf_op jit(solution)/shard_map/ppermute | solution.py:67
  104.7 5.0 %collective-permute-start.47 = (bf16[128,512]{1,0:T(8,128)(2,1)S(1)}, bf16[128,512]{1,0:T(8,128)(2,1)S(1)}, u32[]{:S(2)}, u32[]{:S(2)}) collective-permute-start(bf16[128,512]{1,0:T(8,128)(2,1)S(1)} %collective-permute-done.46.refs_9_), channel_id=1, source_target_pairs={{0,5},{1,2},{2,7},{3,0},{4,1},{5,8},{6,3},{7,10},{8,13},{9,4},{10,... | collective-permute-start | bytes 393224 | tf_op jit(solution)/shard_map/ppermute | solution.py:67
  107.7 4.4 %collective-permute-start.44 = (bf16[128,512]{1,0:T(8,128)(2,1)S(1)}, bf16[128,512]{1,0:T(8,128)(2,1)S(1)}, u32[]{:S(2)}, u32[]{:S(2)}) collective-permute-start(bf16[128,512]{1,0:T(8,128)(2,1)S(1)} %collective-permute-done.43.refs_10_), channel_id=1, source_target_pairs={{0,5},{1,2},{2,7},{3,0},{4,1},{5,8},{6,3},{7,10},{8,13},{9,4},{10,... | collective-permute-start | bytes 393224 | tf_op jit(solution)/shard_map/ppermute | solution.py:67
  109.2 5.3 %collective-permute-start.50 = (bf16[128,512]{1,0:T(8,128)(2,1)S(1)}, bf16[128,512]{1,0:T(8,128)(2,1)S(1)}, u32[]{:S(2)}, u32[]{:S(2)}) collective-permute-start(bf16[128,512]{1,0:T(8,128)(2,1)S(1)} %collective-permute-done.42.refs_8_), channel_id=1, source_target_pairs={{0,1},{1,0},{2,3},{3,2},{4,5},{5,4},{6,7},{7,6},{8,9},{9,8},{10,11... | collective-permute-start | bytes 393224 | tf_op jit(solution)/shard_map/ppermute | solution.py:70
  109.2 5.3 %collective-permute-start.51 = (bf16[128,512]{1,0:T(8,128)(2,1)S(1)}, bf16[128,512]{1,0:T(8,128)(2,1)S(1)}, u32[]{:S(2)}, u32[]{:S(2)}) collective-permute-start(bf16[128,512]{1,0:T(8,128)(2,1)S(1)} %collective-permute-done.46.refs_9_), channel_id=1, source_target_pairs={{0,1},{1,0},{2,3},{3,2},{4,5},{5,4},{6,7},{7,6},{8,9},{9,8},{10,11... | collective-permute-start | bytes 393224 | tf_op jit(solution)/shard_map/ppermute | solution.py:70
  112.1 4.4 %collective-permute-start.49 = (bf16[128,512]{1,0:T(8,128)(2,1)S(1)}, bf16[128,512]{1,0:T(8,128)(2,1)S(1)}, u32[]{:S(2)}, u32[]{:S(2)}) collective-permute-start(bf16[128,512]{1,0:T(8,128)(2,1)S(1)} %collective-permute-done.44.refs_10_), channel_id=1, source_target_pairs={{0,5},{1,2},{2,7},{3,0},{4,1},{5,8},{6,3},{7,10},{8,13},{9,4},{10,... | collective-permute-start | bytes 393224 | tf_op jit(solution)/shard_map/ppermute | solution.py:67
  113.6 4.4 %collective-permute-start.48 = (bf16[128,512]{1,0:T(8,128)(2,1)S(1)}, bf16[128,512]{1,0:T(8,128)(2,1)S(1)}, u32[]{:S(2)}, u32[]{:S(2)}) collective-permute-start(bf16[128,512]{1,0:T(8,128)(2,1)S(1)} %collective-permute-done.47.refs_11_), channel_id=1, source_target_pairs={{0,5},{1,2},{2,7},{3,0},{4,1},{5,8},{6,3},{7,10},{8,13},{9,4},{10,... | collective-permute-start | bytes 393224 | tf_op jit(solution)/shard_map/ppermute | solution.py:67
  113.7 5.5 %collective-permute-start.52 = (bf16[128,512]{1,0:T(8,128)(2,1)S(1)}, bf16[128,512]{1,0:T(8,128)(2,1)S(1)}, u32[]{:S(2)}, u32[]{:S(2)}) collective-permute-start(bf16[128,512]{1,0:T(8,128)(2,1)S(1)} %collective-permute-done.43.refs_10_), channel_id=1, source_target_pairs={{0,1},{1,0},{2,3},{3,2},{4,5},{5,4},{6,7},{7,6},{8,9},{9,8},{10,11... | collective-permute-start | bytes 393224 | tf_op jit(solution)/shard_map/ppermute | solution.py:70
  114.5 4.6 %collective-permute-start.53 = (bf16[128,512]{1,0:T(8,128)(2,1)S(1)}, bf16[128,512]{1,0:T(8,128)(2,1)S(1)}, u32[]{:S(2)}, u32[]{:S(2)}) collective-permute-start(bf16[128,512]{1,0:T(8,128)(2,1)S(1)} %collective-permute-done.47.refs_11_), channel_id=1, source_target_pairs={{0,1},{1,0},{2,3},{3,2},{4,5},{5,4},{6,7},{7,6},{8,9},{9,8},{10,11... | collective-permute-start | bytes 393224 | tf_op jit(solution)/shard_map/ppermute | solution.py:70
  114.5 4.6 %collective-permute-start.54 = (bf16[128,512]{1,0:T(8,128)(2,1)S(1)}, bf16[128,512]{1,0:T(8,128)(2,1)S(1)}, u32[]{:S(2)}, u32[]{:S(2)}) collective-permute-start(bf16[128,512]{1,0:T(8,128)(2,1)S(1)} %collective-permute-done.44.refs_10_), channel_id=1, source_target_pairs={{0,1},{1,0},{2,3},{3,2},{4,5},{5,4},{6,7},{7,6},{8,9},{9,8},{10,11... | collective-permute-start | bytes 393224 | tf_op jit(solution)/shard_map/ppermute | solution.py:70
  116.5 2.7 %collective-permute-start.56 = (bf16[128,512]{1,0:T(8,128)(2,1)S(1)}, bf16[128,512]{1,0:T(8,128)(2,1)S(1)}, u32[]{:S(2)}, u32[]{:S(2)}) collective-permute-start(bf16[128,512]{1,0:T(8,128)(2,1)S(1)} %collective-permute-done.49.refs_12_), channel_id=1, source_target_pairs={{0,1},{1,0},{2,3},{3,2},{4,5},{5,4},{6,7},{7,6},{8,9},{9,8},{10,11... | collective-permute-start | bytes 393224 | tf_op jit(solution)/shard_map/ppermute | solution.py:70
  118.0 1.4 %collective-permute-start.55 = (bf16[128,512]{1,0:T(8,128)(2,1)S(1)}, bf16[128,512]{1,0:T(8,128)(2,1)S(1)}, u32[]{:S(2)}, u32[]{:S(2)}) collective-permute-start(bf16[128,512]{1,0:T(8,128)(2,1)S(1)} %collective-permute-done.48.refs_11_), channel_id=1, source_target_pairs={{0,1},{1,0},{2,3},{3,2},{4,5},{5,4},{6,7},{7,6},{8,9},{9,8},{10,11... | collective-permute-start | bytes 393224 | tf_op jit(solution)/shard_map/ppermute | solution.py:70

commit v4 on v3

--- a/solution.py
+++ b/solution.py
@@ -23,6 +23,12 @@
 FREE = pl.CostEstimate(flops=0, bytes_accessed=0, transcendentals=0)
 
 
+def took(microseconds):
+    return pl.CostEstimate(
+        flops=int(microseconds * 1.15e9), bytes_accessed=0, transcendentals=0
+    )
+
+
 class Ring:
     def __init__(self, devices, columns):
         self.chips = devices // 2
@@ -35,21 +41,21 @@
 
     def locate(self, key_share):
         device = lax.axis_index("ctx")
-        core, chip = device % 2, device // 2
+        two = jnp.int32(2)
+        core, chip = lax.rem(device, two), lax.div(device, two)
         middle = self.chips // 2
+        place = chip
         if self.snake:
-            place = jnp.where(chip % 2 == 0, chip // 2, self.chips - 1 - chip // 2)
-        else:
-            place = chip
-        sign = 1 - 2 * ((core + place) % 2)
+            place = jnp.where(lax.rem(chip, two) == 0, lax.div(chip, two), self.chips - 1 - lax.div(chip, two))
+        sign = 1 - 2 * lax.rem(core + place, two)
         names, values = ["self", "pair"], [device, device + 1 - 2 * core]
         for step in range(-self.rounds, self.rounds + 1):
-            owner = (place - sign * step + self.chips) % self.chips
+            owner = lax.rem(place - sign * step + self.chips, jnp.int32(self.chips))
             if self.snake:
                 owner = jnp.where(owner < middle, 2 * owner, 2 * (self.chips - 1 - owner) + 1)
             names += [(step, True), (step, False), step]
             half = core if step % 2 == 0 else 1 - core
-            values += [2 * owner + half, 2 * owner + 1 - half, owner // key_share]
+            values += [2 * owner + half, 2 * owner + 1 - half, lax.div(owner, jnp.int32(key_share))]
         values = lax.optimization_barrier([x.astype(jnp.int32) for x in values])
         self.numbers = dict(zip(names, values))
         return values
@@ -146,7 +152,7 @@
         in_specs=[SCALARS, SCALARS, VMEM],
         out_specs=[VMEM] * 2,
         compiler_params=limit(8),
-        cost_estimate=FREE,
+        cost_estimate=took(0.09),
         name="prepare",
     )(ring.number("self"), ring.number("pair"), near(last))
 
@@ -165,7 +171,7 @@
         out_specs=VMEM,
         scratch_shapes=[pltpu.SemaphoreType.DMA],
         compiler_params=limit(8),
-        cost_estimate=FREE,
+        cost_estimate=took(0.8999999999999999),
         name="stage",
     )(far(weight))
 
@@ -184,7 +190,7 @@
         out_specs=[VMEM] * 2,
         scratch_shapes=[pltpu.SemaphoreType.DMA((4,))],
         compiler_params=limit(8),
-        cost_estimate=FREE,
+        cost_estimate=took(0.36),
         name="fetch",
     )(head, far(cache[0]), cache[1], far(cache[2]), cache[3])
 
@@ -200,27 +206,34 @@
     rows = q.shape[0] // parts
     diag = diagonal()
     biases = jnp.concatenate([bias[...]] * (chunk // bias.shape[0]), axis=0)
-    for part, out in enumerate(outs):
-        stats = []
-        for start in range(0, rows, chunk):
-            query = jnp.concatenate(
-                [q[pl.ds(part * rows + start, chunk), :], biases], axis=1
-            )
-            keys = jnp.concatenate([key[...], onehot[...]], axis=1)
-            scores = lax.dot_general(
-                query, keys, (((1,), (1,)), ((), ())), preferred_element_type=F32
-            )
-            peak = jnp.max(scores, axis=1, keepdims=True)
-            weights = jnp.exp2(scores - peak).astype(BF16)
-            values = jnp.concatenate([value[...], jnp.ones(value.shape, BF16)], axis=1)
-            sums = jnp.dot(weights, values, preferred_element_type=F32)
-            total = sums[:, LANES:]
-            out[pl.ds(start, chunk), :] = (sums[:, :LANES] / total).astype(BF16)
-            level = peak + jnp.log2(total)
-            for b in range(chunk // LANES):
-                block = level[b * LANES : (b + 1) * LANES]
-                stats.append(jnp.sum(jnp.where(diag, block, 0.0), axis=0, keepdims=True))
-        out[pl.ds(rows, stat_rows(rows)), :] = pack_stats(stats)
+
+    def scores(start):
+        query = jnp.concatenate([q[pl.ds(start, chunk), :], biases], axis=1)
+        keys = jnp.concatenate([key[...], onehot[...]], axis=1)
+        return lax.dot_general(
+            query, keys, (((1,), (1,)), ((), ())), preferred_element_type=F32
+        )
+
+    starts = range(0, parts * rows, chunk)
+    coming, stats = scores(0), []
+    for start in starts:
+        score = coming
+        if start + chunk < parts * rows:
+            coming = scores(start + chunk)
+        peak = jnp.max(score, axis=1, keepdims=True)
+        weights = jnp.exp2(score - peak).astype(BF16)
+        values = jnp.concatenate([value[...], jnp.ones(value.shape, BF16)], axis=1)
+        sums = jnp.dot(weights, values, preferred_element_type=F32)
+        total = sums[:, LANES:]
+        out, inside = outs[start // rows], start % rows
+        out[pl.ds(inside, chunk), :] = (sums[:, :LANES] / total).astype(BF16)
+        level = peak + jnp.log2(total)
+        for b in range(chunk // LANES):
+            block = level[b * LANES : (b + 1) * LANES]
+            stats.append(jnp.sum(jnp.where(diag, block, 0.0), axis=0, keepdims=True))
+        if inside + chunk == rows:
+            out[pl.ds(rows, stat_rows(rows)), :] = pack_stats(stats)
+            stats = []
     for copy in copies:
         copy.wait()
 
@@ -243,7 +256,11 @@
         out_specs=[VMEM] * len(shapes),
         scratch_shapes=scratch,
         compiler_params=limit(16),
-        cost_estimate=FREE,
+        cost_estimate=pl.CostEstimate(
+            flops=16 * parts * rows * head[0].shape[0] * width,
+            bytes_accessed=8 * head[0].size,
+            transcendentals=parts * rows * head[0].shape[0],
+        ),
         name="attend",
     )(*arrays)
     return out[:parts], out[parts:]
@@ -285,113 +302,162 @@
         out_shape=pltpu.VMEM(two.shape, BF16),
         in_specs=[VMEM, VMEM],
         out_specs=VMEM,
-        cost_estimate=FREE,
+        cost_estimate=took(0.075),
         compiler_params=limit(8),
         name="merge",
     )(near(one), near(two))
 
 
 def finish_kernel(rows, queries, *refs):
+    parts, out = refs[:-1], refs[-1]
     diag = diagonal()
-    for half in range(2):
-        parts, out = refs[3 * half : 3 * half + 3], refs[6 + half]
-        width = parts[0].shape[1]
-        stats = [unpack_stats(part, rows) for part in parts]
-        for b in range(rows // LANES):
-            here = pl.ds(b * LANES, LANES)
-            levels = [stat[b : b + 1] for stat in stats]
-            peak = functools.reduce(jnp.maximum, levels)
-            shares = [jnp.exp2(level - peak) for level in levels]
-            total = sum(shares)
-            value = sum(
-                spread(diag, share / total) * part[here, :].astype(F32)
-                for share, part in zip(shares, parts)
-            ).astype(BF16)
-            for piece in range(LANES // queries):
-                head = (b * LANES) // queries + piece
-                out[:, pl.ds(head * width, width)] = value[piece * queries : (piece + 1) * queries]
-
-
-def finish(rows, queries, own, other):
-    width = own[0].shape[1]
-    shape = pltpu.VMEM((queries, rows // queries * width), BF16)
+    width = parts[0].shape[1]
+    stats = [unpack_stats(part, rows) for part in parts]
+    for b in range(rows // LANES):
+        here = pl.ds(b * LANES, LANES)
+        levels = [stat[b : b + 1] for stat in stats]
+        peak = functools.reduce(jnp.maximum, levels)
+        shares = [jnp.exp2(level - peak) for level in levels]
+        total = sum(shares)
+        value = sum(
+            spread(diag, share / total) * part[here, :].astype(F32)
+            for share, part in zip(shares, parts)
+        ).astype(BF16)
+        for piece in range(LANES // queries):
+            head = (b * LANES) // queries + piece
+            out[:, pl.ds(head * width, width)] = value[piece * queries : (piece + 1) * queries]
+
+
+def finish(rows, queries, parts):
+    width = parts[0].shape[1]
     return pl.pallas_call(
         functools.partial(finish_kernel, rows, queries),
-        out_shape=[shape, shape],
-        in_specs=[VMEM] * 6,
-        out_specs=[VMEM] * 2,
-        cost_estimate=FREE,
-        compiler_params=limit(8),
+        out_shape=pltpu.VMEM((queries, rows // queries * width), BF16),
+        in_specs=[VMEM] * len(parts),
+        out_specs=VMEM,
+        compiler_params=limit(8),
+        cost_estimate=took(0.105),
         name="finish",
-    )(*[near(x) for x in (*own, *other)])
-
-
-def project_kernel(count, queries, features, scale, carried, begun, *refs):
-    blocks, parts = refs[:count], refs[count : 2 * count]
-    gains, row = (parts, queries) if carried else (refs[2 * count : 3 * count], queries + 1)
-    weight, *rest = refs[(2 if carried else 3) * count :]
-    total, square = 0.0, 0.0
-    if begun:
-        total, square = rest[0][...], rest[1][...]
-    rest = rest[2 if begun else 0 :]
-    for block, part, gain in zip(blocks, parts, gains):
-        width = part.shape[1]
+    )(*[near(x) for x in parts])
+
+
+def weight_rows(weight, block, target, sem):
+    width = target.shape[0]
+    start = pl.multiple_of(block[0] * width, width)
+    copy = pltpu.make_async_copy(weight.at[pl.ds(start, width), :], target, sem)
+    copy.start()
+    return copy
+
+
+def project_kernel(plan, *refs):
+    queries, features, scale, carried, begun, count, coming, fetched = plan
+    refs = list(refs)
+    take = lambda n: [refs.pop(0) for _ in range(n)]
+    blocks, later = take(0 if fetched else count), take(coming)
+    parts = take(count)
+    gains, row = (parts, queries) if carried else (take(count), queries + 1)
+    weights = take(count) if fetched else take(1)
+    state = take(2 if begun else 0)
+    head_gain = take(1 if scale else 0)
+    outs, targets = take(1 if features else 2), take(coming)
+    copies = []
+    if not fetched:
+        pieces, sems = take(2)
+        copies = [
+            weight_rows(weights[0], block, pieces.at[i], sems.at[i])
+            for i, block in enumerate(blocks)
+        ]
+        weights_at = [pieces.at[i] for i in range(count)]
+        ahead = [
+            weight_rows(weights[0], block, target, sems.at[count + i])
+            for i, (block, target) in enumerate(zip(later, targets))
+        ]
+    else:
+        weights_at, ahead = weights, []
+    total, square = (state[0][...], state[1][...]) if begun else (0.0, 0.0)
+    scaled = []
+    for part, gain in zip(parts, gains):
         values = part[...][:queries].astype(F32)
-        scaled = (values * gain[...][row : row + 1].astype(F32)).astype(BF16)
-        piece = weight[pl.ds(pl.multiple_of(block[0] * width, width), width), :]
-        total += jnp.dot(scaled, piece, preferred_element_type=F32)
-        for lane in range(0, width, LANES):
+        scaled.append((values * gain[...][row : row + 1].astype(F32)).astype(BF16))
+        for lane in range(0, part.shape[1], LANES):
             square += values[:, lane : lane + LANES] * values[:, lane : lane + LANES]
+    for i, weight in enumerate(weights_at):
+        if copies:
+            copies[i].wait()
+        total += jnp.dot(scaled[i], weight[...], preferred_element_type=F32)
     if not features:
-        rest[0][...] = total
-        rest[1][...] = square
-        return
-    factor = lax.rsqrt(jnp.sum(square, axis=1, keepdims=True) / features + EPSILON)
-    if scale is None:
-        rest[0][...] = (total * factor).astype(BF16)
-        return
-    gain, out = rest
-    width = gain.shape[1]
-    for head in range(total.shape[1] // width):
-        value = total[:, head * width : (head + 1) * width] * factor
-        mean = jnp.mean(value * value, axis=1, keepdims=True)
-        out[pl.ds(head * queries, queries), :] = (
-            value * lax.rsqrt(mean + EPSILON) * (gain[...].astype(F32) * scale)
-        ).astype(BF16)
-
-
-def project(queries, blocks, parts, gains, weight, state, last=False, head_gain=None):
-    arrays = [*parts, *(gains or ()), weight, *(state or ())]
-    width, scale = weight.shape[1], None
+        outs[0][...] = total
+        outs[1][...] = square
+    else:
+        factor = lax.rsqrt(jnp.sum(square, axis=1, keepdims=True) / features + EPSILON)
+        if not scale:
+            outs[0][...] = (total * factor).astype(BF16)
+        else:
+            gain = head_gain[0][...].astype(F32) * scale
+            width = gain.shape[1]
+            for head in range(total.shape[1] // width):
+                value = total[:, head * width : (head + 1) * width] * factor
+                mean = jnp.mean(value * value, axis=1, keepdims=True)
+                outs[0][pl.ds(head * queries, queries), :] = (
+                    value * lax.rsqrt(mean + EPSILON) * gain
+                ).astype(BF16)
+    for copy in ahead:
+        copy.wait()
+
+
+def project(queries, blocks, later, parts, gains, weight, state, fetched=None, last=False, head_gain=None):
+    count, depth, width = len(parts), parts[0].shape[1], weight.shape[1]
+    scale = 0.0
     shapes = [pltpu.VMEM((queries, width), F32), pltpu.VMEM((queries, LANES), F32)]
+    scalars = [] if fetched else [*blocks, *later]
+    arrays = [near(x) for x in (*parts, *(gains or ()), *(fetched or ()))]
+    specs = [VMEM] * len(arrays)
+    if not fetched:
+        arrays.append(far(weight))
+        specs.append(ANYWHERE)
+    arrays += [near(x) for x in state or ()]
     if head_gain is not None:
-        arrays.append(head_gain[None, :])
-        depth = head_gain.shape[0]
-        scale = depth**-0.5 * math.log2(math.e)
-        shapes = [pltpu.VMEM((width // depth * queries, depth), BF16)]
+        arrays.append(near(head_gain[None, :]))
+        size = head_gain.shape[0]
+        scale = size**-0.5 * math.log2(math.e)
+        shapes = [pltpu.VMEM((width // size * queries, size), BF16)]
     elif last:
         shapes = [jax.ShapeDtypeStruct((queries, width), BF16)]
+    specs += [VMEM] * (len(arrays) - len(specs))
+    shapes += [pltpu.VMEM((depth, width), BF16)] * len(later)
     features = weight.shape[0] if last else 0
-    return pl.pallas_call(
-        functools.partial(
-            project_kernel, len(parts), queries, features, scale, not gains, bool(state)
-        ),
+    plan = queries, features, scale, not gains, bool(state), count, len(later), bool(fetched)
+    scratch = []
+    if not fetched:
+        scratch = [
+            pltpu.VMEM((count, depth, width), BF16),
+            pltpu.SemaphoreType.DMA((count + len(later),)),
+        ]
+    out = pl.pallas_call(
+        functools.partial(project_kernel, plan),
         out_shape=shapes,
-        in_specs=[SCALARS] * len(blocks) + [VMEM] * len(arrays),
+        in_specs=[SCALARS] * len(scalars) + specs,
         out_specs=[VMEM] * len(shapes),
-        compiler_params=limit(8),
-        cost_estimate=FREE,
+        scratch_shapes=scratch,
+        compiler_params=limit(16),
+        cost_estimate=took(0.6),
         name="project",
-    )(*blocks, *[near(x) for x in arrays])
-
-
-def gather_project(ring, queries, own, other, carriers, weight, beside=None, head_gain=None):
-    arrived, waiting, swapped, state = {}, [], [], None
-
-    def flush(names, state, **how):
+    )(*scalars, *arrays)
+    edge = len(out) - len(later)
+    return out[:edge], out[edge:]
+
+
+def gather_project(ring, queries, own, other, carriers, weight, beside=None, head_gain=None, meanwhile=None):
+    arrived, waiting, state = {}, [], None
+    rounds = ring.rounds
+    final = [(rounds, True), (-rounds, False), (rounds - 1, False), (1 - rounds, True)]
+
+    def flush(names, later=(), **how):
+        waiting[:] = [name for name in waiting if name not in names]
         return project(
             queries,
             [ring.number(name) for name in names],
+            [ring.number(name) for name in later],
             [arrived[name] for name in names],
             carriers and [carriers[name] for name in names],
             weight,
@@ -399,23 +465,32 @@
             **how,
         )
 
-    for step in range(ring.rounds + 1):
-        halves = (True, False) if step < ring.rounds else (True,)
-        for mine, part in zip(halves, (own, other)):
-            arrived[step, mine] = part
-            waiting.append((step, mine))
-        if step < ring.rounds:
-            own = after(own, *(beside or {}).get(step + 1, ()), *(state or ()))
-            own = ring.send(own, 1)
-        if step < ring.rounds - 1:
+    def keep(name, part):
+        arrived[name] = part
+        waiting.append(name)
+
+    keep((0, True), own)
+    keep((0, False), other)
+    for step in range(1, rounds + 1):
+        own = ring.send(after(own, *(beside or {}).get(step, ()), *(state or ())), 1)
+        if step < rounds:
             other = ring.send(other, 1)
-        for mine in halves if step else ():
-            arrived[-step, not mine] = ring.swap(arrived[step, mine])
-            swapped.append((-step, not mine))
-        if carriers and step % 3 == 2 and step < ring.rounds:
-            state, waiting = flush(waiting, state), []
-    (result,) = flush(waiting + swapped, state, last=True, head_gain=head_gain)
-    return result, arrived
+            if len(waiting) > 16:
+                state, _ = flush([name for name in waiting if abs(name[0]) < step - 1])
+            keep((step, True), own)
+            keep((-step, False), ring.swap(own))
+            keep((step, False), other)
+            if step < rounds - 1:
+                keep((-step, True), ring.swap(other))
+    state, fetched = flush([name for name in waiting if name not in final], final)
+    before = arrived[rounds - 1, True]
+    own, other, before = after(own, *state), after(other, own, *state), after(before, own, *state)
+    extra = meanwhile(own) if meanwhile else ()
+    keep((rounds, True), own)
+    keep((-rounds, False), after(ring.swap(own), *extra))
+    keep((1 - rounds, True), ring.swap(other))
+    (result,), _ = flush(final, fetched=fetched, last=True, head_gain=head_gain)
+    return result, arrived, extra
 
 
 def mix_kernel(count, *refs):
@@ -435,7 +510,7 @@
         in_specs=[SCALARS] * len(blocks) + [VMEM] * 4,
         out_specs=[VMEM] * len(blocks),
         compiler_params=limit(8),
-        cost_estimate=FREE,
+        cost_estimate=took(0.18),
         name="mix",
     )(*blocks, *[near(x) for x in (one, two, one_weight, two_weight)])
 
@@ -452,7 +527,7 @@
         in_specs=[VMEM] * len(parts),
         out_specs=VMEM,
         compiler_params=limit(8),
-        cost_estimate=FREE,
+        cost_estimate=took(0.03),
         name="add",
     )(*[near(x) for x in parts])
 
@@ -470,7 +545,7 @@
         in_specs=[VMEM, VMEM],
         out_specs=VMEM,
         compiler_params=limit(8),
-        cost_estimate=FREE,
+        cost_estimate=took(0.03),
         name="join",
     )(near(one), near(two))
 
@@ -486,7 +561,7 @@
         in_specs=[VMEM],
         out_specs=VMEM,
         compiler_params=limit(8),
-        cost_estimate=FREE,
+        cost_estimate=took(0.03),
         name="first_half",
     )(near(both))
 
@@ -527,43 +602,40 @@
     other_keys = ring.swap(after(key_cache, other))
     other_values = ring.swap(after(value_cache, other))
     cache = (key_cache, other_keys, value_cache, other_values)
-    onehot, bias = prepare(ring, last, 2 * key_cache.shape[0])
-    head = fetch(ring.number(0), cache)
-    beside = {rounds - 1: (other_keys,), rounds: (*head, bias)}
-    own_heads, carriers = gather_project(
-        ring, queries, own, other, None, q_weight, beside, q_gain
+    beside = {rounds - 1: (other_keys,), rounds: (other_values,)}
+
+    def meanwhile(token):
+        onehot, bias = prepare(ring, after(last, token), 2 * key_cache.shape[0])
+        ready = after(key_cache, token), other_keys, after(value_cache, token), other_values
+        return onehot, bias, *fetch(ring.number(0), ready)
+
+    own_heads, carriers, (onehot, bias, *head) = gather_project(
+        ring, queries, own, other, None, q_weight, beside, q_gain, meanwhile
     )
-    other_heads = ring.swap(own_heads)
-    other_weight = ring.swap(after(out_weight, other_heads))
-
-    partials = []
-    done = own_heads
-    for step in range(rounds + 1):
+    other_weight = ring.swap(after(out_weight, own_heads))
+
+    travelling, running, done = own_heads, None, own_heads
+    for step in range(ring.chips):
+        last = step + 1 == ring.chips
+        if not last:
+            coming = ring.send(travelling, 1)
+        following = step + 1 if step < rounds else step + 1 - ring.chips
+        (part,), head = attend(
+            None if last else ring.number(following),
+            after(travelling, done),
+            1,
+            bias,
+            onehot,
+            head,
+            cache,
+        )
         if step == 0:
-            coming = join(ring.send(own_heads, 1), ring.send(other_heads, 1))
-        elif step < rounds:
-            block = travelling if step < rounds - 1 else first_half(travelling)
-            coming = ring.send(after(block, done), 1)
-        following = ring.number(step + 1) if step < rounds else None
-        if step == 0:
-            parts, head = attend(following, own_heads, 1, bias, onehot, head, cache)
-            local_other = ring.swap(parts[0])
+            local = part
         else:
-            count = 2 if step < rounds else 1
-            parts, head = attend(following, travelling, count, bias, onehot, head, cache)
-        partials.append(parts)
-        done = parts[0]
-        travelling = coming
-    own = ring.send(partials[rounds][0], -1)
-    other = ring.send(partials[rounds - 1][1], -1)
-    for step in range(rounds - 1, 0, -1):
-        own = ring.send(merge(rows, own, partials[step][0]), -1)
-        if step > 1:
-            other = ring.send(merge(rows, other, partials[step - 1][1]), -1)
-    own_far, other_far = ring.swap(own), ring.swap(other)
-    attended, attended_other = finish(
-        rows, queries, (own, other_far, partials[0][0]), (other, own_far, local_other)
-    )
+            running = ring.send(part if running is None else merge(rows, running, part), 1)
+        travelling, done = coming, part
+    attended = finish(rows, queries, (running, local))
+    attended_other = ring.swap(attended)
 
     def mixed(kind, places):
         blocks = [ring.number(place) for place in places]
@@ -582,7 +654,7 @@
     own_far, other_far = ring.swap(own), ring.swap(other)
     new_own = add(shares[0, True], own, other_far, carriers[0, True])
     new_other = add(shares[0, False], other, own_far, carriers[0, False])
-    next_queries, _ = gather_project(ring, queries, new_own, new_other, carriers, next_weight)
+    next_queries, _, _ = gather_project(ring, queries, new_own, new_other, carriers, next_weight)
     return new_own, next_queries
 
 

time: 121 us -> 116 us (0.959)
  waiting for transfers between devices: 35.5 us -> 25.3 us
  Pallas kernels: 30.2 us -> 32.9 us
  starting transfers between devices: 51.5 us -> 54.1 us
    ppermute x33 -> x35, waiting for transfers between devices: 31.2 us -> 22.9 us  [send(): return lax.ppermute(block, 'ctx', sorted(route))]
    ppermute x33 -> x35, starting transfers between devices: 41.3 us -> 47.2 us  [send(): return lax.ppermute(block, 'ctx', sorted(route))]
    pallas_call x5 -> x4, Pallas kernels: 3.85 us -> 9.34 us  [project(): pl.pallas_call(functools.partial(project_kernel, plan), out_shape=shapes,...]
    ppermute x24 -> x21, starting transfers between devices: 10.2 us -> 6.93 us  [swap(): lax.ppermute(block, 'ctx', [(i, i ^ 1) for i in range(2 * self.chips)])]
    pallas_call x5 -> x8, Pallas kernels: 21.1 us -> 18.3 us  [attend(): pl.pallas_call(functools.partial(attend_kernel, chunk, parts), out_shape=...]
    ppermute x24 -> x21, waiting for transfers between devices: 4.3 us -> 2.39 us  [swap(): lax.ppermute(block, 'ctx', [(i, i ^ 1) for i in range(2 * self.chips)])]
  transfers between devices with their start and end apart: 57 -> 56, of which waited for: 26 -> 19; matrix products, arithmetic and copies ran while one was open for 1% -> 1% of each run, Pallas kernels for 22% -> 26%
where the time goes in v4:
time: 116 us
  starting transfers between devices  54.1 us (47%)
  Pallas kernels  32.9 us (28%)
  waiting for transfers between devices  25.3 us (22%)
  local copies, waits for them, and re-layouts  1.59 us (1%)
  between operations  1.3 us (1%)
    ppermute x35, starting transfers between devices, send(): return lax.ppermute(block, 'ctx', sorted(route))  47.2 us
    ppermute x35, waiting for transfers between devices, send(): return lax.ppermute(block, 'ctx', sorted(route))  22.9 us
    pallas_call x8, Pallas kernels, attend(): pl.pallas_call(functools.partial(attend_kernel, chunk, parts), out_shape=...  18.3 us
    pallas_call x4, Pallas kernels, project(): pl.pallas_call(functools.partial(project_kernel, plan), out_shape=shapes,...  9.34 us
    ppermute x21, starting transfers between devices, swap(): lax.ppermute(block, 'ctx', [(i, i ^ 1) for i in range(2 * self.chips)])  6.93 us
    ppermute x21, waiting for transfers between devices, swap(): lax.ppermute(block, 'ctx', [(i, i ^ 1) for i in range(2 * self.chips)])  2.39 us
  transfers between devices with their start and end apart: 56, of which 19 were waited for; matrix products, arithmetic and copies ran while one was open for 1% of the time, Pallas kernels for 26%

profile of v4, /device:TPU:0, one launch (start us, length us, event | category | flops | bytes accessed | tf_op | source)
XLA Modules:
  0.0 116.3 jit_solution(15016275685860990408)
XLA Ops:
  0.9 1.0 select_select_fusion.refs_16_.refs_3_.refs_28_
  2.5 1.0 collective-permute-done.2.refs_17_.refs_3_.refs_29_
  4.0 2.7 %collective-permute-start = (bf16[130,512]{1,0:T(8,128)(2,1)S(1)}, bf16[130,512]{1,0:T(8,128)(2,1)S(1)}, u32[]{:S(2)}, u32[]{:S(2)}) collective-permute-start(bf16[130,512]{1,0:T(8,128)(2,1)S(1)} %select_select_fusion.refs_16_.refs_3_.refs_28_), channel_id=1, source_target_pairs={{0,5},{1,2},{2,7},{3,0},{4,1},{5,8},{6,3},{7,10},{8,13},{9,4},{10,... | collective-permute-start | bytes 399368 | tf_op jit(solution)/shard_map/ppermute | solution.py:73
  6.7 1.5 %collective-permute-start.8 = (bf16[130,512]{1,0:T(8,128)(2,1)S(1)}, bf16[130,512]{1,0:T(8,128)(2,1)S(1)}, u32[]{:S(2)}, u32[]{:S(2)}) collective-permute-start(bf16[130,512]{1,0:T(8,128)(2,1)S(1)} %collective-permute-done.2.refs_17_.refs_3_.refs_29_), channel_id=1, source_target_pairs={{0,5},{1,2},{2,7},{3,0},{4,1},{5,8},{6,3},{7,10},{8,13},{9,4},{10,... | collective-permute-start | bytes 399368 | tf_op jit(solution)/shard_map/ppermute | solution.py:73
  8.2 1.1 collective-permute-done.refs_18_.refs_30_
  9.3 2.1 %collective-permute-start.1 = (bf16[130,512]{1,0:T(8,128)(2,1)S(1)}, bf16[130,512]{1,0:T(8,128)(2,1)S(1)}, u32[]{:S(2)}, u32[]{:S(2)}) collective-permute-start(bf16[130,512]{1,0:T(8,128)(2,1)S(1)} %collective-permute-done.refs_18_.refs_30_), channel_id=1, source_target_pairs={{0,5},{1,2},{2,7},{3,0},{4,1},{5,8},{6,3},{7,10},{8,13},{9,4},{10,... | collective-permute-start | bytes 399368 | tf_op jit(solution)/shard_map/ppermute | solution.py:73
  11.4 1.2 %collective-permute-start.11 = (bf16[130,512]{1,0:T(8,128)(2,1)S(1)}, bf16[130,512]{1,0:T(8,128)(2,1)S(1)}, u32[]{:S(2)}, u32[]{:S(2)}) collective-permute-start(bf16[130,512]{1,0:T(8,128)(2,1)S(1)} %collective-permute-done.8.refs_20_.refs_32_), channel_id=1, source_target_pairs={{0,5},{1,2},{2,7},{3,0},{4,1},{5,8},{6,3},{7,10},{8,13},{9,4},{10,... | collective-permute-start | bytes 399368 | tf_op jit(solution)/shard_map/ppermute | solution.py:73
  12.7 1.4 %collective-permute-done.1.refs_22_.refs_34_ = bf16[130,512]{1,0:T(8,128)(2,1)S(1)} collective-permute-done((bf16[130,512]{1,0:T(8,128)(2,1)S(1)}, bf16[130,512]{1,0:T(8,128)(2,1)S(1)}, u32[]{:S(2)}, u32[]{:S(2)}) %collective-permute-start.1) | collective-permute-done | bytes 133152 | tf_op jit(solution)/shard_map/ppermute | solution.py:73
  14.1 2.1 %collective-permute-start.4 = (bf16[130,512]{1,0:T(8,128)(2,1)S(1)}, bf16[130,512]{1,0:T(8,128)(2,1)S(1)}, u32[]{:S(2)}, u32[]{:S(2)}) collective-permute-start(bf16[130,512]{1,0:T(8,128)(2,1)S(1)} %collective-permute-done.1.refs_22_.refs_34_), channel_id=1, source_target_pairs={{0,5},{1,2},{2,7},{3,0},{4,1},{5,8},{6,3},{7,10},{8,13},{9,4},{10,... | collective-permute-start | bytes 399368 | tf_op jit(solution)/shard_map/ppermute | solution.py:73
  17.3 1.7 %collective-permute-done.4.refs_26_.refs_38_ = bf16[130,512]{1,0:T(8,128)(2,1)S(1)} collective-permute-done((bf16[130,512]{1,0:T(8,128)(2,1)S(1)}, bf16[130,512]{1,0:T(8,128)(2,1)S(1)}, u32[]{:S(2)}, u32[]{:S(2)}) %collective-permute-start.4) | collective-permute-done | bytes 133152 | tf_op jit(solution)/shard_map/ppermute | solution.py:73
  19.3 1.4 %collective-permute-start.6 = (bf16[130,512]{1,0:T(8,128)(2,1)S(1)}, bf16[130,512]{1,0:T(8,128)(2,1)S(1)}, u32[]{:S(2)}, u32[]{:S(2)}) collective-permute-start(bf16[130,512]{1,0:T(8,128)(2,1)S(1)} %collective-permute-done.4.refs_26_.refs_38_), channel_id=1, source_target_pairs={{0,5},{1,2},{2,7},{3,0},{4,1},{5,8},{6,3},{7,10},{8,13},{9,4},{10,... | collective-permute-start | bytes 399368 | tf_op jit(solution)/shard_map/ppermute | solution.py:73
  20.7 1.7 %collective-permute-start.15 = (bf16[130,512]{1,0:T(8,128)(2,1)S(1)}, bf16[130,512]{1,0:T(8,128)(2,1)S(1)}, u32[]{:S(2)}, u32[]{:S(2)}) collective-permute-start(bf16[130,512]{1,0:T(8,128)(2,1)S(1)} %collective-permute-done.11.refs_24_.refs_36_), channel_id=1, source_target_pairs={{0,5},{1,2},{2,7},{3,0},{4,1},{5,8},{6,3},{7,10},{8,13},{9,4},{10,... | collective-permute-start | bytes 399368 | tf_op jit(solution)/shard_map/ppermute | solution.py:73
  22.4 3.8 %project.4 = (f32[128,512]{1,0:T(8,128)S(1)}, f32[128,128]{1,0:T(8,128)S(1)}, bf16[512,512]{1,0:T(8,128)(2,1)S(1)}, bf16[512,512]{1,0:T(8,128)(2,1)S(1)}, bf16[5...) custom-call(s32[1]{0:T(128)} %bitcast.5.refs_0_.refs_5_, s32[1]{0:T(128)} %bitcast.6.refs_1_.refs_6_, ...), custom_call_target="tpu_custom_call" | custom-call | flops 690000000 | tf_op jit(solution)/shard_map/project/pallas_call | solution.py:436
  27.1 1.5 %fetch.1 = (bf16[3072,128]{1,0:T(8,128)(2,1)S(1)}, bf16[3072,128]{1,0:T(8,128)(2,1)S(1)}) custom-call(s32[1]{0:T(128)} %bitcast.18.head, bf16[1536,1024]{1,0:T(8,128)(2,1)} %refs_1_.13, bf16[1536,1024]{1,0:T(8,128)(2,1)S(1)} %collective-permute-done.3.k1.refs_2_, bf16[1536,1024]{1,0:T(8,128)(2,1)} %refs_3_.13, ...), custom_call_target="tpu_custom_call" | custom-call | flops 414000000 | tf_op jit(solution)/shard_map/fetch/pallas_call | solution.py:186
  29.3 0.8 slice-done.1
  30.2 1.2 %collective-permute-start.17 = (bf16[512,128]{1,0:T(8,128)(2,1)S(1)}, bf16[512,128]{1,0:T(8,128)(2,1)S(1)}, u32[]{:S(2)}, u32[]{:S(2)}) collective-permute-start(bf16[512,128]{1,0:T(8,128)(2,1)S(1)} %project.5.q), channel_id=1, source_target_pairs={{0,5},{1,2},{2,7},{3,0},{4,1},{5,8},{6,3},{7,10},{8,13},{9,4},{10,... | collective-permute-start | bytes 393224 | tf_op jit(solution)/shard_map/ppermute | solution.py:73
  31.4 2.3 %attend.8 = (bf16[528,128]{1,0:T(8,128)(2,1)S(1)}, bf16[3072,128]{1,0:T(8,128)(2,1)S(1)}, bf16[3072,128]{1,0:T(8,128)(2,1)S(1)}) custom-call(bf16[512,128]{1,0:T(8,128)(2,1)S(1)} %project.5.q, bf16[128,128]{1,0:T(8,128)(2,1)S(1)} %get-tuple-element.140.bias, bf16[3072,128]{1,0:T(8,128)(2,1)S(1)} %get-tuple-element.139.onehot, ...), custom_call_target="tpu_custom_call" | custom-call | flops 3221225472 | bytes 3145728 | tf_op jit(solution)/shard_map/attend/pallas_call | solution.py:252
  33.7 0.9 collective-permute-done.17.q
  34.6 1.3 %collective-permute-start.19 = (bf16[512,128]{1,0:T(8,128)(2,1)S(1)}, bf16[512,128]{1,0:T(8,128)(2,1)S(1)}, u32[]{:S(2)}, u32[]{:S(2)}) collective-permute-start(bf16[512,128]{1,0:T(8,128)(2,1)S(1)} %collective-permute-done.17.q), channel_id=1, source_target_pairs={{0,5},{1,2},{2,7},{3,0},{4,1},{5,8},{6,3},{7,10},{8,13},{9,4},{10,... | collective-permute-start | bytes 393224 | tf_op jit(solution)/shard_map/ppermute | solution.py:73
  35.9 2.3 %attend.9 = (bf16[528,128]{1,0:T(8,128)(2,1)S(1)}, bf16[3072,128]{1,0:T(8,128)(2,1)S(1)}, bf16[3072,128]{1,0:T(8,128)(2,1)S(1)}) custom-call(bf16[512,128]{1,0:T(8,128)(2,1)S(1)} %collective-permute-done.17.q, bf16[128,128]{1,0:T(8,128)(2,1)S(1)} %get-tuple-element.140.bias, bf16[3072,128]{1,0:T(8,128)(2,1)S(1)} %get-tuple-element.139.onehot, ...), custom_call_target="tpu_custom_call" | custom-call | flops 3221225472 | bytes 3145728 | tf_op jit(solution)/shard_map/attend/pallas_call | solution.py:252
  38.1 1.6 %collective-permute-start.18 = (bf16[528,128]{1,0:T(8,128)(2,1)S(1)}, bf16[528,128]{1,0:T(8,128)(2,1)S(1)}, u32[]{:S(2)}, u32[]{:S(2)}) collective-permute-start(bf16[528,128]{1,0:T(8,128)(2,1)S(1)} %get-tuple-element.156), channel_id=1, source_target_pairs={{0,5},{1,2},{2,7},{3,0},{4,1},{5,8},{6,3},{7,10},{8,13},{9,4},{10,... | collective-permute-start | bytes 405512 | tf_op jit(solution)/shard_map/ppermute | solution.py:73
  40.2 2.4 %attend.10 = (bf16[528,128]{1,0:T(8,128)(2,1)S(1)}, bf16[3072,128]{1,0:T(8,128)(2,1)S(1)}, bf16[3072,128]{1,0:T(8,128)(2,1)S(1)}) custom-call(bf16[512,128]{1,0:T(8,128)(2,1)S(1)} %collective-permute-done.19.q, bf16[128,128]{1,0:T(8,128)(2,1)S(1)} %get-tuple-element.140.bias, bf16[3072,128]{1,0:T(8,128)(2,1)S(1)} %get-tuple-element.139.onehot, ...), custom_call_target="tpu_custom_call" | custom-call | flops 3221225472 | bytes 3145728 | tf_op jit(solution)/shard_map/attend/pallas_call | solution.py:252
  42.9 1.9 %collective-permute-start.20 = (bf16[528,128]{1,0:T(8,128)(2,1)S(1)}, bf16[528,128]{1,0:T(8,128)(2,1)S(1)}, u32[]{:S(2)}, u32[]{:S(2)}) collective-permute-start(bf16[528,128]{1,0:T(8,128)(2,1)S(1)} %merge.6), channel_id=1, source_target_pairs={{0,5},{1,2},{2,7},{3,0},{4,1},{5,8},{6,3},{7,10},{8,13},{9,4},{10,... | collective-permute-start | bytes 405512 | tf_op jit(solution)/shard_map/ppermute | solution.py:73
  44.7 0.8 collective-permute-start.23
  45.5 2.3 %attend.11 = (bf16[528,128]{1,0:T(8,128)(2,1)S(1)}, bf16[3072,128]{1,0:T(8,128)(2,1)S(1)}, bf16[3072,128]{1,0:T(8,128)(2,1)S(1)}) custom-call(bf16[512,128]{1,0:T(8,128)(2,1)S(1)} %collective-permute-done.21.q, bf16[128,128]{1,0:T(8,128)(2,1)S(1)} %get-tuple-element.140.bias, bf16[3072,128]{1,0:T(8,128)(2,1)S(1)} %get-tuple-element.139.onehot, ...), custom_call_target="tpu_custom_call" | custom-call | flops 3221225472 | bytes 3145728 | tf_op jit(solution)/shard_map/attend/pallas_call | solution.py:252
  48.1 1.6 %collective-permute-start.22 = (bf16[528,128]{1,0:T(8,128)(2,1)S(1)}, bf16[528,128]{1,0:T(8,128)(2,1)S(1)}, u32[]{:S(2)}, u32[]{:S(2)}) collective-permute-start(bf16[528,128]{1,0:T(8,128)(2,1)S(1)} %merge.7), channel_id=1, source_target_pairs={{0,5},{1,2},{2,7},{3,0},{4,1},{5,8},{6,3},{7,10},{8,13},{9,4},{10,... | collective-permute-start | bytes 405512 | tf_op jit(solution)/shard_map/ppermute | solution.py:73
  49.7 0.8 collective-permute-start.25
  50.6 2.3 %attend.12 = (bf16[528,128]{1,0:T(8,128)(2,1)S(1)}, bf16[3072,128]{1,0:T(8,128)(2,1)S(1)}, bf16[3072,128]{1,0:T(8,128)(2,1)S(1)}) custom-call(bf16[512,128]{1,0:T(8,128)(2,1)S(1)} %collective-permute-done.23.q, bf16[128,128]{1,0:T(8,128)(2,1)S(1)} %get-tuple-element.140.bias, bf16[3072,128]{1,0:T(8,128)(2,1)S(1)} %get-tuple-element.139.onehot, ...), custom_call_target="tpu_custom_call" | custom-call | flops 3221225472 | bytes 3145728 | tf_op jit(solution)/shard_map/attend/pallas_call | solution.py:252
  53.1 1.6 %collective-permute-start.24 = (bf16[528,128]{1,0:T(8,128)(2,1)S(1)}, bf16[528,128]{1,0:T(8,128)(2,1)S(1)}, u32[]{:S(2)}, u32[]{:S(2)}) collective-permute-start(bf16[528,128]{1,0:T(8,128)(2,1)S(1)} %merge.8), channel_id=1, source_target_pairs={{0,5},{1,2},{2,7},{3,0},{4,1},{5,8},{6,3},{7,10},{8,13},{9,4},{10,... | collective-permute-start | bytes 405512 | tf_op jit(solution)/shard_map/ppermute | solution.py:73
  54.7 0.9 collective-permute-start.27
  55.6 2.3 %attend.13 = (bf16[528,128]{1,0:T(8,128)(2,1)S(1)}, bf16[3072,128]{1,0:T(8,128)(2,1)S(1)}, bf16[3072,128]{1,0:T(8,128)(2,1)S(1)}) custom-call(bf16[512,128]{1,0:T(8,128)(2,1)S(1)} %collective-permute-done.25.q, bf16[128,128]{1,0:T(8,128)(2,1)S(1)} %get-tuple-element.140.bias, bf16[3072,128]{1,0:T(8,128)(2,1)S(1)} %get-tuple-element.139.onehot, ...), custom_call_target="tpu_custom_call" | custom-call | flops 3221225472 | bytes 3145728 | tf_op jit(solution)/shard_map/attend/pallas_call | solution.py:252
  58.2 1.4 %collective-permute-start.26 = (bf16[528,128]{1,0:T(8,128)(2,1)S(1)}, bf16[528,128]{1,0:T(8,128)(2,1)S(1)}, u32[]{:S(2)}, u32[]{:S(2)}) collective-permute-start(bf16[528,128]{1,0:T(8,128)(2,1)S(1)} %merge.9), channel_id=1, source_target_pairs={{0,5},{1,2},{2,7},{3,0},{4,1},{5,8},{6,3},{7,10},{8,13},{9,4},{10,... | collective-permute-start | bytes 405512 | tf_op jit(solution)/shard_map/ppermute | solution.py:73
  59.6 0.9 collective-permute-start.29
  60.5 2.3 %attend.14 = (bf16[528,128]{1,0:T(8,128)(2,1)S(1)}, bf16[3072,128]{1,0:T(8,128)(2,1)S(1)}, bf16[3072,128]{1,0:T(8,128)(2,1)S(1)}) custom-call(bf16[512,128]{1,0:T(8,128)(2,1)S(1)} %collective-permute-done.27.q, bf16[128,128]{1,0:T(8,128)(2,1)S(1)} %get-tuple-element.140.bias, bf16[3072,128]{1,0:T(8,128)(2,1)S(1)} %get-tuple-element.139.onehot, ...), custom_call_target="tpu_custom_call" | custom-call | flops 3221225472 | bytes 3145728 | tf_op jit(solution)/shard_map/attend/pallas_call | solution.py:252
  63.1 1.5 %collective-permute-start.28 = (bf16[528,128]{1,0:T(8,128)(2,1)S(1)}, bf16[528,128]{1,0:T(8,128)(2,1)S(1)}, u32[]{:S(2)}, u32[]{:S(2)}) collective-permute-start(bf16[528,128]{1,0:T(8,128)(2,1)S(1)} %merge.10), channel_id=1, source_target_pairs={{0,5},{1,2},{2,7},{3,0},{4,1},{5,8},{6,3},{7,10},{8,13},{9,4},{10,... | collective-permute-start | bytes 405512 | tf_op jit(solution)/shard_map/ppermute | solution.py:73
  64.6 2.1 %attend.15.two = bf16[528,128]{1,0:T(8,128)(2,1)S(1)} custom-call(bf16[512,128]{1,0:T(8,128)(2,1)S(1)} %collective-permute-done.29.q, bf16[128,128]{1,0:T(8,128)(2,1)S(1)} %get-tuple-element.140.bias, bf16[3072,128]{1,0:T(8,128)(2,1)S(1)} %get-tuple-element.139.onehot, bf16[3072,128]{1,0:T(8,128)(2,1)S(1)} %get-tuple-element.178.key, ...), custom_call_target="tpu_custom_call" | custom-call | flops 3221225472 | bytes 3145728 | tf_op jit(solution)/shard_map/attend/pallas_call | solution.py:252
  66.7 0.8 collective-permute-done.28.one
  67.8 1.8 %collective-permute-start.30 = (bf16[528,128]{1,0:T(8,128)(2,1)S(1)}, bf16[528,128]{1,0:T(8,128)(2,1)S(1)}, u32[]{:S(2)}, u32[]{:S(2)}) collective-permute-start(bf16[528,128]{1,0:T(8,128)(2,1)S(1)} %merge.11), channel_id=1, source_target_pairs={{0,5},{1,2},{2,7},{3,0},{4,1},{5,8},{6,3},{7,10},{8,13},{9,4},{10,... | collective-permute-start | bytes 405512 | tf_op jit(solution)/shard_map/ppermute | solution.py:73
  69.6 2.9 %collective-permute-done.30.refs_0_ = bf16[528,128]{1,0:T(8,128)(2,1)S(1)} collective-permute-done((bf16[528,128]{1,0:T(8,128)(2,1)S(1)}, bf16[528,128]{1,0:T(8,128)(2,1)S(1)}, u32[]{:S(2)}, u32[]{:S(2)}) %collective-permute-start.30) | collective-permute-done | bytes 135200 | tf_op jit(solution)/shard_map/ppermute | solution.py:73
  73.4 1.0 collective-permute-done.31.refs_8_.refs_3_
  74.8 1.0 collective-permute-start.33
  75.8 0.9 collective-permute-start.37
  76.7 1.1 mix.2
  77.8 1.5 %collective-permute-done.33.refs_1_ = bf16[128,512]{1,0:T(8,128)(2,1)S(1)} collective-permute-done((bf16[128,512]{1,0:T(8,128)(2,1)S(1)}, bf16[128,512]{1,0:T(8,128)(2,1)S(1)}, u32[]{:S(2)}, u32[]{:S(2)}) %collective-permute-start.33) | collective-permute-done | bytes 131104 | tf_op jit(solution)/shard_map/ppermute | solution.py:73
  79.3 1.3 %collective-permute-start.34 = (bf16[128,512]{1,0:T(8,128)(2,1)S(1)}, bf16[128,512]{1,0:T(8,128)(2,1)S(1)}, u32[]{:S(2)}, u32[]{:S(2)}) collective-permute-start(bf16[128,512]{1,0:T(8,128)(2,1)S(1)} %add.161), channel_id=1, source_target_pairs={{0,3},{1,4},{2,1},{3,6},{4,9},{5,0},{6,11},{7,2},{8,5},{9,12},{10,... | collective-permute-start | bytes 393224 | tf_op jit(solution)/shard_map/ppermute | solution.py:73
  80.7 1.0 collective-permute-start.38
  81.7 2.1 %collective-permute-done.34.refs_1_ = bf16[128,512]{1,0:T(8,128)(2,1)S(1)} collective-permute-done((bf16[128,512]{1,0:T(8,128)(2,1)S(1)}, bf16[128,512]{1,0:T(8,128)(2,1)S(1)}, u32[]{:S(2)}, u32[]{:S(2)}) %collective-permute-start.34) | collective-permute-done | bytes 131104 | tf_op jit(solution)/shard_map/ppermute | solution.py:73
  83.8 1.6 %collective-permute-start.35 = (bf16[128,512]{1,0:T(8,128)(2,1)S(1)}, bf16[128,512]{1,0:T(8,128)(2,1)S(1)}, u32[]{:S(2)}, u32[]{:S(2)}) collective-permute-start(bf16[128,512]{1,0:T(8,128)(2,1)S(1)} %add.162), channel_id=1, source_target_pairs={{0,3},{1,4},{2,1},{3,6},{4,9},{5,0},{6,11},{7,2},{8,5},{9,12},{10,... | collective-permute-start | bytes 393224 | tf_op jit(solution)/shard_map/ppermute | solution.py:73
  85.4 1.1 collective-permute-start.39
  86.5 2.0 %collective-permute-done.35.refs_1_ = bf16[128,512]{1,0:T(8,128)(2,1)S(1)} collective-permute-done((bf16[128,512]{1,0:T(8,128)(2,1)S(1)}, bf16[128,512]{1,0:T(8,128)(2,1)S(1)}, u32[]{:S(2)}, u32[]{:S(2)}) %collective-permute-start.35) | collective-permute-done | bytes 131104 | tf_op jit(solution)/shard_map/ppermute | solution.py:73
  88.5 1.6 %collective-permute-start.36 = (bf16[128,512]{1,0:T(8,128)(2,1)S(1)}, bf16[128,512]{1,0:T(8,128)(2,1)S(1)}, u32[]{:S(2)}, u32[]{:S(2)}) collective-permute-start(bf16[128,512]{1,0:T(8,128)(2,1)S(1)} %add.163), channel_id=1, source_target_pairs={{0,3},{1,4},{2,1},{3,6},{4,9},{5,0},{6,11},{7,2},{8,5},{9,12},{10,... | collective-permute-start | bytes 393224 | tf_op jit(solution)/shard_map/ppermute | solution.py:73
  90.6 2.6 %collective-permute-done.36.refs_1_ = bf16[128,512]{1,0:T(8,128)(2,1)S(1)} collective-permute-done((bf16[128,512]{1,0:T(8,128)(2,1)S(1)}, bf16[128,512]{1,0:T(8,128)(2,1)S(1)}, u32[]{:S(2)}, u32[]{:S(2)}) %collective-permute-start.36) | collective-permute-done | bytes 131104 | tf_op jit(solution)/shard_map/ppermute | solution.py:73
  94.0 1.1 collective-permute-start.41
  95.2 1.3 %collective-permute-start.47 = (bf16[128,512]{1,0:T(8,128)(2,1)S(1)}, bf16[128,512]{1,0:T(8,128)(2,1)S(1)}, u32[]{:S(2)}, u32[]{:S(2)}) collective-permute-start(bf16[128,512]{1,0:T(8,128)(2,1)S(1)} %add.167.refs_17_), channel_id=1, source_target_pairs={{0,5},{1,2},{2,7},{3,0},{4,1},{5,8},{6,3},{7,10},{8,13},{9,4},{10,... | collective-permute-start | bytes 393224 | tf_op jit(solution)/shard_map/ppermute | solution.py:73
  96.4 2.0 %collective-permute-done.41.refs_18_ = bf16[128,512]{1,0:T(8,128)(2,1)S(1)} collective-permute-done((bf16[128,512]{1,0:T(8,128)(2,1)S(1)}, bf16[128,512]{1,0:T(8,128)(2,1)S(1)}, u32[]{:S(2)}, u32[]{:S(2)}) %collective-permute-start.41) | collective-permute-done | bytes 131104 | tf_op jit(solution)/shard_map/ppermute | solution.py:73
  98.5 1.3 %collective-permute-start.42 = (bf16[128,512]{1,0:T(8,128)(2,1)S(1)}, bf16[128,512]{1,0:T(8,128)(2,1)S(1)}, u32[]{:S(2)}, u32[]{:S(2)}) collective-permute-start(bf16[128,512]{1,0:T(8,128)(2,1)S(1)} %collective-permute-done.41.refs_18_), channel_id=1, source_target_pairs={{0,5},{1,2},{2,7},{3,0},{4,1},{5,8},{6,3},{7,10},{8,13},{9,4},{10,... | collective-permute-start | bytes 393224 | tf_op jit(solution)/shard_map/ppermute | solution.py:73
  99.9 1.1 collective-permute-start.50
  101.0 1.9 %collective-permute-done.42.refs_22_ = bf16[128,512]{1,0:T(8,128)(2,1)S(1)} collective-permute-done((bf16[128,512]{1,0:T(8,128)(2,1)S(1)}, bf16[128,512]{1,0:T(8,128)(2,1)S(1)}, u32[]{:S(2)}, u32[]{:S(2)}) %collective-permute-start.42) | collective-permute-done | bytes 131104 | tf_op jit(solution)/shard_map/ppermute | solution.py:73
  102.9 1.6 %collective-permute-start.43 = (bf16[128,512]{1,0:T(8,128)(2,1)S(1)}, bf16[128,512]{1,0:T(8,128)(2,1)S(1)}, u32[]{:S(2)}, u32[]{:S(2)}) collective-permute-start(bf16[128,512]{1,0:T(8,128)(2,1)S(1)} %collective-permute-done.42.refs_22_), channel_id=1, source_target_pairs={{0,5},{1,2},{2,7},{3,0},{4,1},{5,8},{6,3},{7,10},{8,13},{9,4},{10,... | collective-permute-start | bytes 393224 | tf_op jit(solution)/shard_map/ppermute | solution.py:73
  105.5 1.8 %collective-permute-done.43.refs_26_ = bf16[128,512]{1,0:T(8,128)(2,1)S(1)} collective-permute-done((bf16[128,512]{1,0:T(8,128)(2,1)S(1)}, bf16[128,512]{1,0:T(8,128)(2,1)S(1)}, u32[]{:S(2)}, u32[]{:S(2)}) %collective-permute-start.43) | collective-permute-done | bytes 131104 | tf_op jit(solution)/shard_map/ppermute | solution.py:73
  107.9 1.0 collective-permute-start.44
  108.9 0.8 collective-permute-start.54
  109.7 3.9 %project.6 = (f32[128,512]{1,0:T(8,128)S(1)}, f32[128,128]{1,0:T(8,128)S(1)}, bf16[512,512]{1,0:T(8,128)(2,1)S(1)}, bf16[512,512]{1,0:T(8,128)(2,1)S(1)}, bf16[5...) custom-call(s32[1]{0:T(128)} %bitcast.5.refs_0_.refs_5_, s32[1]{0:T(128)} %bitcast.6.refs_1_.refs_6_, ...), custom_call_target="tpu_custom_call" | custom-call | flops 690000000 | tf_op jit(solution)/shard_map/project/pallas_call | solution.py:436
  115.2 1.1 project.7
  (91 shorter events, 12.1 us)
Async XLA Ops:
  0.6 26.2 %copy-start.1 = (s32[128]{0:T(128)S(1)}, s32[128]{0:T(128)}, u32[]{:S(2)}) copy-start(s32[128]{0:T(128)} %param.16) | copy-start | bytes 1540
  2.0 1.5 %collective-permute-start.2 = (bf16[130,512]{1,0:T(8,128)(2,1)S(1)}, bf16[130,512]{1,0:T(8,128)(2,1)S(1)}, u32[]{:S(2)}, u32[]{:S(2)}) collective-permute-start(bf16[130,512]{1,0:T(8,128)(2,1)S(1)} %select_select_fusion.refs_16_.refs_3_.refs_28_), channel_id=1, source_target_pairs={{0,1},{1,0},{2,3},{3,2},{4,5},{5,4},{6,7},{7,6},{8,9},{9,8},{10,11... | collective-permute-start | bytes 399368 | tf_op jit(solution)/shard_map/ppermute | solution.py:76
  3.5 10.7 %collective-permute-start.3 = (bf16[1536,1024]{1,0:T(8,128)(2,1)}, bf16[1536,1024]{1,0:T(8,128)(2,1)S(1)}, u32[]{:S(2)}, u32[]{:S(2)}) collective-permute-start(bf16[1536,1024]{1,0:T(8,128)(2,1)} %refs_1_.13), channel_id=1, source_target_pairs={{0,1},{1,0},{2,3},{3,2},{4,5},{5,4},{6,7},{7,6},{8,9},{9,8},{10,11... | collective-permute-start | bytes 9437192 | tf_op jit(solution)/shard_map/ppermute | solution.py:76
  3.8 12.9 %collective-permute-start.5 = (bf16[1536,1024]{1,0:T(8,128)(2,1)}, bf16[1536,1024]{1,0:T(8,128)(2,1)S(1)}, u32[]{:S(2)}, u32[]{:S(2)}) collective-permute-start(bf16[1536,1024]{1,0:T(8,128)(2,1)} %refs_3_.13), channel_id=1, source_target_pairs={{0,1},{1,0},{2,3},{3,2},{4,5},{5,4},{6,7},{7,6},{8,9},{9,8},{10,11... | collective-permute-start | bytes 9437192 | tf_op jit(solution)/shard_map/ppermute | solution.py:76
  4.0 5.4 %collective-permute-start = (bf16[130,512]{1,0:T(8,128)(2,1)S(1)}, bf16[130,512]{1,0:T(8,128)(2,1)S(1)}, u32[]{:S(2)}, u32[]{:S(2)}) collective-permute-start(bf16[130,512]{1,0:T(8,128)(2,1)S(1)} %select_select_fusion.refs_16_.refs_3_.refs_28_), channel_id=1, source_target_pairs={{0,5},{1,2},{2,7},{3,0},{4,1},{5,8},{6,3},{7,10},{8,13},{9,4},{10,... | collective-permute-start | bytes 399368 | tf_op jit(solution)/shard_map/ppermute | solution.py:73
  6.7 4.8 %collective-permute-start.8 = (bf16[130,512]{1,0:T(8,128)(2,1)S(1)}, bf16[130,512]{1,0:T(8,128)(2,1)S(1)}, u32[]{:S(2)}, u32[]{:S(2)}) collective-permute-start(bf16[130,512]{1,0:T(8,128)(2,1)S(1)} %collective-permute-done.2.refs_17_.refs_3_.refs_29_), channel_id=1, source_target_pairs={{0,5},{1,2},{2,7},{3,0},{4,1},{5,8},{6,3},{7,10},{8,13},{9,4},{10,... | collective-permute-start | bytes 399368 | tf_op jit(solution)/shard_map/ppermute | solution.py:73
  9.3 4.8 %collective-permute-start.1 = (bf16[130,512]{1,0:T(8,128)(2,1)S(1)}, bf16[130,512]{1,0:T(8,128)(2,1)S(1)}, u32[]{:S(2)}, u32[]{:S(2)}) collective-permute-start(bf16[130,512]{1,0:T(8,128)(2,1)S(1)} %collective-permute-done.refs_18_.refs_30_), channel_id=1, source_target_pairs={{0,5},{1,2},{2,7},{3,0},{4,1},{5,8},{6,3},{7,10},{8,13},{9,4},{10,... | collective-permute-start | bytes 399368 | tf_op jit(solution)/shard_map/ppermute | solution.py:73
  11.4 5.3 %collective-permute-start.11 = (bf16[130,512]{1,0:T(8,128)(2,1)S(1)}, bf16[130,512]{1,0:T(8,128)(2,1)S(1)}, u32[]{:S(2)}, u32[]{:S(2)}) collective-permute-start(bf16[130,512]{1,0:T(8,128)(2,1)S(1)} %collective-permute-done.8.refs_20_.refs_32_), channel_id=1, source_target_pairs={{0,5},{1,2},{2,7},{3,0},{4,1},{5,8},{6,3},{7,10},{8,13},{9,4},{10,... | collective-permute-start | bytes 399368 | tf_op jit(solution)/shard_map/ppermute | solution.py:73
  14.1 4.8 %collective-permute-start.4 = (bf16[130,512]{1,0:T(8,128)(2,1)S(1)}, bf16[130,512]{1,0:T(8,128)(2,1)S(1)}, u32[]{:S(2)}, u32[]{:S(2)}) collective-permute-start(bf16[130,512]{1,0:T(8,128)(2,1)S(1)} %collective-permute-done.1.refs_22_.refs_34_), channel_id=1, source_target_pairs={{0,5},{1,2},{2,7},{3,0},{4,1},{5,8},{6,3},{7,10},{8,13},{9,4},{10,... | collective-permute-start | bytes 399368 | tf_op jit(solution)/shard_map/ppermute | solution.py:73
  16.2 3.1 %collective-permute-start.7 = (bf16[130,512]{1,0:T(8,128)(2,1)S(1)}, bf16[130,512]{1,0:T(8,128)(2,1)S(1)}, u32[]{:S(2)}, u32[]{:S(2)}) collective-permute-start(bf16[130,512]{1,0:T(8,128)(2,1)S(1)} %collective-permute-done.refs_18_.refs_30_), channel_id=1, source_target_pairs={{0,1},{1,0},{2,3},{3,2},{4,5},{5,4},{6,7},{7,6},{8,9},{9,8},{10,11... | collective-permute-start | bytes 399368 | tf_op jit(solution)/shard_map/ppermute | solution.py:76
  16.2 4.5 %collective-permute-start.9 = (bf16[130,512]{1,0:T(8,128)(2,1)S(1)}, bf16[130,512]{1,0:T(8,128)(2,1)S(1)}, u32[]{:S(2)}, u32[]{:S(2)}) collective-permute-start(bf16[130,512]{1,0:T(8,128)(2,1)S(1)} %collective-permute-done.8.refs_20_.refs_32_), channel_id=1, source_target_pairs={{0,1},{1,0},{2,3},{3,2},{4,5},{5,4},{6,7},{7,6},{8,9},{9,8},{10,11... | collective-permute-start | bytes 399368 | tf_op jit(solution)/shard_map/ppermute | solution.py:76
  16.7 5.7 %collective-permute-start.10 = (bf16[130,512]{1,0:T(8,128)(2,1)S(1)}, bf16[130,512]{1,0:T(8,128)(2,1)S(1)}, u32[]{:S(2)}, u32[]{:S(2)}) collective-permute-start(bf16[130,512]{1,0:T(8,128)(2,1)S(1)} %collective-permute-done.1.refs_22_.refs_34_), channel_id=1, source_target_pairs={{0,1},{1,0},{2,3},{3,2},{4,5},{5,4},{6,7},{7,6},{8,9},{9,8},{10,11... | collective-permute-start | bytes 399368 | tf_op jit(solution)/shard_map/ppermute | solution.py:76
  16.7 5.7 %collective-permute-start.12 = (bf16[130,512]{1,0:T(8,128)(2,1)S(1)}, bf16[130,512]{1,0:T(8,128)(2,1)S(1)}, u32[]{:S(2)}, u32[]{:S(2)}) collective-permute-start(bf16[130,512]{1,0:T(8,128)(2,1)S(1)} %collective-permute-done.11.refs_24_.refs_36_), channel_id=1, source_target_pairs={{0,1},{1,0},{2,3},{3,2},{4,5},{5,4},{6,7},{7,6},{8,9},{9,8},{10,11... | collective-permute-start | bytes 399368 | tf_op jit(solution)/shard_map/ppermute | solution.py:76
  18.9 3.5 %collective-permute-start.13 = (bf16[130,512]{1,0:T(8,128)(2,1)S(1)}, bf16[130,512]{1,0:T(8,128)(2,1)S(1)}, u32[]{:S(2)}, u32[]{:S(2)}) collective-permute-start(bf16[130,512]{1,0:T(8,128)(2,1)S(1)} %collective-permute-done.4.refs_26_.refs_38_), channel_id=1, source_target_pairs={{0,1},{1,0},{2,3},{3,2},{4,5},{5,4},{6,7},{7,6},{8,9},{9,8},{10,11... | collective-permute-start | bytes 399368 | tf_op jit(solution)/shard_map/ppermute | solution.py:76
  19.3 6.9 %collective-permute-start.6 = (bf16[130,512]{1,0:T(8,128)(2,1)S(1)}, bf16[130,512]{1,0:T(8,128)(2,1)S(1)}, u32[]{:S(2)}, u32[]{:S(2)}) collective-permute-start(bf16[130,512]{1,0:T(8,128)(2,1)S(1)} %collective-permute-done.4.refs_26_.refs_38_), channel_id=1, source_target_pairs={{0,5},{1,2},{2,7},{3,0},{4,1},{5,8},{6,3},{7,10},{8,13},{9,4},{10,... | collective-permute-start | bytes 399368 | tf_op jit(solution)/shard_map/ppermute | solution.py:73
  20.7 5.6 %collective-permute-start.15 = (bf16[130,512]{1,0:T(8,128)(2,1)S(1)}, bf16[130,512]{1,0:T(8,128)(2,1)S(1)}, u32[]{:S(2)}, u32[]{:S(2)}) collective-permute-start(bf16[130,512]{1,0:T(8,128)(2,1)S(1)} %collective-permute-done.11.refs_24_.refs_36_), channel_id=1, source_target_pairs={{0,5},{1,2},{2,7},{3,0},{4,1},{5,8},{6,3},{7,10},{8,13},{9,4},{10,... | collective-permute-start | bytes 399368 | tf_op jit(solution)/shard_map/ppermute | solution.py:73
  26.2 2.5 %copy-start = (bf16[128]{0:T(256)(128)(2,1)S(1)}, bf16[128]{0:T(256)(128)(2,1)}, u32[]{:S(2)}) copy-start(bf16[128]{0:T(256)(128)(2,1)} %param.13) | copy-start | bytes 772
  26.2 3.1 %slice-start = ((s8[8388608]{0:T(1024)(128)(4,1)}), s8[4194304]{0:T(1024)(128)(4,1)S(1)}, s32[]{:S(2)}) async-start(s8[8388608]{0:T(1024)(128)(4,1)} %bitcast.27), calls=%async_computation | async-start | bytes 8388608
  26.2 2.5 %collective-permute-start.14 = (bf16[130,512]{1,0:T(8,128)(2,1)S(1)}, bf16[130,512]{1,0:T(8,128)(2,1)S(1)}, u32[]{:S(2)}, u32[]{:S(2)}) collective-permute-start(bf16[130,512]{1,0:T(8,128)(2,1)S(1)} %collective-permute-done.6.refs_0_.refs_4_), channel_id=1, source_target_pairs={{0,1},{1,0},{2,3},{3,2},{4,5},{5,4},{6,7},{7,6},{8,9},{9,8},{10,11... | collective-permute-start | bytes 399368 | tf_op jit(solution)/shard_map/ppermute | solution.py:76
  26.3 2.4 %collective-permute-start.16 = (bf16[130,512]{1,0:T(8,128)(2,1)S(1)}, bf16[130,512]{1,0:T(8,128)(2,1)S(1)}, u32[]{:S(2)}, u32[]{:S(2)}) collective-permute-start(bf16[130,512]{1,0:T(8,128)(2,1)S(1)} %collective-permute-done.15.refs_2_.refs_6_), channel_id=1, source_target_pairs={{0,1},{1,0},{2,3},{3,2},{4,5},{5,4},{6,7},{7,6},{8,9},{9,8},{10,11... | collective-permute-start | bytes 399368 | tf_op jit(solution)/shard_map/ppermute | solution.py:76
  27.1 3.0 %slice-start.1 = ((s8[8388608]{0:T(1024)(128)(4,1)}), s8[4194304]{0:T(1024)(128)(4,1)S(1)}, s32[]{:S(2)}) async-start(s8[8388608]{0:T(1024)(128)(4,1)} %bitcast.27), calls=%async_computation.1 | async-start | bytes 8388608
  30.2 44.2 %collective-permute-start.32 = (bf16[512,8192]{1,0:T(8,128)(2,1)S(1)}, bf16[512,8192]{1,0:T(8,128)(2,1)S(1)}, u32[]{:S(2)}, u32[]{:S(2)}) collective-permute-start(bf16[512,8192]{1,0:T(8,128)(2,1)S(1)} %bitcast.28), channel_id=1, source_target_pairs={{0,1},{1,0},{2,3},{3,2},{4,5},{5,4},{6,7},{7,6},{8,9},{9,8},{10,11... | collective-permute-start | bytes 25165832 | tf_op jit(solution)/shard_map/ppermute | solution.py:76
  30.2 4.4 %collective-permute-start.17 = (bf16[512,128]{1,0:T(8,128)(2,1)S(1)}, bf16[512,128]{1,0:T(8,128)(2,1)S(1)}, u32[]{:S(2)}, u32[]{:S(2)}) collective-permute-start(bf16[512,128]{1,0:T(8,128)(2,1)S(1)} %project.5.q), channel_id=1, source_target_pairs={{0,5},{1,2},{2,7},{3,0},{4,1},{5,8},{6,3},{7,10},{8,13},{9,4},{10,... | collective-permute-start | bytes 393224 | tf_op jit(solution)/shard_map/ppermute | solution.py:73
  34.6 5.2 %collective-permute-start.19 = (bf16[512,128]{1,0:T(8,128)(2,1)S(1)}, bf16[512,128]{1,0:T(8,128)(2,1)S(1)}, u32[]{:S(2)}, u32[]{:S(2)}) collective-permute-start(bf16[512,128]{1,0:T(8,128)(2,1)S(1)} %collective-permute-done.17.q), channel_id=1, source_target_pairs={{0,5},{1,2},{2,7},{3,0},{4,1},{5,8},{6,3},{7,10},{8,13},{9,4},{10,... | collective-permute-start | bytes 393224 | tf_op jit(solution)/shard_map/ppermute | solution.py:73
  38.1 4.5 %collective-permute-start.18 = (bf16[528,128]{1,0:T(8,128)(2,1)S(1)}, bf16[528,128]{1,0:T(8,128)(2,1)S(1)}, u32[]{:S(2)}, u32[]{:S(2)}) collective-permute-start(bf16[528,128]{1,0:T(8,128)(2,1)S(1)} %get-tuple-element.156), channel_id=1, source_target_pairs={{0,5},{1,2},{2,7},{3,0},{4,1},{5,8},{6,3},{7,10},{8,13},{9,4},{10,... | collective-permute-start | bytes 405512 | tf_op jit(solution)/shard_map/ppermute | solution.py:73
  39.7 5.0 %collective-permute-start.21 = (bf16[512,128]{1,0:T(8,128)(2,1)S(1)}, bf16[512,128]{1,0:T(8,128)(2,1)S(1)}, u32[]{:S(2)}, u32[]{:S(2)}) collective-permute-start(bf16[512,128]{1,0:T(8,128)(2,1)S(1)} %collective-permute-done.19.q), channel_id=1, source_target_pairs={{0,5},{1,2},{2,7},{3,0},{4,1},{5,8},{6,3},{7,10},{8,13},{9,4},{10,... | collective-permute-start | bytes 393224 | tf_op jit(solution)/shard_map/ppermute | solution.py:73
  42.9 5.0 %collective-permute-start.20 = (bf16[528,128]{1,0:T(8,128)(2,1)S(1)}, bf16[528,128]{1,0:T(8,128)(2,1)S(1)}, u32[]{:S(2)}, u32[]{:S(2)}) collective-permute-start(bf16[528,128]{1,0:T(8,128)(2,1)S(1)} %merge.6), channel_id=1, source_target_pairs={{0,5},{1,2},{2,7},{3,0},{4,1},{5,8},{6,3},{7,10},{8,13},{9,4},{10,... | collective-permute-start | bytes 405512 | tf_op jit(solution)/shard_map/ppermute | solution.py:73
  44.7 5.0 %collective-permute-start.23 = (bf16[512,128]{1,0:T(8,128)(2,1)S(1)}, bf16[512,128]{1,0:T(8,128)(2,1)S(1)}, u32[]{:S(2)}, u32[]{:S(2)}) collective-permute-start(bf16[512,128]{1,0:T(8,128)(2,1)S(1)} %collective-permute-done.21.q), channel_id=1, source_target_pairs={{0,5},{1,2},{2,7},{3,0},{4,1},{5,8},{6,3},{7,10},{8,13},{9,4},{10,... | collective-permute-start | bytes 393224 | tf_op jit(solution)/shard_map/ppermute | solution.py:73
  48.1 4.7 %collective-permute-start.22 = (bf16[528,128]{1,0:T(8,128)(2,1)S(1)}, bf16[528,128]{1,0:T(8,128)(2,1)S(1)}, u32[]{:S(2)}, u32[]{:S(2)}) collective-permute-start(bf16[528,128]{1,0:T(8,128)(2,1)S(1)} %merge.7), channel_id=1, source_target_pairs={{0,5},{1,2},{2,7},{3,0},{4,1},{5,8},{6,3},{7,10},{8,13},{9,4},{10,... | collective-permute-start | bytes 405512 | tf_op jit(solution)/shard_map/ppermute | solution.py:73
  49.7 4.9 %collective-permute-start.25 = (bf16[512,128]{1,0:T(8,128)(2,1)S(1)}, bf16[512,128]{1,0:T(8,128)(2,1)S(1)}, u32[]{:S(2)}, u32[]{:S(2)}) collective-permute-start(bf16[512,128]{1,0:T(8,128)(2,1)S(1)} %collective-permute-done.23.q), channel_id=1, source_target_pairs={{0,5},{1,2},{2,7},{3,0},{4,1},{5,8},{6,3},{7,10},{8,13},{9,4},{10,... | collective-permute-start | bytes 393224 | tf_op jit(solution)/shard_map/ppermute | solution.py:73
  53.1 4.8 %collective-permute-start.24 = (bf16[528,128]{1,0:T(8,128)(2,1)S(1)}, bf16[528,128]{1,0:T(8,128)(2,1)S(1)}, u32[]{:S(2)}, u32[]{:S(2)}) collective-permute-start(bf16[528,128]{1,0:T(8,128)(2,1)S(1)} %merge.8), channel_id=1, source_target_pairs={{0,5},{1,2},{2,7},{3,0},{4,1},{5,8},{6,3},{7,10},{8,13},{9,4},{10,... | collective-permute-start | bytes 405512 | tf_op jit(solution)/shard_map/ppermute | solution.py:73
  54.7 4.9 %collective-permute-start.27 = (bf16[512,128]{1,0:T(8,128)(2,1)S(1)}, bf16[512,128]{1,0:T(8,128)(2,1)S(1)}, u32[]{:S(2)}, u32[]{:S(2)}) collective-permute-start(bf16[512,128]{1,0:T(8,128)(2,1)S(1)} %collective-permute-done.25.q), channel_id=1, source_target_pairs={{0,5},{1,2},{2,7},{3,0},{4,1},{5,8},{6,3},{7,10},{8,13},{9,4},{10,... | collective-permute-start | bytes 393224 | tf_op jit(solution)/shard_map/ppermute | solution.py:73
  58.2 4.7 %collective-permute-start.26 = (bf16[528,128]{1,0:T(8,128)(2,1)S(1)}, bf16[528,128]{1,0:T(8,128)(2,1)S(1)}, u32[]{:S(2)}, u32[]{:S(2)}) collective-permute-start(bf16[528,128]{1,0:T(8,128)(2,1)S(1)} %merge.9), channel_id=1, source_target_pairs={{0,5},{1,2},{2,7},{3,0},{4,1},{5,8},{6,3},{7,10},{8,13},{9,4},{10,... | collective-permute-start | bytes 405512 | tf_op jit(solution)/shard_map/ppermute | solution.py:73
  59.6 5.0 %collective-permute-start.29 = (bf16[512,128]{1,0:T(8,128)(2,1)S(1)}, bf16[512,128]{1,0:T(8,128)(2,1)S(1)}, u32[]{:S(2)}, u32[]{:S(2)}) collective-permute-start(bf16[512,128]{1,0:T(8,128)(2,1)S(1)} %collective-permute-done.27.q), channel_id=1, source_target_pairs={{0,5},{1,2},{2,7},{3,0},{4,1},{5,8},{6,3},{7,10},{8,13},{9,4},{10,... | collective-permute-start | bytes 393224 | tf_op jit(solution)/shard_map/ppermute | solution.py:73
  63.1 4.5 %collective-permute-start.28 = (bf16[528,128]{1,0:T(8,128)(2,1)S(1)}, bf16[528,128]{1,0:T(8,128)(2,1)S(1)}, u32[]{:S(2)}, u32[]{:S(2)}) collective-permute-start(bf16[528,128]{1,0:T(8,128)(2,1)S(1)} %merge.10), channel_id=1, source_target_pairs={{0,5},{1,2},{2,7},{3,0},{4,1},{5,8},{6,3},{7,10},{8,13},{9,4},{10,... | collective-permute-start | bytes 405512 | tf_op jit(solution)/shard_map/ppermute | solution.py:73
  67.8 4.7 %collective-permute-start.30 = (bf16[528,128]{1,0:T(8,128)(2,1)S(1)}, bf16[528,128]{1,0:T(8,128)(2,1)S(1)}, u32[]{:S(2)}, u32[]{:S(2)}) collective-permute-start(bf16[528,128]{1,0:T(8,128)(2,1)S(1)} %merge.11), channel_id=1, source_target_pairs={{0,5},{1,2},{2,7},{3,0},{4,1},{5,8},{6,3},{7,10},{8,13},{9,4},{10,... | collective-permute-start | bytes 405512 | tf_op jit(solution)/shard_map/ppermute | solution.py:73
  72.8 1.5 %collective-permute-start.31 = (bf16[128,512]{1,0:T(8,128)(2,1)S(1)}, bf16[128,512]{1,0:T(8,128)(2,1)S(1)}, u32[]{:S(2)}, u32[]{:S(2)}) collective-permute-start(bf16[128,512]{1,0:T(8,128)(2,1)S(1)} %finish.1.refs_7_.refs_2_), channel_id=1, source_target_pairs={{0,1},{1,0},{2,3},{3,2},{4,5},{5,4},{6,7},{7,6},{8,9},{9,8},{10,11... | collective-permute-start | bytes 393224 | tf_op jit(solution)/shard_map/ppermute | solution.py:76
  74.8 4.4 %collective-permute-start.33 = (bf16[128,512]{1,0:T(8,128)(2,1)S(1)}, bf16[128,512]{1,0:T(8,128)(2,1)S(1)}, u32[]{:S(2)}, u32[]{:S(2)}) collective-permute-start(bf16[128,512]{1,0:T(8,128)(2,1)S(1)} %get-tuple-element.185), channel_id=1, source_target_pairs={{0,3},{1,4},{2,1},{3,6},{4,9},{5,0},{6,11},{7,2},{8,5},{9,12},{10,... | collective-permute-start | bytes 393224 | tf_op jit(solution)/shard_map/ppermute | solution.py:73
  75.8 4.9 %collective-permute-start.37 = (bf16[128,512]{1,0:T(8,128)(2,1)S(1)}, bf16[128,512]{1,0:T(8,128)(2,1)S(1)}, u32[]{:S(2)}, u32[]{:S(2)}) collective-permute-start(bf16[128,512]{1,0:T(8,128)(2,1)S(1)} %get-tuple-element.188), channel_id=1, source_target_pairs={{0,3},{1,4},{2,1},{3,6},{4,9},{5,0},{6,11},{7,2},{8,5},{9,12},{10,... | collective-permute-start | bytes 393224 | tf_op jit(solution)/shard_map/ppermute | solution.py:73
  79.3 4.4 %collective-permute-start.34 = (bf16[128,512]{1,0:T(8,128)(2,1)S(1)}, bf16[128,512]{1,0:T(8,128)(2,1)S(1)}, u32[]{:S(2)}, u32[]{:S(2)}) collective-permute-start(bf16[128,512]{1,0:T(8,128)(2,1)S(1)} %add.161), channel_id=1, source_target_pairs={{0,3},{1,4},{2,1},{3,6},{4,9},{5,0},{6,11},{7,2},{8,5},{9,12},{10,... | collective-permute-start | bytes 393224 | tf_op jit(solution)/shard_map/ppermute | solution.py:73
  80.7 4.7 %collective-permute-start.38 = (bf16[128,512]{1,0:T(8,128)(2,1)S(1)}, bf16[128,512]{1,0:T(8,128)(2,1)S(1)}, u32[]{:S(2)}, u32[]{:S(2)}) collective-permute-start(bf16[128,512]{1,0:T(8,128)(2,1)S(1)} %add.164), channel_id=1, source_target_pairs={{0,3},{1,4},{2,1},{3,6},{4,9},{5,0},{6,11},{7,2},{8,5},{9,12},{10,... | collective-permute-start | bytes 393224 | tf_op jit(solution)/shard_map/ppermute | solution.py:73
  83.8 4.7 %collective-permute-start.35 = (bf16[128,512]{1,0:T(8,128)(2,1)S(1)}, bf16[128,512]{1,0:T(8,128)(2,1)S(1)}, u32[]{:S(2)}, u32[]{:S(2)}) collective-permute-start(bf16[128,512]{1,0:T(8,128)(2,1)S(1)} %add.162), channel_id=1, source_target_pairs={{0,3},{1,4},{2,1},{3,6},{4,9},{5,0},{6,11},{7,2},{8,5},{9,12},{10,... | collective-permute-start | bytes 393224 | tf_op jit(solution)/shard_map/ppermute | solution.py:73
  85.4 4.7 %collective-permute-start.39 = (bf16[128,512]{1,0:T(8,128)(2,1)S(1)}, bf16[128,512]{1,0:T(8,128)(2,1)S(1)}, u32[]{:S(2)}, u32[]{:S(2)}) collective-permute-start(bf16[128,512]{1,0:T(8,128)(2,1)S(1)} %add.165), channel_id=1, source_target_pairs={{0,3},{1,4},{2,1},{3,6},{4,9},{5,0},{6,11},{7,2},{8,5},{9,12},{10,... | collective-permute-start | bytes 393224 | tf_op jit(solution)/shard_map/ppermute | solution.py:73
  88.5 4.7 %collective-permute-start.36 = (bf16[128,512]{1,0:T(8,128)(2,1)S(1)}, bf16[128,512]{1,0:T(8,128)(2,1)S(1)}, u32[]{:S(2)}, u32[]{:S(2)}) collective-permute-start(bf16[128,512]{1,0:T(8,128)(2,1)S(1)} %add.163), channel_id=1, source_target_pairs={{0,3},{1,4},{2,1},{3,6},{4,9},{5,0},{6,11},{7,2},{8,5},{9,12},{10,... | collective-permute-start | bytes 393224 | tf_op jit(solution)/shard_map/ppermute | solution.py:73
  90.1 3.8 %collective-permute-start.40 = (bf16[128,512]{1,0:T(8,128)(2,1)S(1)}, bf16[128,512]{1,0:T(8,128)(2,1)S(1)}, u32[]{:S(2)}, u32[]{:S(2)}) collective-permute-start(bf16[128,512]{1,0:T(8,128)(2,1)S(1)} %collective-permute-done.39.refs_1_), channel_id=1, source_target_pairs={{0,1},{1,0},{2,3},{3,2},{4,5},{5,4},{6,7},{7,6},{8,9},{9,8},{10,11... | collective-permute-start | bytes 393224 | tf_op jit(solution)/shard_map/ppermute | solution.py:76
  93.2 1.9 %collective-permute-start.45 = (bf16[128,512]{1,0:T(8,128)(2,1)S(1)}, bf16[128,512]{1,0:T(8,128)(2,1)S(1)}, u32[]{:S(2)}, u32[]{:S(2)}) collective-permute-start(bf16[128,512]{1,0:T(8,128)(2,1)S(1)} %collective-permute-done.36.refs_1_), channel_id=1, source_target_pairs={{0,1},{1,0},{2,3},{3,2},{4,5},{5,4},{6,7},{7,6},{8,9},{9,8},{10,11... | collective-permute-start | bytes 393224 | tf_op jit(solution)/shard_map/ppermute | solution.py:76
  94.0 4.4 %collective-permute-start.41 = (bf16[128,512]{1,0:T(8,128)(2,1)S(1)}, bf16[128,512]{1,0:T(8,128)(2,1)S(1)}, u32[]{:S(2)}, u32[]{:S(2)}) collective-permute-start(bf16[128,512]{1,0:T(8,128)(2,1)S(1)} %add.166.refs_16_), channel_id=1, source_target_pairs={{0,5},{1,2},{2,7},{3,0},{4,1},{5,8},{6,3},{7,10},{8,13},{9,4},{10,... | collective-permute-start | bytes 393224 | tf_op jit(solution)/shard_map/ppermute | solution.py:73
  95.2 4.7 %collective-permute-start.47 = (bf16[128,512]{1,0:T(8,128)(2,1)S(1)}, bf16[128,512]{1,0:T(8,128)(2,1)S(1)}, u32[]{:S(2)}, u32[]{:S(2)}) collective-permute-start(bf16[128,512]{1,0:T(8,128)(2,1)S(1)} %add.167.refs_17_), channel_id=1, source_target_pairs={{0,5},{1,2},{2,7},{3,0},{4,1},{5,8},{6,3},{7,10},{8,13},{9,4},{10,... | collective-permute-start | bytes 393224 | tf_op jit(solution)/shard_map/ppermute | solution.py:73
  98.5 4.4 %collective-permute-start.42 = (bf16[128,512]{1,0:T(8,128)(2,1)S(1)}, bf16[128,512]{1,0:T(8,128)(2,1)S(1)}, u32[]{:S(2)}, u32[]{:S(2)}) collective-permute-start(bf16[128,512]{1,0:T(8,128)(2,1)S(1)} %collective-permute-done.41.refs_18_), channel_id=1, source_target_pairs={{0,5},{1,2},{2,7},{3,0},{4,1},{5,8},{6,3},{7,10},{8,13},{9,4},{10,... | collective-permute-start | bytes 393224 | tf_op jit(solution)/shard_map/ppermute | solution.py:73
  99.9 5.1 %collective-permute-start.50 = (bf16[128,512]{1,0:T(8,128)(2,1)S(1)}, bf16[128,512]{1,0:T(8,128)(2,1)S(1)}, u32[]{:S(2)}, u32[]{:S(2)}) collective-permute-start(bf16[128,512]{1,0:T(8,128)(2,1)S(1)} %collective-permute-done.47.refs_20_), channel_id=1, source_target_pairs={{0,5},{1,2},{2,7},{3,0},{4,1},{5,8},{6,3},{7,10},{8,13},{9,4},{10,... | collective-permute-start | bytes 393224 | tf_op jit(solution)/shard_map/ppermute | solution.py:73
  102.9 4.4 %collective-permute-start.43 = (bf16[128,512]{1,0:T(8,128)(2,1)S(1)}, bf16[128,512]{1,0:T(8,128)(2,1)S(1)}, u32[]{:S(2)}, u32[]{:S(2)}) collective-permute-start(bf16[128,512]{1,0:T(8,128)(2,1)S(1)} %collective-permute-done.42.refs_22_), channel_id=1, source_target_pairs={{0,5},{1,2},{2,7},{3,0},{4,1},{5,8},{6,3},{7,10},{8,13},{9,4},{10,... | collective-permute-start | bytes 393224 | tf_op jit(solution)/shard_map/ppermute | solution.py:73
  104.5 3.4 %collective-permute-start.46 = (bf16[128,512]{1,0:T(8,128)(2,1)S(1)}, bf16[128,512]{1,0:T(8,128)(2,1)S(1)}, u32[]{:S(2)}, u32[]{:S(2)}) collective-permute-start(bf16[128,512]{1,0:T(8,128)(2,1)S(1)} %collective-permute-done.41.refs_18_), channel_id=1, source_target_pairs={{0,1},{1,0},{2,3},{3,2},{4,5},{5,4},{6,7},{7,6},{8,9},{9,8},{10,11... | collective-permute-start | bytes 393224 | tf_op jit(solution)/shard_map/ppermute | solution.py:76
  104.5 4.4 %collective-permute-start.48 = (bf16[128,512]{1,0:T(8,128)(2,1)S(1)}, bf16[128,512]{1,0:T(8,128)(2,1)S(1)}, u32[]{:S(2)}, u32[]{:S(2)}) collective-permute-start(bf16[128,512]{1,0:T(8,128)(2,1)S(1)} %collective-permute-done.47.refs_20_), channel_id=1, source_target_pairs={{0,1},{1,0},{2,3},{3,2},{4,5},{5,4},{6,7},{7,6},{8,9},{9,8},{10,11... | collective-permute-start | bytes 393224 | tf_op jit(solution)/shard_map/ppermute | solution.py:76
  105.0 4.7 %collective-permute-start.49 = (bf16[128,512]{1,0:T(8,128)(2,1)S(1)}, bf16[128,512]{1,0:T(8,128)(2,1)S(1)}, u32[]{:S(2)}, u32[]{:S(2)}) collective-permute-start(bf16[128,512]{1,0:T(8,128)(2,1)S(1)} %collective-permute-done.42.refs_22_), channel_id=1, source_target_pairs={{0,1},{1,0},{2,3},{3,2},{4,5},{5,4},{6,7},{7,6},{8,9},{9,8},{10,11... | collective-permute-start | bytes 393224 | tf_op jit(solution)/shard_map/ppermute | solution.py:76
  105.0 4.7 %collective-permute-start.51 = (bf16[128,512]{1,0:T(8,128)(2,1)S(1)}, bf16[128,512]{1,0:T(8,128)(2,1)S(1)}, u32[]{:S(2)}, u32[]{:S(2)}) collective-permute-start(bf16[128,512]{1,0:T(8,128)(2,1)S(1)} %collective-permute-done.50.refs_24_), channel_id=1, source_target_pairs={{0,1},{1,0},{2,3},{3,2},{4,5},{5,4},{6,7},{7,6},{8,9},{9,8},{10,11... | collective-permute-start | bytes 393224 | tf_op jit(solution)/shard_map/ppermute | solution.py:76
  107.3 2.4 %collective-permute-start.52 = (bf16[128,512]{1,0:T(8,128)(2,1)S(1)}, bf16[128,512]{1,0:T(8,128)(2,1)S(1)}, u32[]{:S(2)}, u32[]{:S(2)}) collective-permute-start(bf16[128,512]{1,0:T(8,128)(2,1)S(1)} %collective-permute-done.43.refs_26_), channel_id=1, source_target_pairs={{0,1},{1,0},{2,3},{3,2},{4,5},{5,4},{6,7},{7,6},{8,9},{9,8},{10,11... | collective-permute-start | bytes 393224 | tf_op jit(solution)/shard_map/ppermute | solution.py:76
  107.9 5.7 %collective-permute-start.44 = (bf16[128,512]{1,0:T(8,128)(2,1)S(1)}, bf16[128,512]{1,0:T(8,128)(2,1)S(1)}, u32[]{:S(2)}, u32[]{:S(2)}) collective-permute-start(bf16[128,512]{1,0:T(8,128)(2,1)S(1)} %collective-permute-done.43.refs_26_), channel_id=1, source_target_pairs={{0,5},{1,2},{2,7},{3,0},{4,1},{5,8},{6,3},{7,10},{8,13},{9,4},{10,... | collective-permute-start | bytes 393224 | tf_op jit(solution)/shard_map/ppermute | solution.py:73
  108.9 4.8 %collective-permute-start.54 = (bf16[128,512]{1,0:T(8,128)(2,1)S(1)}, bf16[128,512]{1,0:T(8,128)(2,1)S(1)}, u32[]{:S(2)}, u32[]{:S(2)}) collective-permute-start(bf16[128,512]{1,0:T(8,128)(2,1)S(1)} %collective-permute-done.50.refs_24_), channel_id=1, source_target_pairs={{0,5},{1,2},{2,7},{3,0},{4,1},{5,8},{6,3},{7,10},{8,13},{9,4},{10,... | collective-permute-start | bytes 393224 | tf_op jit(solution)/shard_map/ppermute | solution.py:73
  113.6 1.4 %collective-permute-start.53 = (bf16[128,512]{1,0:T(8,128)(2,1)S(1)}, bf16[128,512]{1,0:T(8,128)(2,1)S(1)}, u32[]{:S(2)}, u32[]{:S(2)}) collective-permute-start(bf16[128,512]{1,0:T(8,128)(2,1)S(1)} %collective-permute-done.44.refs_0_), channel_id=1, source_target_pairs={{0,1},{1,0},{2,3},{3,2},{4,5},{5,4},{6,7},{7,6},{8,9},{9,8},{10,11... | collective-permute-start | bytes 393224 | tf_op jit(solution)/shard_map/ppermute | solution.py:76
  113.7 1.5 %collective-permute-start.55 = (bf16[128,512]{1,0:T(8,128)(2,1)S(1)}, bf16[128,512]{1,0:T(8,128)(2,1)S(1)}, u32[]{:S(2)}, u32[]{:S(2)}) collective-permute-start(bf16[128,512]{1,0:T(8,128)(2,1)S(1)} %collective-permute-done.54.refs_2_), channel_id=1, source_target_pairs={{0,1},{1,0},{2,3},{3,2},{4,5},{5,4},{6,7},{7,6},{8,9},{9,8},{10,11... | collective-permute-start | bytes 393224 | tf_op jit(solution)/shard_map/ppermute | solution.py:76

commit v5 on v4

--- a/solution.py
+++ b/solution.py
@@ -257,7 +257,7 @@
         scratch_shapes=scratch,
         compiler_params=limit(16),
         cost_estimate=pl.CostEstimate(
-            flops=16 * parts * rows * head[0].shape[0] * width,
+            flops=32 * parts * rows * head[0].shape[0] * width,
             bytes_accessed=8 * head[0].size,
             transcendentals=parts * rows * head[0].shape[0],
         ),
@@ -350,7 +350,7 @@
 
 
 def project_kernel(plan, *refs):
-    queries, features, scale, carried, begun, count, coming, fetched = plan
+    queries, features, scale, carried, begun, count, coming, fetched, resident = plan
     refs = list(refs)
     take = lambda n: [refs.pop(0) for _ in range(n)]
     blocks, later = take(0 if fetched else count), take(coming)
@@ -361,7 +361,11 @@
     head_gain = take(1 if scale else 0)
     outs, targets = take(1 if features else 2), take(coming)
     copies = []
-    if not fetched:
+    if resident:
+        depth = parts[0].shape[1]
+        starts = [pl.multiple_of(block[0] * depth, depth) for block in blocks]
+        weights_at, ahead = [weights[0].at[pl.ds(start, depth), :] for start in starts], []
+    elif not fetched:
         pieces, sems = take(2)
         copies = [
             weight_rows(weights[0], block, pieces.at[i], sems.at[i])
@@ -405,7 +409,7 @@
         copy.wait()
 
 
-def project(queries, blocks, later, parts, gains, weight, state, fetched=None, last=False, head_gain=None):
+def project(queries, blocks, later, parts, gains, weight, state, fetched=None, last=False, head_gain=None, resident=False):
     count, depth, width = len(parts), parts[0].shape[1], weight.shape[1]
     scale = 0.0
     shapes = [pltpu.VMEM((queries, width), F32), pltpu.VMEM((queries, LANES), F32)]
@@ -413,8 +417,8 @@
     arrays = [near(x) for x in (*parts, *(gains or ()), *(fetched or ()))]
     specs = [VMEM] * len(arrays)
     if not fetched:
-        arrays.append(far(weight))
-        specs.append(ANYWHERE)
+        arrays.append(near(weight) if resident else far(weight))
+        specs.append(VMEM if resident else ANYWHERE)
     arrays += [near(x) for x in state or ()]
     if head_gain is not None:
         arrays.append(near(head_gain[None, :]))
@@ -426,9 +430,9 @@
     specs += [VMEM] * (len(arrays) - len(specs))
     shapes += [pltpu.VMEM((depth, width), BF16)] * len(later)
     features = weight.shape[0] if last else 0
-    plan = queries, features, scale, not gains, bool(state), count, len(later), bool(fetched)
+    plan = queries, features, scale, not gains, bool(state), count, len(later), bool(fetched), resident
     scratch = []
-    if not fetched:
+    if not fetched and not resident:
         scratch = [
             pltpu.VMEM((count, depth, width), BF16),
             pltpu.SemaphoreType.DMA((count + len(later),)),
@@ -462,6 +466,7 @@
             carriers and [carriers[name] for name in names],
             weight,
             state,
+            resident=bool(carriers),
             **how,
         )
 
@@ -482,7 +487,7 @@
             keep((step, False), other)
             if step < rounds - 1:
                 keep((-step, True), ring.swap(other))
-    state, fetched = flush([name for name in waiting if name not in final], final)
+    state, fetched = flush([name for name in waiting if name not in final], () if carriers else final)
     before = arrived[rounds - 1, True]
     own, other, before = after(own, *state), after(other, own, *state), after(before, own, *state)
     extra = meanwhile(own) if meanwhile else ()
@@ -597,8 +602,8 @@
         jnp.where(row == queries, attn_gain[None, :], next_gain[None, :]),
     )
     last = jnp.broadcast_to(block_limit[:, None], (queries, LANES))
+    other = ring.swap(own)
     own, last = after(own, *numbers), after(last, *numbers)
-    other = ring.swap(own)
     other_keys = ring.swap(after(key_cache, other))
     other_values = ring.swap(after(value_cache, other))
     cache = (key_cache, other_keys, value_cache, other_values)

time: 116 us -> 116 us (level)
  Pallas kernels: 32.9 us -> 29.4 us
  waiting for transfers between devices: 25.3 us -> 28.3 us
    pallas_call x4, Pallas kernels: 9.34 us -> 6.47 us  [project(): pl.pallas_call(functools.partial(project_kernel, plan), out_shape=shapes,...]
    ppermute x35, waiting for transfers between devices: 22.9 us -> 25.7 us  [send(): return lax.ppermute(block, 'ctx', sorted(route))]
  transfers between devices with their start and end apart: 56 -> 56, of which waited for: 19 -> 21; matrix products, arithmetic and copies ran while one was open for 1% -> 1% of each run, Pallas kernels for 26% -> 24%
where the time goes in v5:
time: 116 us
  starting transfers between devices  54.5 us (47%)
  Pallas kernels  29.4 us (25%)
  waiting for transfers between devices  28.3 us (24%)
  local copies, waits for them, and re-layouts  1.6 us (1%)
    ppermute x35, starting transfers between devices, send(): return lax.ppermute(block, 'ctx', sorted(route))  47.4 us
    ppermute x35, waiting for transfers between devices, send(): return lax.ppermute(block, 'ctx', sorted(route))  25.7 us
    pallas_call x8, Pallas kernels, attend(): pl.pallas_call(functools.partial(attend_kernel, chunk, parts), out_shape=...  17.5 us
    ppermute x21, starting transfers between devices, swap(): lax.ppermute(block, 'ctx', [(i, i ^ 1) for i in range(2 * self.chips)])  7.12 us
    pallas_call x4, Pallas kernels, project(): pl.pallas_call(functools.partial(project_kernel, plan), out_shape=shapes,...  6.47 us
    ppermute x21, waiting for transfers between devices, swap(): lax.ppermute(block, 'ctx', [(i, i ^ 1) for i in range(2 * self.chips)])  2.6 us
  transfers between devices with their start and end apart: 56, of which 21 were waited for; matrix products, arithmetic and copies ran while one was open for 1% of the time, Pallas kernels for 24%

profile of v5, /device:TPU:0, one launch (start us, length us, event | category | flops | bytes accessed | tf_op | source)
XLA Modules:
  0.0 115.9 jit_solution(12392222676690947185)
XLA Ops:
  0.7 1.0 select_select_fusion.refs_16_.refs_3_.refs_24_
  2.2 1.0 collective-permute-done.2.refs_17_.refs_3_.refs_25_
  3.7 2.7 %collective-permute-start = (bf16[130,512]{1,0:T(8,128)(2,1)S(1)}, bf16[130,512]{1,0:T(8,128)(2,1)S(1)}, u32[]{:S(2)}, u32[]{:S(2)}) collective-permute-start(bf16[130,512]{1,0:T(8,128)(2,1)S(1)} %select_select_fusion.refs_16_.refs_3_.refs_24_), channel_id=1, source_target_pairs={{0,5},{1,2},{2,7},{3,0},{4,1},{5,8},{6,3},{7,10},{8,13},{9,4},{10,... | collective-permute-start | bytes 399368 | tf_op jit(solution)/shard_map/ppermute | solution.py:73
  6.4 1.5 %collective-permute-start.8 = (bf16[130,512]{1,0:T(8,128)(2,1)S(1)}, bf16[130,512]{1,0:T(8,128)(2,1)S(1)}, u32[]{:S(2)}, u32[]{:S(2)}) collective-permute-start(bf16[130,512]{1,0:T(8,128)(2,1)S(1)} %collective-permute-done.2.refs_17_.refs_3_.refs_25_), channel_id=1, source_target_pairs={{0,5},{1,2},{2,7},{3,0},{4,1},{5,8},{6,3},{7,10},{8,13},{9,4},{10,... | collective-permute-start | bytes 399368 | tf_op jit(solution)/shard_map/ppermute | solution.py:73
  8.0 1.1 collective-permute-done.refs_18_.refs_26_
  9.1 2.1 %collective-permute-start.1 = (bf16[130,512]{1,0:T(8,128)(2,1)S(1)}, bf16[130,512]{1,0:T(8,128)(2,1)S(1)}, u32[]{:S(2)}, u32[]{:S(2)}) collective-permute-start(bf16[130,512]{1,0:T(8,128)(2,1)S(1)} %collective-permute-done.refs_18_.refs_26_), channel_id=1, source_target_pairs={{0,5},{1,2},{2,7},{3,0},{4,1},{5,8},{6,3},{7,10},{8,13},{9,4},{10,... | collective-permute-start | bytes 399368 | tf_op jit(solution)/shard_map/ppermute | solution.py:73
  11.2 1.2 %collective-permute-start.11 = (bf16[130,512]{1,0:T(8,128)(2,1)S(1)}, bf16[130,512]{1,0:T(8,128)(2,1)S(1)}, u32[]{:S(2)}, u32[]{:S(2)}) collective-permute-start(bf16[130,512]{1,0:T(8,128)(2,1)S(1)} %collective-permute-done.8.refs_20_.refs_28_), channel_id=1, source_target_pairs={{0,5},{1,2},{2,7},{3,0},{4,1},{5,8},{6,3},{7,10},{8,13},{9,4},{10,... | collective-permute-start | bytes 399368 | tf_op jit(solution)/shard_map/ppermute | solution.py:73
  12.4 1.4 %collective-permute-done.1.refs_22_.refs_30_ = bf16[130,512]{1,0:T(8,128)(2,1)S(1)} collective-permute-done((bf16[130,512]{1,0:T(8,128)(2,1)S(1)}, bf16[130,512]{1,0:T(8,128)(2,1)S(1)}, u32[]{:S(2)}, u32[]{:S(2)}) %collective-permute-start.1) | collective-permute-done | bytes 133152 | tf_op jit(solution)/shard_map/ppermute | solution.py:73
  13.9 2.1 %collective-permute-start.4 = (bf16[130,512]{1,0:T(8,128)(2,1)S(1)}, bf16[130,512]{1,0:T(8,128)(2,1)S(1)}, u32[]{:S(2)}, u32[]{:S(2)}) collective-permute-start(bf16[130,512]{1,0:T(8,128)(2,1)S(1)} %collective-permute-done.1.refs_22_.refs_30_), channel_id=1, source_target_pairs={{0,5},{1,2},{2,7},{3,0},{4,1},{5,8},{6,3},{7,10},{8,13},{9,4},{10,... | collective-permute-start | bytes 399368 | tf_op jit(solution)/shard_map/ppermute | solution.py:73
  17.0 1.7 %collective-permute-done.4.refs_26_.refs_34_ = bf16[130,512]{1,0:T(8,128)(2,1)S(1)} collective-permute-done((bf16[130,512]{1,0:T(8,128)(2,1)S(1)}, bf16[130,512]{1,0:T(8,128)(2,1)S(1)}, u32[]{:S(2)}, u32[]{:S(2)}) %collective-permute-start.4) | collective-permute-done | bytes 133152 | tf_op jit(solution)/shard_map/ppermute | solution.py:73
  19.1 1.4 %collective-permute-start.6 = (bf16[130,512]{1,0:T(8,128)(2,1)S(1)}, bf16[130,512]{1,0:T(8,128)(2,1)S(1)}, u32[]{:S(2)}, u32[]{:S(2)}) collective-permute-start(bf16[130,512]{1,0:T(8,128)(2,1)S(1)} %collective-permute-done.4.refs_26_.refs_34_), channel_id=1, source_target_pairs={{0,5},{1,2},{2,7},{3,0},{4,1},{5,8},{6,3},{7,10},{8,13},{9,4},{10,... | collective-permute-start | bytes 399368 | tf_op jit(solution)/shard_map/ppermute | solution.py:73
  20.5 1.7 %collective-permute-start.15 = (bf16[130,512]{1,0:T(8,128)(2,1)S(1)}, bf16[130,512]{1,0:T(8,128)(2,1)S(1)}, u32[]{:S(2)}, u32[]{:S(2)}) collective-permute-start(bf16[130,512]{1,0:T(8,128)(2,1)S(1)} %collective-permute-done.11.refs_24_.refs_32_), channel_id=1, source_target_pairs={{0,5},{1,2},{2,7},{3,0},{4,1},{5,8},{6,3},{7,10},{8,13},{9,4},{10,... | collective-permute-start | bytes 399368 | tf_op jit(solution)/shard_map/ppermute | solution.py:73
  22.2 3.8 %project.4 = (f32[128,512]{1,0:T(8,128)S(1)}, f32[128,128]{1,0:T(8,128)S(1)}, bf16[512,512]{1,0:T(8,128)(2,1)S(1)}, bf16[512,512]{1,0:T(8,128)(2,1)S(1)}, bf16[5...) custom-call(s32[1]{0:T(128)} %bitcast.5.refs_0_.refs_5_, s32[1]{0:T(128)} %bitcast.6.refs_1_.refs_6_, ...), custom_call_target="tpu_custom_call" | custom-call | flops 690000000 | tf_op jit(solution)/shard_map/project/pallas_call | solution.py:440
  26.9 1.7 %fetch.1 = (bf16[3072,128]{1,0:T(8,128)(2,1)S(1)}, bf16[3072,128]{1,0:T(8,128)(2,1)S(1)}) custom-call(s32[1]{0:T(128)} %bitcast.18.head, bf16[1536,1024]{1,0:T(8,128)(2,1)} %refs_1_.13, bf16[1536,1024]{1,0:T(8,128)(2,1)S(1)} %collective-permute-done.3.k1.refs_2_, bf16[1536,1024]{1,0:T(8,128)(2,1)} %refs_3_.13, ...), custom_call_target="tpu_custom_call" | custom-call | flops 414000000 | tf_op jit(solution)/shard_map/fetch/pallas_call | solution.py:186
  29.2 0.8 slice-done.1
  30.0 1.2 %collective-permute-start.17 = (bf16[512,128]{1,0:T(8,128)(2,1)S(1)}, bf16[512,128]{1,0:T(8,128)(2,1)S(1)}, u32[]{:S(2)}, u32[]{:S(2)}) collective-permute-start(bf16[512,128]{1,0:T(8,128)(2,1)S(1)} %project.5.q), channel_id=1, source_target_pairs={{0,5},{1,2},{2,7},{3,0},{4,1},{5,8},{6,3},{7,10},{8,13},{9,4},{10,... | collective-permute-start | bytes 393224 | tf_op jit(solution)/shard_map/ppermute | solution.py:73
  31.2 2.2 %attend.8 = (bf16[528,128]{1,0:T(8,128)(2,1)S(1)}, bf16[3072,128]{1,0:T(8,128)(2,1)S(1)}, bf16[3072,128]{1,0:T(8,128)(2,1)S(1)}) custom-call(bf16[512,128]{1,0:T(8,128)(2,1)S(1)} %project.5.q, bf16[128,128]{1,0:T(8,128)(2,1)S(1)} %get-tuple-element.136.bias, bf16[3072,128]{1,0:T(8,128)(2,1)S(1)} %get-tuple-element.135.onehot, ...), custom_call_target="tpu_custom_call" | custom-call | flops 6442450944 | bytes 3145728 | tf_op jit(solution)/shard_map/attend/pallas_call | solution.py:252
  33.4 1.0 collective-permute-done.17.q
  34.4 1.3 %collective-permute-start.19 = (bf16[512,128]{1,0:T(8,128)(2,1)S(1)}, bf16[512,128]{1,0:T(8,128)(2,1)S(1)}, u32[]{:S(2)}, u32[]{:S(2)}) collective-permute-start(bf16[512,128]{1,0:T(8,128)(2,1)S(1)} %collective-permute-done.17.q), channel_id=1, source_target_pairs={{0,5},{1,2},{2,7},{3,0},{4,1},{5,8},{6,3},{7,10},{8,13},{9,4},{10,... | collective-permute-start | bytes 393224 | tf_op jit(solution)/shard_map/ppermute | solution.py:73
  35.7 2.2 %attend.9 = (bf16[528,128]{1,0:T(8,128)(2,1)S(1)}, bf16[3072,128]{1,0:T(8,128)(2,1)S(1)}, bf16[3072,128]{1,0:T(8,128)(2,1)S(1)}) custom-call(bf16[512,128]{1,0:T(8,128)(2,1)S(1)} %collective-permute-done.17.q, bf16[128,128]{1,0:T(8,128)(2,1)S(1)} %get-tuple-element.136.bias, bf16[3072,128]{1,0:T(8,128)(2,1)S(1)} %get-tuple-element.135.onehot, ...), custom_call_target="tpu_custom_call" | custom-call | flops 6442450944 | bytes 3145728 | tf_op jit(solution)/shard_map/attend/pallas_call | solution.py:252
  37.9 1.6 %collective-permute-start.18 = (bf16[528,128]{1,0:T(8,128)(2,1)S(1)}, bf16[528,128]{1,0:T(8,128)(2,1)S(1)}, u32[]{:S(2)}, u32[]{:S(2)}) collective-permute-start(bf16[528,128]{1,0:T(8,128)(2,1)S(1)} %get-tuple-element.152), channel_id=1, source_target_pairs={{0,5},{1,2},{2,7},{3,0},{4,1},{5,8},{6,3},{7,10},{8,13},{9,4},{10,... | collective-permute-start | bytes 405512 | tf_op jit(solution)/shard_map/ppermute | solution.py:73
  40.1 2.2 %attend.10 = (bf16[528,128]{1,0:T(8,128)(2,1)S(1)}, bf16[3072,128]{1,0:T(8,128)(2,1)S(1)}, bf16[3072,128]{1,0:T(8,128)(2,1)S(1)}) custom-call(bf16[512,128]{1,0:T(8,128)(2,1)S(1)} %collective-permute-done.19.q, bf16[128,128]{1,0:T(8,128)(2,1)S(1)} %get-tuple-element.136.bias, bf16[3072,128]{1,0:T(8,128)(2,1)S(1)} %get-tuple-element.135.onehot, ...), custom_call_target="tpu_custom_call" | custom-call | flops 6442450944 | bytes 3145728 | tf_op jit(solution)/shard_map/attend/pallas_call | solution.py:252
  42.7 1.9 %collective-permute-start.20 = (bf16[528,128]{1,0:T(8,128)(2,1)S(1)}, bf16[528,128]{1,0:T(8,128)(2,1)S(1)}, u32[]{:S(2)}, u32[]{:S(2)}) collective-permute-start(bf16[528,128]{1,0:T(8,128)(2,1)S(1)} %merge.6), channel_id=1, source_target_pairs={{0,5},{1,2},{2,7},{3,0},{4,1},{5,8},{6,3},{7,10},{8,13},{9,4},{10,... | collective-permute-start | bytes 405512 | tf_op jit(solution)/shard_map/ppermute | solution.py:73
  44.5 0.8 collective-permute-start.23
  45.3 2.2 %attend.11 = (bf16[528,128]{1,0:T(8,128)(2,1)S(1)}, bf16[3072,128]{1,0:T(8,128)(2,1)S(1)}, bf16[3072,128]{1,0:T(8,128)(2,1)S(1)}) custom-call(bf16[512,128]{1,0:T(8,128)(2,1)S(1)} %collective-permute-done.21.q, bf16[128,128]{1,0:T(8,128)(2,1)S(1)} %get-tuple-element.136.bias, bf16[3072,128]{1,0:T(8,128)(2,1)S(1)} %get-tuple-element.135.onehot, ...), custom_call_target="tpu_custom_call" | custom-call | flops 6442450944 | bytes 3145728 | tf_op jit(solution)/shard_map/attend/pallas_call | solution.py:252
  47.8 1.8 %collective-permute-start.22 = (bf16[528,128]{1,0:T(8,128)(2,1)S(1)}, bf16[528,128]{1,0:T(8,128)(2,1)S(1)}, u32[]{:S(2)}, u32[]{:S(2)}) collective-permute-start(bf16[528,128]{1,0:T(8,128)(2,1)S(1)} %merge.7), channel_id=1, source_target_pairs={{0,5},{1,2},{2,7},{3,0},{4,1},{5,8},{6,3},{7,10},{8,13},{9,4},{10,... | collective-permute-start | bytes 405512 | tf_op jit(solution)/shard_map/ppermute | solution.py:73
  49.5 0.8 collective-permute-start.25
  50.4 2.2 %attend.12 = (bf16[528,128]{1,0:T(8,128)(2,1)S(1)}, bf16[3072,128]{1,0:T(8,128)(2,1)S(1)}, bf16[3072,128]{1,0:T(8,128)(2,1)S(1)}) custom-call(bf16[512,128]{1,0:T(8,128)(2,1)S(1)} %collective-permute-done.23.q, bf16[128,128]{1,0:T(8,128)(2,1)S(1)} %get-tuple-element.136.bias, bf16[3072,128]{1,0:T(8,128)(2,1)S(1)} %get-tuple-element.135.onehot, ...), custom_call_target="tpu_custom_call" | custom-call | flops 6442450944 | bytes 3145728 | tf_op jit(solution)/shard_map/attend/pallas_call | solution.py:252
  52.8 1.6 %collective-permute-start.24 = (bf16[528,128]{1,0:T(8,128)(2,1)S(1)}, bf16[528,128]{1,0:T(8,128)(2,1)S(1)}, u32[]{:S(2)}, u32[]{:S(2)}) collective-permute-start(bf16[528,128]{1,0:T(8,128)(2,1)S(1)} %merge.8), channel_id=1, source_target_pairs={{0,5},{1,2},{2,7},{3,0},{4,1},{5,8},{6,3},{7,10},{8,13},{9,4},{10,... | collective-permute-start | bytes 405512 | tf_op jit(solution)/shard_map/ppermute | solution.py:73
  54.4 1.0 collective-permute-start.27
  55.4 2.2 %attend.13 = (bf16[528,128]{1,0:T(8,128)(2,1)S(1)}, bf16[3072,128]{1,0:T(8,128)(2,1)S(1)}, bf16[3072,128]{1,0:T(8,128)(2,1)S(1)}) custom-call(bf16[512,128]{1,0:T(8,128)(2,1)S(1)} %collective-permute-done.25.q, bf16[128,128]{1,0:T(8,128)(2,1)S(1)} %get-tuple-element.136.bias, bf16[3072,128]{1,0:T(8,128)(2,1)S(1)} %get-tuple-element.135.onehot, ...), custom_call_target="tpu_custom_call" | custom-call | flops 6442450944 | bytes 3145728 | tf_op jit(solution)/shard_map/attend/pallas_call | solution.py:252
  57.9 1.6 %collective-permute-start.26 = (bf16[528,128]{1,0:T(8,128)(2,1)S(1)}, bf16[528,128]{1,0:T(8,128)(2,1)S(1)}, u32[]{:S(2)}, u32[]{:S(2)}) collective-permute-start(bf16[528,128]{1,0:T(8,128)(2,1)S(1)} %merge.9), channel_id=1, source_target_pairs={{0,5},{1,2},{2,7},{3,0},{4,1},{5,8},{6,3},{7,10},{8,13},{9,4},{10,... | collective-permute-start | bytes 405512 | tf_op jit(solution)/shard_map/ppermute | solution.py:73
  59.4 0.8 collective-permute-start.29
  60.2 2.2 %attend.14 = (bf16[528,128]{1,0:T(8,128)(2,1)S(1)}, bf16[3072,128]{1,0:T(8,128)(2,1)S(1)}, bf16[3072,128]{1,0:T(8,128)(2,1)S(1)}) custom-call(bf16[512,128]{1,0:T(8,128)(2,1)S(1)} %collective-permute-done.27.q, bf16[128,128]{1,0:T(8,128)(2,1)S(1)} %get-tuple-element.136.bias, bf16[3072,128]{1,0:T(8,128)(2,1)S(1)} %get-tuple-element.135.onehot, ...), custom_call_target="tpu_custom_call" | custom-call | flops 6442450944 | bytes 3145728 | tf_op jit(solution)/shard_map/attend/pallas_call | solution.py:252
  62.7 1.8 %collective-permute-start.28 = (bf16[528,128]{1,0:T(8,128)(2,1)S(1)}, bf16[528,128]{1,0:T(8,128)(2,1)S(1)}, u32[]{:S(2)}, u32[]{:S(2)}) collective-permute-start(bf16[528,128]{1,0:T(8,128)(2,1)S(1)} %merge.10), channel_id=1, source_target_pairs={{0,5},{1,2},{2,7},{3,0},{4,1},{5,8},{6,3},{7,10},{8,13},{9,4},{10,... | collective-permute-start | bytes 405512 | tf_op jit(solution)/shard_map/ppermute | solution.py:73
  64.4 2.1 %attend.15.two = bf16[528,128]{1,0:T(8,128)(2,1)S(1)} custom-call(bf16[512,128]{1,0:T(8,128)(2,1)S(1)} %collective-permute-done.29.q, bf16[128,128]{1,0:T(8,128)(2,1)S(1)} %get-tuple-element.136.bias, bf16[3072,128]{1,0:T(8,128)(2,1)S(1)} %get-tuple-element.135.onehot, bf16[3072,128]{1,0:T(8,128)(2,1)S(1)} %get-tuple-element.174.key, ...), custom_call_target="tpu_custom_call" | custom-call | flops 6442450944 | bytes 3145728 | tf_op jit(solution)/shard_map/attend/pallas_call | solution.py:252
  67.4 2.0 %collective-permute-start.30 = (bf16[528,128]{1,0:T(8,128)(2,1)S(1)}, bf16[528,128]{1,0:T(8,128)(2,1)S(1)}, u32[]{:S(2)}, u32[]{:S(2)}) collective-permute-start(bf16[528,128]{1,0:T(8,128)(2,1)S(1)} %merge.11), channel_id=1, source_target_pairs={{0,5},{1,2},{2,7},{3,0},{4,1},{5,8},{6,3},{7,10},{8,13},{9,4},{10,... | collective-permute-start | bytes 405512 | tf_op jit(solution)/shard_map/ppermute | solution.py:73
  69.4 2.7 %collective-permute-done.30.refs_0_ = bf16[528,128]{1,0:T(8,128)(2,1)S(1)} collective-permute-done((bf16[528,128]{1,0:T(8,128)(2,1)S(1)}, bf16[528,128]{1,0:T(8,128)(2,1)S(1)}, u32[]{:S(2)}, u32[]{:S(2)}) %collective-permute-start.30) | collective-permute-done | bytes 135200 | tf_op jit(solution)/shard_map/ppermute | solution.py:73
  73.2 1.0 collective-permute-done.31.refs_8_.refs_3_
  74.6 0.9 collective-permute-start.33
  75.5 1.0 collective-permute-start.37
  76.5 1.1 mix.2
  77.6 1.5 %collective-permute-done.33.refs_1_ = bf16[128,512]{1,0:T(8,128)(2,1)S(1)} collective-permute-done((bf16[128,512]{1,0:T(8,128)(2,1)S(1)}, bf16[128,512]{1,0:T(8,128)(2,1)S(1)}, u32[]{:S(2)}, u32[]{:S(2)}) %collective-permute-start.33) | collective-permute-done | bytes 131104 | tf_op jit(solution)/shard_map/ppermute | solution.py:73
  79.1 1.2 collective-permute-start.34
  80.5 0.9 collective-permute-start.38
  81.4 2.2 %collective-permute-done.34.refs_1_ = bf16[128,512]{1,0:T(8,128)(2,1)S(1)} collective-permute-done((bf16[128,512]{1,0:T(8,128)(2,1)S(1)}, bf16[128,512]{1,0:T(8,128)(2,1)S(1)}, u32[]{:S(2)}, u32[]{:S(2)}) %collective-permute-start.34) | collective-permute-done | bytes 131104 | tf_op jit(solution)/shard_map/ppermute | solution.py:73
  83.6 1.4 %collective-permute-start.35 = (bf16[128,512]{1,0:T(8,128)(2,1)S(1)}, bf16[128,512]{1,0:T(8,128)(2,1)S(1)}, u32[]{:S(2)}, u32[]{:S(2)}) collective-permute-start(bf16[128,512]{1,0:T(8,128)(2,1)S(1)} %add.162), channel_id=1, source_target_pairs={{0,3},{1,4},{2,1},{3,6},{4,9},{5,0},{6,11},{7,2},{8,5},{9,12},{10,... | collective-permute-start | bytes 393224 | tf_op jit(solution)/shard_map/ppermute | solution.py:73
  85.1 1.1 collective-permute-start.39
  86.1 2.1 %collective-permute-done.35.refs_1_ = bf16[128,512]{1,0:T(8,128)(2,1)S(1)} collective-permute-done((bf16[128,512]{1,0:T(8,128)(2,1)S(1)}, bf16[128,512]{1,0:T(8,128)(2,1)S(1)}, u32[]{:S(2)}, u32[]{:S(2)}) %collective-permute-start.35) | collective-permute-done | bytes 131104 | tf_op jit(solution)/shard_map/ppermute | solution.py:73
  88.3 1.5 %collective-permute-start.36 = (bf16[128,512]{1,0:T(8,128)(2,1)S(1)}, bf16[128,512]{1,0:T(8,128)(2,1)S(1)}, u32[]{:S(2)}, u32[]{:S(2)}) collective-permute-start(bf16[128,512]{1,0:T(8,128)(2,1)S(1)} %add.163), channel_id=1, source_target_pairs={{0,3},{1,4},{2,1},{3,6},{4,9},{5,0},{6,11},{7,2},{8,5},{9,12},{10,... | collective-permute-start | bytes 393224 | tf_op jit(solution)/shard_map/ppermute | solution.py:73
  90.4 2.6 %collective-permute-done.36.refs_1_ = bf16[128,512]{1,0:T(8,128)(2,1)S(1)} collective-permute-done((bf16[128,512]{1,0:T(8,128)(2,1)S(1)}, bf16[128,512]{1,0:T(8,128)(2,1)S(1)}, u32[]{:S(2)}, u32[]{:S(2)}) %collective-permute-start.36) | collective-permute-done | bytes 131104 | tf_op jit(solution)/shard_map/ppermute | solution.py:73
  93.8 1.1 collective-permute-start.41
  95.0 1.3 %collective-permute-start.47 = (bf16[128,512]{1,0:T(8,128)(2,1)S(1)}, bf16[128,512]{1,0:T(8,128)(2,1)S(1)}, u32[]{:S(2)}, u32[]{:S(2)}) collective-permute-start(bf16[128,512]{1,0:T(8,128)(2,1)S(1)} %add.167.refs_13_), channel_id=1, source_target_pairs={{0,5},{1,2},{2,7},{3,0},{4,1},{5,8},{6,3},{7,10},{8,13},{9,4},{10,... | collective-permute-start | bytes 393224 | tf_op jit(solution)/shard_map/ppermute | solution.py:73
  96.2 2.0 %collective-permute-done.41.refs_14_ = bf16[128,512]{1,0:T(8,128)(2,1)S(1)} collective-permute-done((bf16[128,512]{1,0:T(8,128)(2,1)S(1)}, bf16[128,512]{1,0:T(8,128)(2,1)S(1)}, u32[]{:S(2)}, u32[]{:S(2)}) %collective-permute-start.41) | collective-permute-done | bytes 131104 | tf_op jit(solution)/shard_map/ppermute | solution.py:73
  98.3 1.3 %collective-permute-start.42 = (bf16[128,512]{1,0:T(8,128)(2,1)S(1)}, bf16[128,512]{1,0:T(8,128)(2,1)S(1)}, u32[]{:S(2)}, u32[]{:S(2)}) collective-permute-start(bf16[128,512]{1,0:T(8,128)(2,1)S(1)} %collective-permute-done.41.refs_14_), channel_id=1, source_target_pairs={{0,5},{1,2},{2,7},{3,0},{4,1},{5,8},{6,3},{7,10},{8,13},{9,4},{10,... | collective-permute-start | bytes 393224 | tf_op jit(solution)/shard_map/ppermute | solution.py:73
  99.7 1.1 collective-permute-start.50
  100.8 1.9 %collective-permute-done.42.refs_18_ = bf16[128,512]{1,0:T(8,128)(2,1)S(1)} collective-permute-done((bf16[128,512]{1,0:T(8,128)(2,1)S(1)}, bf16[128,512]{1,0:T(8,128)(2,1)S(1)}, u32[]{:S(2)}, u32[]{:S(2)}) %collective-permute-start.42) | collective-permute-done | bytes 131104 | tf_op jit(solution)/shard_map/ppermute | solution.py:73
  102.7 1.6 %collective-permute-start.43 = (bf16[128,512]{1,0:T(8,128)(2,1)S(1)}, bf16[128,512]{1,0:T(8,128)(2,1)S(1)}, u32[]{:S(2)}, u32[]{:S(2)}) collective-permute-start(bf16[128,512]{1,0:T(8,128)(2,1)S(1)} %collective-permute-done.42.refs_18_), channel_id=1, source_target_pairs={{0,5},{1,2},{2,7},{3,0},{4,1},{5,8},{6,3},{7,10},{8,13},{9,4},{10,... | collective-permute-start | bytes 393224 | tf_op jit(solution)/shard_map/ppermute | solution.py:73
  105.3 1.8 %collective-permute-done.43.refs_22_ = bf16[128,512]{1,0:T(8,128)(2,1)S(1)} collective-permute-done((bf16[128,512]{1,0:T(8,128)(2,1)S(1)}, bf16[128,512]{1,0:T(8,128)(2,1)S(1)}, u32[]{:S(2)}, u32[]{:S(2)}) %collective-permute-start.43) | collective-permute-done | bytes 131104 | tf_op jit(solution)/shard_map/ppermute | solution.py:73
  107.7 1.0 collective-permute-start.44
  109.5 1.0 project.6
  110.5 1.5 %collective-permute-done.44.refs_4_ = bf16[128,512]{1,0:T(8,128)(2,1)S(1)} collective-permute-done((bf16[128,512]{1,0:T(8,128)(2,1)S(1)}, bf16[128,512]{1,0:T(8,128)(2,1)S(1)}, u32[]{:S(2)}, u32[]{:S(2)}) %collective-permute-start.44) | collective-permute-done | bytes 131104 | tf_op jit(solution)/shard_map/ppermute | solution.py:73
  112.3 1.1 collective-permute-done.54.refs_6_
  114.8 1.1 project.7
  (96 shorter events, 14.2 us)
Async XLA Ops:
  0.6 25.9 %copy-start.1 = (s32[128]{0:T(128)S(1)}, s32[128]{0:T(128)}, u32[]{:S(2)}) copy-start(s32[128]{0:T(128)} %param.16) | copy-start | bytes 1540
  1.7 1.5 %collective-permute-start.2 = (bf16[130,512]{1,0:T(8,128)(2,1)S(1)}, bf16[130,512]{1,0:T(8,128)(2,1)S(1)}, u32[]{:S(2)}, u32[]{:S(2)}) collective-permute-start(bf16[130,512]{1,0:T(8,128)(2,1)S(1)} %select_select_fusion.refs_16_.refs_3_.refs_24_), channel_id=1, source_target_pairs={{0,1},{1,0},{2,3},{3,2},{4,5},{5,4},{6,7},{7,6},{8,9},{9,8},{10,11... | collective-permute-start | bytes 399368 | tf_op jit(solution)/shard_map/ppermute | solution.py:76
  3.2 10.7 %collective-permute-start.3 = (bf16[1536,1024]{1,0:T(8,128)(2,1)}, bf16[1536,1024]{1,0:T(8,128)(2,1)S(1)}, u32[]{:S(2)}, u32[]{:S(2)}) collective-permute-start(bf16[1536,1024]{1,0:T(8,128)(2,1)} %refs_1_.13), channel_id=1, source_target_pairs={{0,1},{1,0},{2,3},{3,2},{4,5},{5,4},{6,7},{7,6},{8,9},{9,8},{10,11... | collective-permute-start | bytes 9437192 | tf_op jit(solution)/shard_map/ppermute | solution.py:76
  3.6 12.9 %collective-permute-start.5 = (bf16[1536,1024]{1,0:T(8,128)(2,1)}, bf16[1536,1024]{1,0:T(8,128)(2,1)}, u32[]{:S(2)}, u32[]{:S(2)}) collective-permute-start(bf16[1536,1024]{1,0:T(8,128)(2,1)} %refs_3_.13), channel_id=1, source_target_pairs={{0,1},{1,0},{2,3},{3,2},{4,5},{5,4},{6,7},{7,6},{8,9},{9,8},{10,11... | collective-permute-start | bytes 9437192 | tf_op jit(solution)/shard_map/ppermute | solution.py:76
  3.7 5.4 %collective-permute-start = (bf16[130,512]{1,0:T(8,128)(2,1)S(1)}, bf16[130,512]{1,0:T(8,128)(2,1)S(1)}, u32[]{:S(2)}, u32[]{:S(2)}) collective-permute-start(bf16[130,512]{1,0:T(8,128)(2,1)S(1)} %select_select_fusion.refs_16_.refs_3_.refs_24_), channel_id=1, source_target_pairs={{0,5},{1,2},{2,7},{3,0},{4,1},{5,8},{6,3},{7,10},{8,13},{9,4},{10,... | collective-permute-start | bytes 399368 | tf_op jit(solution)/shard_map/ppermute | solution.py:73
  6.4 4.8 %collective-permute-start.8 = (bf16[130,512]{1,0:T(8,128)(2,1)S(1)}, bf16[130,512]{1,0:T(8,128)(2,1)S(1)}, u32[]{:S(2)}, u32[]{:S(2)}) collective-permute-start(bf16[130,512]{1,0:T(8,128)(2,1)S(1)} %collective-permute-done.2.refs_17_.refs_3_.refs_25_), channel_id=1, source_target_pairs={{0,5},{1,2},{2,7},{3,0},{4,1},{5,8},{6,3},{7,10},{8,13},{9,4},{10,... | collective-permute-start | bytes 399368 | tf_op jit(solution)/shard_map/ppermute | solution.py:73
  9.1 4.8 %collective-permute-start.1 = (bf16[130,512]{1,0:T(8,128)(2,1)S(1)}, bf16[130,512]{1,0:T(8,128)(2,1)S(1)}, u32[]{:S(2)}, u32[]{:S(2)}) collective-permute-start(bf16[130,512]{1,0:T(8,128)(2,1)S(1)} %collective-permute-done.refs_18_.refs_26_), channel_id=1, source_target_pairs={{0,5},{1,2},{2,7},{3,0},{4,1},{5,8},{6,3},{7,10},{8,13},{9,4},{10,... | collective-permute-start | bytes 399368 | tf_op jit(solution)/shard_map/ppermute | solution.py:73
  11.2 5.3 %collective-permute-start.11 = (bf16[130,512]{1,0:T(8,128)(2,1)S(1)}, bf16[130,512]{1,0:T(8,128)(2,1)S(1)}, u32[]{:S(2)}, u32[]{:S(2)}) collective-permute-start(bf16[130,512]{1,0:T(8,128)(2,1)S(1)} %collective-permute-done.8.refs_20_.refs_28_), channel_id=1, source_target_pairs={{0,5},{1,2},{2,7},{3,0},{4,1},{5,8},{6,3},{7,10},{8,13},{9,4},{10,... | collective-permute-start | bytes 399368 | tf_op jit(solution)/shard_map/ppermute | solution.py:73
  13.9 4.8 %collective-permute-start.4 = (bf16[130,512]{1,0:T(8,128)(2,1)S(1)}, bf16[130,512]{1,0:T(8,128)(2,1)S(1)}, u32[]{:S(2)}, u32[]{:S(2)}) collective-permute-start(bf16[130,512]{1,0:T(8,128)(2,1)S(1)} %collective-permute-done.1.refs_22_.refs_30_), channel_id=1, source_target_pairs={{0,5},{1,2},{2,7},{3,0},{4,1},{5,8},{6,3},{7,10},{8,13},{9,4},{10,... | collective-permute-start | bytes 399368 | tf_op jit(solution)/shard_map/ppermute | solution.py:73
  16.0 3.1 %collective-permute-start.7 = (bf16[130,512]{1,0:T(8,128)(2,1)S(1)}, bf16[130,512]{1,0:T(8,128)(2,1)S(1)}, u32[]{:S(2)}, u32[]{:S(2)}) collective-permute-start(bf16[130,512]{1,0:T(8,128)(2,1)S(1)} %collective-permute-done.refs_18_.refs_26_), channel_id=1, source_target_pairs={{0,1},{1,0},{2,3},{3,2},{4,5},{5,4},{6,7},{7,6},{8,9},{9,8},{10,11... | collective-permute-start | bytes 399368 | tf_op jit(solution)/shard_map/ppermute | solution.py:76
  16.0 4.5 %collective-permute-start.9 = (bf16[130,512]{1,0:T(8,128)(2,1)S(1)}, bf16[130,512]{1,0:T(8,128)(2,1)S(1)}, u32[]{:S(2)}, u32[]{:S(2)}) collective-permute-start(bf16[130,512]{1,0:T(8,128)(2,1)S(1)} %collective-permute-done.8.refs_20_.refs_28_), channel_id=1, source_target_pairs={{0,1},{1,0},{2,3},{3,2},{4,5},{5,4},{6,7},{7,6},{8,9},{9,8},{10,11... | collective-permute-start | bytes 399368 | tf_op jit(solution)/shard_map/ppermute | solution.py:76
  16.5 5.7 %collective-permute-start.10 = (bf16[130,512]{1,0:T(8,128)(2,1)S(1)}, bf16[130,512]{1,0:T(8,128)(2,1)S(1)}, u32[]{:S(2)}, u32[]{:S(2)}) collective-permute-start(bf16[130,512]{1,0:T(8,128)(2,1)S(1)} %collective-permute-done.1.refs_22_.refs_30_), channel_id=1, source_target_pairs={{0,1},{1,0},{2,3},{3,2},{4,5},{5,4},{6,7},{7,6},{8,9},{9,8},{10,11... | collective-permute-start | bytes 399368 | tf_op jit(solution)/shard_map/ppermute | solution.py:76
  16.5 5.7 %collective-permute-start.12 = (bf16[130,512]{1,0:T(8,128)(2,1)S(1)}, bf16[130,512]{1,0:T(8,128)(2,1)S(1)}, u32[]{:S(2)}, u32[]{:S(2)}) collective-permute-start(bf16[130,512]{1,0:T(8,128)(2,1)S(1)} %collective-permute-done.11.refs_24_.refs_32_), channel_id=1, source_target_pairs={{0,1},{1,0},{2,3},{3,2},{4,5},{5,4},{6,7},{7,6},{8,9},{9,8},{10,11... | collective-permute-start | bytes 399368 | tf_op jit(solution)/shard_map/ppermute | solution.py:76
  18.6 3.5 %collective-permute-start.13 = (bf16[130,512]{1,0:T(8,128)(2,1)S(1)}, bf16[130,512]{1,0:T(8,128)(2,1)S(1)}, u32[]{:S(2)}, u32[]{:S(2)}) collective-permute-start(bf16[130,512]{1,0:T(8,128)(2,1)S(1)} %collective-permute-done.4.refs_26_.refs_34_), channel_id=1, source_target_pairs={{0,1},{1,0},{2,3},{3,2},{4,5},{5,4},{6,7},{7,6},{8,9},{9,8},{10,11... | collective-permute-start | bytes 399368 | tf_op jit(solution)/shard_map/ppermute | solution.py:76
  19.1 6.9 %collective-permute-start.6 = (bf16[130,512]{1,0:T(8,128)(2,1)S(1)}, bf16[130,512]{1,0:T(8,128)(2,1)S(1)}, u32[]{:S(2)}, u32[]{:S(2)}) collective-permute-start(bf16[130,512]{1,0:T(8,128)(2,1)S(1)} %collective-permute-done.4.refs_26_.refs_34_), channel_id=1, source_target_pairs={{0,5},{1,2},{2,7},{3,0},{4,1},{5,8},{6,3},{7,10},{8,13},{9,4},{10,... | collective-permute-start | bytes 399368 | tf_op jit(solution)/shard_map/ppermute | solution.py:73
  20.5 5.6 %collective-permute-start.15 = (bf16[130,512]{1,0:T(8,128)(2,1)S(1)}, bf16[130,512]{1,0:T(8,128)(2,1)S(1)}, u32[]{:S(2)}, u32[]{:S(2)}) collective-permute-start(bf16[130,512]{1,0:T(8,128)(2,1)S(1)} %collective-permute-done.11.refs_24_.refs_32_), channel_id=1, source_target_pairs={{0,5},{1,2},{2,7},{3,0},{4,1},{5,8},{6,3},{7,10},{8,13},{9,4},{10,... | collective-permute-start | bytes 399368 | tf_op jit(solution)/shard_map/ppermute | solution.py:73
  25.9 2.7 %copy-start = (bf16[128]{0:T(256)(128)(2,1)S(1)}, bf16[128]{0:T(256)(128)(2,1)}, u32[]{:S(2)}) copy-start(bf16[128]{0:T(256)(128)(2,1)} %param.13) | copy-start | bytes 772
  25.9 3.2 %slice-start = ((s8[8388608]{0:T(1024)(128)(4,1)}), s8[4194304]{0:T(1024)(128)(4,1)S(1)}, s32[]{:S(2)}) async-start(s8[8388608]{0:T(1024)(128)(4,1)} %bitcast.27), calls=%async_computation | async-start | bytes 8388608
  26.0 2.6 %collective-permute-start.14 = (bf16[130,512]{1,0:T(8,128)(2,1)S(1)}, bf16[130,512]{1,0:T(8,128)(2,1)S(1)}, u32[]{:S(2)}, u32[]{:S(2)}) collective-permute-start(bf16[130,512]{1,0:T(8,128)(2,1)S(1)} %collective-permute-done.6.refs_0_.refs_8_), channel_id=1, source_target_pairs={{0,1},{1,0},{2,3},{3,2},{4,5},{5,4},{6,7},{7,6},{8,9},{9,8},{10,11... | collective-permute-start | bytes 399368 | tf_op jit(solution)/shard_map/ppermute | solution.py:76
  26.1 2.5 %collective-permute-start.16 = (bf16[130,512]{1,0:T(8,128)(2,1)S(1)}, bf16[130,512]{1,0:T(8,128)(2,1)S(1)}, u32[]{:S(2)}, u32[]{:S(2)}) collective-permute-start(bf16[130,512]{1,0:T(8,128)(2,1)S(1)} %collective-permute-done.15.refs_2_.refs_10_), channel_id=1, source_target_pairs={{0,1},{1,0},{2,3},{3,2},{4,5},{5,4},{6,7},{7,6},{8,9},{9,8},{10,11... | collective-permute-start | bytes 399368 | tf_op jit(solution)/shard_map/ppermute | solution.py:76
  26.9 3.2 %slice-start.1 = ((s8[8388608]{0:T(1024)(128)(4,1)}), s8[4194304]{0:T(1024)(128)(4,1)S(1)}, s32[]{:S(2)}) async-start(s8[8388608]{0:T(1024)(128)(4,1)} %bitcast.27), calls=%async_computation.1 | async-start | bytes 8388608
  30.0 44.1 %collective-permute-start.32 = (bf16[512,8192]{1,0:T(8,128)(2,1)S(1)}, bf16[512,8192]{1,0:T(8,128)(2,1)S(1)}, u32[]{:S(2)}, u32[]{:S(2)}) collective-permute-start(bf16[512,8192]{1,0:T(8,128)(2,1)S(1)} %bitcast.28), channel_id=1, source_target_pairs={{0,1},{1,0},{2,3},{3,2},{4,5},{5,4},{6,7},{7,6},{8,9},{9,8},{10,11... | collective-permute-start | bytes 25165832 | tf_op jit(solution)/shard_map/ppermute | solution.py:76
  30.0 4.4 %collective-permute-start.17 = (bf16[512,128]{1,0:T(8,128)(2,1)S(1)}, bf16[512,128]{1,0:T(8,128)(2,1)S(1)}, u32[]{:S(2)}, u32[]{:S(2)}) collective-permute-start(bf16[512,128]{1,0:T(8,128)(2,1)S(1)} %project.5.q), channel_id=1, source_target_pairs={{0,5},{1,2},{2,7},{3,0},{4,1},{5,8},{6,3},{7,10},{8,13},{9,4},{10,... | collective-permute-start | bytes 393224 | tf_op jit(solution)/shard_map/ppermute | solution.py:73
  34.4 5.1 %collective-permute-start.19 = (bf16[512,128]{1,0:T(8,128)(2,1)S(1)}, bf16[512,128]{1,0:T(8,128)(2,1)S(1)}, u32[]{:S(2)}, u32[]{:S(2)}) collective-permute-start(bf16[512,128]{1,0:T(8,128)(2,1)S(1)} %collective-permute-done.17.q), channel_id=1, source_target_pairs={{0,5},{1,2},{2,7},{3,0},{4,1},{5,8},{6,3},{7,10},{8,13},{9,4},{10,... | collective-permute-start | bytes 393224 | tf_op jit(solution)/shard_map/ppermute | solution.py:73
  37.9 4.5 %collective-permute-start.18 = (bf16[528,128]{1,0:T(8,128)(2,1)S(1)}, bf16[528,128]{1,0:T(8,128)(2,1)S(1)}, u32[]{:S(2)}, u32[]{:S(2)}) collective-permute-start(bf16[528,128]{1,0:T(8,128)(2,1)S(1)} %get-tuple-element.152), channel_id=1, source_target_pairs={{0,5},{1,2},{2,7},{3,0},{4,1},{5,8},{6,3},{7,10},{8,13},{9,4},{10,... | collective-permute-start | bytes 405512 | tf_op jit(solution)/shard_map/ppermute | solution.py:73
  39.5 5.0 %collective-permute-start.21 = (bf16[512,128]{1,0:T(8,128)(2,1)S(1)}, bf16[512,128]{1,0:T(8,128)(2,1)S(1)}, u32[]{:S(2)}, u32[]{:S(2)}) collective-permute-start(bf16[512,128]{1,0:T(8,128)(2,1)S(1)} %collective-permute-done.19.q), channel_id=1, source_target_pairs={{0,5},{1,2},{2,7},{3,0},{4,1},{5,8},{6,3},{7,10},{8,13},{9,4},{10,... | collective-permute-start | bytes 393224 | tf_op jit(solution)/shard_map/ppermute | solution.py:73
  42.7 4.9 %collective-permute-start.20 = (bf16[528,128]{1,0:T(8,128)(2,1)S(1)}, bf16[528,128]{1,0:T(8,128)(2,1)S(1)}, u32[]{:S(2)}, u32[]{:S(2)}) collective-permute-start(bf16[528,128]{1,0:T(8,128)(2,1)S(1)} %merge.6), channel_id=1, source_target_pairs={{0,5},{1,2},{2,7},{3,0},{4,1},{5,8},{6,3},{7,10},{8,13},{9,4},{10,... | collective-permute-start | bytes 405512 | tf_op jit(solution)/shard_map/ppermute | solution.py:73
  44.5 5.0 %collective-permute-start.23 = (bf16[512,128]{1,0:T(8,128)(2,1)S(1)}, bf16[512,128]{1,0:T(8,128)(2,1)S(1)}, u32[]{:S(2)}, u32[]{:S(2)}) collective-permute-start(bf16[512,128]{1,0:T(8,128)(2,1)S(1)} %collective-permute-done.21.q), channel_id=1, source_target_pairs={{0,5},{1,2},{2,7},{3,0},{4,1},{5,8},{6,3},{7,10},{8,13},{9,4},{10,... | collective-permute-start | bytes 393224 | tf_op jit(solution)/shard_map/ppermute | solution.py:73
  47.8 4.8 %collective-permute-start.22 = (bf16[528,128]{1,0:T(8,128)(2,1)S(1)}, bf16[528,128]{1,0:T(8,128)(2,1)S(1)}, u32[]{:S(2)}, u32[]{:S(2)}) collective-permute-start(bf16[528,128]{1,0:T(8,128)(2,1)S(1)} %merge.7), channel_id=1, source_target_pairs={{0,5},{1,2},{2,7},{3,0},{4,1},{5,8},{6,3},{7,10},{8,13},{9,4},{10,... | collective-permute-start | bytes 405512 | tf_op jit(solution)/shard_map/ppermute | solution.py:73
  49.5 4.9 %collective-permute-start.25 = (bf16[512,128]{1,0:T(8,128)(2,1)S(1)}, bf16[512,128]{1,0:T(8,128)(2,1)S(1)}, u32[]{:S(2)}, u32[]{:S(2)}) collective-permute-start(bf16[512,128]{1,0:T(8,128)(2,1)S(1)} %collective-permute-done.23.q), channel_id=1, source_target_pairs={{0,5},{1,2},{2,7},{3,0},{4,1},{5,8},{6,3},{7,10},{8,13},{9,4},{10,... | collective-permute-start | bytes 393224 | tf_op jit(solution)/shard_map/ppermute | solution.py:73
  52.8 4.8 %collective-permute-start.24 = (bf16[528,128]{1,0:T(8,128)(2,1)S(1)}, bf16[528,128]{1,0:T(8,128)(2,1)S(1)}, u32[]{:S(2)}, u32[]{:S(2)}) collective-permute-start(bf16[528,128]{1,0:T(8,128)(2,1)S(1)} %merge.8), channel_id=1, source_target_pairs={{0,5},{1,2},{2,7},{3,0},{4,1},{5,8},{6,3},{7,10},{8,13},{9,4},{10,... | collective-permute-start | bytes 405512 | tf_op jit(solution)/shard_map/ppermute | solution.py:73
  54.4 5.0 %collective-permute-start.27 = (bf16[512,128]{1,0:T(8,128)(2,1)S(1)}, bf16[512,128]{1,0:T(8,128)(2,1)S(1)}, u32[]{:S(2)}, u32[]{:S(2)}) collective-permute-start(bf16[512,128]{1,0:T(8,128)(2,1)S(1)} %collective-permute-done.25.q), channel_id=1, source_target_pairs={{0,5},{1,2},{2,7},{3,0},{4,1},{5,8},{6,3},{7,10},{8,13},{9,4},{10,... | collective-permute-start | bytes 393224 | tf_op jit(solution)/shard_map/ppermute | solution.py:73
  57.9 4.6 %collective-permute-start.26 = (bf16[528,128]{1,0:T(8,128)(2,1)S(1)}, bf16[528,128]{1,0:T(8,128)(2,1)S(1)}, u32[]{:S(2)}, u32[]{:S(2)}) collective-permute-start(bf16[528,128]{1,0:T(8,128)(2,1)S(1)} %merge.9), channel_id=1, source_target_pairs={{0,5},{1,2},{2,7},{3,0},{4,1},{5,8},{6,3},{7,10},{8,13},{9,4},{10,... | collective-permute-start | bytes 405512 | tf_op jit(solution)/shard_map/ppermute | solution.py:73
  59.4 5.0 %collective-permute-start.29 = (bf16[512,128]{1,0:T(8,128)(2,1)S(1)}, bf16[512,128]{1,0:T(8,128)(2,1)S(1)}, u32[]{:S(2)}, u32[]{:S(2)}) collective-permute-start(bf16[512,128]{1,0:T(8,128)(2,1)S(1)} %collective-permute-done.27.q), channel_id=1, source_target_pairs={{0,5},{1,2},{2,7},{3,0},{4,1},{5,8},{6,3},{7,10},{8,13},{9,4},{10,... | collective-permute-start | bytes 393224 | tf_op jit(solution)/shard_map/ppermute | solution.py:73
  62.7 4.5 %collective-permute-start.28 = (bf16[528,128]{1,0:T(8,128)(2,1)S(1)}, bf16[528,128]{1,0:T(8,128)(2,1)S(1)}, u32[]{:S(2)}, u32[]{:S(2)}) collective-permute-start(bf16[528,128]{1,0:T(8,128)(2,1)S(1)} %merge.10), channel_id=1, source_target_pairs={{0,5},{1,2},{2,7},{3,0},{4,1},{5,8},{6,3},{7,10},{8,13},{9,4},{10,... | collective-permute-start | bytes 405512 | tf_op jit(solution)/shard_map/ppermute | solution.py:73
  67.4 4.7 %collective-permute-start.30 = (bf16[528,128]{1,0:T(8,128)(2,1)S(1)}, bf16[528,128]{1,0:T(8,128)(2,1)S(1)}, u32[]{:S(2)}, u32[]{:S(2)}) collective-permute-start(bf16[528,128]{1,0:T(8,128)(2,1)S(1)} %merge.11), channel_id=1, source_target_pairs={{0,5},{1,2},{2,7},{3,0},{4,1},{5,8},{6,3},{7,10},{8,13},{9,4},{10,... | collective-permute-start | bytes 405512 | tf_op jit(solution)/shard_map/ppermute | solution.py:73
  72.4 1.7 %collective-permute-start.31 = (bf16[128,512]{1,0:T(8,128)(2,1)S(1)}, bf16[128,512]{1,0:T(8,128)(2,1)S(1)}, u32[]{:S(2)}, u32[]{:S(2)}) collective-permute-start(bf16[128,512]{1,0:T(8,128)(2,1)S(1)} %finish.1.refs_7_.refs_2_), channel_id=1, source_target_pairs={{0,1},{1,0},{2,3},{3,2},{4,5},{5,4},{6,7},{7,6},{8,9},{9,8},{10,11... | collective-permute-start | bytes 393224 | tf_op jit(solution)/shard_map/ppermute | solution.py:76
  74.6 4.4 %collective-permute-start.33 = (bf16[128,512]{1,0:T(8,128)(2,1)S(1)}, bf16[128,512]{1,0:T(8,128)(2,1)S(1)}, u32[]{:S(2)}, u32[]{:S(2)}) collective-permute-start(bf16[128,512]{1,0:T(8,128)(2,1)S(1)} %get-tuple-element.181), channel_id=1, source_target_pairs={{0,3},{1,4},{2,1},{3,6},{4,9},{5,0},{6,11},{7,2},{8,5},{9,12},{10,... | collective-permute-start | bytes 393224 | tf_op jit(solution)/shard_map/ppermute | solution.py:73
  75.5 34.0 %slice-start.2 = ((s8[8388608]{0:T(1024)(128)(4,1)}), s8[4194304]{0:T(1024)(128)(4,1)S(1)}, s32[]{:S(2)}) async-start(s8[8388608]{0:T(1024)(128)(4,1)} %bitcast.29), calls=%async_computation.2 | async-start | bytes 8388608
  75.5 34.0 %slice-start.3 = ((s8[8388608]{0:T(1024)(128)(4,1)}), s8[4194304]{0:T(1024)(128)(4,1)S(1)}, s32[]{:S(2)}) async-start(s8[8388608]{0:T(1024)(128)(4,1)} %bitcast.29), calls=%async_computation.3 | async-start | bytes 8388608
  75.5 5.0 %collective-permute-start.37 = (bf16[128,512]{1,0:T(8,128)(2,1)S(1)}, bf16[128,512]{1,0:T(8,128)(2,1)S(1)}, u32[]{:S(2)}, u32[]{:S(2)}) collective-permute-start(bf16[128,512]{1,0:T(8,128)(2,1)S(1)} %get-tuple-element.184), channel_id=1, source_target_pairs={{0,3},{1,4},{2,1},{3,6},{4,9},{5,0},{6,11},{7,2},{8,5},{9,12},{10,... | collective-permute-start | bytes 393224 | tf_op jit(solution)/shard_map/ppermute | solution.py:73
  79.1 4.4 %collective-permute-start.34 = (bf16[128,512]{1,0:T(8,128)(2,1)S(1)}, bf16[128,512]{1,0:T(8,128)(2,1)S(1)}, u32[]{:S(2)}, u32[]{:S(2)}) collective-permute-start(bf16[128,512]{1,0:T(8,128)(2,1)S(1)} %add.161), channel_id=1, source_target_pairs={{0,3},{1,4},{2,1},{3,6},{4,9},{5,0},{6,11},{7,2},{8,5},{9,12},{10,... | collective-permute-start | bytes 393224 | tf_op jit(solution)/shard_map/ppermute | solution.py:73
  80.5 4.5 %collective-permute-start.38 = (bf16[128,512]{1,0:T(8,128)(2,1)S(1)}, bf16[128,512]{1,0:T(8,128)(2,1)S(1)}, u32[]{:S(2)}, u32[]{:S(2)}) collective-permute-start(bf16[128,512]{1,0:T(8,128)(2,1)S(1)} %add.164), channel_id=1, source_target_pairs={{0,3},{1,4},{2,1},{3,6},{4,9},{5,0},{6,11},{7,2},{8,5},{9,12},{10,... | collective-permute-start | bytes 393224 | tf_op jit(solution)/shard_map/ppermute | solution.py:73
  83.6 4.7 %collective-permute-start.35 = (bf16[128,512]{1,0:T(8,128)(2,1)S(1)}, bf16[128,512]{1,0:T(8,128)(2,1)S(1)}, u32[]{:S(2)}, u32[]{:S(2)}) collective-permute-start(bf16[128,512]{1,0:T(8,128)(2,1)S(1)} %add.162), channel_id=1, source_target_pairs={{0,3},{1,4},{2,1},{3,6},{4,9},{5,0},{6,11},{7,2},{8,5},{9,12},{10,... | collective-permute-start | bytes 393224 | tf_op jit(solution)/shard_map/ppermute | solution.py:73
  85.1 4.7 %collective-permute-start.39 = (bf16[128,512]{1,0:T(8,128)(2,1)S(1)}, bf16[128,512]{1,0:T(8,128)(2,1)S(1)}, u32[]{:S(2)}, u32[]{:S(2)}) collective-permute-start(bf16[128,512]{1,0:T(8,128)(2,1)S(1)} %add.165), channel_id=1, source_target_pairs={{0,3},{1,4},{2,1},{3,6},{4,9},{5,0},{6,11},{7,2},{8,5},{9,12},{10,... | collective-permute-start | bytes 393224 | tf_op jit(solution)/shard_map/ppermute | solution.py:73
  88.3 4.7 %collective-permute-start.36 = (bf16[128,512]{1,0:T(8,128)(2,1)S(1)}, bf16[128,512]{1,0:T(8,128)(2,1)S(1)}, u32[]{:S(2)}, u32[]{:S(2)}) collective-permute-start(bf16[128,512]{1,0:T(8,128)(2,1)S(1)} %add.163), channel_id=1, source_target_pairs={{0,3},{1,4},{2,1},{3,6},{4,9},{5,0},{6,11},{7,2},{8,5},{9,12},{10,... | collective-permute-start | bytes 393224 | tf_op jit(solution)/shard_map/ppermute | solution.py:73
  89.8 4.0 %collective-permute-start.40 = (bf16[128,512]{1,0:T(8,128)(2,1)S(1)}, bf16[128,512]{1,0:T(8,128)(2,1)S(1)}, u32[]{:S(2)}, u32[]{:S(2)}) collective-permute-start(bf16[128,512]{1,0:T(8,128)(2,1)S(1)} %collective-permute-done.39.refs_1_), channel_id=1, source_target_pairs={{0,1},{1,0},{2,3},{3,2},{4,5},{5,4},{6,7},{7,6},{8,9},{9,8},{10,11... | collective-permute-start | bytes 393224 | tf_op jit(solution)/shard_map/ppermute | solution.py:76
  93.0 1.9 %collective-permute-start.45 = (bf16[128,512]{1,0:T(8,128)(2,1)S(1)}, bf16[128,512]{1,0:T(8,128)(2,1)S(1)}, u32[]{:S(2)}, u32[]{:S(2)}) collective-permute-start(bf16[128,512]{1,0:T(8,128)(2,1)S(1)} %collective-permute-done.36.refs_1_), channel_id=1, source_target_pairs={{0,1},{1,0},{2,3},{3,2},{4,5},{5,4},{6,7},{7,6},{8,9},{9,8},{10,11... | collective-permute-start | bytes 393224 | tf_op jit(solution)/shard_map/ppermute | solution.py:76
  93.8 4.4 %collective-permute-start.41 = (bf16[128,512]{1,0:T(8,128)(2,1)S(1)}, bf16[128,512]{1,0:T(8,128)(2,1)S(1)}, u32[]{:S(2)}, u32[]{:S(2)}) collective-permute-start(bf16[128,512]{1,0:T(8,128)(2,1)S(1)} %add.166.refs_12_), channel_id=1, source_target_pairs={{0,5},{1,2},{2,7},{3,0},{4,1},{5,8},{6,3},{7,10},{8,13},{9,4},{10,... | collective-permute-start | bytes 393224 | tf_op jit(solution)/shard_map/ppermute | solution.py:73
  95.0 4.7 %collective-permute-start.47 = (bf16[128,512]{1,0:T(8,128)(2,1)S(1)}, bf16[128,512]{1,0:T(8,128)(2,1)S(1)}, u32[]{:S(2)}, u32[]{:S(2)}) collective-permute-start(bf16[128,512]{1,0:T(8,128)(2,1)S(1)} %add.167.refs_13_), channel_id=1, source_target_pairs={{0,5},{1,2},{2,7},{3,0},{4,1},{5,8},{6,3},{7,10},{8,13},{9,4},{10,... | collective-permute-start | bytes 393224 | tf_op jit(solution)/shard_map/ppermute | solution.py:73
  98.3 4.4 %collective-permute-start.42 = (bf16[128,512]{1,0:T(8,128)(2,1)S(1)}, bf16[128,512]{1,0:T(8,128)(2,1)S(1)}, u32[]{:S(2)}, u32[]{:S(2)}) collective-permute-start(bf16[128,512]{1,0:T(8,128)(2,1)S(1)} %collective-permute-done.41.refs_14_), channel_id=1, source_target_pairs={{0,5},{1,2},{2,7},{3,0},{4,1},{5,8},{6,3},{7,10},{8,13},{9,4},{10,... | collective-permute-start | bytes 393224 | tf_op jit(solution)/shard_map/ppermute | solution.py:73
  99.7 5.1 %collective-permute-start.50 = (bf16[128,512]{1,0:T(8,128)(2,1)S(1)}, bf16[128,512]{1,0:T(8,128)(2,1)S(1)}, u32[]{:S(2)}, u32[]{:S(2)}) collective-permute-start(bf16[128,512]{1,0:T(8,128)(2,1)S(1)} %collective-permute-done.47.refs_16_), channel_id=1, source_target_pairs={{0,5},{1,2},{2,7},{3,0},{4,1},{5,8},{6,3},{7,10},{8,13},{9,4},{10,... | collective-permute-start | bytes 393224 | tf_op jit(solution)/shard_map/ppermute | solution.py:73
  102.7 4.4 %collective-permute-start.43 = (bf16[128,512]{1,0:T(8,128)(2,1)S(1)}, bf16[128,512]{1,0:T(8,128)(2,1)S(1)}, u32[]{:S(2)}, u32[]{:S(2)}) collective-permute-start(bf16[128,512]{1,0:T(8,128)(2,1)S(1)} %collective-permute-done.42.refs_18_), channel_id=1, source_target_pairs={{0,5},{1,2},{2,7},{3,0},{4,1},{5,8},{6,3},{7,10},{8,13},{9,4},{10,... | collective-permute-start | bytes 393224 | tf_op jit(solution)/shard_map/ppermute | solution.py:73
  104.3 3.4 %collective-permute-start.46 = (bf16[128,512]{1,0:T(8,128)(2,1)S(1)}, bf16[128,512]{1,0:T(8,128)(2,1)S(1)}, u32[]{:S(2)}, u32[]{:S(2)}) collective-permute-start(bf16[128,512]{1,0:T(8,128)(2,1)S(1)} %collective-permute-done.41.refs_14_), channel_id=1, source_target_pairs={{0,1},{1,0},{2,3},{3,2},{4,5},{5,4},{6,7},{7,6},{8,9},{9,8},{10,11... | collective-permute-start | bytes 393224 | tf_op jit(solution)/shard_map/ppermute | solution.py:76
  104.3 4.4 %collective-permute-start.48 = (bf16[128,512]{1,0:T(8,128)(2,1)S(1)}, bf16[128,512]{1,0:T(8,128)(2,1)S(1)}, u32[]{:S(2)}, u32[]{:S(2)}) collective-permute-start(bf16[128,512]{1,0:T(8,128)(2,1)S(1)} %collective-permute-done.47.refs_16_), channel_id=1, source_target_pairs={{0,1},{1,0},{2,3},{3,2},{4,5},{5,4},{6,7},{7,6},{8,9},{9,8},{10,11... | collective-permute-start | bytes 393224 | tf_op jit(solution)/shard_map/ppermute | solution.py:76
  104.8 4.7 %collective-permute-start.49 = (bf16[128,512]{1,0:T(8,128)(2,1)S(1)}, bf16[128,512]{1,0:T(8,128)(2,1)S(1)}, u32[]{:S(2)}, u32[]{:S(2)}) collective-permute-start(bf16[128,512]{1,0:T(8,128)(2,1)S(1)} %collective-permute-done.42.refs_18_), channel_id=1, source_target_pairs={{0,1},{1,0},{2,3},{3,2},{4,5},{5,4},{6,7},{7,6},{8,9},{9,8},{10,11... | collective-permute-start | bytes 393224 | tf_op jit(solution)/shard_map/ppermute | solution.py:76
  104.8 4.7 %collective-permute-start.51 = (bf16[128,512]{1,0:T(8,128)(2,1)S(1)}, bf16[128,512]{1,0:T(8,128)(2,1)S(1)}, u32[]{:S(2)}, u32[]{:S(2)}) collective-permute-start(bf16[128,512]{1,0:T(8,128)(2,1)S(1)} %collective-permute-done.50.refs_20_), channel_id=1, source_target_pairs={{0,1},{1,0},{2,3},{3,2},{4,5},{5,4},{6,7},{7,6},{8,9},{9,8},{10,11... | collective-permute-start | bytes 393224 | tf_op jit(solution)/shard_map/ppermute | solution.py:76
  107.1 2.4 %collective-permute-start.52 = (bf16[128,512]{1,0:T(8,128)(2,1)S(1)}, bf16[128,512]{1,0:T(8,128)(2,1)S(1)}, u32[]{:S(2)}, u32[]{:S(2)}) collective-permute-start(bf16[128,512]{1,0:T(8,128)(2,1)S(1)} %collective-permute-done.43.refs_22_), channel_id=1, source_target_pairs={{0,1},{1,0},{2,3},{3,2},{4,5},{5,4},{6,7},{7,6},{8,9},{9,8},{10,11... | collective-permute-start | bytes 393224 | tf_op jit(solution)/shard_map/ppermute | solution.py:76
  107.7 4.4 %collective-permute-start.44 = (bf16[128,512]{1,0:T(8,128)(2,1)S(1)}, bf16[128,512]{1,0:T(8,128)(2,1)S(1)}, u32[]{:S(2)}, u32[]{:S(2)}) collective-permute-start(bf16[128,512]{1,0:T(8,128)(2,1)S(1)} %collective-permute-done.43.refs_22_), channel_id=1, source_target_pairs={{0,5},{1,2},{2,7},{3,0},{4,1},{5,8},{6,3},{7,10},{8,13},{9,4},{10,... | collective-permute-start | bytes 393224 | tf_op jit(solution)/shard_map/ppermute | solution.py:73
  108.7 4.8 %collective-permute-start.54 = (bf16[128,512]{1,0:T(8,128)(2,1)S(1)}, bf16[128,512]{1,0:T(8,128)(2,1)S(1)}, u32[]{:S(2)}, u32[]{:S(2)}) collective-permute-start(bf16[128,512]{1,0:T(8,128)(2,1)S(1)} %collective-permute-done.50.refs_20_), channel_id=1, source_target_pairs={{0,5},{1,2},{2,7},{3,0},{4,1},{5,8},{6,3},{7,10},{8,13},{9,4},{10,... | collective-permute-start | bytes 393224 | tf_op jit(solution)/shard_map/ppermute | solution.py:73
  112.0 2.2 %collective-permute-start.53 = (bf16[128,512]{1,0:T(8,128)(2,1)S(1)}, bf16[128,512]{1,0:T(8,128)(2,1)S(1)}, u32[]{:S(2)}, u32[]{:S(2)}) collective-permute-start(bf16[128,512]{1,0:T(8,128)(2,1)S(1)} %collective-permute-done.44.refs_4_), channel_id=1, source_target_pairs={{0,1},{1,0},{2,3},{3,2},{4,5},{5,4},{6,7},{7,6},{8,9},{9,8},{10,11... | collective-permute-start | bytes 393224 | tf_op jit(solution)/shard_map/ppermute | solution.py:76
  113.4 1.3 %collective-permute-start.55 = (bf16[128,512]{1,0:T(8,128)(2,1)S(1)}, bf16[128,512]{1,0:T(8,128)(2,1)S(1)}, u32[]{:S(2)}, u32[]{:S(2)}) collective-permute-start(bf16[128,512]{1,0:T(8,128)(2,1)S(1)} %collective-permute-done.54.refs_6_), channel_id=1, source_target_pairs={{0,1},{1,0},{2,3},{3,2},{4,5},{5,4},{6,7},{7,6},{8,9},{9,8},{10,11... | collective-permute-start | bytes 393224 | tf_op jit(solution)/shard_map/ppermute | solution.py:76

commit v6 on v5

--- a/solution.py
+++ b/solution.py
@@ -607,14 +607,14 @@
     other_keys = ring.swap(after(key_cache, other))
     other_values = ring.swap(after(value_cache, other))
     cache = (key_cache, other_keys, value_cache, other_values)
-    beside = {rounds - 1: (other_keys,), rounds: (other_values,)}
+    onehot, bias = prepare(ring, last, 2 * key_cache.shape[0])
+    beside = {2: (onehot, bias), rounds - 1: (other_keys,), rounds: (other_values,)}
 
     def meanwhile(token):
-        onehot, bias = prepare(ring, after(last, token), 2 * key_cache.shape[0])
         ready = after(key_cache, token), other_keys, after(value_cache, token), other_values
-        return onehot, bias, *fetch(ring.number(0), ready)
-
-    own_heads, carriers, (onehot, bias, *head) = gather_project(
+        return fetch(ring.number(0), ready)
+
+    own_heads, carriers, head = gather_project(
         ring, queries, own, other, None, q_weight, beside, q_gain, meanwhile
     )
     other_weight = ring.swap(after(out_weight, own_heads))

time: 116 us -> 117 us (level)
  transfers between devices with their start and end apart: 56 -> 56, of which waited for: 21 -> 22; matrix products, arithmetic and copies ran while one was open for 1% -> 1% of each run, Pallas kernels for 24% -> 23%
where the time goes in v6:
time: 117 us
  starting transfers between devices  54.2 us (46%)
  Pallas kernels  29.3 us (25%)
  waiting for transfers between devices  28.9 us (25%)
  local copies, waits for them, and re-layouts  2.55 us (2%)
    ppermute x35, starting transfers between devices, send(): return lax.ppermute(block, 'ctx', sorted(route))  47.2 us
    ppermute x35, waiting for transfers between devices, send(): return lax.ppermute(block, 'ctx', sorted(route))  26.3 us
    pallas_call x8, Pallas kernels, attend(): pl.pallas_call(functools.partial(attend_kernel, chunk, parts), out_shape=...  17.5 us
    ppermute x21, starting transfers between devices, swap(): lax.ppermute(block, 'ctx', [(i, i ^ 1) for i in range(2 * self.chips)])  7.01 us
    pallas_call x4, Pallas kernels, project(): pl.pallas_call(functools.partial(project_kernel, plan), out_shape=shapes,...  6.48 us
    ppermute x21, waiting for transfers between devices, swap(): lax.ppermute(block, 'ctx', [(i, i ^ 1) for i in range(2 * self.chips)])  2.6 us
  transfers between devices with their start and end apart: 56, of which 22 were waited for; matrix products, arithmetic and copies ran while one was open for 1% of the time, Pallas kernels for 23%

profile of v6, /device:TPU:0, one launch (start us, length us, event | category | flops | bytes accessed | tf_op | source)
XLA Modules:
  0.0 117.0 jit_solution(3952145488377668798)
XLA Ops:
  0.6 1.0 select_select_fusion.refs_16_.refs_3_.refs_24_
  2.2 1.0 collective-permute-done.2.refs_17_.refs_3_.refs_25_
  3.7 2.7 %collective-permute-start = (bf16[130,512]{1,0:T(8,128)(2,1)S(1)}, bf16[130,512]{1,0:T(8,128)(2,1)S(1)}, u32[]{:S(2)}, u32[]{:S(2)}) collective-permute-start(bf16[130,512]{1,0:T(8,128)(2,1)S(1)} %select_select_fusion.refs_16_.refs_3_.refs_24_), channel_id=1, source_target_pairs={{0,5},{1,2},{2,7},{3,0},{4,1},{5,8},{6,3},{7,10},{8,13},{9,4},{10,... | collective-permute-start | bytes 399368 | tf_op jit(solution)/shard_map/ppermute | solution.py:73
  7.4 1.7 %collective-permute-done.refs_18_.refs_26_ = bf16[130,512]{1,0:T(8,128)(2,1)S(1)} collective-permute-done((bf16[130,512]{1,0:T(8,128)(2,1)S(1)}, bf16[130,512]{1,0:T(8,128)(2,1)S(1)}, u32[]{:S(2)}, u32[]{:S(2)}) %collective-permute-start) | collective-permute-done | bytes 133152 | tf_op jit(solution)/shard_map/ppermute | solution.py:73
  9.1 1.8 %collective-permute-start.8 = (bf16[130,512]{1,0:T(8,128)(2,1)S(1)}, bf16[130,512]{1,0:T(8,128)(2,1)S(1)}, u32[]{:S(2)}, u32[]{:S(2)}) collective-permute-start(bf16[130,512]{1,0:T(8,128)(2,1)S(1)} %collective-permute-done.2.refs_17_.refs_3_.refs_25_), channel_id=1, source_target_pairs={{0,5},{1,2},{2,7},{3,0},{4,1},{5,8},{6,3},{7,10},{8,13},{9,4},{10,... | collective-permute-start | bytes 399368 | tf_op jit(solution)/shard_map/ppermute | solution.py:73
  10.9 1.5 %collective-permute-start.1 = (bf16[130,512]{1,0:T(8,128)(2,1)S(1)}, bf16[130,512]{1,0:T(8,128)(2,1)S(1)}, u32[]{:S(2)}, u32[]{:S(2)}) collective-permute-start(bf16[130,512]{1,0:T(8,128)(2,1)S(1)} %collective-permute-done.refs_18_.refs_26_), channel_id=1, source_target_pairs={{0,5},{1,2},{2,7},{3,0},{4,1},{5,8},{6,3},{7,10},{8,13},{9,4},{10,... | collective-permute-start | bytes 399368 | tf_op jit(solution)/shard_map/ppermute | solution.py:73
  12.4 1.1 collective-permute-done.8.refs_20_.refs_28_
  13.6 2.1 %collective-permute-start.11 = (bf16[130,512]{1,0:T(8,128)(2,1)S(1)}, bf16[130,512]{1,0:T(8,128)(2,1)S(1)}, u32[]{:S(2)}, u32[]{:S(2)}) collective-permute-start(bf16[130,512]{1,0:T(8,128)(2,1)S(1)} %collective-permute-done.8.refs_20_.refs_28_), channel_id=1, source_target_pairs={{0,5},{1,2},{2,7},{3,0},{4,1},{5,8},{6,3},{7,10},{8,13},{9,4},{10,... | collective-permute-start | bytes 399368 | tf_op jit(solution)/shard_map/ppermute | solution.py:73
  15.7 1.3 %collective-permute-start.4 = (bf16[130,512]{1,0:T(8,128)(2,1)S(1)}, bf16[130,512]{1,0:T(8,128)(2,1)S(1)}, u32[]{:S(2)}, u32[]{:S(2)}) collective-permute-start(bf16[130,512]{1,0:T(8,128)(2,1)S(1)} %collective-permute-done.1.refs_22_.refs_30_), channel_id=1, source_target_pairs={{0,5},{1,2},{2,7},{3,0},{4,1},{5,8},{6,3},{7,10},{8,13},{9,4},{10,... | collective-permute-start | bytes 399368 | tf_op jit(solution)/shard_map/ppermute | solution.py:73
  17.4 0.9 collective-permute-done.11.refs_24_.refs_32_
  19.1 1.1 collective-permute-done.4.refs_26_.refs_34_
  20.3 1.4 %collective-permute-start.6 = (bf16[130,512]{1,0:T(8,128)(2,1)S(1)}, bf16[130,512]{1,0:T(8,128)(2,1)S(1)}, u32[]{:S(2)}, u32[]{:S(2)}) collective-permute-start(bf16[130,512]{1,0:T(8,128)(2,1)S(1)} %collective-permute-done.4.refs_26_.refs_34_), channel_id=1, source_target_pairs={{0,5},{1,2},{2,7},{3,0},{4,1},{5,8},{6,3},{7,10},{8,13},{9,4},{10,... | collective-permute-start | bytes 399368 | tf_op jit(solution)/shard_map/ppermute | solution.py:73
  21.7 1.6 %collective-permute-start.15 = (bf16[130,512]{1,0:T(8,128)(2,1)S(1)}, bf16[130,512]{1,0:T(8,128)(2,1)S(1)}, u32[]{:S(2)}, u32[]{:S(2)}) collective-permute-start(bf16[130,512]{1,0:T(8,128)(2,1)S(1)} %collective-permute-done.11.refs_24_.refs_32_), channel_id=1, source_target_pairs={{0,5},{1,2},{2,7},{3,0},{4,1},{5,8},{6,3},{7,10},{8,13},{9,4},{10,... | collective-permute-start | bytes 399368 | tf_op jit(solution)/shard_map/ppermute | solution.py:73
  23.3 3.8 %project.4 = (f32[128,512]{1,0:T(8,128)S(1)}, f32[128,128]{1,0:T(8,128)S(1)}, bf16[512,512]{1,0:T(8,128)(2,1)S(1)}, bf16[512,512]{1,0:T(8,128)(2,1)S(1)}, bf16[5...) custom-call(s32[1]{0:T(128)} %bitcast.5.refs_0_.refs_5_, s32[1]{0:T(128)} %bitcast.6.refs_1_.refs_6_, ...), custom_call_target="tpu_custom_call" | custom-call | flops 690000000 | tf_op jit(solution)/shard_map/project/pallas_call | solution.py:440
  27.7 1.6 %fetch.1 = (bf16[3072,128]{1,0:T(8,128)(2,1)S(1)}, bf16[3072,128]{1,0:T(8,128)(2,1)S(1)}) custom-call(s32[1]{0:T(128)} %bitcast.18.head, bf16[1536,1024]{1,0:T(8,128)(2,1)} %refs_1_.13, bf16[1536,1024]{1,0:T(8,128)(2,1)S(1)} %collective-permute-done.3.k1.refs_2_, bf16[1536,1024]{1,0:T(8,128)(2,1)} %refs_3_.13, ...), custom_call_target="tpu_custom_call" | custom-call | flops 414000000 | tf_op jit(solution)/shard_map/fetch/pallas_call | solution.py:186
  30.0 1.1 slice-done.1
  31.2 1.2 %collective-permute-start.17 = (bf16[512,128]{1,0:T(8,128)(2,1)S(1)}, bf16[512,128]{1,0:T(8,128)(2,1)S(1)}, u32[]{:S(2)}, u32[]{:S(2)}) collective-permute-start(bf16[512,128]{1,0:T(8,128)(2,1)S(1)} %project.5.q), channel_id=1, source_target_pairs={{0,5},{1,2},{2,7},{3,0},{4,1},{5,8},{6,3},{7,10},{8,13},{9,4},{10,... | collective-permute-start | bytes 393224 | tf_op jit(solution)/shard_map/ppermute | solution.py:73
  32.4 2.2 %attend.8 = (bf16[528,128]{1,0:T(8,128)(2,1)S(1)}, bf16[3072,128]{1,0:T(8,128)(2,1)S(1)}, bf16[3072,128]{1,0:T(8,128)(2,1)S(1)}) custom-call(bf16[512,128]{1,0:T(8,128)(2,1)S(1)} %project.5.q, bf16[128,128]{1,0:T(8,128)(2,1)S(1)} %get-tuple-element.128.bias, bf16[3072,128]{1,0:T(8,128)(2,1)S(1)} %get-tuple-element.127.onehot, ...), custom_call_target="tpu_custom_call" | custom-call | flops 6442450944 | bytes 3145728 | tf_op jit(solution)/shard_map/attend/pallas_call | solution.py:252
  34.6 1.0 collective-permute-done.17.q
  35.6 1.3 %collective-permute-start.19 = (bf16[512,128]{1,0:T(8,128)(2,1)S(1)}, bf16[512,128]{1,0:T(8,128)(2,1)S(1)}, u32[]{:S(2)}, u32[]{:S(2)}) collective-permute-start(bf16[512,128]{1,0:T(8,128)(2,1)S(1)} %collective-permute-done.17.q), channel_id=1, source_target_pairs={{0,5},{1,2},{2,7},{3,0},{4,1},{5,8},{6,3},{7,10},{8,13},{9,4},{10,... | collective-permute-start | bytes 393224 | tf_op jit(solution)/shard_map/ppermute | solution.py:73
  36.9 2.2 %attend.9 = (bf16[528,128]{1,0:T(8,128)(2,1)S(1)}, bf16[3072,128]{1,0:T(8,128)(2,1)S(1)}, bf16[3072,128]{1,0:T(8,128)(2,1)S(1)}) custom-call(bf16[512,128]{1,0:T(8,128)(2,1)S(1)} %collective-permute-done.17.q, bf16[128,128]{1,0:T(8,128)(2,1)S(1)} %get-tuple-element.128.bias, bf16[3072,128]{1,0:T(8,128)(2,1)S(1)} %get-tuple-element.127.onehot, ...), custom_call_target="tpu_custom_call" | custom-call | flops 6442450944 | bytes 3145728 | tf_op jit(solution)/shard_map/attend/pallas_call | solution.py:252
  39.1 1.5 %collective-permute-start.18 = (bf16[528,128]{1,0:T(8,128)(2,1)S(1)}, bf16[528,128]{1,0:T(8,128)(2,1)S(1)}, u32[]{:S(2)}, u32[]{:S(2)}) collective-permute-start(bf16[528,128]{1,0:T(8,128)(2,1)S(1)} %get-tuple-element.152), channel_id=1, source_target_pairs={{0,5},{1,2},{2,7},{3,0},{4,1},{5,8},{6,3},{7,10},{8,13},{9,4},{10,... | collective-permute-start | bytes 405512 | tf_op jit(solution)/shard_map/ppermute | solution.py:73
  41.3 2.2 %attend.10 = (bf16[528,128]{1,0:T(8,128)(2,1)S(1)}, bf16[3072,128]{1,0:T(8,128)(2,1)S(1)}, bf16[3072,128]{1,0:T(8,128)(2,1)S(1)}) custom-call(bf16[512,128]{1,0:T(8,128)(2,1)S(1)} %collective-permute-done.19.q, bf16[128,128]{1,0:T(8,128)(2,1)S(1)} %get-tuple-element.128.bias, bf16[3072,128]{1,0:T(8,128)(2,1)S(1)} %get-tuple-element.127.onehot, ...), custom_call_target="tpu_custom_call" | custom-call | flops 6442450944 | bytes 3145728 | tf_op jit(solution)/shard_map/attend/pallas_call | solution.py:252
  43.8 1.8 %collective-permute-start.20 = (bf16[528,128]{1,0:T(8,128)(2,1)S(1)}, bf16[528,128]{1,0:T(8,128)(2,1)S(1)}, u32[]{:S(2)}, u32[]{:S(2)}) collective-permute-start(bf16[528,128]{1,0:T(8,128)(2,1)S(1)} %merge.6), channel_id=1, source_target_pairs={{0,5},{1,2},{2,7},{3,0},{4,1},{5,8},{6,3},{7,10},{8,13},{9,4},{10,... | collective-permute-start | bytes 405512 | tf_op jit(solution)/shard_map/ppermute | solution.py:73
  46.4 2.2 %attend.11 = (bf16[528,128]{1,0:T(8,128)(2,1)S(1)}, bf16[3072,128]{1,0:T(8,128)(2,1)S(1)}, bf16[3072,128]{1,0:T(8,128)(2,1)S(1)}) custom-call(bf16[512,128]{1,0:T(8,128)(2,1)S(1)} %collective-permute-done.21.q, bf16[128,128]{1,0:T(8,128)(2,1)S(1)} %get-tuple-element.128.bias, bf16[3072,128]{1,0:T(8,128)(2,1)S(1)} %get-tuple-element.127.onehot, ...), custom_call_target="tpu_custom_call" | custom-call | flops 6442450944 | bytes 3145728 | tf_op jit(solution)/shard_map/attend/pallas_call | solution.py:252
  48.9 1.8 %collective-permute-start.22 = (bf16[528,128]{1,0:T(8,128)(2,1)S(1)}, bf16[528,128]{1,0:T(8,128)(2,1)S(1)}, u32[]{:S(2)}, u32[]{:S(2)}) collective-permute-start(bf16[528,128]{1,0:T(8,128)(2,1)S(1)} %merge.7), channel_id=1, source_target_pairs={{0,5},{1,2},{2,7},{3,0},{4,1},{5,8},{6,3},{7,10},{8,13},{9,4},{10,... | collective-permute-start | bytes 405512 | tf_op jit(solution)/shard_map/ppermute | solution.py:73
  51.5 2.2 %attend.12 = (bf16[528,128]{1,0:T(8,128)(2,1)S(1)}, bf16[3072,128]{1,0:T(8,128)(2,1)S(1)}, bf16[3072,128]{1,0:T(8,128)(2,1)S(1)}) custom-call(bf16[512,128]{1,0:T(8,128)(2,1)S(1)} %collective-permute-done.23.q, bf16[128,128]{1,0:T(8,128)(2,1)S(1)} %get-tuple-element.128.bias, bf16[3072,128]{1,0:T(8,128)(2,1)S(1)} %get-tuple-element.127.onehot, ...), custom_call_target="tpu_custom_call" | custom-call | flops 6442450944 | bytes 3145728 | tf_op jit(solution)/shard_map/attend/pallas_call | solution.py:252
  53.9 1.6 %collective-permute-start.24 = (bf16[528,128]{1,0:T(8,128)(2,1)S(1)}, bf16[528,128]{1,0:T(8,128)(2,1)S(1)}, u32[]{:S(2)}, u32[]{:S(2)}) collective-permute-start(bf16[528,128]{1,0:T(8,128)(2,1)S(1)} %merge.8), channel_id=1, source_target_pairs={{0,5},{1,2},{2,7},{3,0},{4,1},{5,8},{6,3},{7,10},{8,13},{9,4},{10,... | collective-permute-start | bytes 405512 | tf_op jit(solution)/shard_map/ppermute | solution.py:73
  55.5 1.0 collective-permute-start.27
  56.5 2.2 %attend.13 = (bf16[528,128]{1,0:T(8,128)(2,1)S(1)}, bf16[3072,128]{1,0:T(8,128)(2,1)S(1)}, bf16[3072,128]{1,0:T(8,128)(2,1)S(1)}) custom-call(bf16[512,128]{1,0:T(8,128)(2,1)S(1)} %collective-permute-done.25.q, bf16[128,128]{1,0:T(8,128)(2,1)S(1)} %get-tuple-element.128.bias, bf16[3072,128]{1,0:T(8,128)(2,1)S(1)} %get-tuple-element.127.onehot, ...), custom_call_target="tpu_custom_call" | custom-call | flops 6442450944 | bytes 3145728 | tf_op jit(solution)/shard_map/attend/pallas_call | solution.py:252
  59.0 1.6 %collective-permute-start.26 = (bf16[528,128]{1,0:T(8,128)(2,1)S(1)}, bf16[528,128]{1,0:T(8,128)(2,1)S(1)}, u32[]{:S(2)}, u32[]{:S(2)}) collective-permute-start(bf16[528,128]{1,0:T(8,128)(2,1)S(1)} %merge.9), channel_id=1, source_target_pairs={{0,5},{1,2},{2,7},{3,0},{4,1},{5,8},{6,3},{7,10},{8,13},{9,4},{10,... | collective-permute-start | bytes 405512 | tf_op jit(solution)/shard_map/ppermute | solution.py:73
  60.5 0.8 collective-permute-start.29
  61.4 2.2 %attend.14 = (bf16[528,128]{1,0:T(8,128)(2,1)S(1)}, bf16[3072,128]{1,0:T(8,128)(2,1)S(1)}, bf16[3072,128]{1,0:T(8,128)(2,1)S(1)}) custom-call(bf16[512,128]{1,0:T(8,128)(2,1)S(1)} %collective-permute-done.27.q, bf16[128,128]{1,0:T(8,128)(2,1)S(1)} %get-tuple-element.128.bias, bf16[3072,128]{1,0:T(8,128)(2,1)S(1)} %get-tuple-element.127.onehot, ...), custom_call_target="tpu_custom_call" | custom-call | flops 6442450944 | bytes 3145728 | tf_op jit(solution)/shard_map/attend/pallas_call | solution.py:252
  63.8 1.7 %collective-permute-start.28 = (bf16[528,128]{1,0:T(8,128)(2,1)S(1)}, bf16[528,128]{1,0:T(8,128)(2,1)S(1)}, u32[]{:S(2)}, u32[]{:S(2)}) collective-permute-start(bf16[528,128]{1,0:T(8,128)(2,1)S(1)} %merge.10), channel_id=1, source_target_pairs={{0,5},{1,2},{2,7},{3,0},{4,1},{5,8},{6,3},{7,10},{8,13},{9,4},{10,... | collective-permute-start | bytes 405512 | tf_op jit(solution)/shard_map/ppermute | solution.py:73
  65.5 2.1 %attend.15.two = bf16[528,128]{1,0:T(8,128)(2,1)S(1)} custom-call(bf16[512,128]{1,0:T(8,128)(2,1)S(1)} %collective-permute-done.29.q, bf16[128,128]{1,0:T(8,128)(2,1)S(1)} %get-tuple-element.128.bias, bf16[3072,128]{1,0:T(8,128)(2,1)S(1)} %get-tuple-element.127.onehot, bf16[3072,128]{1,0:T(8,128)(2,1)S(1)} %get-tuple-element.174.key, ...), custom_call_target="tpu_custom_call" | custom-call | flops 6442450944 | bytes 3145728 | tf_op jit(solution)/shard_map/attend/pallas_call | solution.py:252
  68.5 1.9 %collective-permute-start.30 = (bf16[528,128]{1,0:T(8,128)(2,1)S(1)}, bf16[528,128]{1,0:T(8,128)(2,1)S(1)}, u32[]{:S(2)}, u32[]{:S(2)}) collective-permute-start(bf16[528,128]{1,0:T(8,128)(2,1)S(1)} %merge.11), channel_id=1, source_target_pairs={{0,5},{1,2},{2,7},{3,0},{4,1},{5,8},{6,3},{7,10},{8,13},{9,4},{10,... | collective-permute-start | bytes 405512 | tf_op jit(solution)/shard_map/ppermute | solution.py:73
  70.5 2.8 %collective-permute-done.30.refs_0_ = bf16[528,128]{1,0:T(8,128)(2,1)S(1)} collective-permute-done((bf16[528,128]{1,0:T(8,128)(2,1)S(1)}, bf16[528,128]{1,0:T(8,128)(2,1)S(1)}, u32[]{:S(2)}, u32[]{:S(2)}) %collective-permute-start.30) | collective-permute-done | bytes 135200 | tf_op jit(solution)/shard_map/ppermute | solution.py:73
  74.3 1.0 collective-permute-done.31.refs_8_.refs_3_
  75.7 0.9 collective-permute-start.33
  76.6 1.0 collective-permute-start.37
  77.6 1.1 mix.2
  78.7 1.5 %collective-permute-done.33.refs_1_ = bf16[128,512]{1,0:T(8,128)(2,1)S(1)} collective-permute-done((bf16[128,512]{1,0:T(8,128)(2,1)S(1)}, bf16[128,512]{1,0:T(8,128)(2,1)S(1)}, u32[]{:S(2)}, u32[]{:S(2)}) %collective-permute-start.33) | collective-permute-done | bytes 131104 | tf_op jit(solution)/shard_map/ppermute | solution.py:73
  80.2 1.2 collective-permute-start.34
  81.6 0.9 collective-permute-start.38
  82.4 2.2 %collective-permute-done.34.refs_1_ = bf16[128,512]{1,0:T(8,128)(2,1)S(1)} collective-permute-done((bf16[128,512]{1,0:T(8,128)(2,1)S(1)}, bf16[128,512]{1,0:T(8,128)(2,1)S(1)}, u32[]{:S(2)}, u32[]{:S(2)}) %collective-permute-start.34) | collective-permute-done | bytes 131104 | tf_op jit(solution)/shard_map/ppermute | solution.py:73
  84.7 1.4 %collective-permute-start.35 = (bf16[128,512]{1,0:T(8,128)(2,1)S(1)}, bf16[128,512]{1,0:T(8,128)(2,1)S(1)}, u32[]{:S(2)}, u32[]{:S(2)}) collective-permute-start(bf16[128,512]{1,0:T(8,128)(2,1)S(1)} %add.162), channel_id=1, source_target_pairs={{0,3},{1,4},{2,1},{3,6},{4,9},{5,0},{6,11},{7,2},{8,5},{9,12},{10,... | collective-permute-start | bytes 393224 | tf_op jit(solution)/shard_map/ppermute | solution.py:73
  86.1 1.1 collective-permute-start.39
  87.2 2.1 %collective-permute-done.35.refs_1_ = bf16[128,512]{1,0:T(8,128)(2,1)S(1)} collective-permute-done((bf16[128,512]{1,0:T(8,128)(2,1)S(1)}, bf16[128,512]{1,0:T(8,128)(2,1)S(1)}, u32[]{:S(2)}, u32[]{:S(2)}) %collective-permute-start.35) | collective-permute-done | bytes 131104 | tf_op jit(solution)/shard_map/ppermute | solution.py:73
  89.4 1.5 %collective-permute-start.36 = (bf16[128,512]{1,0:T(8,128)(2,1)S(1)}, bf16[128,512]{1,0:T(8,128)(2,1)S(1)}, u32[]{:S(2)}, u32[]{:S(2)}) collective-permute-start(bf16[128,512]{1,0:T(8,128)(2,1)S(1)} %add.163), channel_id=1, source_target_pairs={{0,3},{1,4},{2,1},{3,6},{4,9},{5,0},{6,11},{7,2},{8,5},{9,12},{10,... | collective-permute-start | bytes 393224 | tf_op jit(solution)/shard_map/ppermute | solution.py:73
  91.5 2.6 %collective-permute-done.36.refs_1_ = bf16[128,512]{1,0:T(8,128)(2,1)S(1)} collective-permute-done((bf16[128,512]{1,0:T(8,128)(2,1)S(1)}, bf16[128,512]{1,0:T(8,128)(2,1)S(1)}, u32[]{:S(2)}, u32[]{:S(2)}) %collective-permute-start.36) | collective-permute-done | bytes 131104 | tf_op jit(solution)/shard_map/ppermute | solution.py:73
  94.9 1.1 collective-permute-start.41
  96.1 1.3 %collective-permute-start.47 = (bf16[128,512]{1,0:T(8,128)(2,1)S(1)}, bf16[128,512]{1,0:T(8,128)(2,1)S(1)}, u32[]{:S(2)}, u32[]{:S(2)}) collective-permute-start(bf16[128,512]{1,0:T(8,128)(2,1)S(1)} %add.167.refs_13_), channel_id=1, source_target_pairs={{0,5},{1,2},{2,7},{3,0},{4,1},{5,8},{6,3},{7,10},{8,13},{9,4},{10,... | collective-permute-start | bytes 393224 | tf_op jit(solution)/shard_map/ppermute | solution.py:73
  97.3 2.0 %collective-permute-done.41.refs_14_ = bf16[128,512]{1,0:T(8,128)(2,1)S(1)} collective-permute-done((bf16[128,512]{1,0:T(8,128)(2,1)S(1)}, bf16[128,512]{1,0:T(8,128)(2,1)S(1)}, u32[]{:S(2)}, u32[]{:S(2)}) %collective-permute-start.41) | collective-permute-done | bytes 131104 | tf_op jit(solution)/shard_map/ppermute | solution.py:73
  99.4 1.3 %collective-permute-start.42 = (bf16[128,512]{1,0:T(8,128)(2,1)S(1)}, bf16[128,512]{1,0:T(8,128)(2,1)S(1)}, u32[]{:S(2)}, u32[]{:S(2)}) collective-permute-start(bf16[128,512]{1,0:T(8,128)(2,1)S(1)} %collective-permute-done.41.refs_14_), channel_id=1, source_target_pairs={{0,5},{1,2},{2,7},{3,0},{4,1},{5,8},{6,3},{7,10},{8,13},{9,4},{10,... | collective-permute-start | bytes 393224 | tf_op jit(solution)/shard_map/ppermute | solution.py:73
  100.8 1.1 collective-permute-start.50
  101.9 1.9 %collective-permute-done.42.refs_18_ = bf16[128,512]{1,0:T(8,128)(2,1)S(1)} collective-permute-done((bf16[128,512]{1,0:T(8,128)(2,1)S(1)}, bf16[128,512]{1,0:T(8,128)(2,1)S(1)}, u32[]{:S(2)}, u32[]{:S(2)}) %collective-permute-start.42) | collective-permute-done | bytes 131104 | tf_op jit(solution)/shard_map/ppermute | solution.py:73
  103.8 1.6 %collective-permute-start.43 = (bf16[128,512]{1,0:T(8,128)(2,1)S(1)}, bf16[128,512]{1,0:T(8,128)(2,1)S(1)}, u32[]{:S(2)}, u32[]{:S(2)}) collective-permute-start(bf16[128,512]{1,0:T(8,128)(2,1)S(1)} %collective-permute-done.42.refs_18_), channel_id=1, source_target_pairs={{0,5},{1,2},{2,7},{3,0},{4,1},{5,8},{6,3},{7,10},{8,13},{9,4},{10,... | collective-permute-start | bytes 393224 | tf_op jit(solution)/shard_map/ppermute | solution.py:73
  106.4 1.8 %collective-permute-done.43.refs_22_ = bf16[128,512]{1,0:T(8,128)(2,1)S(1)} collective-permute-done((bf16[128,512]{1,0:T(8,128)(2,1)S(1)}, bf16[128,512]{1,0:T(8,128)(2,1)S(1)}, u32[]{:S(2)}, u32[]{:S(2)}) %collective-permute-start.43) | collective-permute-done | bytes 131104 | tf_op jit(solution)/shard_map/ppermute | solution.py:73
  108.7 1.0 collective-permute-start.44
  109.8 0.8 collective-permute-start.54
  110.7 1.0 project.6
  111.7 1.5 %collective-permute-done.44.refs_4_ = bf16[128,512]{1,0:T(8,128)(2,1)S(1)} collective-permute-done((bf16[128,512]{1,0:T(8,128)(2,1)S(1)}, bf16[128,512]{1,0:T(8,128)(2,1)S(1)}, u32[]{:S(2)}, u32[]{:S(2)}) %collective-permute-start.44) | collective-permute-done | bytes 131104 | tf_op jit(solution)/shard_map/ppermute | solution.py:73
  113.4 1.1 collective-permute-done.54.refs_6_
  115.9 1.1 project.7
  (94 shorter events, 15.7 us)
Async XLA Ops:
  1.7 1.5 %collective-permute-start.2 = (bf16[130,512]{1,0:T(8,128)(2,1)S(1)}, bf16[130,512]{1,0:T(8,128)(2,1)S(1)}, u32[]{:S(2)}, u32[]{:S(2)}) collective-permute-start(bf16[130,512]{1,0:T(8,128)(2,1)S(1)} %select_select_fusion.refs_16_.refs_3_.refs_24_), channel_id=1, source_target_pairs={{0,1},{1,0},{2,3},{3,2},{4,5},{5,4},{6,7},{7,6},{8,9},{9,8},{10,11... | collective-permute-start | bytes 399368 | tf_op jit(solution)/shard_map/ppermute | solution.py:76
  3.2 12.5 %collective-permute-start.3 = (bf16[1536,1024]{1,0:T(8,128)(2,1)}, bf16[1536,1024]{1,0:T(8,128)(2,1)S(1)}, u32[]{:S(2)}, u32[]{:S(2)}) collective-permute-start(bf16[1536,1024]{1,0:T(8,128)(2,1)} %refs_1_.13), channel_id=1, source_target_pairs={{0,1},{1,0},{2,3},{3,2},{4,5},{5,4},{6,7},{7,6},{8,9},{9,8},{10,11... | collective-permute-start | bytes 9437192 | tf_op jit(solution)/shard_map/ppermute | solution.py:76
  3.6 15.5 %collective-permute-start.5 = (bf16[1536,1024]{1,0:T(8,128)(2,1)}, bf16[1536,1024]{1,0:T(8,128)(2,1)}, u32[]{:S(2)}, u32[]{:S(2)}) collective-permute-start(bf16[1536,1024]{1,0:T(8,128)(2,1)} %refs_3_.13), channel_id=1, source_target_pairs={{0,1},{1,0},{2,3},{3,2},{4,5},{5,4},{6,7},{7,6},{8,9},{9,8},{10,11... | collective-permute-start | bytes 9437192 | tf_op jit(solution)/shard_map/ppermute | solution.py:76
  3.7 5.4 %collective-permute-start = (bf16[130,512]{1,0:T(8,128)(2,1)S(1)}, bf16[130,512]{1,0:T(8,128)(2,1)S(1)}, u32[]{:S(2)}, u32[]{:S(2)}) collective-permute-start(bf16[130,512]{1,0:T(8,128)(2,1)S(1)} %select_select_fusion.refs_16_.refs_3_.refs_24_), channel_id=1, source_target_pairs={{0,5},{1,2},{2,7},{3,0},{4,1},{5,8},{6,3},{7,10},{8,13},{9,4},{10,... | collective-permute-start | bytes 399368 | tf_op jit(solution)/shard_map/ppermute | solution.py:73
  9.1 4.5 %collective-permute-start.8 = (bf16[130,512]{1,0:T(8,128)(2,1)S(1)}, bf16[130,512]{1,0:T(8,128)(2,1)S(1)}, u32[]{:S(2)}, u32[]{:S(2)}) collective-permute-start(bf16[130,512]{1,0:T(8,128)(2,1)S(1)} %collective-permute-done.2.refs_17_.refs_3_.refs_25_), channel_id=1, source_target_pairs={{0,5},{1,2},{2,7},{3,0},{4,1},{5,8},{6,3},{7,10},{8,13},{9,4},{10,... | collective-permute-start | bytes 399368 | tf_op jit(solution)/shard_map/ppermute | solution.py:73
  10.9 4.8 %collective-permute-start.1 = (bf16[130,512]{1,0:T(8,128)(2,1)S(1)}, bf16[130,512]{1,0:T(8,128)(2,1)S(1)}, u32[]{:S(2)}, u32[]{:S(2)}) collective-permute-start(bf16[130,512]{1,0:T(8,128)(2,1)S(1)} %collective-permute-done.refs_18_.refs_26_), channel_id=1, source_target_pairs={{0,5},{1,2},{2,7},{3,0},{4,1},{5,8},{6,3},{7,10},{8,13},{9,4},{10,... | collective-permute-start | bytes 399368 | tf_op jit(solution)/shard_map/ppermute | solution.py:73
  13.6 4.8 %collective-permute-start.11 = (bf16[130,512]{1,0:T(8,128)(2,1)S(1)}, bf16[130,512]{1,0:T(8,128)(2,1)S(1)}, u32[]{:S(2)}, u32[]{:S(2)}) collective-permute-start(bf16[130,512]{1,0:T(8,128)(2,1)S(1)} %collective-permute-done.8.refs_20_.refs_28_), channel_id=1, source_target_pairs={{0,5},{1,2},{2,7},{3,0},{4,1},{5,8},{6,3},{7,10},{8,13},{9,4},{10,... | collective-permute-start | bytes 399368 | tf_op jit(solution)/shard_map/ppermute | solution.py:73
  15.7 4.5 %collective-permute-start.4 = (bf16[130,512]{1,0:T(8,128)(2,1)S(1)}, bf16[130,512]{1,0:T(8,128)(2,1)S(1)}, u32[]{:S(2)}, u32[]{:S(2)}) collective-permute-start(bf16[130,512]{1,0:T(8,128)(2,1)S(1)} %collective-permute-done.1.refs_22_.refs_30_), channel_id=1, source_target_pairs={{0,5},{1,2},{2,7},{3,0},{4,1},{5,8},{6,3},{7,10},{8,13},{9,4},{10,... | collective-permute-start | bytes 399368 | tf_op jit(solution)/shard_map/ppermute | solution.py:73
  16.9 3.4 %collective-permute-start.7 = (bf16[130,512]{1,0:T(8,128)(2,1)S(1)}, bf16[130,512]{1,0:T(8,128)(2,1)S(1)}, u32[]{:S(2)}, u32[]{:S(2)}) collective-permute-start(bf16[130,512]{1,0:T(8,128)(2,1)S(1)} %collective-permute-done.refs_18_.refs_26_), channel_id=1, source_target_pairs={{0,1},{1,0},{2,3},{3,2},{4,5},{5,4},{6,7},{7,6},{8,9},{9,8},{10,11... | collective-permute-start | bytes 399368 | tf_op jit(solution)/shard_map/ppermute | solution.py:76
  17.3 4.4 %collective-permute-start.9 = (bf16[130,512]{1,0:T(8,128)(2,1)S(1)}, bf16[130,512]{1,0:T(8,128)(2,1)S(1)}, u32[]{:S(2)}, u32[]{:S(2)}) collective-permute-start(bf16[130,512]{1,0:T(8,128)(2,1)S(1)} %collective-permute-done.8.refs_20_.refs_28_), channel_id=1, source_target_pairs={{0,1},{1,0},{2,3},{3,2},{4,5},{5,4},{6,7},{7,6},{8,9},{9,8},{10,11... | collective-permute-start | bytes 399368 | tf_op jit(solution)/shard_map/ppermute | solution.py:76
  18.3 5.0 %collective-permute-start.10 = (bf16[130,512]{1,0:T(8,128)(2,1)S(1)}, bf16[130,512]{1,0:T(8,128)(2,1)S(1)}, u32[]{:S(2)}, u32[]{:S(2)}) collective-permute-start(bf16[130,512]{1,0:T(8,128)(2,1)S(1)} %collective-permute-done.1.refs_22_.refs_30_), channel_id=1, source_target_pairs={{0,1},{1,0},{2,3},{3,2},{4,5},{5,4},{6,7},{7,6},{8,9},{9,8},{10,11... | collective-permute-start | bytes 399368 | tf_op jit(solution)/shard_map/ppermute | solution.py:76
  19.1 4.3 %collective-permute-start.12 = (bf16[130,512]{1,0:T(8,128)(2,1)S(1)}, bf16[130,512]{1,0:T(8,128)(2,1)S(1)}, u32[]{:S(2)}, u32[]{:S(2)}) collective-permute-start(bf16[130,512]{1,0:T(8,128)(2,1)S(1)} %collective-permute-done.11.refs_24_.refs_32_), channel_id=1, source_target_pairs={{0,1},{1,0},{2,3},{3,2},{4,5},{5,4},{6,7},{7,6},{8,9},{9,8},{10,11... | collective-permute-start | bytes 399368 | tf_op jit(solution)/shard_map/ppermute | solution.py:76
  20.1 3.2 %collective-permute-start.13 = (bf16[130,512]{1,0:T(8,128)(2,1)S(1)}, bf16[130,512]{1,0:T(8,128)(2,1)S(1)}, u32[]{:S(2)}, u32[]{:S(2)}) collective-permute-start(bf16[130,512]{1,0:T(8,128)(2,1)S(1)} %collective-permute-done.4.refs_26_.refs_34_), channel_id=1, source_target_pairs={{0,1},{1,0},{2,3},{3,2},{4,5},{5,4},{6,7},{7,6},{8,9},{9,8},{10,11... | collective-permute-start | bytes 399368 | tf_op jit(solution)/shard_map/ppermute | solution.py:76
  20.3 6.9 %collective-permute-start.6 = (bf16[130,512]{1,0:T(8,128)(2,1)S(1)}, bf16[130,512]{1,0:T(8,128)(2,1)S(1)}, u32[]{:S(2)}, u32[]{:S(2)}) collective-permute-start(bf16[130,512]{1,0:T(8,128)(2,1)S(1)} %collective-permute-done.4.refs_26_.refs_34_), channel_id=1, source_target_pairs={{0,5},{1,2},{2,7},{3,0},{4,1},{5,8},{6,3},{7,10},{8,13},{9,4},{10,... | collective-permute-start | bytes 399368 | tf_op jit(solution)/shard_map/ppermute | solution.py:73
  21.7 5.5 %collective-permute-start.15 = (bf16[130,512]{1,0:T(8,128)(2,1)S(1)}, bf16[130,512]{1,0:T(8,128)(2,1)S(1)}, u32[]{:S(2)}, u32[]{:S(2)}) collective-permute-start(bf16[130,512]{1,0:T(8,128)(2,1)S(1)} %collective-permute-done.11.refs_24_.refs_32_), channel_id=1, source_target_pairs={{0,5},{1,2},{2,7},{3,0},{4,1},{5,8},{6,3},{7,10},{8,13},{9,4},{10,... | collective-permute-start | bytes 399368 | tf_op jit(solution)/shard_map/ppermute | solution.py:73
  27.1 2.3 %copy-start = (bf16[128]{0:T(256)(128)(2,1)S(1)}, bf16[128]{0:T(256)(128)(2,1)}, u32[]{:S(2)}) copy-start(bf16[128]{0:T(256)(128)(2,1)} %param.13) | copy-start | bytes 772
  27.1 2.9 %slice-start = ((s8[8388608]{0:T(1024)(128)(4,1)}), s8[4194304]{0:T(1024)(128)(4,1)S(1)}, s32[]{:S(2)}) async-start(s8[8388608]{0:T(1024)(128)(4,1)} %bitcast.27), calls=%async_computation | async-start | bytes 8388608
  27.1 2.2 %collective-permute-start.14 = (bf16[130,512]{1,0:T(8,128)(2,1)S(1)}, bf16[130,512]{1,0:T(8,128)(2,1)S(1)}, u32[]{:S(2)}, u32[]{:S(2)}) collective-permute-start(bf16[130,512]{1,0:T(8,128)(2,1)S(1)} %collective-permute-done.6.refs_0_.refs_8_), channel_id=1, source_target_pairs={{0,1},{1,0},{2,3},{3,2},{4,5},{5,4},{6,7},{7,6},{8,9},{9,8},{10,11... | collective-permute-start | bytes 399368 | tf_op jit(solution)/shard_map/ppermute | solution.py:76
  27.2 2.1 %collective-permute-start.16 = (bf16[130,512]{1,0:T(8,128)(2,1)S(1)}, bf16[130,512]{1,0:T(8,128)(2,1)S(1)}, u32[]{:S(2)}, u32[]{:S(2)}) collective-permute-start(bf16[130,512]{1,0:T(8,128)(2,1)S(1)} %collective-permute-done.15.refs_2_.refs_10_), channel_id=1, source_target_pairs={{0,1},{1,0},{2,3},{3,2},{4,5},{5,4},{6,7},{7,6},{8,9},{9,8},{10,11... | collective-permute-start | bytes 399368 | tf_op jit(solution)/shard_map/ppermute | solution.py:76
  27.7 3.4 %slice-start.1 = ((s8[8388608]{0:T(1024)(128)(4,1)}), s8[4194304]{0:T(1024)(128)(4,1)S(1)}, s32[]{:S(2)}) async-start(s8[8388608]{0:T(1024)(128)(4,1)} %bitcast.27), calls=%async_computation.1 | async-start | bytes 8388608
  31.1 44.1 %collective-permute-start.32 = (bf16[512,8192]{1,0:T(8,128)(2,1)S(1)}, bf16[512,8192]{1,0:T(8,128)(2,1)S(1)}, u32[]{:S(2)}, u32[]{:S(2)}) collective-permute-start(bf16[512,8192]{1,0:T(8,128)(2,1)S(1)} %bitcast.28), channel_id=1, source_target_pairs={{0,1},{1,0},{2,3},{3,2},{4,5},{5,4},{6,7},{7,6},{8,9},{9,8},{10,11... | collective-permute-start | bytes 25165832 | tf_op jit(solution)/shard_map/ppermute | solution.py:76
  31.2 4.4 %collective-permute-start.17 = (bf16[512,128]{1,0:T(8,128)(2,1)S(1)}, bf16[512,128]{1,0:T(8,128)(2,1)S(1)}, u32[]{:S(2)}, u32[]{:S(2)}) collective-permute-start(bf16[512,128]{1,0:T(8,128)(2,1)S(1)} %project.5.q), channel_id=1, source_target_pairs={{0,5},{1,2},{2,7},{3,0},{4,1},{5,8},{6,3},{7,10},{8,13},{9,4},{10,... | collective-permute-start | bytes 393224 | tf_op jit(solution)/shard_map/ppermute | solution.py:73
  35.6 5.0 %collective-permute-start.19 = (bf16[512,128]{1,0:T(8,128)(2,1)S(1)}, bf16[512,128]{1,0:T(8,128)(2,1)S(1)}, u32[]{:S(2)}, u32[]{:S(2)}) collective-permute-start(bf16[512,128]{1,0:T(8,128)(2,1)S(1)} %collective-permute-done.17.q), channel_id=1, source_target_pairs={{0,5},{1,2},{2,7},{3,0},{4,1},{5,8},{6,3},{7,10},{8,13},{9,4},{10,... | collective-permute-start | bytes 393224 | tf_op jit(solution)/shard_map/ppermute | solution.py:73
  39.1 4.5 %collective-permute-start.18 = (bf16[528,128]{1,0:T(8,128)(2,1)S(1)}, bf16[528,128]{1,0:T(8,128)(2,1)S(1)}, u32[]{:S(2)}, u32[]{:S(2)}) collective-permute-start(bf16[528,128]{1,0:T(8,128)(2,1)S(1)} %get-tuple-element.152), channel_id=1, source_target_pairs={{0,5},{1,2},{2,7},{3,0},{4,1},{5,8},{6,3},{7,10},{8,13},{9,4},{10,... | collective-permute-start | bytes 405512 | tf_op jit(solution)/shard_map/ppermute | solution.py:73
  40.6 5.0 %collective-permute-start.21 = (bf16[512,128]{1,0:T(8,128)(2,1)S(1)}, bf16[512,128]{1,0:T(8,128)(2,1)S(1)}, u32[]{:S(2)}, u32[]{:S(2)}) collective-permute-start(bf16[512,128]{1,0:T(8,128)(2,1)S(1)} %collective-permute-done.19.q), channel_id=1, source_target_pairs={{0,5},{1,2},{2,7},{3,0},{4,1},{5,8},{6,3},{7,10},{8,13},{9,4},{10,... | collective-permute-start | bytes 393224 | tf_op jit(solution)/shard_map/ppermute | solution.py:73
  43.8 4.8 %collective-permute-start.20 = (bf16[528,128]{1,0:T(8,128)(2,1)S(1)}, bf16[528,128]{1,0:T(8,128)(2,1)S(1)}, u32[]{:S(2)}, u32[]{:S(2)}) collective-permute-start(bf16[528,128]{1,0:T(8,128)(2,1)S(1)} %merge.6), channel_id=1, source_target_pairs={{0,5},{1,2},{2,7},{3,0},{4,1},{5,8},{6,3},{7,10},{8,13},{9,4},{10,... | collective-permute-start | bytes 405512 | tf_op jit(solution)/shard_map/ppermute | solution.py:73
  45.6 5.0 %collective-permute-start.23 = (bf16[512,128]{1,0:T(8,128)(2,1)S(1)}, bf16[512,128]{1,0:T(8,128)(2,1)S(1)}, u32[]{:S(2)}, u32[]{:S(2)}) collective-permute-start(bf16[512,128]{1,0:T(8,128)(2,1)S(1)} %collective-permute-done.21.q), channel_id=1, source_target_pairs={{0,5},{1,2},{2,7},{3,0},{4,1},{5,8},{6,3},{7,10},{8,13},{9,4},{10,... | collective-permute-start | bytes 393224 | tf_op jit(solution)/shard_map/ppermute | solution.py:73
  48.9 4.8 %collective-permute-start.22 = (bf16[528,128]{1,0:T(8,128)(2,1)S(1)}, bf16[528,128]{1,0:T(8,128)(2,1)S(1)}, u32[]{:S(2)}, u32[]{:S(2)}) collective-permute-start(bf16[528,128]{1,0:T(8,128)(2,1)S(1)} %merge.7), channel_id=1, source_target_pairs={{0,5},{1,2},{2,7},{3,0},{4,1},{5,8},{6,3},{7,10},{8,13},{9,4},{10,... | collective-permute-start | bytes 405512 | tf_op jit(solution)/shard_map/ppermute | solution.py:73
  50.6 4.9 %collective-permute-start.25 = (bf16[512,128]{1,0:T(8,128)(2,1)S(1)}, bf16[512,128]{1,0:T(8,128)(2,1)S(1)}, u32[]{:S(2)}, u32[]{:S(2)}) collective-permute-start(bf16[512,128]{1,0:T(8,128)(2,1)S(1)} %collective-permute-done.23.q), channel_id=1, source_target_pairs={{0,5},{1,2},{2,7},{3,0},{4,1},{5,8},{6,3},{7,10},{8,13},{9,4},{10,... | collective-permute-start | bytes 393224 | tf_op jit(solution)/shard_map/ppermute | solution.py:73
  53.9 4.8 %collective-permute-start.24 = (bf16[528,128]{1,0:T(8,128)(2,1)S(1)}, bf16[528,128]{1,0:T(8,128)(2,1)S(1)}, u32[]{:S(2)}, u32[]{:S(2)}) collective-permute-start(bf16[528,128]{1,0:T(8,128)(2,1)S(1)} %merge.8), channel_id=1, source_target_pairs={{0,5},{1,2},{2,7},{3,0},{4,1},{5,8},{6,3},{7,10},{8,13},{9,4},{10,... | collective-permute-start | bytes 405512 | tf_op jit(solution)/shard_map/ppermute | solution.py:73
  55.5 5.0 %collective-permute-start.27 = (bf16[512,128]{1,0:T(8,128)(2,1)S(1)}, bf16[512,128]{1,0:T(8,128)(2,1)S(1)}, u32[]{:S(2)}, u32[]{:S(2)}) collective-permute-start(bf16[512,128]{1,0:T(8,128)(2,1)S(1)} %collective-permute-done.25.q), channel_id=1, source_target_pairs={{0,5},{1,2},{2,7},{3,0},{4,1},{5,8},{6,3},{7,10},{8,13},{9,4},{10,... | collective-permute-start | bytes 393224 | tf_op jit(solution)/shard_map/ppermute | solution.py:73
  59.0 4.6 %collective-permute-start.26 = (bf16[528,128]{1,0:T(8,128)(2,1)S(1)}, bf16[528,128]{1,0:T(8,128)(2,1)S(1)}, u32[]{:S(2)}, u32[]{:S(2)}) collective-permute-start(bf16[528,128]{1,0:T(8,128)(2,1)S(1)} %merge.9), channel_id=1, source_target_pairs={{0,5},{1,2},{2,7},{3,0},{4,1},{5,8},{6,3},{7,10},{8,13},{9,4},{10,... | collective-permute-start | bytes 405512 | tf_op jit(solution)/shard_map/ppermute | solution.py:73
  60.5 5.0 %collective-permute-start.29 = (bf16[512,128]{1,0:T(8,128)(2,1)S(1)}, bf16[512,128]{1,0:T(8,128)(2,1)S(1)}, u32[]{:S(2)}, u32[]{:S(2)}) collective-permute-start(bf16[512,128]{1,0:T(8,128)(2,1)S(1)} %collective-permute-done.27.q), channel_id=1, source_target_pairs={{0,5},{1,2},{2,7},{3,0},{4,1},{5,8},{6,3},{7,10},{8,13},{9,4},{10,... | collective-permute-start | bytes 393224 | tf_op jit(solution)/shard_map/ppermute | solution.py:73
  63.8 4.5 %collective-permute-start.28 = (bf16[528,128]{1,0:T(8,128)(2,1)S(1)}, bf16[528,128]{1,0:T(8,128)(2,1)S(1)}, u32[]{:S(2)}, u32[]{:S(2)}) collective-permute-start(bf16[528,128]{1,0:T(8,128)(2,1)S(1)} %merge.10), channel_id=1, source_target_pairs={{0,5},{1,2},{2,7},{3,0},{4,1},{5,8},{6,3},{7,10},{8,13},{9,4},{10,... | collective-permute-start | bytes 405512 | tf_op jit(solution)/shard_map/ppermute | solution.py:73
  68.5 4.7 %collective-permute-start.30 = (bf16[528,128]{1,0:T(8,128)(2,1)S(1)}, bf16[528,128]{1,0:T(8,128)(2,1)S(1)}, u32[]{:S(2)}, u32[]{:S(2)}) collective-permute-start(bf16[528,128]{1,0:T(8,128)(2,1)S(1)} %merge.11), channel_id=1, source_target_pairs={{0,5},{1,2},{2,7},{3,0},{4,1},{5,8},{6,3},{7,10},{8,13},{9,4},{10,... | collective-permute-start | bytes 405512 | tf_op jit(solution)/shard_map/ppermute | solution.py:73
  73.6 1.7 %collective-permute-start.31 = (bf16[128,512]{1,0:T(8,128)(2,1)S(1)}, bf16[128,512]{1,0:T(8,128)(2,1)S(1)}, u32[]{:S(2)}, u32[]{:S(2)}) collective-permute-start(bf16[128,512]{1,0:T(8,128)(2,1)S(1)} %finish.1.refs_7_.refs_2_), channel_id=1, source_target_pairs={{0,1},{1,0},{2,3},{3,2},{4,5},{5,4},{6,7},{7,6},{8,9},{9,8},{10,11... | collective-permute-start | bytes 393224 | tf_op jit(solution)/shard_map/ppermute | solution.py:76
  75.7 4.4 %collective-permute-start.33 = (bf16[128,512]{1,0:T(8,128)(2,1)S(1)}, bf16[128,512]{1,0:T(8,128)(2,1)S(1)}, u32[]{:S(2)}, u32[]{:S(2)}) collective-permute-start(bf16[128,512]{1,0:T(8,128)(2,1)S(1)} %get-tuple-element.181), channel_id=1, source_target_pairs={{0,3},{1,4},{2,1},{3,6},{4,9},{5,0},{6,11},{7,2},{8,5},{9,12},{10,... | collective-permute-start | bytes 393224 | tf_op jit(solution)/shard_map/ppermute | solution.py:73
  76.6 34.1 %slice-start.2 = ((s8[8388608]{0:T(1024)(128)(4,1)}), s8[4194304]{0:T(1024)(128)(4,1)S(1)}, s32[]{:S(2)}) async-start(s8[8388608]{0:T(1024)(128)(4,1)} %bitcast.29), calls=%async_computation.2 | async-start | bytes 8388608
  76.6 34.1 %slice-start.3 = ((s8[8388608]{0:T(1024)(128)(4,1)}), s8[4194304]{0:T(1024)(128)(4,1)S(1)}, s32[]{:S(2)}) async-start(s8[8388608]{0:T(1024)(128)(4,1)} %bitcast.29), calls=%async_computation.3 | async-start | bytes 8388608
  76.6 5.0 %collective-permute-start.37 = (bf16[128,512]{1,0:T(8,128)(2,1)S(1)}, bf16[128,512]{1,0:T(8,128)(2,1)S(1)}, u32[]{:S(2)}, u32[]{:S(2)}) collective-permute-start(bf16[128,512]{1,0:T(8,128)(2,1)S(1)} %get-tuple-element.184), channel_id=1, source_target_pairs={{0,3},{1,4},{2,1},{3,6},{4,9},{5,0},{6,11},{7,2},{8,5},{9,12},{10,... | collective-permute-start | bytes 393224 | tf_op jit(solution)/shard_map/ppermute | solution.py:73
  80.2 4.4 %collective-permute-start.34 = (bf16[128,512]{1,0:T(8,128)(2,1)S(1)}, bf16[128,512]{1,0:T(8,128)(2,1)S(1)}, u32[]{:S(2)}, u32[]{:S(2)}) collective-permute-start(bf16[128,512]{1,0:T(8,128)(2,1)S(1)} %add.161), channel_id=1, source_target_pairs={{0,3},{1,4},{2,1},{3,6},{4,9},{5,0},{6,11},{7,2},{8,5},{9,12},{10,... | collective-permute-start | bytes 393224 | tf_op jit(solution)/shard_map/ppermute | solution.py:73
  81.6 4.5 %collective-permute-start.38 = (bf16[128,512]{1,0:T(8,128)(2,1)S(1)}, bf16[128,512]{1,0:T(8,128)(2,1)S(1)}, u32[]{:S(2)}, u32[]{:S(2)}) collective-permute-start(bf16[128,512]{1,0:T(8,128)(2,1)S(1)} %add.164), channel_id=1, source_target_pairs={{0,3},{1,4},{2,1},{3,6},{4,9},{5,0},{6,11},{7,2},{8,5},{9,12},{10,... | collective-permute-start | bytes 393224 | tf_op jit(solution)/shard_map/ppermute | solution.py:73
  84.7 4.7 %collective-permute-start.35 = (bf16[128,512]{1,0:T(8,128)(2,1)S(1)}, bf16[128,512]{1,0:T(8,128)(2,1)S(1)}, u32[]{:S(2)}, u32[]{:S(2)}) collective-permute-start(bf16[128,512]{1,0:T(8,128)(2,1)S(1)} %add.162), channel_id=1, source_target_pairs={{0,3},{1,4},{2,1},{3,6},{4,9},{5,0},{6,11},{7,2},{8,5},{9,12},{10,... | collective-permute-start | bytes 393224 | tf_op jit(solution)/shard_map/ppermute | solution.py:73
  86.1 4.7 %collective-permute-start.39 = (bf16[128,512]{1,0:T(8,128)(2,1)S(1)}, bf16[128,512]{1,0:T(8,128)(2,1)S(1)}, u32[]{:S(2)}, u32[]{:S(2)}) collective-permute-start(bf16[128,512]{1,0:T(8,128)(2,1)S(1)} %add.165), channel_id=1, source_target_pairs={{0,3},{1,4},{2,1},{3,6},{4,9},{5,0},{6,11},{7,2},{8,5},{9,12},{10,... | collective-permute-start | bytes 393224 | tf_op jit(solution)/shard_map/ppermute | solution.py:73
  89.4 4.7 %collective-permute-start.36 = (bf16[128,512]{1,0:T(8,128)(2,1)S(1)}, bf16[128,512]{1,0:T(8,128)(2,1)S(1)}, u32[]{:S(2)}, u32[]{:S(2)}) collective-permute-start(bf16[128,512]{1,0:T(8,128)(2,1)S(1)} %add.163), channel_id=1, source_target_pairs={{0,3},{1,4},{2,1},{3,6},{4,9},{5,0},{6,11},{7,2},{8,5},{9,12},{10,... | collective-permute-start | bytes 393224 | tf_op jit(solution)/shard_map/ppermute | solution.py:73
  90.9 4.0 %collective-permute-start.40 = (bf16[128,512]{1,0:T(8,128)(2,1)S(1)}, bf16[128,512]{1,0:T(8,128)(2,1)S(1)}, u32[]{:S(2)}, u32[]{:S(2)}) collective-permute-start(bf16[128,512]{1,0:T(8,128)(2,1)S(1)} %collective-permute-done.39.refs_1_), channel_id=1, source_target_pairs={{0,1},{1,0},{2,3},{3,2},{4,5},{5,4},{6,7},{7,6},{8,9},{9,8},{10,11... | collective-permute-start | bytes 393224 | tf_op jit(solution)/shard_map/ppermute | solution.py:76
  94.1 1.9 %collective-permute-start.45 = (bf16[128,512]{1,0:T(8,128)(2,1)S(1)}, bf16[128,512]{1,0:T(8,128)(2,1)S(1)}, u32[]{:S(2)}, u32[]{:S(2)}) collective-permute-start(bf16[128,512]{1,0:T(8,128)(2,1)S(1)} %collective-permute-done.36.refs_1_), channel_id=1, source_target_pairs={{0,1},{1,0},{2,3},{3,2},{4,5},{5,4},{6,7},{7,6},{8,9},{9,8},{10,11... | collective-permute-start | bytes 393224 | tf_op jit(solution)/shard_map/ppermute | solution.py:76
  94.9 4.4 %collective-permute-start.41 = (bf16[128,512]{1,0:T(8,128)(2,1)S(1)}, bf16[128,512]{1,0:T(8,128)(2,1)S(1)}, u32[]{:S(2)}, u32[]{:S(2)}) collective-permute-start(bf16[128,512]{1,0:T(8,128)(2,1)S(1)} %add.166.refs_12_), channel_id=1, source_target_pairs={{0,5},{1,2},{2,7},{3,0},{4,1},{5,8},{6,3},{7,10},{8,13},{9,4},{10,... | collective-permute-start | bytes 393224 | tf_op jit(solution)/shard_map/ppermute | solution.py:73
  96.1 4.7 %collective-permute-start.47 = (bf16[128,512]{1,0:T(8,128)(2,1)S(1)}, bf16[128,512]{1,0:T(8,128)(2,1)S(1)}, u32[]{:S(2)}, u32[]{:S(2)}) collective-permute-start(bf16[128,512]{1,0:T(8,128)(2,1)S(1)} %add.167.refs_13_), channel_id=1, source_target_pairs={{0,5},{1,2},{2,7},{3,0},{4,1},{5,8},{6,3},{7,10},{8,13},{9,4},{10,... | collective-permute-start | bytes 393224 | tf_op jit(solution)/shard_map/ppermute | solution.py:73
  99.4 4.4 %collective-permute-start.42 = (bf16[128,512]{1,0:T(8,128)(2,1)S(1)}, bf16[128,512]{1,0:T(8,128)(2,1)S(1)}, u32[]{:S(2)}, u32[]{:S(2)}) collective-permute-start(bf16[128,512]{1,0:T(8,128)(2,1)S(1)} %collective-permute-done.41.refs_14_), channel_id=1, source_target_pairs={{0,5},{1,2},{2,7},{3,0},{4,1},{5,8},{6,3},{7,10},{8,13},{9,4},{10,... | collective-permute-start | bytes 393224 | tf_op jit(solution)/shard_map/ppermute | solution.py:73
  100.8 5.1 %collective-permute-start.50 = (bf16[128,512]{1,0:T(8,128)(2,1)S(1)}, bf16[128,512]{1,0:T(8,128)(2,1)S(1)}, u32[]{:S(2)}, u32[]{:S(2)}) collective-permute-start(bf16[128,512]{1,0:T(8,128)(2,1)S(1)} %collective-permute-done.47.refs_16_), channel_id=1, source_target_pairs={{0,5},{1,2},{2,7},{3,0},{4,1},{5,8},{6,3},{7,10},{8,13},{9,4},{10,... | collective-permute-start | bytes 393224 | tf_op jit(solution)/shard_map/ppermute | solution.py:73
  103.8 4.4 %collective-permute-start.43 = (bf16[128,512]{1,0:T(8,128)(2,1)S(1)}, bf16[128,512]{1,0:T(8,128)(2,1)S(1)}, u32[]{:S(2)}, u32[]{:S(2)}) collective-permute-start(bf16[128,512]{1,0:T(8,128)(2,1)S(1)} %collective-permute-done.42.refs_18_), channel_id=1, source_target_pairs={{0,5},{1,2},{2,7},{3,0},{4,1},{5,8},{6,3},{7,10},{8,13},{9,4},{10,... | collective-permute-start | bytes 393224 | tf_op jit(solution)/shard_map/ppermute | solution.py:73
  105.4 3.4 %collective-permute-start.46 = (bf16[128,512]{1,0:T(8,128)(2,1)S(1)}, bf16[128,512]{1,0:T(8,128)(2,1)S(1)}, u32[]{:S(2)}, u32[]{:S(2)}) collective-permute-start(bf16[128,512]{1,0:T(8,128)(2,1)S(1)} %collective-permute-done.41.refs_14_), channel_id=1, source_target_pairs={{0,1},{1,0},{2,3},{3,2},{4,5},{5,4},{6,7},{7,6},{8,9},{9,8},{10,11... | collective-permute-start | bytes 393224 | tf_op jit(solution)/shard_map/ppermute | solution.py:76
  105.4 4.4 %collective-permute-start.48 = (bf16[128,512]{1,0:T(8,128)(2,1)S(1)}, bf16[128,512]{1,0:T(8,128)(2,1)S(1)}, u32[]{:S(2)}, u32[]{:S(2)}) collective-permute-start(bf16[128,512]{1,0:T(8,128)(2,1)S(1)} %collective-permute-done.47.refs_16_), channel_id=1, source_target_pairs={{0,1},{1,0},{2,3},{3,2},{4,5},{5,4},{6,7},{7,6},{8,9},{9,8},{10,11... | collective-permute-start | bytes 393224 | tf_op jit(solution)/shard_map/ppermute | solution.py:76
  105.9 4.7 %collective-permute-start.49 = (bf16[128,512]{1,0:T(8,128)(2,1)S(1)}, bf16[128,512]{1,0:T(8,128)(2,1)S(1)}, u32[]{:S(2)}, u32[]{:S(2)}) collective-permute-start(bf16[128,512]{1,0:T(8,128)(2,1)S(1)} %collective-permute-done.42.refs_18_), channel_id=1, source_target_pairs={{0,1},{1,0},{2,3},{3,2},{4,5},{5,4},{6,7},{7,6},{8,9},{9,8},{10,11... | collective-permute-start | bytes 393224 | tf_op jit(solution)/shard_map/ppermute | solution.py:76
  105.9 4.7 %collective-permute-start.51 = (bf16[128,512]{1,0:T(8,128)(2,1)S(1)}, bf16[128,512]{1,0:T(8,128)(2,1)S(1)}, u32[]{:S(2)}, u32[]{:S(2)}) collective-permute-start(bf16[128,512]{1,0:T(8,128)(2,1)S(1)} %collective-permute-done.50.refs_20_), channel_id=1, source_target_pairs={{0,1},{1,0},{2,3},{3,2},{4,5},{5,4},{6,7},{7,6},{8,9},{9,8},{10,11... | collective-permute-start | bytes 393224 | tf_op jit(solution)/shard_map/ppermute | solution.py:76
  108.1 2.5 %collective-permute-start.52 = (bf16[128,512]{1,0:T(8,128)(2,1)S(1)}, bf16[128,512]{1,0:T(8,128)(2,1)S(1)}, u32[]{:S(2)}, u32[]{:S(2)}) collective-permute-start(bf16[128,512]{1,0:T(8,128)(2,1)S(1)} %collective-permute-done.43.refs_22_), channel_id=1, source_target_pairs={{0,1},{1,0},{2,3},{3,2},{4,5},{5,4},{6,7},{7,6},{8,9},{9,8},{10,11... | collective-permute-start | bytes 393224 | tf_op jit(solution)/shard_map/ppermute | solution.py:76
  108.7 4.4 %collective-permute-start.44 = (bf16[128,512]{1,0:T(8,128)(2,1)S(1)}, bf16[128,512]{1,0:T(8,128)(2,1)S(1)}, u32[]{:S(2)}, u32[]{:S(2)}) collective-permute-start(bf16[128,512]{1,0:T(8,128)(2,1)S(1)} %collective-permute-done.43.refs_22_), channel_id=1, source_target_pairs={{0,5},{1,2},{2,7},{3,0},{4,1},{5,8},{6,3},{7,10},{8,13},{9,4},{10,... | collective-permute-start | bytes 393224 | tf_op jit(solution)/shard_map/ppermute | solution.py:73
  109.8 4.8 %collective-permute-start.54 = (bf16[128,512]{1,0:T(8,128)(2,1)S(1)}, bf16[128,512]{1,0:T(8,128)(2,1)S(1)}, u32[]{:S(2)}, u32[]{:S(2)}) collective-permute-start(bf16[128,512]{1,0:T(8,128)(2,1)S(1)} %collective-permute-done.50.refs_20_), channel_id=1, source_target_pairs={{0,5},{1,2},{2,7},{3,0},{4,1},{5,8},{6,3},{7,10},{8,13},{9,4},{10,... | collective-permute-start | bytes 393224 | tf_op jit(solution)/shard_map/ppermute | solution.py:73
  113.1 2.2 %collective-permute-start.53 = (bf16[128,512]{1,0:T(8,128)(2,1)S(1)}, bf16[128,512]{1,0:T(8,128)(2,1)S(1)}, u32[]{:S(2)}, u32[]{:S(2)}) collective-permute-start(bf16[128,512]{1,0:T(8,128)(2,1)S(1)} %collective-permute-done.44.refs_4_), channel_id=1, source_target_pairs={{0,1},{1,0},{2,3},{3,2},{4,5},{5,4},{6,7},{7,6},{8,9},{9,8},{10,11... | collective-permute-start | bytes 393224 | tf_op jit(solution)/shard_map/ppermute | solution.py:76
  114.5 1.3 %collective-permute-start.55 = (bf16[128,512]{1,0:T(8,128)(2,1)S(1)}, bf16[128,512]{1,0:T(8,128)(2,1)S(1)}, u32[]{:S(2)}, u32[]{:S(2)}) collective-permute-start(bf16[128,512]{1,0:T(8,128)(2,1)S(1)} %collective-permute-done.54.refs_6_), channel_id=1, source_target_pairs={{0,1},{1,0},{2,3},{3,2},{4,5},{5,4},{6,7},{7,6},{8,9},{9,8},{10,11... | collective-permute-start | bytes 393224 | tf_op jit(solution)/shard_map/ppermute | solution.py:76
